TPU v7x, 32 devices: a whole 2x2x4 slice. The times are simulated.
32 devices in a mesh: dp: 4 (over y, core), tensor: 8 (over z, x).
Axes of the slice: x: 2, y: 2, z: 4, core: 2. Of those that a mesh axis runs over, the one named last changes fastest.
Arguments:
- hidden_in: bfloat16 [8192, 2048], P(('dp', 'tensor')), may hold values from -6 to 6
- out_grad: bfloat16 [8192, 2048], P(('dp', 'tensor')), may hold values from -6 to 6
- segment_ids: int32 [4, 2048], P('dp'), may hold values from 0 to 2, never falling along the last dimension, each value on 1 to 1024 neighbouring positions
- step_count: int32 [1], replicated, may hold values from 2 to 20
- query_weight: float32 [2048, 2048], P('dp', 'tensor'), may hold values from -0.125 to 0.125
- keyvalue_weight: float32 [2048, 512], P(('dp', 'tensor')), may hold values from -0.125 to 0.125
- output_weight: float32 [2048, 2048], P('tensor', 'dp'), may hold values from -0.5 to 0.5
- gateup_weight: float32 [2, 2048, 5632], P(None, 'dp', 'tensor'), may hold values from -0.125 to 0.125
- down_weight: float32 [5632, 2048], P('tensor', 'dp'), may hold values from -0.078125 to 0.078125
- norm_gains: float32 [2, 2048], P(None, ('dp', 'tensor')), may hold values from 0.5 to 1.5
- query_first: float32 [2048, 2048], P('dp', 'tensor'), may hold values from -16 to 16
- keyvalue_first: float32 [2048, 512], P(('dp', 'tensor')), may hold values from -64 to 64
- output_first: float32 [2048, 2048], P('tensor', 'dp'), may hold values from -6 to 6
- gateup_first: float32 [2, 2048, 5632], P(None, 'dp', 'tensor'), may hold values from -12 to 12
- down_first: float32 [5632, 2048], P('tensor', 'dp'), may hold values from -16 to 16
- gains_first: float32 [2, 2048], P(None, ('dp', 'tensor')), may hold values from -32 to 32
- query_second: float32 [2048, 2048], P('dp', 'tensor'), may hold values from 36.864 to 294.912
- keyvalue_second: float32 [2048, 512], P(('dp', 'tensor')), may hold values from 409.6 to 3276.8
- output_second: float32 [2048, 2048], P('tensor', 'dp'), may hold values from 4.096 to 32.768
- gateup_second: float32 [2, 2048, 5632], P(None, 'dp', 'tensor'), may hold values from 16.384 to 131.072
- down_second: float32 [5632, 2048], P('tensor', 'dp'), may hold values from 36.864 to 294.912
- gains_second: float32 [2, 2048], P(None, ('dp', 'tensor')), may hold values from 102.4 to 819.2
Outputs:
- hidden_out: bfloat16 [8192, 2048], P(('dp', 'tensor'))
- input_grad: float32 [8192, 2048], P(('dp', 'tensor'))
- updated_query: float32 [2048, 2048], P('dp', 'tensor')
- updated_keyvalue: float32 [2048, 512], P(('dp', 'tensor'))
- updated_output: float32 [2048, 2048], P('tensor', 'dp')
- updated_gateup: float32 [2, 2048, 5632], P(None, 'dp', 'tensor')
- updated_down: float32 [5632, 2048], P('tensor', 'dp')
- updated_gains: float32 [2, 2048], P(None, ('dp', 'tensor'))
- updated_query_first: float32 [2048, 2048], P('dp', 'tensor')
- updated_keyvalue_first: float32 [2048, 512], P(('dp', 'tensor'))
- updated_output_first: float32 [2048, 2048], P('tensor', 'dp')
- updated_gateup_first: float32 [2, 2048, 5632], P(None, 'dp', 'tensor')
- updated_down_first: float32 [5632, 2048], P('tensor', 'dp')
- updated_gains_first: float32 [2, 2048], P(None, ('dp', 'tensor'))
- updated_query_second: float32 [2048, 2048], P('dp', 'tensor')
- updated_keyvalue_second: float32 [2048, 512], P(('dp', 'tensor'))
- updated_output_second: float32 [2048, 2048], P('tensor', 'dp')
- updated_gateup_second: float32 [2, 2048, 5632], P(None, 'dp', 'tensor')
- updated_down_second: float32 [5632, 2048], P('tensor', 'dp')
- updated_gains_second: float32 [2, 2048], P(None, ('dp', 'tensor'))
Inputs may be any that keep to these rules, and one draw needn't show every extreme that they name: `segment_ids`: along a pack the document numbers never fall; each of the 3 numbers names 1 to 1024 consecutive tokens, and one document of every pack has exactly 1024.
All inputs are finite; a program needn't handle non-finite values.
Results may differ from a plain program's by a relative error of at most 0.025.
Values may be sent and summed in bfloat16 or wider, within the bound.
A program may use at most 192 MiB of HBM per device.

v0:
```python
import jax
import jax.numpy as jnp
from jax import lax
from jax.sharding import PartitionSpec as P

D = 2048
H = 32
KVH = 4
HD = 64
FF = 5632


NORM_EPS = 1e-05
ADAM_EPS = 1e-08
BETA_ONE = 0.9
BETA_TWO = 0.95
DECAY = 0.1
GAIN_RATE = 1.0
NEG_FILL = -1e30
ROPE_BASE = 10000.0


def rope_tables(seg_row):
    length = seg_row.shape[0]
    earlier = jnp.sum((seg_row[None, :] < seg_row[:, None]).astype(jnp.int32), axis=1)
    position = (jnp.arange(length, dtype=jnp.int32) - earlier).astype(jnp.float32)
    half_dim = HD // 2
    frequency = jnp.power(ROPE_BASE, -2.0 * jnp.arange(half_dim, dtype=jnp.float32) / HD)
    angles = position[:, None] * frequency[None, :]
    return (jnp.cos(angles), jnp.sin(angles))


def rotate(values, cos_table, sin_table):
    half_dim = values.shape[-1] // 2
    front_half = values[..., :half_dim]
    back_half = values[..., half_dim:]
    return jnp.concatenate(
        [
            front_half * cos_table - back_half * sin_table,
            back_half * cos_table + front_half * sin_table,
        ],
        axis=-1,
    )


def rotate_back(grads, cos_table, sin_table):
    half_dim = grads.shape[-1] // 2
    front_half = grads[..., :half_dim]
    back_half = grads[..., half_dim:]
    return jnp.concatenate(
        [
            front_half * cos_table + back_half * sin_table,
            back_half * cos_table - front_half * sin_table,
        ],
        axis=-1,
    )


def contract_rows(left, right):
    return lax.dot_general(
        left, right, (((0,), (0,)), ((), ())), preferred_element_type=jnp.float32
    )


def contract_cols(left, right):
    return lax.dot_general(
        left, right, (((1,), (1,)), ((), ())), preferred_element_type=jnp.float32
    )


def norm_back(upstream, inputs, inverse, gain):
    scaled = gain * upstream
    inner = jnp.mean(scaled * inputs, axis=1, keepdims=True)
    return (
        inverse * scaled - inputs * inverse * inverse * inverse * inner,
        jnp.sum(upstream * inputs * inverse, axis=0),
    )


def adam_step(weight, grad, first_old, second_old, rate, decay, step_value):
    first_new = BETA_ONE * first_old + (1.0 - BETA_ONE) * grad
    second_new = BETA_TWO * second_old + (1.0 - BETA_TWO) * grad * grad
    fix_one = 1.0 - jnp.power(jnp.float32(BETA_ONE), step_value)
    fix_two = 1.0 - jnp.power(jnp.float32(BETA_TWO), step_value)
    update = first_new / fix_one / (jnp.sqrt(second_new / fix_two) + ADAM_EPS)
    return (weight - rate * (update + decay * weight), first_new, second_new)


def body(
    hidden_in,
    out_grad,
    segment_ids,
    step_count,
    query_weight,
    keyvalue_weight,
    output_weight,
    gateup_weight,
    down_weight,
    norm_gains,
    query_first,
    keyvalue_first,
    output_first,
    gateup_first,
    down_first,
    gains_first,
    query_second,
    keyvalue_second,
    output_second,
    gateup_second,
    down_second,
    gains_second,
):
    inputs = hidden_in.astype(jnp.float32)
    query_full, output_full, gateup_full, down_full = (
        lax.all_gather(query_weight.astype(jnp.bfloat16), "dp", axis=0, tiled=True),
        lax.all_gather(output_weight.astype(jnp.bfloat16), "dp", axis=1, tiled=True),
        lax.all_gather(gateup_weight.astype(jnp.bfloat16), "dp", axis=1, tiled=True),
        lax.all_gather(down_weight.astype(jnp.bfloat16), "dp", axis=1, tiled=True),
    )
    keyvalue_full, gains_full = (
        lax.all_gather(keyvalue_weight.astype(jnp.bfloat16), ("dp", "tensor"), axis=0, tiled=True),
        lax.all_gather(norm_gains.astype(jnp.bfloat16), ("dp", "tensor"), axis=1, tiled=True),
    )
    gain_attn = gains_full[0].astype(jnp.float32)
    gain_mlp = gains_full[1].astype(jnp.float32)
    heads_here = query_full.shape[1] // HD
    share_size = H // KVH
    key_heads = max(1, heads_here // share_size)
    repeat_count = heads_here // key_heads
    key_first = lax.axis_index("tensor") * heads_here // share_size
    key_cols = key_heads * HD
    key_proj = lax.dynamic_slice_in_dim(keyvalue_full, key_first * HD, key_cols, 1)
    value_proj = lax.dynamic_slice_in_dim(keyvalue_full, (KVH + key_first) * HD, key_cols, 1)
    pair_proj = jnp.concatenate([key_proj, value_proj], axis=1)
    seg_row = segment_ids[0]
    group_rows = seg_row.shape[0]
    cos_table, sin_table = rope_tables(seg_row)
    scale = HD ** (-0.5)
    inverse_one = lax.rsqrt(jnp.mean(inputs * inputs, axis=1, keepdims=True) + NORM_EPS)
    normed_one = (inputs * inverse_one * gain_attn).astype(jnp.bfloat16)
    rows_one = lax.all_gather(normed_one, "tensor", axis=0, tiled=True)
    query_pre = jnp.dot(rows_one, query_full, preferred_element_type=jnp.float32)
    pair_pre = jnp.dot(rows_one, pair_proj, preferred_element_type=jnp.float32)
    query_heads = query_pre.reshape(group_rows, key_heads, repeat_count, HD).transpose(1, 2, 0, 3)
    query_rot = rotate(query_heads, cos_table, sin_table).astype(jnp.bfloat16)
    key_pre = pair_pre[:, :key_cols].reshape(group_rows, key_heads, HD).transpose(1, 0, 2)
    key_rot = rotate(key_pre, cos_table, sin_table).astype(jnp.bfloat16)
    value_heads = (
        pair_pre[:, key_cols:]
        .reshape(group_rows, key_heads, HD)
        .transpose(1, 0, 2)
        .astype(jnp.bfloat16)
    )
    block_rows = min(512, group_rows)
    block_count = group_rows // block_rows
    key_places = jnp.arange(group_rows, dtype=jnp.int32)

    def soft_scores(block_index):
        begin_row = block_index * block_rows
        query_block = lax.dynamic_slice_in_dim(query_rot, begin_row, block_rows, 2)
        query_segs = lax.dynamic_slice_in_dim(seg_row, begin_row, block_rows, 0)
        query_places = begin_row + jnp.arange(block_rows, dtype=jnp.int32)
        allowed = (query_segs[:, None] == seg_row[None, :]) & (
            key_places[None, :] <= query_places[:, None]
        )
        scores = (
            jnp.einsum("krqd,kjd->krqj", query_block, key_rot, preferred_element_type=jnp.float32)
            * scale
        )
        return (query_block, jnp.where(allowed, scores, NEG_FILL))

    def attend_block(block_index):
        query_block, scores = soft_scores(block_index)
        row_max = jnp.max(scores, axis=-1, keepdims=True)
        log_total = row_max + jnp.log(jnp.sum(jnp.exp(scores - row_max), axis=-1, keepdims=True))
        probability = jnp.exp(scores - log_total).astype(jnp.bfloat16)
        attended = jnp.einsum(
            "krqj,kjd->krqd", probability, value_heads, preferred_element_type=jnp.float32
        )
        return (attended.astype(jnp.bfloat16), log_total)

    attended_blocks, log_totals = lax.map(attend_block, jnp.arange(block_count, dtype=jnp.int32))
    attended_flat = attended_blocks.transpose(0, 3, 1, 2, 4).reshape(group_rows, heads_here * HD)
    piece = attended_flat
    attn_out = lax.psum_scatter(
        jnp.dot(piece, output_full, preferred_element_type=jnp.float32).astype(jnp.bfloat16),
        "tensor",
        scatter_dimension=0,
        tiled=True,
    ).astype(jnp.float32)
    residual_mid = inputs + attn_out
    inverse_two = lax.rsqrt(jnp.mean(residual_mid * residual_mid, axis=1, keepdims=True) + NORM_EPS)
    normed_two = (residual_mid * inverse_two * gain_mlp).astype(jnp.bfloat16)
    rows_two = lax.all_gather(normed_two, "tensor", axis=0, tiled=True)
    gate_proj = jnp.dot(rows_two, gateup_full[0], preferred_element_type=jnp.float32)
    up_proj = jnp.dot(rows_two, gateup_full[1], preferred_element_type=jnp.float32)
    sigmoid_gate = jax.nn.sigmoid(gate_proj)
    silu_gate = gate_proj * sigmoid_gate
    hidden_mlp = (silu_gate * up_proj).astype(jnp.bfloat16)
    piece = hidden_mlp
    mlp_out = lax.psum_scatter(
        jnp.dot(piece, down_full, preferred_element_type=jnp.float32).astype(jnp.bfloat16),
        "tensor",
        scatter_dimension=0,
        tiled=True,
    ).astype(jnp.float32)
    hidden_out = (residual_mid + mlp_out).astype(jnp.bfloat16)
    grad_rows = lax.all_gather(out_grad, "tensor", axis=0, tiled=True)
    down_grad = contract_rows(hidden_mlp, grad_rows)
    hidden_grad = contract_cols(grad_rows, down_full)
    gate_grad = (
        hidden_grad * up_proj * sigmoid_gate * (1.0 + gate_proj * (1.0 - sigmoid_gate))
    ).astype(jnp.bfloat16)
    up_grad = (hidden_grad * silu_gate).astype(jnp.bfloat16)
    gateup_grad = jnp.stack([contract_rows(rows_two, gate_grad), contract_rows(rows_two, up_grad)])
    normed_two_grad = lax.psum_scatter(
        (contract_cols(gate_grad, gateup_full[0]) + contract_cols(up_grad, gateup_full[1])).astype(
            jnp.bfloat16
        ),
        "tensor",
        scatter_dimension=0,
        tiled=True,
    ).astype(jnp.float32)
    mid_back, gain_mlp_grad = norm_back(normed_two_grad, residual_mid, inverse_two, gain_mlp)
    mid_grad = out_grad.astype(jnp.float32) + mid_back
    attn_grad_rows = lax.all_gather(mid_grad.astype(jnp.bfloat16), "tensor", axis=0, tiled=True)
    output_grad = contract_rows(attended_flat, attn_grad_rows)
    attended_grad = contract_cols(attn_grad_rows, output_full).astype(jnp.bfloat16)
    attended_heads_grad = attended_grad.reshape(group_rows, key_heads, repeat_count, HD).transpose(
        1, 2, 0, 3
    )

    def back_block(carry, block_index):
        key_acc, value_acc = carry
        query_block, scores = soft_scores(block_index)
        begin_row = block_index * block_rows
        grad_block = lax.dynamic_slice_in_dim(attended_heads_grad, begin_row, block_rows, 2)
        probability = jnp.exp(scores - log_totals[block_index])
        weights_grad = jnp.einsum(
            "krqd,kjd->krqj", grad_block, value_heads, preferred_element_type=jnp.float32
        )
        row_inner = jnp.sum(probability * weights_grad, axis=-1, keepdims=True)
        scores_grad = (probability * (weights_grad - row_inner)).astype(jnp.bfloat16)
        query_grad = (
            jnp.einsum("krqj,kjd->krqd", scores_grad, key_rot, preferred_element_type=jnp.float32)
            * scale
        )
        key_acc = (
            key_acc
            + jnp.einsum(
                "krqj,krqd->kjd", scores_grad, query_block, preferred_element_type=jnp.float32
            )
            * scale
        )
        value_acc = value_acc + jnp.einsum(
            "krqj,krqd->kjd",
            probability.astype(jnp.bfloat16),
            grad_block,
            preferred_element_type=jnp.float32,
        )
        return ((key_acc, value_acc), query_grad)

    zero_heads = jnp.zeros((key_heads, group_rows, HD), jnp.float32)
    (key_acc, value_acc), query_grads = lax.scan(
        back_block, (zero_heads, zero_heads), jnp.arange(block_count, dtype=jnp.int32)
    )
    query_grads = query_grads.transpose(1, 2, 0, 3, 4).reshape(
        key_heads, repeat_count, group_rows, HD
    )
    query_back = (
        rotate_back(query_grads, cos_table, sin_table)
        .transpose(2, 0, 1, 3)
        .reshape(group_rows, heads_here * HD)
        .astype(jnp.bfloat16)
    )
    key_back = (
        rotate_back(key_acc, cos_table, sin_table).transpose(1, 0, 2).reshape(group_rows, key_cols)
    )
    value_back = value_acc.transpose(1, 0, 2).reshape(group_rows, key_cols)
    pair_back = jnp.concatenate([key_back, value_back], axis=1).astype(jnp.bfloat16)
    query_wgrad = contract_rows(rows_one, query_back)
    pair_wgrad = contract_rows(rows_one, pair_back)
    keyvalue_grad = jnp.zeros((keyvalue_full.shape[0], keyvalue_full.shape[1]), jnp.float32)
    keyvalue_grad = lax.dynamic_update_slice_in_dim(
        keyvalue_grad, pair_wgrad[:, :key_cols], key_first * HD, 1
    )
    keyvalue_grad = lax.dynamic_update_slice_in_dim(
        keyvalue_grad, pair_wgrad[:, key_cols:], (KVH + key_first) * HD, 1
    )
    normed_one_grad = lax.psum_scatter(
        (contract_cols(query_back, query_full) + contract_cols(pair_back, pair_proj)).astype(
            jnp.bfloat16
        ),
        "tensor",
        scatter_dimension=0,
        tiled=True,
    ).astype(jnp.float32)
    input_back, gain_attn_grad = norm_back(normed_one_grad, inputs, inverse_one, gain_attn)
    input_grad = mid_grad + input_back
    gains_grad = jnp.stack([gain_attn_grad, gain_mlp_grad])
    query_sum, output_sum, gateup_sum, down_sum = (
        lax.psum_scatter(
            query_wgrad.astype(jnp.bfloat16), "dp", scatter_dimension=0, tiled=True
        ).astype(jnp.float32),
        lax.psum_scatter(
            output_grad.astype(jnp.bfloat16), "dp", scatter_dimension=1, tiled=True
        ).astype(jnp.float32),
        lax.psum_scatter(
            gateup_grad.astype(jnp.bfloat16), "dp", scatter_dimension=1, tiled=True
        ).astype(jnp.float32),
        lax.psum_scatter(
            down_grad.astype(jnp.bfloat16), "dp", scatter_dimension=1, tiled=True
        ).astype(jnp.float32),
    )
    keyvalue_sum, gains_sum = (
        lax.psum_scatter(keyvalue_grad, ("dp", "tensor"), scatter_dimension=0, tiled=True),
        lax.psum_scatter(gains_grad, ("dp", "tensor"), scatter_dimension=1, tiled=True),
    )
    step_value = step_count[0].astype(jnp.float32)
    query_new, query_mone, query_mtwo = adam_step(
        query_weight, query_sum, query_first, query_second, D ** (-0.5), DECAY, step_value
    )
    pair_new, pair_mone, pair_mtwo = adam_step(
        keyvalue_weight,
        keyvalue_sum,
        keyvalue_first,
        keyvalue_second,
        D ** (-0.5),
        DECAY,
        step_value,
    )
    output_new, output_mone, output_mtwo = adam_step(
        output_weight,
        output_sum,
        output_first,
        output_second,
        (H * HD // 16) ** (-0.5),
        DECAY,
        step_value,
    )
    gateup_new, gateup_mone, gateup_mtwo = adam_step(
        gateup_weight, gateup_sum, gateup_first, gateup_second, D ** (-0.5), DECAY, step_value
    )
    down_new, down_mone, down_mtwo = adam_step(
        down_weight, down_sum, down_first, down_second, FF ** (-0.5), DECAY, step_value
    )
    gains_new, gains_mone, gains_mtwo = adam_step(
        norm_gains, gains_sum, gains_first, gains_second, GAIN_RATE, 0.0, step_value
    )
    return (
        hidden_out,
        input_grad,
        query_new,
        pair_new,
        output_new,
        gateup_new,
        down_new,
        gains_new,
        query_mone,
        pair_mone,
        output_mone,
        gateup_mone,
        down_mone,
        gains_mone,
        query_mtwo,
        pair_mtwo,
        output_mtwo,
        gateup_mtwo,
        down_mtwo,
        gains_mtwo,
    )


def solution(mesh):
    return jax.shard_map(
        body,
        mesh=mesh,
        in_specs=(
            P(("dp", "tensor"), None),
            P(("dp", "tensor"), None),
            P("dp", None),
            P(),
            P("dp", "tensor"),
            P(("dp", "tensor"), None),
            P("tensor", "dp"),
            P(None, "dp", "tensor"),
            P("tensor", "dp"),
            P(None, ("dp", "tensor")),
            P("dp", "tensor"),
            P(("dp", "tensor"), None),
            P("tensor", "dp"),
            P(None, "dp", "tensor"),
            P("tensor", "dp"),
            P(None, ("dp", "tensor")),
            P("dp", "tensor"),
            P(("dp", "tensor"), None),
            P("tensor", "dp"),
            P(None, "dp", "tensor"),
            P("tensor", "dp"),
            P(None, ("dp", "tensor")),
        ),
        out_specs=(
            P(("dp", "tensor"), None),
            P(("dp", "tensor"), None),
            P("dp", "tensor"),
            P(("dp", "tensor"), None),
            P("tensor", "dp"),
            P(None, "dp", "tensor"),
            P("tensor", "dp"),
            P(None, ("dp", "tensor")),
            P("dp", "tensor"),
            P(("dp", "tensor"), None),
            P("tensor", "dp"),
            P(None, "dp", "tensor"),
            P("tensor", "dp"),
            P(None, ("dp", "tensor")),
            P("dp", "tensor"),
            P(("dp", "tensor"), None),
            P("tensor", "dp"),
            P(None, "dp", "tensor"),
            P("tensor", "dp"),
            P(None, ("dp", "tensor")),
        ),
        check_vma=False,
    )
```

profile of v0, /device:TPU:0, one launch (start us, length us, event | category | flops | bytes accessed | tf_op | source)
XLA Modules:
  0.0 1912.9 jit_solution(14565001015085654138)
XLA Ops:
  9.6 69.3 %all-gather = bf16[32,64,2]{1,2,0:T(2,128)(2,1)S(1)} all-gather(bf16[1,64,2]{1,2,0:T(2,128)(2,1)S(1)} %convert_bitcast_fusion.1), channel_id=1, replica_groups=mesh['dp'=4,'tensor'=8] {'dp','tensor'}, dimensions={0}, use_global_device_ids=true | all-gather | bytes 8448 | tf_op jit(solution)/shard_map/all_gather | solution.py:122
  89.6 114.9 %all-gather.11.cloned.1.call-done = bf16[2048,2048]{1,0:T(8,128)(2,1)} async-done(((bf16[256,2048]{1,0:T(8,128)(2,1)}), bf16[2048,2048]{1,0:T(8,128)(2,1)}) %all-gather.11.cloned.1.call-update) | async-done | bytes 8388624 | tf_op jit(solution)/shard_map/all_gather | solution.py:141
  204.5 6.3 fusion.106
  212.7 8.9 all-gather.13.cloned.1.call-done
  221.6 6.0 fusion.123
  228.0 60.7 %while.28 = (s32[]{:T(128)}, bf16[4,1,4,512,64]{3,4,2,1,0:T(8,128)(2,1)S(1)}, f32[4,1,4,512,1]{3,2,4,1,0:T(4,128)}, s32[4]{0:T(128)S(1)}, s32[2048]{0:T(1024)S(1...) while((s32[]{:T(128)}, ...), condition=%wide.region_5.6_spmd.clone, body=%wide.region_2.5_spmd.clone.sunk | while | flops 1123154432 | bytes 55658704 | solution.py:182
  290.0 7.3 convolution_convert_fusion.1
  300.6 145.8 %reduce-scatter.13.cloned.1.call-done = bf16[256,2048]{1,0:T(8,128)(2,1)} async-done(((bf16[2048,2048]{1,0:T(8,128)(2,1)}), bf16[256,2048]{1,0:T(8,128)(2,1)}) %reduce-scatter.13.cloned.1.call-update) | async-done | bytes 1048592 | tf_op jit(solution)/shard_map/reduce_scatter | solution.py:185
  452.5 38.4 %all-gather.21.cloned.1.call-done = bf16[2,2048,704]{1,2,0:T(8,128)(2,1)} async-done(((bf16[2,512,704]{1,2,0:T(8,128)(2,1)}), bf16[2,2048,704]{1,2,0:T(8,128)(2,1)}) %all-gather.21.cloned.1.call-update) | async-done | bytes 5767184 | tf_op jit(solution)/shard_map/all_gather | solution.py:117
  491.0 127.9 %all-gather.19.cloned.1.call-done = bf16[2048,2048]{1,0:T(8,128)(2,1)} async-done(((bf16[256,2048]{1,0:T(8,128)(2,1)}), bf16[2048,2048]{1,0:T(8,128)(2,1)}) %all-gather.19.cloned.1.call-update) | async-done | bytes 8388624 | tf_op jit(solution)/shard_map/all_gather | solution.py:194
  618.8 12.2 fusion.61
  631.1 8.0 fusion.60
  639.0 7.3 all-gather.23.cloned.1.call-done
  646.3 127.3 %all-gather.25.cloned.1.call-done = bf16[2048,2048]{1,0:T(8,128)(2,1)} async-done(((bf16[256,2048]{1,0:T(8,128)(2,1)}), bf16[2048,2048]{1,0:T(8,128)(2,1)}) %all-gather.25.cloned.1.call-update) | async-done | bytes 8388624 | tf_op jit(solution)/shard_map/all_gather | solution.py:208
  773.6 15.1 multiply_convert_fusion.1
  788.7 14.2 fusion.59
  802.9 13.1 add_convert_fusion.1
  816.2 147.3 %reduce-scatter.17.cloned.1.call-done = bf16[256,2048]{1,0:T(8,128)(2,1)} async-done(((bf16[2048,2048]{1,0:T(8,128)(2,1)}), bf16[256,2048]{1,0:T(8,128)(2,1)}) %reduce-scatter.17.cloned.1.call-update) | async-done | bytes 1048592 | tf_op jit(solution)/shard_map/reduce_scatter | solution.py:216
  968.8 10.6 convolution_convert_fusion.4
  981.2 9.1 fusion.56
  990.4 8.6 fusion.55
  1002.0 90.8 %all-gather.27.cloned.1.call-done = bf16[2048,2048]{1,0:T(8,128)(2,1)} async-done(((bf16[256,2048]{1,0:T(8,128)(2,1)}), bf16[2048,2048]{1,0:T(8,128)(2,1)}) %all-gather.27.cloned.1.call-update) | async-done | bytes 8388624 | tf_op jit(solution)/shard_map/all_gather | solution.py:226
  1092.9 6.7 convolution_convert_fusion.7
  1099.6 162.0 %while.29 = (s32[]{:T(128)}, f32[1,2048,64]{1,2,0:T(8,128)}, f32[1,2048,64]{1,2,0:T(8,128)}, f32[4,1,4,512,64]{3,4,2,1,0:T(8,128)}, s32[4]{0:T(128)S(1)}, /*inde...) while((s32[]{:T(128)}, f32[1,2048,64]{1,2,0:T(8,128)}, ...), condition=%wide.region_13.14_spmd.clone, body=%wide.region_11.13_spmd.clone.sunk | while | flops 2751199744 | bytes 139864496 | solution.py:264
  1108.4 6.5 fusion.187
  1114.9 10.6 multiply_reduce_fusion.3
  1125.4 8.4 multiply_convert_fusion.6
  1148.7 6.7 fusion.187
  1155.4 10.6 multiply_reduce_fusion.3
  1165.9 8.5 multiply_convert_fusion.6
  1189.2 6.7 fusion.187
  1195.9 10.6 multiply_reduce_fusion.3
  1206.4 8.4 multiply_convert_fusion.6
  1229.6 6.7 fusion.187
  1236.2 10.6 multiply_reduce_fusion.3
  1246.8 8.4 multiply_convert_fusion.6
  1269.4 6.7 convolution_convert_fusion.5
  1289.4 6.3 dynamic_update_slice.18
  1295.7 5.9 dynamic_update_slice.19
  1302.0 9.5 fusion.124
  1311.6 11.6 add_convert_fusion
  1325.0 10.9 convolution_convert_fusion
  1342.4 6.2 multiply_subtract_fusion
  1353.9 113.0 %reduce-scatter.23.cloned.1.call-done = f32[64,512]{1,0:T(8,128)} async-done(((f32[2048,512]{1,0:T(8,128)}), f32[64,512]{1,0:T(8,128)}) %reduce-scatter.23.cloned.1.call-update) | async-done | bytes 131088 | tf_op jit(solution)/shard_map/reduce_scatter | solution.py:316
  1468.8 147.7 %reduce-scatter.19.cloned.1.call-done = bf16[256,2048]{1,0:T(8,128)(2,1)} async-done(((bf16[2048,2048]{1,0:T(8,128)(2,1)}), bf16[256,2048]{1,0:T(8,128)(2,1)}) %reduce-scatter.19.cloned.1.call-update) | async-done | bytes 1048592 | tf_op jit(solution)/shard_map/reduce_scatter | solution.py:290
  1619.8 148.6 %reduce-scatter.15.cloned.1.call-done = bf16[256,2048]{1,0:T(8,128)(2,1)} async-done(((bf16[2048,2048]{1,0:T(8,128)(2,1)}), bf16[256,2048]{1,0:T(8,128)(2,1)}) %reduce-scatter.15.cloned.1.call-update) | async-done | bytes 1048592 | tf_op jit(solution)/shard_map/reduce_scatter | solution.py:201
  1768.5 5.4 fusion.71
  1773.9 130.8 %reduce-scatter.31.cloned.1.call-done = f32[64,2]{1,0:T(8,128)} async-done(((f32[2048,2]{1,0:T(8,128)}), f32[64,2]{1,0:T(8,128)}) %reduce-scatter.31.cloned.1.call-update) | async-done | bytes 528
  (325 shorter events, 182.7 us)
Async XLA Ops:
  7.2 76.0 %copy-start.27 = (f32[512,256]{1,0:T(8,128)S(1)}, f32[512,256]{1,0:T(8,128)}, u32[]{:S(2)}) copy-start(f32[512,256]{1,0:T(8,128)} %param.30) | copy-start | bytes 1572868
  7.2 76.8 %copy-start.29 = (f32[256,512]{1,0:T(8,128)S(1)}, f32[256,512]{1,0:T(8,128)}, u32[]{:S(2)}) copy-start(f32[256,512]{1,0:T(8,128)} %param.32) | copy-start | bytes 1572868
  7.2 80.6 %all-gather.15.cloned.1.call-start = ((), (), s32[]{:S(2)}) async-start(), calls=%async_computation.12 | async-start | bytes 2162688 | tf_op jit(solution)/shard_map/all_gather | solution.py:121
  8.9 195.6 %all-gather.11.cloned.1.call-start = ((), (), s32[]{:S(2)}) async-start(), calls=%async_computation.10 | async-start | bytes 9437184 | tf_op jit(solution)/shard_map/all_gather | solution.py:141
  80.6 885.5 %copy-start.38 = (f32[1,2048]{1,0:T(1,128)}, f32[1,2048]{1,0:T(1,128)S(1)}, u32[]{:S(2)}) copy-start(f32[1,2048]{1,0:T(1,128)S(1)} %get-tuple-element.297) | copy-start | bytes 24580
  83.1 138.5 %all-gather.13.cloned.1.call-start = ((), (), s32[]{:S(2)}) async-start(), calls=%async_computation.11 | async-start | bytes 1310720 | tf_op jit(solution)/shard_map/all_gather | solution.py:115
  83.9 206.0 %all-gather.17.cloned.1.call-start = ((), (), s32[]{:S(2)}) async-start(), calls=%async_computation.13 | async-start | bytes 1310720 | tf_op jit(solution)/shard_map/all_gather | solution.py:116
  84.8 361.7 %reduce-scatter.13.cloned.1.call-start = ((), (), s32[]{:S(2)}) async-start(), calls=%async_computation.14 | async-start | bytes 9437184 | tf_op jit(solution)/shard_map/reduce_scatter | solution.py:185
  84.9 126.1 %copy-start.51 = (f32[32]{0:T(128)}, f32[32]{0:T(128)S(1)}, u32[]{:S(2)}) copy-start(f32[32]{0:T(128)S(1)} %multiply_power_fusion) | copy-start | bytes 388
  86.7 124.3 %copy-start.40 = (f32[2048]{0:T(1024)}, f32[2048]{0:T(1024)S(1)}, u32[]{:S(2)}) copy-start(f32[2048]{0:T(1024)S(1)} %subtract_convert_fusion.2) | copy-start | bytes 24580
  87.7 139.9 %copy-start.23 = (f32[2048,32]{0,1:T(8,128)}, f32[2048,32]{0,1:T(8,128)S(1)}, u32[]{:S(2)}) copy-start(f32[2048,32]{0,1:T(8,128)S(1)} %get-tuple-element.295) | copy-start | bytes 786436
  87.7 139.9 %copy-start.25 = (f32[2048,32]{0,1:T(8,128)}, f32[2048,32]{0,1:T(8,128)S(1)}, u32[]{:S(2)}) copy-start(f32[2048,32]{0,1:T(8,128)S(1)} %get-tuple-element.296) | copy-start | bytes 786436
  89.6 121.3 %copy-start.19 = (bf16[2048,64]{1,0:T(8,128)(2,1)}, bf16[2048,64]{1,0:T(8,128)(2,1)S(1)}, u32[]{:S(2)}) copy-start(bf16[2048,64]{1,0:T(8,128)(2,1)S(1)} %get-tuple-element.287) | copy-start | bytes 786436
  89.6 121.3 %copy-start.21 = (bf16[2048,64]{1,0:T(8,128)(2,1)}, bf16[2048,64]{1,0:T(8,128)(2,1)S(1)}, u32[]{:S(2)}) copy-start(bf16[2048,64]{1,0:T(8,128)(2,1)S(1)} %get-tuple-element.288) | copy-start | bytes 786436
  297.3 149.1 %copy-start.1 = (bf16[256,2048]{1,0:T(8,128)(2,1)S(1)}, bf16[256,2048]{1,0:T(8,128)(2,1)}, u32[]{:S(2)}) copy-start(bf16[256,2048]{1,0:T(8,128)(2,1)} %param.26) | copy-start | bytes 3145732
  297.3 193.6 %all-gather.21.cloned.1.call-start = ((), (), s32[]{:S(2)}) async-start(), calls=%async_computation.16 | async-start | bytes 7208960 | tf_op jit(solution)/shard_map/all_gather | solution.py:117
  300.6 150.2 %copy-start.16 = (f32[704,512]{1,0:T(8,128)S(1)}, f32[704,512]{1,0:T(8,128)}, u32[]{:S(2)}) copy-start(f32[704,512]{1,0:T(8,128)} %param.34) | copy-start | bytes 4325380
  300.6 318.3 %all-gather.19.cloned.1.call-start = ((), (), s32[]{:S(2)}) async-start(), calls=%async_computation.15 | async-start | bytes 9437184 | tf_op jit(solution)/shard_map/all_gather | solution.py:194
  448.1 518.0 %copy-start.45 = (f32[256]{0:T(256)}, f32[256]{0:T(256)S(1)}, u32[]{:S(2)}) copy-start(f32[256]{0:T(256)S(1)} %add_rsqrt_fusion) | copy-start | bytes 3076
  450.7 195.6 %all-gather.23.cloned.1.call-start = ((), (), s32[]{:S(2)}) async-start(), calls=%async_computation.17 | async-start | bytes 3604480 | tf_op jit(solution)/shard_map/all_gather | solution.py:118
  451.8 321.9 %all-gather.25.cloned.1.call-start = ((), (), s32[]{:S(2)}) async-start(), calls=%async_computation.19 | async-start | bytes 9437184 | tf_op jit(solution)/shard_map/all_gather | solution.py:208
  452.5 510.9 %reduce-scatter.17.cloned.1.call-start = ((), (), s32[]{:S(2)}) async-start(), calls=%async_computation.20 | async-start | bytes 9437184 | tf_op jit(solution)/shard_map/reduce_scatter | solution.py:216
  788.7 14.2 copy-start.59
  816.1 147.4 %copy-start.5 = (bf16[256,2048]{1,0:T(8,128)(2,1)S(1)}, bf16[256,2048]{1,0:T(8,128)(2,1)}, u32[]{:S(2)}) copy-start(bf16[256,2048]{1,0:T(8,128)(2,1)} %reduce-scatter.13.cloned.1.call-done) | copy-start | bytes 3145732
  816.1 150.6 %copy-start.13 = (bf16[256,2048]{1,0:T(8,128)(2,1)S(1)}, bf16[256,2048]{1,0:T(8,128)(2,1)}, u32[]{:S(2)}) copy-start(bf16[256,2048]{1,0:T(8,128)(2,1)} %param.27) | copy-start | bytes 3145732
  816.1 276.7 %all-gather.27.cloned.1.call-start = ((), (), s32[]{:S(2)}) async-start(), calls=%async_computation.21 | async-start | bytes 9437184 | tf_op jit(solution)/shard_map/all_gather | solution.py:226
  968.8 368.1 %reduce-scatter.29.cloned.1.call-start = ((), (), s32[]{:S(2)}) async-start(), calls=%async_computation.27 | async-start | bytes 3604480 | tf_op jit(solution)/shard_map/reduce_scatter | solution.py:311
  979.4 362.9 %reduce-scatter.27.cloned.1.call-start = ((), (), s32[]{:S(2)}) async-start(), calls=%async_computation.26 | async-start | bytes 7208960 | tf_op jit(solution)/shard_map/reduce_scatter | solution.py:308
  1001.9 90.9 %copy-start.34 = (bf16[256,2048]{1,0:T(8,128)(2,1)S(1)}, bf16[256,2048]{1,0:T(8,128)(2,1)}, u32[]{:S(2)}) copy-start(bf16[256,2048]{1,0:T(8,128)(2,1)} %all-gather.17.cloned.1.call-done) | copy-start | bytes 3145732
  1002.0 346.6 %reduce-scatter.21.cloned.1.call-start = ((), (), s32[]{:S(2)}) async-start(), calls=%async_computation.23 | async-start | bytes 1310720 | tf_op jit(solution)/shard_map/reduce_scatter | solution.py:302
  1269.4 82.1 %reduce-scatter.25.cloned.1.call-start = ((), (), s32[]{:S(2)}) async-start(), calls=%async_computation.25 | async-start | bytes 1310720 | tf_op jit(solution)/shard_map/reduce_scatter | solution.py:305
  1276.2 190.7 %reduce-scatter.23.cloned.1.call-start = ((), (), s32[]{:S(2)}) async-start(), calls=%async_computation.24 | async-start | bytes 4325376 | tf_op jit(solution)/shard_map/reduce_scatter | solution.py:316
  1301.6 314.9 %reduce-scatter.19.cloned.1.call-start = ((), (), s32[]{:S(2)}) async-start(), calls=%async_computation.22 | async-start | bytes 9437184 | tf_op jit(solution)/shard_map/reduce_scatter | solution.py:290
  1323.2 445.2 %reduce-scatter.15.cloned.1.call-start = ((), (), s32[]{:S(2)}) async-start(), calls=%async_computation.18 | async-start | bytes 9437184 | tf_op jit(solution)/shard_map/reduce_scatter | solution.py:201
  1335.9 568.8 %reduce-scatter.31.cloned.1.call-start = ((), (), s32[]{:S(2)}) async-start(), calls=%async_computation.28 | async-start | bytes 1081344
  1348.6 118.4 %copy-start.37 = (f32[64,512]{1,0:T(8,128)S(1)}, f32[64,512]{1,0:T(8,128)}, u32[]{:S(2)}) copy-start(f32[64,512]{1,0:T(8,128)} %param.31) | copy-start | bytes 393220
  1351.4 265.1 %copy-start.2 = (bf16[256,2048]{1,0:T(8,128)(2,1)S(1)}, bf16[256,2048]{1,0:T(8,128)(2,1)}, u32[]{:S(2)}) copy-start(bf16[256,2048]{1,0:T(8,128)(2,1)} %param.26) | copy-start | bytes 3145732
  1351.4 265.1 %copy-start.43 = (f32[1,2048]{1,0:T(1,128)S(1)}, f32[1,2048]{1,0:T(1,128)}, u32[]{:S(2)}) copy-start(f32[1,2048]{1,0:T(1,128)} %copy-done.42) | copy-start | bytes 24580
  1351.4 265.1 %copy-start.48 = (f32[256]{0:T(256)S(1)}, f32[256]{0:T(256)}, u32[]{:S(2)}) copy-start(f32[256]{0:T(256)} %copy-done.47) | copy-start | bytes 3076
  1351.4 267.0 %copy-start.44 = (f32[2048]{0:T(1024)S(1)}, f32[2048]{0:T(1024)}, u32[]{:S(2)}) copy-start(f32[2048]{0:T(1024)} %get-tuple-element.208) | copy-start | bytes 24580
  1353.9 414.5 %copy-start.6 = (bf16[256,2048]{1,0:T(8,128)(2,1)S(1)}, bf16[256,2048]{1,0:T(8,128)(2,1)}, u32[]{:S(2)}) copy-start(bf16[256,2048]{1,0:T(8,128)(2,1)} %reduce-scatter.13.cloned.1.call-done) | copy-start | bytes 3145732
  1353.9 414.6 %copy-start.14 = (bf16[256,2048]{1,0:T(8,128)(2,1)S(1)}, bf16[256,2048]{1,0:T(8,128)(2,1)}, u32[]{:S(2)}) copy-start(bf16[256,2048]{1,0:T(8,128)(2,1)} %param.27) | copy-start | bytes 3145732
  1353.9 414.6 %copy-start.39 = (f32[1,2048]{1,0:T(1,128)S(1)}, f32[1,2048]{1,0:T(1,128)}, u32[]{:S(2)}) copy-start(f32[1,2048]{1,0:T(1,128)} %copy-done.38) | copy-start | bytes 24580
  1353.9 414.6 %copy-start.46 = (f32[256]{0:T(256)S(1)}, f32[256]{0:T(256)}, u32[]{:S(2)}) copy-start(f32[256]{0:T(256)} %copy-done.45) | copy-start | bytes 3076
  1353.9 414.5 %copy-start.50 = (f32[256]{0:T(256)S(1)}, f32[256]{0:T(256)}, u32[]{:S(2)}) copy-start(f32[256]{0:T(256)} %copy-done.49) | copy-start | bytes 3076
  1619.8 285.8 %copy-start.53 = (f32[2,64]{1,0:T(2,128)S(1)}, f32[2,64]{1,0:T(2,128)}, u32[]{:S(2)}) copy-start(f32[2,64]{1,0:T(2,128)} %param.35) | copy-start | bytes 1540
  1619.8 285.8 %copy-start.54 = (f32[2,64]{1,0:T(2,128)S(1)}, f32[2,64]{1,0:T(2,128)}, u32[]{:S(2)}) copy-start(f32[2,64]{1,0:T(2,128)} %param.47) | copy-start | bytes 1540
  1619.8 285.8 %copy-start.55 = (f32[2,64]{1,0:T(2,128)S(1)}, f32[2,64]{1,0:T(2,128)}, u32[]{:S(2)}) copy-start(f32[2,64]{1,0:T(2,128)} %param.41) | copy-start | bytes 1540
  (49 other events, 265.9 us)
Sparse Core Ops, SparseCore 0:
  11.6 59.2 all-gather.14
  83.3 121.1 all-gather.10
  206.6 14.9 all-gather.12
  223.6 16.7 all-gather.16
  297.4 148.9 reduce-scatter.12
  448.5 42.4 all-gather.20
  493.9 124.9 all-gather.18
  621.1 25.2 all-gather.22
  648.7 124.9 all-gather.24
  816.2 147.1 reduce-scatter.16
  968.9 123.9 all-gather.26
  1095.2 34.5 reduce-scatter.28
  1132.5 54.8 reduce-scatter.26
  1269.5 23.2 reduce-scatter.20
  1295.8 24.9 reduce-scatter.24
  1322.9 143.9 reduce-scatter.22
  1470.4 146.0 reduce-scatter.18
  1620.4 147.9 reduce-scatter.14
  1770.7 134.0 reduce-scatter.30
where the time goes:
time: 1920 us; the launch traced here: 1910 us
  waiting for transfers between devices  1350 us (70%)
  matrix products  302 us (16%)
  other arithmetic  121 us (6%)
  blocking collectives  69.3 us (4%)
  local copies, waits for them, and re-layouts  39.8 us (2%)
    reduce_scatter x1, waiting for transfers between devices, body(): lax.psum_scatter(jnp.dot(piece, down_full, preferred_element_type=jnp.flo...  149 us
    reduce_scatter x1, waiting for transfers between devices, body(): lax.psum_scatter((contract_cols(query_back, query_full) + contract_cols(p...  148 us
    reduce_scatter x1, waiting for transfers between devices, body(): lax.psum_scatter((contract_cols(gate_grad, gateup_full[0]) + contract_col...  147 us
    reduce_scatter x1, waiting for transfers between devices, body(): lax.psum_scatter(jnp.dot(piece, output_full, preferred_element_type=jnp.f...  146 us
    unnamed x20, waiting for transfers between devices  132 us
    all_gather x1, waiting for transfers between devices, body(): rows_two = lax.all_gather(normed_two, 'tensor', axis=0, tiled=True)  128 us
    all_gather x1, waiting for transfers between devices, body(): grad_rows = lax.all_gather(out_grad, 'tensor', axis=0, tiled=True)  127 us
    all_gather x1, waiting for transfers between devices, body(): rows_one = lax.all_gather(normed_one, 'tensor', axis=0, tiled=True)  115 us
  transfers between devices with their start and end apart: 19, of which 13 were waited for; matrix products, arithmetic and copies ran while one was open for 21% of the time, Pallas kernels for 0%

commit v1 on v0

v1 whole, which is shorter than its diff:
```python
import functools

import jax
import jax.numpy as jnp
from jax import lax
from jax.experimental import pallas as pl
from jax.experimental.pallas import tpu as pltpu
from jax.sharding import Mesh
from jax.sharding import PartitionSpec as P

D = 2048
H = 32
KVH = 4
HD = 64
FF = 5632
HALF = HD // 2

NORM_EPS = 1e-05
ADAM_EPS = 1e-08
BETA_ONE = 0.9
BETA_TWO = 0.95
DECAY = 0.1
GAIN_RATE = 1.0
NEG_FILL = -1e30
ROPE_BASE = 10000.0

AXES = ("h", "y", "c", "zh", "zl", "x")
GROUP = ("c", "zl", "x")
KEYS_BACK = 1024
QUERY_BLOCK = 256
SCALE = HD ** (-0.5)


def dot_nn(left, right):
    return lax.dot_general(
        left, right, (((1,), (0,)), ((), ())), preferred_element_type=jnp.float32
    )


def dot_nt(left, right):
    return lax.dot_general(
        left, right, (((1,), (1,)), ((), ())), preferred_element_type=jnp.float32
    )


def dot_tn(left, right):
    return lax.dot_general(
        left, right, (((0,), (0,)), ((), ())), preferred_element_type=jnp.float32
    )


def dot_tt(left, right):
    return lax.dot_general(
        left, right, (((0,), (1,)), ((), ())), preferred_element_type=jnp.float32
    )


TO_AWAY_CORE = [(0, 2), (3, 1)]


def own_shard(weight, h_size):
    shard = weight.astype(jnp.bfloat16)
    return lax.all_gather(shard, "h", axis=0) if h_size > 1 else shard[None]


def halves(grad, h_size):
    grad = grad.astype(jnp.bfloat16)
    if h_size > 1:
        return lax.psum_scatter(grad, "h", scatter_dimension=2, tiled=False)
    return grad[:, :, 0]


def add_swapped(grad, came):
    keep = lax.dynamic_index_in_dim(grad, lax.axis_index("y"), 0, keepdims=False)
    return (keep.astype(jnp.float32) + came.astype(jnp.float32)).astype(jnp.bfloat16)


def to_owners(part, deep):
    total = part.astype(jnp.float32) + deep.astype(jnp.float32)
    first = lax.axis_index("c") == 0
    mine = jnp.where(first, total[0], total[1])
    partners = jnp.where(first, total[1], total[0]).astype(jnp.bfloat16)
    got = lax.ppermute(partners, ("c", "zh"), TO_AWAY_CORE)
    return jnp.where(lax.axis_index("c") == lax.axis_index("zh"), mine, got.astype(jnp.float32))


MESH_ID = pl.DeviceIdType.MESH
CHUNKS = 2
ROW_STRIP = 32
PARTNERS = (("c",), ("x",), ("zl",), ("y",), ("y", "c"), ("zh",), ("zh", "c"))


def flipped(*axes):
    return {axis: 1 - lax.axis_index(axis) for axis in axes}


def greet():
    barrier = pltpu.get_barrier_semaphore()
    for axes in PARTNERS:
        pl.semaphore_signal(barrier, inc=1, device_id=flipped(*axes), device_id_type=MESH_ID)
    pl.semaphore_wait(barrier, len(PARTNERS))


def far_copy(src, dst, send, recv, device):
    return pltpu.make_async_remote_copy(
        src_ref=src,
        dst_ref=dst,
        send_sem=send,
        recv_sem=recv,
        device_id=device,
        device_id_type=MESH_ID,
    )


class Spread:
    def __init__(self, shard):
        self.inputs = [shard]
        self.outputs = [jax.ShapeDtypeStruct((4,) + shard.shape, shard.dtype)]
        self.sems = [3, 4]
        self.alias = {}

    def begin(self, ins, outs, sems):
        (src,), (dst,), (send, recv) = ins, outs, sems
        core, z_high, y_at = (lax.axis_index(a) for a in ("c", "zh", "y"))
        slot = 2 * y_at + core
        target = dst.at[slot]

        @pl.when(core == z_high)
        def _():
            pltpu.make_async_copy(src, target, send.at[0]).start()

        @pl.when(core != z_high)
        def _():
            far_copy(src, target, send.at[0], recv.at[slot], {"c": z_high}).start()

        far_copy(src, target, send.at[1], recv.at[slot], {"y": 1 - y_at, "c": z_high}).start()
        far_copy(src, target, send.at[2], recv.at[slot], {"zh": 1 - z_high, "c": z_high}).start()

    def finish(self, ins, outs, sems):
        (src,), (dst,), (send, recv) = ins, outs, sems
        core, z_high, y_at = (lax.axis_index(a) for a in ("c", "zh", "y"))

        def arrived(slot):
            far_copy(src, dst.at[slot], send.at[1], recv.at[slot], flipped("y")).wait_recv()

        @pl.when(core == z_high)
        def _():
            pltpu.make_async_copy(src, dst.at[2 * y_at + core], send.at[0]).wait()
            arrived(2 * y_at + 1 - core)
            arrived(2 * (1 - y_at))
            arrived(2 * (1 - y_at) + 1)

        @pl.when(core != z_high)
        def _():
            far_copy(src, dst.at[0], send.at[0], recv.at[0], flipped("c")).wait_send()
            arrived(2 * y_at)
            arrived(2 * y_at + 1)

        far_copy(src, dst.at[0], send.at[1], recv.at[0], flipped("y")).wait_send()
        far_copy(src, dst.at[0], send.at[2], recv.at[0], flipped("zh")).wait_send()


class Pass:
    def __init__(self, gathered):
        self.inputs = [gathered]
        self.outputs = [jax.ShapeDtypeStruct(gathered.shape, gathered.dtype)]
        self.sems = [1, 1]
        self.alias = {0: 0}

    def copy(self, outs, sems, y_from):
        (dst,), (send, recv) = outs, sems
        part = dst.at[pl.ds(2 * y_from, 2)]
        return far_copy(part, part, send.at[0], recv.at[0], flipped("y"))

    def begin(self, ins, outs, sems):
        @pl.when(lax.axis_index("c") != lax.axis_index("zh"))
        def _():
            self.copy(outs, sems, lax.axis_index("y")).start()

    def finish(self, ins, outs, sems):
        @pl.when(lax.axis_index("c") != lax.axis_index("zh"))
        def _():
            self.copy(outs, sems, lax.axis_index("y")).wait_send()
            self.copy(outs, sems, 1 - lax.axis_index("y")).wait_recv()


class Swap:
    def __init__(self, grad):
        self.inputs = [grad]
        self.outputs = [jax.ShapeDtypeStruct(grad.shape[1:], grad.dtype)]
        self.sems = [1, 1]
        self.alias = {}

    def copy(self, ins, outs, sems):
        (src,), (dst,), (send, recv) = ins, outs, sems
        return far_copy(
            src.at[1 - lax.axis_index("y")], dst, send.at[0], recv.at[0], flipped("y")
        )

    def begin(self, ins, outs, sems):
        self.copy(ins, outs, sems).start()

    def finish(self, ins, outs, sems):
        self.copy(ins, outs, sems).wait()


class Move:
    def __init__(self, array, axis, sends):
        self.inputs = [array]
        self.outputs = [jax.ShapeDtypeStruct(array.shape, array.dtype)]
        self.sems = [1, 1]
        self.alias = {}
        self.axis, self.sends = axis, sends

    def copy(self, ins, outs, sems):
        (src,), (dst,), (send, recv) = ins, outs, sems
        return far_copy(src, dst, send.at[0], recv.at[0], flipped(self.axis))

    def begin(self, ins, outs, sems):
        @pl.when(self.sends())
        def _():
            self.copy(ins, outs, sems).start()

    def finish(self, ins, outs, sems):
        @pl.when(self.sends())
        def _():
            self.copy(ins, outs, sems).wait_send()

        @pl.when(jnp.logical_not(self.sends()))
        def _():
            self.copy(ins, outs, sems).wait_recv()


def at_home():
    return lax.axis_index("c") == lax.axis_index("zh")


def not_home():
    return lax.axis_index("c") != lax.axis_index("zh")


def group_index(core, z_low, x_at):
    return (core * 2 + z_low) * 2 + x_at


class GatherRows:
    def __init__(self, block):
        self.inputs = [block]
        self.outputs = [jax.ShapeDtypeStruct((8,) + block.shape, block.dtype)]
        self.sems = [(7, CHUNKS), (8, CHUNKS)]
        self.alias = {}

    def places(self):
        return tuple(lax.axis_index(a) for a in ("c", "zl", "x"))

    def part(self, ref, k):
        rows = ref.shape[0] // CHUNKS
        return ref.at[pl.ds(k * rows, rows)]

    def begin(self, ins, outs, sems):
        (src,), (dst,), (send, recv) = ins, outs, sems
        core, z_low, x_at = self.places()
        own = group_index(core, z_low, x_at)
        for k in range(CHUNKS):
            for way, axis in enumerate(("x", "zl", "c")):
                far_copy(
                    self.part(src, k),
                    self.part(dst.at[own], k),
                    send.at[way, k],
                    recv.at[own, k],
                    flipped(axis),
                ).start()

    def finish(self, ins, outs, sems):
        (src,), (dst,), (send, recv) = ins, outs, sems
        core, z_low, x_at = self.places()
        own = group_index(core, z_low, x_at)
        beside = group_index(core, z_low, 1 - x_at)
        below = group_index(core, 1 - z_low, x_at)
        across = group_index(core, 1 - z_low, 1 - x_at)
        turn = jnp.where(core == 0, below, beside)
        onward = {
            "x": jnp.where(core == 0, 1 - x_at, x_at),
            "zl": jnp.where(core == 0, z_low, 1 - z_low),
        }

        def pass_on(block, k, way, device):
            part = self.part(dst.at[block], k)
            return far_copy(part, part, send.at[way, k], recv.at[block, k], device)

        pltpu.sync_copy(src, dst.at[own])
        for k in range(CHUNKS):
            pass_on(beside, k, 0, flipped("x")).wait_recv()
            pass_on(below, k, 0, flipped("x")).wait_recv()
            pass_on(turn, k, 3, onward).start()
            pass_on(beside, k, 4, flipped("c")).start()
            pass_on(below, k, 5, flipped("c")).start()
        for k in range(CHUNKS):
            pass_on(across, k, 0, flipped("x")).wait_recv()
            pass_on(across, k, 6, flipped("c")).start()
        for k in range(CHUNKS):
            for z_of in (0, 1):
                for x_of in (0, 1):
                    block = group_index(1 - core, z_of, x_of)
                    pass_on(block, k, 0, flipped("c")).wait_recv()
            for way in range(7):
                pass_on(own, k, way, flipped("c")).wait_send()


class ScatterRows:
    alias = {}

    def __init__(self, partial):
        self.inputs = [partial]
        self.in_spaces = [pltpu.VMEM]
        self.rows, cols = partial.shape[0] // 8, partial.shape[1]
        block = (self.rows, cols)
        self.outputs = [jax.ShapeDtypeStruct(block, jnp.float32)]
        self.out_spaces = [pltpu.VMEM]
        self.sems = [(7, CHUNKS), (7, CHUNKS)]
        kind = partial.dtype
        self.scratch = [pltpu.VMEM((4,) + block, kind)] * 2 + [pltpu.VMEM(block, kind)] * 3

    def begin(self, ins, outs, sems, scratch):
        (partial,) = ins
        came, sums, turned, direct_in, late_in = scratch
        send, recv = sems
        core, z_low, x_at = (lax.axis_index(a) for a in ("c", "zl", "x"))
        rows, size = self.rows, self.rows // CHUNKS
        own, beside, below, across = (
            2 * z_low + x_at,
            2 * z_low + 1 - x_at,
            2 * (1 - z_low) + x_at,
            2 * (1 - z_low) + 1 - x_at,
        )
        direct = jnp.where(core == 0, beside, below)
        late = jnp.where(core == 0, below, beside)
        direct_way = {
            "x": jnp.where(core == 0, 1 - x_at, x_at),
            "zl": jnp.where(core == 0, z_low, 1 - z_low),
        }
        late_way = {
            "x": jnp.where(core == 0, x_at, 1 - x_at),
            "zl": jnp.where(core == 0, 1 - z_low, z_low),
        }
        self.blocks = (across, direct, late, own)

        def to_core(n, k):
            block = self.blocks[n]
            at = (4 * (1 - core) + block) * rows + k * size
            return far_copy(
                partial.at[pl.ds(pl.multiple_of(at, size), size)],
                came.at[block, pl.ds(k * size, size)],
                send.at[n, k],
                recv.at[block, k],
                flipped("c"),
            )

        def add(n, k, target, *others):
            block = self.blocks[n]

            @pl.loop(0, size // ROW_STRIP)
            def _(strip):
                inner = pl.multiple_of(k * size + strip * ROW_STRIP, ROW_STRIP)
                at = pl.ds(inner, ROW_STRIP)
                there = pl.multiple_of((4 * core + block) * rows + inner, ROW_STRIP)
                total = partial[pl.ds(there, ROW_STRIP)].astype(jnp.float32)
                total += came[block, at].astype(jnp.float32)
                for other in others:
                    total += other[at].astype(jnp.float32)
                target[at] = total.astype(target.dtype)

        def send_sum(n, way, k, target, device):
            at = pl.ds(k * size, size)
            return far_copy(
                sums.at[self.blocks[n], at],
                target.at[at],
                send.at[way, k],
                recv.at[way, k],
                device,
            )

        self.to_core, self.add, self.send_sum = to_core, add, send_sum
        self.turn = lambda k: send_sum(0, 4, k, turned, direct_way)
        self.straight = lambda k: send_sum(1, 5, k, direct_in, direct_way)
        self.last = lambda k: send_sum(2, 6, k, late_in, late_way)
        for n in range(4):
            for k in range(CHUNKS):
                to_core(n, k).start()

    def finish(self, ins, outs, sems, scratch):
        (out,) = outs
        came, sums, turned, direct_in, late_in = scratch
        across, direct, late, own = self.blocks
        for k in range(CHUNKS):
            self.to_core(0, k).wait_recv()
            self.add(0, k, sums.at[across])
            self.turn(k).start()
        for k in range(CHUNKS):
            self.to_core(1, k).wait_recv()
            self.add(1, k, sums.at[direct])
            self.straight(k).start()
        for k in range(CHUNKS):
            self.to_core(2, k).wait_recv()
            self.turn(k).wait_recv()
            self.add(2, k, sums.at[late], turned)
            self.last(k).start()
        for k in range(CHUNKS):
            self.to_core(3, k).wait_recv()
            self.straight(k).wait_recv()
            self.last(k).wait_recv()
            self.add(3, k, out, direct_in, late_in)
        for k in range(CHUNKS):
            for n in range(4):
                self.to_core(n, k).wait_send()
            self.turn(k).wait_send()
            self.straight(k).wait_send()
            self.last(k).wait_send()


class Everyone:
    everyone = True
    alias = {}

    def __init__(self, parts, pick, devices):
        self.inputs = [parts]
        self.outputs = [jax.ShapeDtypeStruct((devices,) + parts.shape[1:], parts.dtype)]
        self.sems = [devices, devices]
        self.pick, self.devices = pick, devices

    def copy(self, ins, outs, sems, step):
        (src,), (dst,), (send, recv) = ins, outs, sems
        me = my_number()
        to = lax.rem(me + step, self.devices)
        return pltpu.make_async_remote_copy(
            src_ref=src.at[self.pick(to)],
            dst_ref=dst.at[me],
            send_sem=send.at[step],
            recv_sem=recv.at[me],
            device_id=to,
            device_id_type=pl.DeviceIdType.LOGICAL,
        )

    def begin(self, ins, outs, sems):
        @pl.loop(1, self.devices)
        def _(step):
            self.copy(ins, outs, sems, step).start()

    def finish(self, ins, outs, sems):
        (src,), (dst,), (send, recv) = ins, outs, sems
        me = my_number()
        pltpu.sync_copy(src.at[self.pick(me)], dst.at[me])

        @pl.loop(1, self.devices)
        def _(step):
            self.copy(ins, outs, sems, step).wait_send()
            origin = lax.rem(me + step, self.devices)
            pltpu.make_async_remote_copy(
                src_ref=src.at[0],
                dst_ref=dst.at[origin],
                send_sem=send.at[step],
                recv_sem=recv.at[origin],
                device_id=origin,
                device_id_type=pl.DeviceIdType.LOGICAL,
            ).wait_recv()


def my_number():
    number = 0
    for axis in AXES:
        number = number * lax.axis_size(axis) + lax.axis_index(axis)
    return number


def greet_everyone(devices):
    barrier = pltpu.get_barrier_semaphore()
    me = my_number()

    @pl.loop(1, devices)
    def _(step):
        pl.semaphore_signal(
            barrier,
            inc=1,
            device_id=lax.rem(me + step, devices),
            device_id_type=pl.DeviceIdType.LOGICAL,
        )

    pl.semaphore_wait(barrier, devices - 1)


def run(collective_id, *tasks):
    arrays, in_specs, shapes, out_specs, scratch, counts, aliases = [], [], [], [], [], [], {}
    devices = 0
    for task in tasks:
        for a, b in task.alias.items():
            aliases[len(arrays) + a] = len(shapes) + b
        extra = getattr(task, "scratch", None)
        kinds = [pltpu.SemaphoreType.DMA(s if isinstance(s, tuple) else (s,)) for s in task.sems]
        counts.append(
            (len(task.inputs), len(task.outputs), len(kinds), len(extra) if extra else None)
        )
        arrays += task.inputs
        shapes += task.outputs
        scratch += kinds + (extra or [])
        spaces = getattr(task, "in_spaces", [pl.ANY] * len(task.inputs))
        in_specs += [pl.BlockSpec(memory_space=s) for s in spaces]
        spaces = getattr(task, "out_spaces", [pl.ANY] * len(task.outputs))
        out_specs += [pl.BlockSpec(memory_space=s) for s in spaces]
        if getattr(task, "everyone", False):
            devices = task.devices

    def kernel(*refs):
        ins = refs[: len(arrays)]
        outs = refs[len(arrays) : len(arrays) + len(shapes)]
        rest = refs[len(arrays) + len(shapes) :]
        if devices:
            greet_everyone(devices)
        else:
            greet()
        bound = []
        for i, o, s, e in counts:
            mine = [ins[:i], outs[:o], rest[:s]]
            ins, outs, rest = ins[i:], outs[o:], rest[s:]
            if e is not None:
                mine.append(rest[:e])
                rest = rest[e:]
            bound.append(mine)
        for task, mine in zip(tasks, bound):
            task.begin(*mine)
        for task, mine in zip(tasks, bound):
            task.finish(*mine)

    results = pl.pallas_call(
        kernel,
        in_specs=in_specs,
        out_specs=out_specs,
        out_shape=shapes,
        scratch_shapes=scratch,
        input_output_aliases=aliases,
        compiler_params=pltpu.CompilerParams(
            collective_id=collective_id, has_side_effects=True, vmem_limit_bytes=56 * 2**20
        ),
    )(*arrays)
    grouped, at = [], 0
    for task in tasks:
        count = len(task.outputs)
        grouped.append(results[at] if count == 1 else results[at : at + count])
        at += count
    return grouped


def attn_mask(start_row, block, count):
    key_at = (block + 5 - count) * QUERY_BLOCK
    shape = (count * QUERY_BLOCK, QUERY_BLOCK)
    keys = key_at + lax.broadcasted_iota(jnp.int32, shape, 0)
    rows = KEYS_BACK + block * QUERY_BLOCK + lax.broadcasted_iota(jnp.int32, shape, 1)
    return (keys >= start_row) & (keys <= rows)


def attn_fwd_kernel(heads, first_ref, start_ref, q_ref, kt_ref, vt_ref, o_ref, lse_ref, k_s):
    pack, block = pl.program_id(0), pl.program_id(1)

    @pl.when(block == 0)
    def _():
        k_s[...] = kt_ref[0].astype(jnp.float32).T.astype(jnp.bfloat16)

    needed = block + 5 - first_ref[pack, block] // QUERY_BLOCK
    for count in range(1, 6):

        @pl.when(needed == count)
        def _():
            key_at = pl.multiple_of((block + 5 - count) * QUERY_BLOCK, QUERY_BLOCK)
            window = pl.ds(key_at, count * QUERY_BLOCK)
            allowed = attn_mask(start_ref[0], block, count)
            keys = k_s[window, :]
            values_t = vt_ref[0, :, window]
            for head in range(heads):
                scores = dot_nn(keys, q_ref[head * HD : (head + 1) * HD, :])
                scores = jnp.where(allowed, scores, NEG_FILL)
                top = jnp.max(scores, axis=0, keepdims=True)
                weights = jnp.exp(scores - top)
                total = jnp.sum(weights, axis=0, keepdims=True)
                mixed = dot_nn(values_t, weights.astype(jnp.bfloat16))
                o_ref[head * HD : (head + 1) * HD, :] = (mixed / total).astype(jnp.bfloat16)
                lse_ref[0, head : head + 1, :] = top + jnp.log(total)


def attn_bwd_kernel(
    heads,
    first_ref,
    start_ref,
    q_ref,
    o_ref,
    do_ref,
    lse_ref,
    kt_ref,
    vt_ref,
    dq_ref,
    dk_ref,
    dv_ref,
    k_s,
    v_s,
    dk_s,
    dv_s,
):
    pack, block = pl.program_id(0), pl.program_id(1)

    @pl.when(block == 0)
    def _():
        k_s[...] = kt_ref[0].astype(jnp.float32).T.astype(jnp.bfloat16)
        v_s[...] = vt_ref[0].astype(jnp.float32).T.astype(jnp.bfloat16)
        dk_s[...] = jnp.zeros_like(dk_s)
        dv_s[...] = jnp.zeros_like(dv_s)

    needed = block + 5 - first_ref[pack, block] // QUERY_BLOCK
    for count in range(1, 6):

        @pl.when(needed == count)
        def _():
            key_at = pl.multiple_of((block + 5 - count) * QUERY_BLOCK, QUERY_BLOCK)
            window = pl.ds(key_at, count * QUERY_BLOCK)
            allowed = attn_mask(start_ref[0], block, count)
            keys = k_s[window, :]
            values = v_s[window, :]
            keys_t = kt_ref[0, :, window]
            for head in range(heads):
                here = slice(head * HD, (head + 1) * HD)
                query_t = q_ref[here, :]
                grad_t = do_ref[here, :]
                grad_f = grad_t.astype(jnp.float32)
                delta = jnp.sum(grad_f * o_ref[here, :].astype(jnp.float32), axis=0, keepdims=True)
                scores = jnp.where(allowed, dot_nn(keys, query_t), NEG_FILL)
                weights = jnp.exp(scores - lse_ref[0, head : head + 1, :])
                weights_grad = dot_nn(values, grad_t)
                scores_grad = (weights * (weights_grad - delta)).astype(jnp.bfloat16)
                dq_ref[here, :] = dot_nn(keys_t, scores_grad) * SCALE
                query = query_t.astype(jnp.float32).T.astype(jnp.bfloat16)
                grad = grad_f.T.astype(jnp.bfloat16)
                dk_s[window, :] += dot_nn(scores_grad, query)
                dv_s[window, :] += dot_nn(weights.astype(jnp.bfloat16), grad)

    @pl.when(block == pl.num_programs(1) - 1)
    def _():
        dk_ref[0] = dk_s[...].T
        dv_ref[0] = dv_s[...].T


def attn_fwd(first, start, query_t, keys_t, values_t):
    packs, _, window = keys_t.shape
    rows = query_t.shape[1] // packs
    blocks = rows // QUERY_BLOCK
    heads = query_t.shape[0] // HD
    width = query_t.shape[0]
    col = lambda p, b, s: (0, p * blocks + b)
    return pl.pallas_call(
        functools.partial(attn_fwd_kernel, heads),
        grid_spec=pltpu.PrefetchScalarGridSpec(
            num_scalar_prefetch=1,
            grid=(packs, blocks),
            in_specs=[
                pl.BlockSpec((1, 1, QUERY_BLOCK), lambda p, b, s: (p, 0, b)),
                pl.BlockSpec((width, QUERY_BLOCK), col),
                pl.BlockSpec((1, HD, window), lambda p, b, s: (p, 0, 0)),
                pl.BlockSpec((1, HD, window), lambda p, b, s: (p, 0, 0)),
            ],
            out_specs=[
                pl.BlockSpec((width, QUERY_BLOCK), col),
                pl.BlockSpec((1, heads, QUERY_BLOCK), lambda p, b, s: (p, 0, b)),
            ],
            scratch_shapes=[pltpu.VMEM((window, HD), jnp.bfloat16)],
        ),
        out_shape=[
            jax.ShapeDtypeStruct(query_t.shape, jnp.bfloat16),
            jax.ShapeDtypeStruct((packs, heads, rows), jnp.float32),
        ],
        compiler_params=pltpu.CompilerParams(vmem_limit_bytes=48 * 2**20),
    )(first, start, query_t, keys_t, values_t)


def attn_bwd(first, start, query_t, out_t, grad_t, lse, keys_t, values_t):
    packs, _, window = keys_t.shape
    rows = query_t.shape[1] // packs
    blocks = rows // QUERY_BLOCK
    heads = query_t.shape[0] // HD
    width = query_t.shape[0]
    col = lambda p, b, s: (0, p * blocks + b)
    whole = lambda p, b, s: (p, 0, 0)
    return pl.pallas_call(
        functools.partial(attn_bwd_kernel, heads),
        grid_spec=pltpu.PrefetchScalarGridSpec(
            num_scalar_prefetch=1,
            grid=(packs, blocks),
            in_specs=[
                pl.BlockSpec((1, 1, QUERY_BLOCK), lambda p, b, s: (p, 0, b)),
                pl.BlockSpec((width, QUERY_BLOCK), col),
                pl.BlockSpec((width, QUERY_BLOCK), col),
                pl.BlockSpec((width, QUERY_BLOCK), col),
                pl.BlockSpec((1, heads, QUERY_BLOCK), lambda p, b, s: (p, 0, b)),
                pl.BlockSpec((1, HD, window), whole),
                pl.BlockSpec((1, HD, window), whole),
            ],
            out_specs=[
                pl.BlockSpec((width, QUERY_BLOCK), col),
                pl.BlockSpec((1, HD, window), whole),
                pl.BlockSpec((1, HD, window), whole),
            ],
            scratch_shapes=[
                pltpu.VMEM((window, HD), jnp.bfloat16),
                pltpu.VMEM((window, HD), jnp.bfloat16),
                pltpu.VMEM((window, HD), jnp.float32),
                pltpu.VMEM((window, HD), jnp.float32),
            ],
        ),
        out_shape=[
            jax.ShapeDtypeStruct(query_t.shape, jnp.float32),
            jax.ShapeDtypeStruct((packs, HD, window), jnp.float32),
            jax.ShapeDtypeStruct((packs, HD, window), jnp.float32),
        ],
        compiler_params=pltpu.CompilerParams(vmem_limit_bytes=48 * 2**20),
    )(first, start, query_t, out_t, grad_t, lse, keys_t, values_t)


def rotate(values, cos_table, sin_table):
    front, back = values[:, :HALF], values[:, HALF:]
    return jnp.concatenate(
        [front * cos_table - back * sin_table, back * cos_table + front * sin_table], axis=1
    )


def rotate_back(grads, cos_table, sin_table):
    front, back = grads[:, :HALF], grads[:, HALF:]
    return jnp.concatenate(
        [front * cos_table + back * sin_table, back * cos_table - front * sin_table], axis=1
    )


def norm_back(upstream, inputs, inverse, gain):
    scaled = gain * upstream
    inner = jnp.mean(scaled * inputs, axis=1, keepdims=True)
    return (
        inverse * scaled - inputs * inverse * inverse * inverse * inner,
        jnp.sum(upstream * inputs * inverse, axis=0),
    )


def adam_step(weight, grad, first_old, second_old, rate, decay, step_value):
    first_new = BETA_ONE * first_old + (1.0 - BETA_ONE) * grad
    second_new = BETA_TWO * second_old + (1.0 - BETA_TWO) * grad * grad
    fix_one = 1.0 - jnp.power(jnp.float32(BETA_ONE), step_value)
    fix_two = 1.0 - jnp.power(jnp.float32(BETA_TWO), step_value)
    update = first_new / fix_one / (jnp.sqrt(second_new / fix_two) + ADAM_EPS)
    return (weight - rate * (update + decay * weight), first_new, second_new)


def rows_of(blocks):
    _, h, rows, cols = blocks.shape
    y = c = 2
    blocks = blocks.reshape(y, c, h, rows, cols)
    return blocks.transpose(2, 0, 1, 3, 4).reshape(h * y * c * rows, cols)


def cols_of(blocks):
    _, h, rows, cols = blocks.shape
    y = c = 2
    blocks = blocks.reshape(y, c, h, rows, cols)
    return blocks.transpose(3, 2, 0, 1, 4).reshape(rows, h * y * c * cols)


def as_row_blocks(whole, h_size):
    rows, cols = whole.shape
    parts = whole.reshape(h_size, 2, 2, rows // (4 * h_size), cols)
    return parts.transpose(1, 2, 0, 3, 4)


def as_col_blocks(whole, h_size):
    rows, cols = whole.shape
    parts = whole.reshape(rows, h_size, 2, 2, cols // (4 * h_size))
    return parts.transpose(2, 3, 1, 0, 4)


def body(
    h_size,
    tensor_size,
    hidden_in,
    out_grad,
    segment_ids,
    step_count,
    query_weight,
    keyvalue_weight,
    output_weight,
    gateup_weight,
    down_weight,
    norm_gains,
    query_first,
    keyvalue_first,
    output_first,
    gateup_first,
    down_first,
    gains_first,
    query_second,
    keyvalue_second,
    output_second,
    gateup_second,
    down_second,
    gains_second,
):
    zl_size = tensor_size // 4
    core, z_high = lax.axis_index("c"), lax.axis_index("zh")
    z_low, x_at = lax.axis_index("zl"), lax.axis_index("x")
    inputs = hidden_in.astype(jnp.float32)
    devices = h_size * 4 * tensor_size

    pair_rows = keyvalue_weight.shape[0]
    gain_cols = norm_gains.shape[1]
    small_rows = -(-(2 * gain_cols) // (2 * HD))
    pad_rows = 16 * (-(-small_rows // 16))
    by_head = (
        keyvalue_weight.reshape(pair_rows, 2, KVH, HD)
        .transpose(2, 0, 1, 3)
        .reshape(KVH, pair_rows, 2 * HD)
    )
    flat_gains = jnp.pad(norm_gains.reshape(-1), (0, pad_rows * 2 * HD - 2 * gain_cols))
    flat_gains = jnp.broadcast_to(flat_gains.reshape(1, pad_rows, 2 * HD), (KVH, pad_rows, 2 * HD))
    small = jnp.concatenate([by_head, flat_gains], axis=1).astype(jnp.bfloat16)

    def head_of(device):
        low = lax.rem(lax.div(device, 2), zl_size)
        at_core = lax.rem(lax.div(device, tensor_size), 2)
        return lax.div((at_core * zl_size + low) * 2 * (H // tensor_size), H // KVH)

    small_all, query_parts = run(
        0, Everyone(small, head_of, devices), Spread(own_shard(query_weight, h_size))
    )
    pair_proj = small_all[:, :pair_rows].reshape(devices * pair_rows, 2 * HD)
    gains_full = (
        small_all[:, pair_rows:]
        .reshape(devices, pad_rows * 2 * HD)[:, : 2 * gain_cols]
        .reshape(devices, 2, gain_cols)
        .transpose(1, 0, 2)
        .reshape(2, devices * gain_cols)
    )
    gain_attn = gains_full[0].astype(jnp.float32)
    gain_mlp = gains_full[1].astype(jnp.float32)

    heads_here = query_weight.shape[1] // HD

    seg_mine = segment_ids
    seg_other = lax.ppermute(seg_mine, "c", [(0, 1), (1, 0)])
    seg_packs = jnp.where(
        core == 0,
        jnp.concatenate([seg_mine, seg_other]),
        jnp.concatenate([seg_other, seg_mine]),
    )
    pack_rows = seg_packs.shape[1]
    half_rows = pack_rows // 2
    sizes = [jnp.sum((seg_packs == n).astype(jnp.int32), axis=1, keepdims=True) for n in (0, 1)]
    seg_half = lax.dynamic_slice_in_dim(seg_packs, z_high * half_rows, half_rows, 1)
    earlier = jnp.where(seg_half >= 1, sizes[0], 0) + jnp.where(seg_half >= 2, sizes[1], 0)
    place = z_high * half_rows + jnp.arange(half_rows, dtype=jnp.int32)[None, :]
    position = place - earlier
    start = KEYS_BACK + jnp.arange(half_rows, dtype=jnp.int32)[None, :] - position
    frequency = jnp.power(ROPE_BASE, -2.0 * jnp.arange(HALF, dtype=jnp.float32) / HD)
    angles = frequency[:, None] * position.reshape(1, 2 * half_rows).astype(jnp.float32)
    cos_table, sin_table = jnp.cos(angles), jnp.sin(angles)
    block_first = start[:, ::QUERY_BLOCK]
    start = start[:, None, :]

    inverse_one = lax.rsqrt(jnp.mean(inputs * inputs, axis=1, keepdims=True) + NORM_EPS)
    normed_one = (inputs * inverse_one * gain_attn).astype(jnp.bfloat16)
    rows_one, query_parts, output_parts, gate_parts = run(
        1,
        GatherRows(normed_one),
        Pass(query_parts),
        Spread(own_shard(output_weight, h_size)),
        Spread(own_shard(gateup_weight[0], h_size)),
    )
    block_rows = rows_one.shape[1]
    group_rows = 8 * block_rows
    rows_one = rows_one.reshape(group_rows, D)
    query_full = rows_of(query_parts)
    query_pre = dot_tt(query_full, rows_one).reshape(heads_here, HD, group_rows)
    pair_pre = dot_tt(pair_proj, rows_one).reshape(2, HD, group_rows)
    query_rot = (rotate(query_pre, cos_table, sin_table).astype(jnp.bfloat16) * SCALE).astype(
        jnp.bfloat16
    )
    query_rot = query_rot.reshape(heads_here * HD, group_rows)
    key_rot = rotate(pair_pre[:1], cos_table, sin_table).astype(jnp.bfloat16)
    pair_rot = jnp.concatenate([key_rot, pair_pre[1:].astype(jnp.bfloat16)])
    grad_rows, pair_back_half, output_parts, gate_parts, up_parts = run(
        2,
        GatherRows(out_grad),
        Move(pair_rot, "zh", lambda: lax.axis_index("zh") == 0),
        Pass(output_parts),
        Pass(gate_parts),
        Spread(own_shard(gateup_weight[1], h_size)),
    )
    grad_rows = grad_rows.reshape(group_rows, D)
    pair_back_half = jnp.where(z_high == 1, pair_back_half, 0)
    output_full = cols_of(output_parts)
    gate_full = rows_of(gate_parts)
    pair_window = jnp.concatenate(
        [
            pair_back_half.reshape(2, HD, 2, half_rows),
            pair_rot.reshape(2, HD, 2, half_rows),
        ],
        axis=3,
    ).transpose(0, 2, 1, 3)
    keys_t, values_t = pair_window[0], pair_window[1]
    attended_t, log_totals = attn_fwd(block_first, start, query_rot, keys_t, values_t)
    attn_out, up_parts, down_parts = run(
        3,
        ScatterRows(dot_tn(attended_t, output_full).astype(jnp.bfloat16)),
        Pass(up_parts),
        Spread(own_shard(down_weight, h_size)),
    )

    residual_mid = inputs + attn_out
    inverse_two = lax.rsqrt(jnp.mean(residual_mid * residual_mid, axis=1, keepdims=True) + NORM_EPS)
    normed_two = (residual_mid * inverse_two * gain_mlp).astype(jnp.bfloat16)
    rows_two, down_parts = run(4, GatherRows(normed_two), Pass(down_parts))
    rows_two = rows_two.reshape(group_rows, D)
    up_full = rows_of(up_parts)
    down_full = cols_of(down_parts)
    gate_proj = dot_nn(rows_two, gate_full)
    up_proj = dot_nn(rows_two, up_full)
    sigmoid_gate = jax.nn.sigmoid(gate_proj)
    silu_gate = gate_proj * sigmoid_gate
    hidden_mlp = (silu_gate * up_proj).astype(jnp.bfloat16)

    down_grad = halves(as_col_blocks(dot_tn(hidden_mlp, grad_rows), h_size), h_size)
    mlp_out, down_came = run(
        5,
        ScatterRows(dot_nn(hidden_mlp, down_full).astype(jnp.bfloat16)),
        Swap(down_grad),
    )
    hidden_out = (residual_mid + mlp_out).astype(jnp.bfloat16)
    down_part = add_swapped(down_grad, down_came)
    hidden_grad = dot_nt(grad_rows, down_full)
    gate_grad = (
        hidden_grad * up_proj * sigmoid_gate * (1.0 + gate_proj * (1.0 - sigmoid_gate))
    ).astype(jnp.bfloat16)
    up_grad = (hidden_grad * silu_gate).astype(jnp.bfloat16)
    gate_wgrad = halves(as_row_blocks(dot_tn(rows_two, gate_grad), h_size), h_size)
    up_wgrad = halves(as_row_blocks(dot_tn(rows_two, up_grad), h_size), h_size)
    normed_two_grad, gate_came, down_deep = run(
        6,
        ScatterRows(
            (dot_nt(gate_grad, gate_full) + dot_nt(up_grad, up_full)).astype(jnp.bfloat16)
        ),
        Swap(gate_wgrad),
        Move(down_part, "zh", not_home),
    )
    gate_part = add_swapped(gate_wgrad, gate_came)
    mid_back, gain_mlp_grad = norm_back(normed_two_grad, residual_mid, inverse_two, gain_mlp)
    mid_grad = out_grad.astype(jnp.float32) + mid_back
    attn_grad_rows, up_came, gate_deep = run(
        7,
        GatherRows(mid_grad.astype(jnp.bfloat16)),
        Swap(up_wgrad),
        Move(gate_part, "zh", not_home),
    )
    attn_grad_rows = attn_grad_rows.reshape(group_rows, D)
    up_part = add_swapped(up_wgrad, up_came)
    output_grad = halves(as_col_blocks(dot_nn(attended_t, attn_grad_rows), h_size), h_size)
    attended_grad = dot_nt(output_full, attn_grad_rows).astype(jnp.bfloat16)
    query_grads, key_grads, value_grads = attn_bwd(
        block_first, start, query_rot, attended_t, attended_grad, log_totals, keys_t, values_t
    )
    query_back = (
        rotate_back(query_grads.reshape(heads_here, HD, group_rows), cos_table, sin_table)
        .astype(jnp.bfloat16)
        .reshape(heads_here * HD, group_rows)
    )
    pair_grads = jnp.stack([key_grads, value_grads]).transpose(0, 2, 1, 3)
    pair_later, up_deep, output_came = run(
        8,
        Move(
            pair_grads[..., :KEYS_BACK].astype(jnp.bfloat16),
            "zh",
            lambda: lax.axis_index("zh") == 1,
        ),
        Move(up_part, "zh", not_home),
        Swap(output_grad),
    )
    output_part = add_swapped(output_grad, output_came)
    pair_later = jnp.where(z_high == 0, pair_later, 0).astype(jnp.float32)
    pair_sum = (pair_grads[..., KEYS_BACK:] + pair_later).reshape(2, HD, group_rows)
    pair_back = jnp.concatenate(
        [rotate_back(pair_sum[:1], cos_table, sin_table), pair_sum[1:]]
    ).astype(jnp.bfloat16)
    pair_back = pair_back.reshape(2 * HD, group_rows)
    query_wgrad = halves(as_row_blocks(dot_tt(rows_one, query_back), h_size), h_size)
    pair_wgrad = dot_tt(rows_one, pair_back)
    normed_one_grad, query_came, output_deep = run(
        9,
        ScatterRows(
            (dot_tt(query_back, query_full) + dot_tt(pair_back, pair_proj)).astype(jnp.bfloat16)
        ),
        Swap(query_wgrad),
        Move(output_part, "zh", not_home),
    )
    query_part = add_swapped(query_wgrad, query_came)
    input_back, gain_attn_grad = norm_back(normed_one_grad, inputs, inverse_one, gain_attn)
    input_grad = mid_grad + input_back
    gains_grad = jnp.stack([gain_attn_grad, gain_mlp_grad]).reshape(2, devices, gain_cols)
    gains_grad = gains_grad.transpose(1, 0, 2).reshape(devices, 2 * gain_cols)
    gains_grad = jnp.pad(gains_grad, ((0, 0), (0, pad_rows * 2 * HD - 2 * gain_cols)))
    small_grads = jnp.concatenate(
        [
            pair_wgrad.reshape(devices, pair_rows, 2 * HD),
            gains_grad.reshape(devices, pad_rows, 2 * HD),
        ],
        axis=1,
    ).astype(jnp.bfloat16)
    small_sums, query_deep = run(
        10,
        Everyone(small_grads, lambda device: device, devices),
        Move(query_part, "zh", not_home),
    )
    small_sums = small_sums.astype(jnp.float32)
    pair_sums = (
        small_sums[:, :pair_rows]
        .reshape(h_size * 2, 2, 2, zl_size * 2, pair_rows, 2 * HD)
        .sum(axis=(0, 2))
        .reshape(KVH, tensor_size // KVH, pair_rows, 2, HD)
        .sum(axis=1)
    )
    keyvalue_sum = pair_sums.transpose(1, 2, 0, 3).reshape(pair_rows, 2 * KVH * HD)
    gains_sum = (
        small_sums[:, pair_rows:]
        .sum(axis=0)
        .reshape(pad_rows * 2 * HD)[: 2 * gain_cols]
        .reshape(2, gain_cols)
    )
    query_sum = to_owners(query_part, query_deep)
    output_sum = to_owners(output_part, output_deep)
    gateup_sum = jnp.stack([to_owners(gate_part, gate_deep), to_owners(up_part, up_deep)])
    down_sum = to_owners(down_part, down_deep)
    step_value = step_count[0].astype(jnp.float32)
    query_new, query_mone, query_mtwo = adam_step(
        query_weight, query_sum, query_first, query_second, D ** (-0.5), DECAY, step_value
    )
    pair_new, pair_mone, pair_mtwo = adam_step(
        keyvalue_weight,
        keyvalue_sum,
        keyvalue_first,
        keyvalue_second,
        D ** (-0.5),
        DECAY,
        step_value,
    )
    output_new, output_mone, output_mtwo = adam_step(
        output_weight,
        output_sum,
        output_first,
        output_second,
        (H * HD // 16) ** (-0.5),
        DECAY,
        step_value,
    )
    gateup_new, gateup_mone, gateup_mtwo = adam_step(
        gateup_weight, gateup_sum, gateup_first, gateup_second, D ** (-0.5), DECAY, step_value
    )
    down_new, down_mone, down_mtwo = adam_step(
        down_weight, down_sum, down_first, down_second, FF ** (-0.5), DECAY, step_value
    )
    gains_new, gains_mone, gains_mtwo = adam_step(
        norm_gains, gains_sum, gains_first, gains_second, GAIN_RATE, 0.0, step_value
    )
    return (
        hidden_out,
        input_grad,
        query_new,
        pair_new,
        output_new,
        gateup_new,
        down_new,
        gains_new,
        query_mone,
        pair_mone,
        output_mone,
        gateup_mone,
        down_mone,
        gains_mone,
        query_mtwo,
        pair_mtwo,
        output_mtwo,
        gateup_mtwo,
        down_mtwo,
        gains_mtwo,
    )


def solution(mesh):
    dp_size, tensor_size = mesh.shape["dp"], mesh.shape["tensor"]
    h_size = dp_size // 4
    fine = Mesh(mesh.devices.reshape(h_size, 2, 2, 2, tensor_size // 4, 2), AXES)
    dp, tensor = AXES[:3], AXES[3:]
    rows = P(AXES, None)
    weights = (
        P(dp, tensor),
        P(AXES, None),
        P(tensor, dp),
        P(None, dp, tensor),
        P(tensor, dp),
        P(None, AXES),
    )
    return jax.shard_map(
        functools.partial(body, h_size, tensor_size),
        mesh=fine,
        in_specs=(rows, rows, P(dp, None), P()) + weights * 3,
        out_specs=(rows, rows) + weights * 3,
        check_vma=False,
    )
```

time: 1920 us -> 1030 us (0.54)
  waiting for transfers between devices: 1350 us -> 0.02 us
  Pallas kernels: 0 us -> 647 us
  matrix products: 302 us -> 154 us
  local copies, waits for them, and re-layouts: 39.8 us -> 116 us
  blocking collectives: 69.3 us -> 0 us
  other arithmetic: 121 us -> 91.9 us
    reduce_scatter x9 -> x0, waiting for transfers between devices: 703 us -> none  [the longest x1 149 us: body(): lax.psum_scatter(jnp.dot(piece, down_full, preferred_element_type=jnp.flo...]
    pallas_call x0 -> x13, Pallas kernels: none -> 647 us  [the longest x11 608 us: run(): pl.pallas_call(kernel, in_specs=in_specs, out_specs=out_specs, out_shape=...]
    all_gather x9 -> x0, waiting for transfers between devices: 516 us -> none  [the longest x1 128 us: body(): rows_two = lax.all_gather(normed_two, 'tensor', axis=0, tiled=True)]
    dot_general x46 -> x18, matrix products: 302 us -> 154 us  [the longest x4 45.1 us: dot_nt(): lax.dot_general(left, right, (((1,), (1,)), ((), ())), preferred_element_...]
    unnamed x20 -> x0, waiting for transfers between devices: 132 us -> none
    all_gather x1 -> x0, blocking collectives: 69.3 us -> none  [body(): lax.all_gather(norm_gains.astype(jnp.bfloat16), ('dp', 'tensor'), axis=1,...]
    dot_general x0 -> x5, local copies, waits for them, and re-layouts: none -> 50.9 us  [the longest x2 24.6 us: dot_tn(): lax.dot_general(left, right, (((0,), (0,)), ((), ())), preferred_element_...]
    convert_element_type x10 -> x12, other arithmetic: 40.8 us -> 17.3 us  [the longest x5 10.4 us: add_swapped(): (keep.astype(jnp.float32) + came.astype(jnp.float32)).astype(jnp.bfloat16)]
  transfers between devices with their start and end apart: 19 -> 6, of which waited for: 13 -> 0; matrix products, arithmetic and copies ran while one was open for 21% -> 11% of each run, Pallas kernels for 0% -> 11%
where the time goes in v1:
time: 1030 us; the launch traced here: 1020 us
  Pallas kernels  647 us (63%)
  matrix products  154 us (15%)
  local copies, waits for them, and re-layouts  116 us (11%)
  other arithmetic  91.9 us (9%)
  starting transfers between devices  11.2 us (1%)
    pallas_call x11, Pallas kernels, run(): pl.pallas_call(kernel, in_specs=in_specs, out_specs=out_specs, out_shape=...  608 us
    dot_general x4, matrix products, dot_nt(): lax.dot_general(left, right, (((1,), (1,)), ((), ())), preferred_element_...  45.1 us
    dot_general x6, matrix products, dot_tt(): lax.dot_general(left, right, (((0,), (1,)), ((), ())), preferred_element_...  43 us
    dot_general x4, matrix products, dot_nn(): lax.dot_general(left, right, (((1,), (0,)), ((), ())), preferred_element_...  35.7 us
    dot_general x4, matrix products, dot_tn(): lax.dot_general(left, right, (((0,), (0,)), ((), ())), preferred_element_...  29.8 us
    unnamed x193, local copies, waits for them, and re-layouts  26.1 us
    dot_general x2, local copies, waits for them, and re-layouts, dot_tn(): lax.dot_general(left, right, (((0,), (0,)), ((), ())), preferred_element_...  24.6 us
    pallas_call x1, Pallas kernels, attn_bwd(): pl.pallas_call(functools.partial(attn_bwd_kernel, heads), grid_spec=pltpu...  22.3 us
  transfers between devices with their start and end apart: 6, of which 0 were waited for; matrix products, arithmetic and copies ran while one was open for 11% of the time, Pallas kernels for 11%

profile of v1, /device:TPU:0, one launch (start us, length us, event | category | flops | bytes accessed | tf_op | source)
XLA Modules:
  0.0 1023.1 jit_solution(4116982687338913773)
XLA Ops:
  5.6 27.9 %shard_map.365 = (bf16[32,80,128]{2,1,0:T(8,128)(2,1)}, bf16[4,1,512,256]{3,2,1,0:T(8,128)(2,1)}) custom-call(bf16[4,80,128]{2,1,0:T(8,128)(2,1)} %pad_maximum_fusion.5.refs_0_, bf16[1,512,256]{2,1,0:T(8,128)(2,1)} %convert_bitcast_fusion.2.refs_1_), custom_call_target="tpu_custom_call" | custom-call | tf_op jit(solution)/shard_map/pallas_call | solution.py:533
  43.5 87.1 %shard_map.366 = (bf16[8,256,2048]{2,1,0:T(8,128)(2,1)}, bf16[4,1,512,256]{3,2,1,0:T(8,128)(2,1)}, bf16[4,1,256,512]{3,2,1,0:T(8,128)(2,1)}, bf16[4,1,512,704]{3,2,1,0:T(8,128)(2,1)}) custom-call(bf16[256,2048]{1,0:T(8,128)(2,1)} %fusion.22.refs_0_, bf16[4,1,512,256]{3,2,1,0:T(8,128)(2,1)} %get-tuple-element.58.refs_1_, ...), custom_call_target="tpu_custom_call", output_to_operand_aliasing={{1}: (1, {})} | custom-call | tf_op jit(solution)/shard_map/pallas_call | solution.py:533
  130.6 6.4 fusion.79
  142.2 7.4 fusion.78
  151.9 3.6 copy.198
  158.0 12.5 %copy.193 = bf16[2048,2048]{1,0:T(8,128)(2,1)} copy(bf16[2048,2048]{0,1:T(8,128)(2,1)} %bitcast.253) | data formatting | bytes 16777216 | tf_op jit(solution)/shard_map/dot_general | solution.py:53
  175.4 76.4 %shard_map.367 = (bf16[8,256,2048]{2,1,0:T(8,128)(2,1)}, bf16[2,64,2048]{2,1,0:T(8,128)(2,1)}, bf16[4,1,256,512]{3,2,1,0:T(8,128)(2,1)}, bf16[4,1,512,704]{3,2,1,0:T(8,128)(2,1)}, bf16[4,1,512,704]{3,2,1,0:T(8,128)(2,1)}) custom-call(bf16[256,2048]{1,0:T(8,128)(2,1)} %refs_0_.1, ...), custom_call_target="tpu_custom_call", output_to_operand_aliasing={{2}: (2, {}), {3}: (3, {})} | custom-call | tf_op jit(solution)/shard_map/pallas_call | solution.py:533
  256.3 16.8 %shard_map.368 = (bf16[256,2048]{1,0:T(8,128)(2,1)S(1)}, f32[2,4,1024]{2,1,0:T(4,128)S(1)}) custom-call(s32[2,4]{1,0:T(2,128)S(1)} %slice.139.first_ref, s32[2,1,1024]{2,1,0:T(1,128)S(1)} %broadcast_in_dim.40.start_ref, bf16[256,2048]{1,0:T(8,128)(2,1)S(1)} %bitcast.249, bf16[2,64,2048]{2,1,0:T(8,128)(2,1)S(1)} %get-tuple-element.257.kt_ref, ...), custom_call_target="tpu_custom_call" | custom-call | tf_op jit(solution)/shard_map/pallas_call | solution.py:655
  273.2 5.7 convolution_convert_fusion.1.refs_0_
  278.9 61.3 %shard_map.369 = (f32[256,2048]{1,0:T(8,128)}, bf16[4,1,512,704]{3,2,1,0:T(8,128)(2,1)}, bf16[4,1,704,512]{3,2,1,0:T(8,128)(2,1)}) custom-call(bf16[2048,2048]{1,0:T(8,128)(2,1)} %convolution_convert_fusion.1.refs_0_, bf16[4,1,512,704]{3,2,1,0:T(8,128)(2,1)} %get-tuple-element.66.refs_1_, ...), custom_call_target="tpu_custom_call", output_to_operand_aliasing={{1}: (1, {})} | custom-call | tf_op jit(solution)/shard_map/pallas_call | solution.py:533
  344.8 51.4 %shard_map.370 = (bf16[8,256,2048]{2,1,0:T(8,128)(2,1)}, bf16[4,1,704,512]{3,2,1,0:T(8,128)(2,1)}) custom-call(bf16[256,2048]{1,0:T(8,128)(2,1)} %multiply_convert_fusion.3.refs_0_, bf16[4,1,704,512]{3,2,1,0:T(8,128)(2,1)} %get-tuple-element.68.refs_1_), custom_call_target="tpu_custom_call", output_to_operand_aliasing={{1}: (1, {})} | custom-call | tf_op jit(solution)/shard_map/pallas_call | solution.py:533
  396.2 11.4 %fusion.81 = f32[2048,704]{0,1:T(8,128)} fusion(bf16[2048,2048]{1,0:T(8,128)(2,1)} %bitcast.264, bf16[2048,704]{1,0:T(8,128)(2,1)S(1)} %bitcast.286), kind=kOutput, calls=%fused_computation.190 | convolution fusion | flops 5905580032 | bytes 17039360 | tf_op jit(solution)/shard_map/dot_general | solution.py:35
  407.7 8.3 fusion.80
  416.0 4.5 copy.233
  420.5 7.8 reshape.506
  428.3 12.3 %copy.186 = bf16[2048,2048]{1,0:T(8,128)(2,1)} copy(bf16[2048,2048]{0,1:T(8,128)(2,1)} %bitcast.262) | data formatting | bytes 16777216 | tf_op jit(solution)/shard_map/dot_general | solution.py:47
  440.6 15.7 %multiply_convert_fusion = (bf16[2048,704]{0,1:T(8,128)(2,1)}, bf16[2048,704]{0,1:T(8,128)(2,1)}, bf16[2048,704]{0,1:T(8,128)(2,1)S(1)}) fusion(f32[2048,704]{0,1:T(8,128)} %fusion.80, f32[2048,704]{0,1:T(8,128)} %fusion.81, bf16[2048,2048]{1,0:T(8,128)(2,1)} %bitcast.263, bf16[704,2048]{1,0:T(8,128)(2,1)} %reshape.506), kind=kOutput, calls=%fused_computation.4 | convolution fusion | flops 5927206912 | bytes 31457280 | tf_op jit(solution)/shard_map/dot_general | solution.py:41
  456.4 9.1 convolution_convert_fusion.refs_0_
  465.4 7.7 fusion.19
  473.1 12.3 %copy.187 = bf16[2048,2048]{1,0:T(8,128)(2,1)} copy(bf16[2048,2048]{0,1:T(8,128)(2,1)} %bitcast.265) | data formatting | bytes 16777216 | tf_op jit(solution)/shard_map/dot_general | solution.py:47
  485.4 13.1 %fusion.82 = f32[2048,2048]{1,0:T(8,128)} fusion(bf16[2048,704]{0,1:T(8,128)(2,1)} %get-tuple-element.246, bf16[2048,704]{1,0:T(8,128)(2,1)} %bitcast.284), kind=kOutput, calls=%fused_computation.191 | convolution fusion | flops 5905580032 | bytes 22544384 | tf_op jit(solution)/shard_map/dot_general | solution.py:41
  498.6 8.2 fusion.13.refs_1_
  506.8 8.2 fusion.16.refs_1_
  515.0 12.9 %add_convert_fusion.1.refs_0_ = bf16[2048,2048]{1,0:T(8,128)(2,1)} fusion(f32[2048,2048]{1,0:T(8,128)} %fusion.82, bf16[2048,704]{0,1:T(8,128)(2,1)S(1)} %copy-done.87, bf16[2048,704]{1,0:T(8,128)(2,1)S(1)} %bitcast.287), kind=kOutput, calls=%fused_computation.1 | convolution fusion | flops 5913968640 | bytes 30932992 | tf_op jit(solution)/shard_map/dot_general | solution.py:41
  527.9 45.5 %shard_map.371 = (f32[256,2048]{1,0:T(8,128)}, bf16[2,704,512]{2,1,0:T(8,128)(2,1)}) custom-call(bf16[2048,2048]{1,0:T(8,128)(2,1)} %convolution_convert_fusion.refs_0_, bf16[2,2,704,512]{3,2,1,0:T(8,128)(2,1)} %bitcast.273), custom_call_target="tpu_custom_call" | custom-call | tf_op jit(solution)/shard_map/pallas_call | solution.py:533
  573.4 2.9 fusion.6.refs_2_
  576.3 52.9 %shard_map.372 = (f32[256,2048]{1,0:T(8,128)}, bf16[2,512,704]{2,1,0:T(8,128)(2,1)}, bf16[2,704,512]{2,1,0:T(8,128)(2,1)}) custom-call(bf16[2048,2048]{1,0:T(8,128)(2,1)} %add_convert_fusion.1.refs_0_, bf16[2,2,512,704]{3,2,1,0:T(8,128)(2,1)} %fusion.13.refs_1_, bf16[2,704,512]{2,1,0:T(8,128)(2,1)} %fusion.6.refs_2_), custom_call_target="tpu_custom_call" | custom-call | tf_op jit(solution)/shard_map/pallas_call | solution.py:533
  629.2 3.1 fusion.3.refs_2_
  635.3 62.7 %shard_map.373 = (bf16[8,256,2048]{2,1,0:T(8,128)(2,1)}, bf16[2,512,704]{2,1,0:T(8,128)(2,1)}, bf16[2,512,704]{2,1,0:T(8,128)(2,1)}) custom-call(bf16[256,2048]{1,0:T(8,128)(2,1)} %fusion.69.refs_0_, bf16[2,2,512,704]{3,2,1,0:T(8,128)(2,1)} %fusion.16.refs_1_, bf16[2,512,704]{2,1,0:T(8,128)(2,1)} %fusion.3.refs_2_), custom_call_target="tpu_custom_call" | custom-call | tf_op jit(solution)/shard_map/pallas_call | solution.py:533
  698.0 12.4 %copy.192 = bf16[2048,2048]{1,0:T(8,128)(2,1)} copy(bf16[2048,2048]{0,1:T(8,128)(2,1)} %bitcast.267) | data formatting | bytes 16777216 | tf_op jit(solution)/shard_map/dot_general | solution.py:35
  710.5 6.9 convolution_convert_fusion.4
  718.9 3.4 convolution_convert_fusion.2.do_ref
  722.3 22.3 %shard_map.374 = (f32[256,2048]{1,0:T(8,128)}, f32[2,64,2048]{2,1,0:T(8,128)S(1)}, f32[2,64,2048]{2,1,0:T(8,128)S(1)}) custom-call(s32[2,4]{1,0:T(2,128)S(1)} %slice.139.first_ref, s32[2,1,1024]{2,1,0:T(1,128)S(1)} %broadcast_in_dim.40.start_ref, bf16[256,2048]{1,0:T(8,128)(2,1)S(1)} %bitcast.250, bf16[256,2048]{1,0:T(8,128)(2,1)S(1)} %copy-done.3, ...), custom_call_target="tpu_custom_call" | custom-call | tf_op jit(solution)/shard_map/pallas_call | solution.py:688
  748.5 63.8 %shard_map.375 = (bf16[2,64,2,1024]{3,2,1,0:T(2,128)(2,1)}, bf16[2,512,704]{2,1,0:T(8,128)(2,1)}, bf16[2,256,512]{2,1,0:T(8,128)(2,1)}) custom-call(bf16[2,64,2,1024]{3,2,1,0:T(2,128)(2,1)} %slice.308.refs_0_, bf16[2,512,704]{2,1,0:T(8,128)(2,1)} %fusion.2.refs_1_, bf16[2,2,256,512]{3,2,1,0:T(8,128)(2,1)} %bitcast.288), custom_call_target="tpu_custom_call" | custom-call | tf_op jit(solution)/shard_map/pallas_call | solution.py:533
  816.7 2.7 fusion.55
  822.4 8.2 fusion.83
  830.8 11.6 %add_convert_fusion.refs_0_ = bf16[2048,2048]{1,0:T(8,128)(2,1)} fusion(f32[2048,2048]{1,0:T(8,128)} %fusion.83, bf16[128,2048]{1,0:T(8,128)(2,1)S(1)} %bitcast.290, bf16[2048,128]{1,0:T(8,128)(2,1)S(1)} %bitcast.275), kind=kOutput, calls=%fused_computation | convolution fusion | flops 1082130432 | bytes 26214400 | tf_op jit(solution)/shard_map/dot_general | solution.py:53
  842.4 3.4 convolution_convert_fusion.3.refs_1_
  845.8 41.5 %shard_map.376 = (f32[256,2048]{1,0:T(8,128)}, bf16[2,512,256]{2,1,0:T(8,128)(2,1)}, bf16[2,256,512]{2,1,0:T(8,128)(2,1)}) custom-call(bf16[2048,2048]{1,0:T(8,128)(2,1)} %add_convert_fusion.refs_0_, bf16[2,2,512,256]{3,2,1,0:T(8,128)(2,1)} %convolution_convert_fusion.3.refs_1_, bf16[2,256,512]{2,1,0:T(8,128)(2,1)} %fusion.35.refs_2_), custom_call_target="tpu_custom_call" | custom-call | tf_op jit(solution)/shard_map/pallas_call | solution.py:533
  892.3 5.9 convolution_convert_fusion.5
  899.1 37.7 %shard_map.377 = (bf16[32,80,128]{2,1,0:T(8,128)(2,1)}, bf16[2,512,256]{2,1,0:T(8,128)(2,1)}) custom-call(bf16[32,80,128]{2,1,0:T(8,128)(2,1)} %pad_maximum_fusion.2.refs_0_, bf16[2,512,256]{2,1,0:T(8,128)(2,1)} %fusion.34.refs_1_), custom_call_target="tpu_custom_call" | custom-call | tf_op jit(solution)/shard_map/pallas_call | solution.py:533
  975.9 6.3 fusion.26
  984.4 3.2 multiply_subtract_fusion.2
  987.7 3.3 multiply_subtract_fusion.3
  1001.3 6.7 multiply_subtract_fusion
  1008.0 3.6 copy.206
  1013.8 3.6 copy.208
  1017.4 5.5 multiply_subtract_fusion.1
  (308 shorter events, 113.0 us)
Async XLA Ops:
  0.7 36.0 %copy-start.12 = (bf16[256,2048]{1,0:T(8,128)(2,1)S(1)}, bf16[256,2048]{1,0:T(8,128)(2,1)}, u32[]{:S(2)}) copy-start(bf16[256,2048]{1,0:T(8,128)(2,1)} %param.22) | copy-start | bytes 3145732
  0.7 169.8 %collective-permute-start = (s32[1,2048]{1,0:T(1,128)}, s32[1,2048]{1,0:T(1,128)}, u32[]{:S(2)}, u32[]{:S(2)}) collective-permute-start(s32[1,2048]{1,0:T(1,128)} %param.24), channel_id=1, source_target_pairs={{0,8},{8,0},{1,9},{9,1},{2,10},{10,2},{3,11},{11,3},{4,12},{12,4},... | collective-permute-start | bytes 24584 | tf_op jit(solution)/shard_map/ppermute | solution.py:848
  41.5 89.1 %copy-start.40 = (bf16[32,64,128]{2,1,0:T(8,128)(2,1)S(1)}, bf16[32,64,128]{2,1,0:T(8,128)(2,1)}, u32[]{:S(2)}) copy-start(bf16[32,64,128]{2,1,0:T(8,128)(2,1)} %slice.146) | copy-start | bytes 1572868
  130.6 9.2 copy-start.27
  151.2 191.1 %copy-start.69 = (f32[2048]{0:T(1024)}, f32[2048]{0:T(1024)S(1)}, u32[]{:S(2)}) copy-start(f32[2048]{0:T(1024)S(1)} %reshape.520) | copy-start | bytes 24580
  157.9 12.5 %copy-start.85 = (s32[1,2048]{1,0:T(1,128)S(1)}, s32[1,2048]{1,0:T(1,128)}, u32[]{:S(2)}) copy-start(s32[1,2048]{1,0:T(1,128)} %param.24) | copy-start | bytes 24580
  157.9 13.5 %copy-start.83 = (s32[1024]{0:T(1024)S(1)}, s32[1024]{0:T(1024)}, u32[]{:S(2)}) copy-start(s32[1024]{0:T(1024)} %iota_add_fusion) | copy-start | bytes 12292
  157.9 13.6 %copy-start.82 = (s32[1024]{0:T(1024)S(1)}, s32[1024]{0:T(1024)}, u32[]{:S(2)}) copy-start(s32[1024]{0:T(1024)} %iota_add_fusion.1) | copy-start | bytes 12292
  157.9 13.7 %copy-start.86 = (f32[32]{0:T(128)S(1)}, f32[32]{0:T(128)}, u32[]{:S(2)}) copy-start(f32[32]{0:T(128)} %multiply_power_fusion) | copy-start | bytes 388
  157.9 15.5 %copy-start.57 = (f32[1,64,2048]{2,1,0:T(8,128)S(1)}, f32[1,64,2048]{2,1,0:T(8,128)}, u32[]{:S(2)}) copy-start(f32[1,64,2048]{2,1,0:T(8,128)} %slice_bitcast_fusion.2) | copy-start | bytes 1572868
  158.0 16.6 %copy-start.62 = (bf16[1,64,2048]{2,1,0:T(8,128)(2,1)S(1)}, bf16[1,64,2048]{2,1,0:T(8,128)(2,1)}, u32[]{:S(2)}) copy-start(bf16[1,64,2048]{2,1,0:T(8,128)(2,1)} %slice_bitcast_fusion.3) | copy-start | bytes 786436
  171.6 80.2 %copy-start.73 = (f32[1,8,2,128]{3,1,2,0:T(8,128)}, f32[1,8,2,128]{3,1,2,0:T(8,128)S(1)}, u32[]{:S(2)}) copy-start(f32[1,8,2,128]{3,1,2,0:T(8,128)S(1)} %copy.240) | copy-start | bytes 24580
  173.4 80.4 %copy-start.51 = (f32[32,2048]{1,0:T(8,128)}, f32[32,2048]{1,0:T(8,128)S(1)}, u32[]{:S(2)}) copy-start(f32[32,2048]{1,0:T(8,128)S(1)} %get-tuple-element.262) | copy-start | bytes 786436
  175.4 76.6 %copy-start.64 = (bf16[1,64,2,1024]{3,1,2,0:T(8,128)(2,1)S(1)}, bf16[1,64,2,1024]{3,1,2,0:T(8,128)(2,1)}, u32[]{:S(2)}) copy-start(bf16[1,64,2,1024]{3,1,2,0:T(8,128)(2,1)} %copy.182) | copy-start | bytes 786436
  253.7 19.4 %copy-start.44 = (bf16[2,2,1,256,512]{3,4,1,0,2:T(8,128)(2,1)}, bf16[2,2,1,256,512]{3,4,1,0,2:T(8,128)(2,1)S(1)}, u32[]{:S(2)}) copy-start(bf16[2,2,1,256,512]{3,4,1,0,2:T(8,128)(2,1)S(1)} %copy.184) | copy-start | bytes 3145732
  256.3 22.6 %copy-start = (bf16[4,64,2048]{2,1,0:T(8,128)(2,1)}, bf16[4,64,2048]{2,1,0:T(8,128)(2,1)S(1)}, u32[]{:S(2)}) copy-start(bf16[4,64,2048]{2,1,0:T(8,128)(2,1)S(1)} %maximum_multiply_fusion) | copy-start | bytes 3145732
  278.9 61.3 %copy-start.14 = (bf16[256,2048]{1,0:T(8,128)(2,1)S(1)}, bf16[256,2048]{1,0:T(8,128)(2,1)}, u32[]{:S(2)}) copy-start(bf16[256,2048]{1,0:T(8,128)(2,1)} %param.22) | copy-start | bytes 3145732
  342.2 54.0 %copy-start.77 = (f32[256]{0:T(256)}, f32[256]{0:T(256)S(1)}, u32[]{:S(2)}) copy-start(f32[256]{0:T(256)S(1)} %add_rsqrt_fusion) | copy-start | bytes 3076
  343.5 52.7 %copy-start.47 = (bf16[4,1,512,704]{3,2,1,0:T(8,128)(2,1)S(1)}, bf16[4,1,512,704]{3,2,1,0:T(8,128)(2,1)}, u32[]{:S(2)}) copy-start(bf16[4,1,512,704]{3,2,1,0:T(8,128)(2,1)} %get-tuple-element.71) | copy-start | bytes 8650756
  396.2 11.5 %copy-start.30 = (bf16[8,256,2048]{2,1,0:T(8,128)(2,1)S(1)}, bf16[8,256,2048]{2,1,0:T(8,128)(2,1)}, u32[]{:S(2)}) copy-start(bf16[8,256,2048]{2,1,0:T(8,128)(2,1)} %get-tuple-element.69) | copy-start | bytes 25165828
  396.2 11.4 %copy-start.46 = (bf16[4,1,512,704]{3,2,1,0:T(8,128)(2,1)S(1)}, bf16[4,1,512,704]{3,2,1,0:T(8,128)(2,1)}, u32[]{:S(2)}) copy-start(bf16[4,1,512,704]{3,2,1,0:T(8,128)(2,1)} %get-tuple-element.70) | copy-start | bytes 8650756
  407.7 8.3 copy-start.26
  440.6 15.7 %copy-start.50 = (bf16[704,2048]{1,0:T(8,128)(2,1)S(1)}, bf16[704,2048]{1,0:T(8,128)(2,1)}, u32[]{:S(2)}) copy-start(bf16[704,2048]{1,0:T(8,128)(2,1)} %reshape.506) | copy-start | bytes 8650756
  456.3 9.1 copy-start.32
  485.4 13.1 %copy-start.33 = (bf16[2048,2048]{1,0:T(8,128)(2,1)S(1)}, bf16[2048,2048]{1,0:T(8,128)(2,1)}, u32[]{:S(2)}) copy-start(bf16[2048,2048]{1,0:T(8,128)(2,1)} %copy.187) | copy-start | bytes 25165828
  485.4 13.1 %copy-start.88 = (bf16[2048,704]{0,1:T(8,128)(2,1)S(1)}, bf16[2048,704]{0,1:T(8,128)(2,1)}, u32[]{:S(2)}) copy-start(bf16[2048,704]{0,1:T(8,128)(2,1)} %get-tuple-element.246) | copy-start | bytes 8650756
  498.6 8.2 copy-start.87
  527.9 45.5 %copy-start.38 = (bf16[704,2,2,512]{3,0,2,1:T(8,128)(2,1)S(1)}, bf16[704,2,2,512]{3,0,2,1:T(8,128)(2,1)}, u32[]{:S(2)}) copy-start(bf16[704,2,2,512]{3,0,2,1:T(8,128)(2,1)} %fusion.19) | copy-start | bytes 8650756
  576.3 53.0 %copy-start.35 = (bf16[2,2,512,704]{3,2,1,0:T(8,128)(2,1)S(1)}, bf16[2,2,512,704]{3,2,1,0:T(8,128)(2,1)}, u32[]{:S(2)}) copy-start(bf16[2,2,512,704]{3,2,1,0:T(8,128)(2,1)} %fusion.13.refs_1_) | copy-start | bytes 8650756
  698.0 12.4 %copy-start.3 = (bf16[256,2048]{1,0:T(8,128)(2,1)S(1)}, bf16[256,2048]{1,0:T(8,128)(2,1)}, u32[]{:S(2)}) copy-start(bf16[256,2048]{1,0:T(8,128)(2,1)} %copy-done.2) | copy-start | bytes 3145732
  710.5 8.4 copy-start.31
  822.4 8.3 copy-start.63
  822.4 8.3 copy-start.68
  822.4 8.3 copy-start.41
  822.4 20.0 %slice-start = ((s8[8388608]{0:T(1024)(128)(4,1)}), s8[4194304]{0:T(1024)(128)(4,1)S(1)}, s32[]{:S(2)}) async-start(s8[8388608]{0:T(1024)(128)(4,1)} %bitcast.259), calls=%async_computation | async-start | bytes 8388608
  830.7 11.7 %copy-start.56 = (bf16[2,64,2048]{2,1,0:T(8,128)(2,1)}, bf16[2,64,2048]{2,1,0:T(8,128)(2,1)S(1)}, u32[]{:S(2)}) copy-start(bf16[2,64,2048]{2,1,0:T(8,128)(2,1)S(1)} %pad_maximum_fusion.4) | copy-start | bytes 1572868
  830.7 11.7 %slice-start.1 = ((s8[8388608]{0:T(1024)(128)(4,1)}), s8[4194304]{0:T(1024)(128)(4,1)S(1)}, s32[]{:S(2)}) async-start(s8[8388608]{0:T(1024)(128)(4,1)} %bitcast.259), calls=%async_computation.1 | async-start | bytes 8388608
  845.8 41.5 %copy-start.55 = (bf16[2,2,512,256]{3,2,1,0:T(8,128)(2,1)S(1)}, bf16[2,2,512,256]{3,2,1,0:T(8,128)(2,1)}, u32[]{:S(2)}) copy-start(bf16[2,2,512,256]{3,2,1,0:T(8,128)(2,1)} %convolution_convert_fusion.3.refs_1_) | copy-start | bytes 3145732
  845.8 43.5 %copy-start.15 = (bf16[256,2048]{1,0:T(8,128)(2,1)S(1)}, bf16[256,2048]{1,0:T(8,128)(2,1)}, u32[]{:S(2)}) copy-start(bf16[256,2048]{1,0:T(8,128)(2,1)} %param.22) | copy-start | bytes 3145732
  845.8 43.5 %copy-start.72 = (f32[2048]{0:T(1024)S(1)}, f32[2048]{0:T(1024)}, u32[]{:S(2)}) copy-start(f32[2048]{0:T(1024)} %copy-done.71) | copy-start | bytes 24580
  845.8 43.5 %copy-start.80 = (f32[256]{0:T(256)S(1)}, f32[256]{0:T(256)}, u32[]{:S(2)}) copy-start(f32[256]{0:T(256)} %copy-done.79) | copy-start | bytes 3076
  899.1 42.1 %copy-start.23 = (bf16[2,704,512]{2,1,0:T(8,128)(2,1)S(1)}, bf16[2,704,512]{2,1,0:T(8,128)(2,1)}, u32[]{:S(2)}) copy-start(bf16[2,704,512]{2,1,0:T(8,128)(2,1)} %fusion.6.refs_2_) | copy-start | bytes 4325380
  899.1 42.1 %copy-start.61 = (bf16[2,704,512]{2,1,0:T(8,128)(2,1)S(1)}, bf16[2,704,512]{2,1,0:T(8,128)(2,1)}, u32[]{:S(2)}) copy-start(bf16[2,704,512]{2,1,0:T(8,128)(2,1)} %get-tuple-element.93) | copy-start | bytes 4325380
  942.7 74.7 %collective-permute-start.5 = (bf16[704,512]{1,0:T(8,128)(2,1)}, bf16[704,512]{1,0:T(8,128)(2,1)}, u32[]{:S(2)}, u32[]{:S(2)}) collective-permute-start(bf16[704,512]{1,0:T(8,128)(2,1)} %fusion.39), channel_id=1, source_target_pairs={{0,8},{12,4},{1,9},{13,5},{2,10},{14,6},{3,11},{15,7},{16,24},{28,... | collective-permute-start | bytes 2162696 | tf_op jit(solution)/shard_map/ppermute | solution.py:83
  950.3 40.7 %collective-permute-start.3 = (bf16[512,704]{0,1:T(8,128)(2,1)}, bf16[512,704]{0,1:T(8,128)(2,1)}, u32[]{:S(2)}, u32[]{:S(2)}) collective-permute-start(bf16[512,704]{0,1:T(8,128)(2,1)} %copy.199), channel_id=1, source_target_pairs={{0,8},{12,4},{1,9},{13,5},{2,10},{14,6},{3,11},{15,7},{16,24},{28,... | collective-permute-start | bytes 2162696 | tf_op jit(solution)/shard_map/ppermute | solution.py:83
  959.6 36.2 %collective-permute-start.4 = (bf16[512,704]{0,1:T(8,128)(2,1)}, bf16[512,704]{0,1:T(8,128)(2,1)}, u32[]{:S(2)}, u32[]{:S(2)}) collective-permute-start(bf16[512,704]{0,1:T(8,128)(2,1)} %copy.201), channel_id=1, source_target_pairs={{0,8},{12,4},{1,9},{13,5},{2,10},{14,6},{3,11},{15,7},{16,24},{28,... | collective-permute-start | bytes 2162696 | tf_op jit(solution)/shard_map/ppermute | solution.py:83
  964.1 20.3 %collective-permute-start.2 = (bf16[256,512]{1,0:T(8,128)(2,1)}, bf16[256,512]{1,0:T(8,128)(2,1)}, u32[]{:S(2)}, u32[]{:S(2)}) collective-permute-start(bf16[256,512]{1,0:T(8,128)(2,1)} %fusion.59), channel_id=1, source_target_pairs={{0,8},{12,4},{1,9},{13,5},{2,10},{14,6},{3,11},{15,7},{16,24},{28,... | collective-permute-start | bytes 786440 | tf_op jit(solution)/shard_map/ppermute | solution.py:83
  967.9 19.7 %collective-permute-start.1 = (bf16[512,256]{1,0:T(8,128)(2,1)}, bf16[512,256]{1,0:T(8,128)(2,1)}, u32[]{:S(2)}, u32[]{:S(2)}) collective-permute-start(bf16[512,256]{1,0:T(8,128)(2,1)} %fusion.58), channel_id=1, source_target_pairs={{0,8},{12,4},{1,9},{13,5},{2,10},{14,6},{3,11},{15,7},{16,24},{28,... | collective-permute-start | bytes 786440 | tf_op jit(solution)/shard_map/ppermute | solution.py:83
  (49 other events, 189.9 us)

commit v2 on v1

--- a/solution.py
+++ b/solution.py
@@ -75,13 +75,62 @@
     return (keep.astype(jnp.float32) + came.astype(jnp.float32)).astype(jnp.bfloat16)
 
 
-def to_owners(part, deep):
-    total = part.astype(jnp.float32) + deep.astype(jnp.float32)
-    first = lax.axis_index("c") == 0
-    mine = jnp.where(first, total[0], total[1])
-    partners = jnp.where(first, total[1], total[0]).astype(jnp.bfloat16)
-    got = lax.ppermute(partners, ("c", "zh"), TO_AWAY_CORE)
-    return jnp.where(lax.axis_index("c") == lax.axis_index("zh"), mine, got.astype(jnp.float32))
+def for_partner(part, deep):
+    at = 1 - lax.axis_index("c")
+    pick = lambda a: lax.dynamic_index_in_dim(a, at, 0, keepdims=False).astype(jnp.float32)
+    return (pick(part) + pick(deep)).astype(jnp.bfloat16)
+
+
+def adam_kernel(rate, decay, groups, place_ref, fix_ref, w_ref, m_ref, v_ref, *refs):
+    grads, (w_out, m_out, v_out) = refs[: 3 * groups], refs[3 * groups :]
+    home = place_ref[1] == 1
+    grad = None
+    for n in range(groups):
+        part, deep, got = grads[3 * n : 3 * n + 3]
+        mine = part[0].astype(jnp.float32) + deep[0].astype(jnp.float32)
+        found = jnp.where(home, mine, got[...].astype(jnp.float32))
+        grad = found if n == 0 else jnp.where(pl.program_id(0) == n, found, grad)
+    first_new = BETA_ONE * m_ref[0] + (1.0 - BETA_ONE) * grad
+    second_new = BETA_TWO * v_ref[0] + (1.0 - BETA_TWO) * grad * grad
+    update = first_new / fix_ref[0] / (jnp.sqrt(second_new / fix_ref[1]) + ADAM_EPS)
+    weight = w_ref[0]
+    w_out[0] = weight - rate * (update + decay * weight)
+    m_out[0] = first_new
+    v_out[0] = second_new
+
+
+def adam_shard(weight, first, second, grads, rate, fixes):
+    groups, rows, cols = weight.shape
+    size = min(rows, 128)
+    while rows % size:
+        size //= 2
+    steps = rows // size
+    place = jnp.stack([lax.axis_index("c"), (lax.axis_index("c") == lax.axis_index("zh"))])
+    state = pl.BlockSpec((1, size, cols), lambda g, i, s: (g, i, 0))
+
+    def at(n):
+        if groups == 1:
+            return lambda g, i: i
+        return lambda g, i: jnp.where(g == n, i, jnp.where(g < n, 0, steps - 1))
+
+    specs, arrays = [], []
+    for n, (part, deep, got) in enumerate(grads):
+        where = at(n)
+        half = pl.BlockSpec((1, size, cols), lambda g, i, s, f=where: (s[0], f(g, i), 0))
+        specs += [half, half, pl.BlockSpec((size, cols), lambda g, i, s, f=where: (f(g, i), 0))]
+        arrays += [part, deep, got]
+    kind = jax.ShapeDtypeStruct(weight.shape, jnp.float32)
+    return pl.pallas_call(
+        functools.partial(adam_kernel, rate, DECAY, groups),
+        grid_spec=pltpu.PrefetchScalarGridSpec(
+            num_scalar_prefetch=1,
+            grid=(groups, steps),
+            in_specs=[pl.BlockSpec(memory_space=pltpu.SMEM)] + [state] * 3 + specs,
+            out_specs=[state] * 3,
+        ),
+        out_shape=[kind] * 3,
+        compiler_params=pltpu.CompilerParams(vmem_limit_bytes=32 * 2**20),
+    )(place.astype(jnp.int32), fixes, weight, first, second, *arrays)
 
 
 MESH_ID = pl.DeviceIdType.MESH
@@ -244,11 +293,12 @@
 
 
 class GatherRows:
-    def __init__(self, block):
+    def __init__(self, block, along_x=False):
         self.inputs = [block]
         self.outputs = [jax.ShapeDtypeStruct((8,) + block.shape, block.dtype)]
-        self.sems = [(7, CHUNKS), (8, CHUNKS)]
+        self.sems = [(7, CHUNKS), (8, CHUNKS), 1]
         self.alias = {}
+        self.along_x = along_x
 
     def places(self):
         return tuple(lax.axis_index(a) for a in ("c", "zl", "x"))
@@ -258,7 +308,7 @@
         return ref.at[pl.ds(k * rows, rows)]
 
     def begin(self, ins, outs, sems):
-        (src,), (dst,), (send, recv) = ins, outs, sems
+        (src,), (dst,), (send, recv, local) = ins, outs, sems
         core, z_low, x_at = self.places()
         own = group_index(core, z_low, x_at)
         for k in range(CHUNKS):
@@ -270,25 +320,26 @@
                     recv.at[own, k],
                     flipped(axis),
                 ).start()
+        pltpu.make_async_copy(src, dst.at[own], local.at[0]).start()
 
     def finish(self, ins, outs, sems):
-        (src,), (dst,), (send, recv) = ins, outs, sems
+        (src,), (dst,), (send, recv, local) = ins, outs, sems
         core, z_low, x_at = self.places()
         own = group_index(core, z_low, x_at)
         beside = group_index(core, z_low, 1 - x_at)
         below = group_index(core, 1 - z_low, x_at)
         across = group_index(core, 1 - z_low, 1 - x_at)
-        turn = jnp.where(core == 0, below, beside)
+        by_x = True if self.along_x else core == 0
+        turn = jnp.where(by_x, below, beside)
         onward = {
-            "x": jnp.where(core == 0, 1 - x_at, x_at),
-            "zl": jnp.where(core == 0, z_low, 1 - z_low),
+            "x": jnp.where(by_x, 1 - x_at, x_at),
+            "zl": jnp.where(by_x, z_low, 1 - z_low),
         }
 
         def pass_on(block, k, way, device):
             part = self.part(dst.at[block], k)
             return far_copy(part, part, send.at[way, k], recv.at[block, k], device)
 
-        pltpu.sync_copy(src, dst.at[own])
         for k in range(CHUNKS):
             pass_on(beside, k, 0, flipped("x")).wait_recv()
             pass_on(below, k, 0, flipped("x")).wait_recv()
@@ -305,6 +356,7 @@
                     pass_on(block, k, 0, flipped("c")).wait_recv()
             for way in range(7):
                 pass_on(own, k, way, flipped("c")).wait_send()
+        pltpu.make_async_copy(src, dst.at[own], local.at[0]).wait()
 
 
 class ScatterRows:
@@ -869,7 +921,7 @@
     normed_one = (inputs * inverse_one * gain_attn).astype(jnp.bfloat16)
     rows_one, query_parts, output_parts, gate_parts = run(
         1,
-        GatherRows(normed_one),
+        GatherRows(normed_one, along_x=True),
         Pass(query_parts),
         Spread(own_shard(output_weight, h_size)),
         Spread(own_shard(gateup_weight[0], h_size)),
@@ -888,7 +940,7 @@
     pair_rot = jnp.concatenate([key_rot, pair_pre[1:].astype(jnp.bfloat16)])
     grad_rows, pair_back_half, output_parts, gate_parts, up_parts = run(
         2,
-        GatherRows(out_grad),
+        GatherRows(out_grad, along_x=True),
         Move(pair_rot, "zh", lambda: lax.axis_index("zh") == 0),
         Pass(output_parts),
         Pass(gate_parts),
@@ -953,11 +1005,12 @@
     gate_part = add_swapped(gate_wgrad, gate_came)
     mid_back, gain_mlp_grad = norm_back(normed_two_grad, residual_mid, inverse_two, gain_mlp)
     mid_grad = out_grad.astype(jnp.float32) + mid_back
-    attn_grad_rows, up_came, gate_deep = run(
+    attn_grad_rows, up_came, gate_deep, down_got = run(
         7,
         GatherRows(mid_grad.astype(jnp.bfloat16)),
         Swap(up_wgrad),
         Move(gate_part, "zh", not_home),
+        Move(for_partner(down_part, down_deep), "c", at_home),
     )
     attn_grad_rows = attn_grad_rows.reshape(group_rows, D)
     up_part = add_swapped(up_wgrad, up_came)
@@ -972,7 +1025,7 @@
         .reshape(heads_here * HD, group_rows)
     )
     pair_grads = jnp.stack([key_grads, value_grads]).transpose(0, 2, 1, 3)
-    pair_later, up_deep, output_came = run(
+    pair_later, up_deep, output_came, gate_got = run(
         8,
         Move(
             pair_grads[..., :KEYS_BACK].astype(jnp.bfloat16),
@@ -981,6 +1034,7 @@
         ),
         Move(up_part, "zh", not_home),
         Swap(output_grad),
+        Move(for_partner(gate_part, gate_deep), "c", at_home),
     )
     output_part = add_swapped(output_grad, output_came)
     pair_later = jnp.where(z_high == 0, pair_later, 0).astype(jnp.float32)
@@ -991,13 +1045,14 @@
     pair_back = pair_back.reshape(2 * HD, group_rows)
     query_wgrad = halves(as_row_blocks(dot_tt(rows_one, query_back), h_size), h_size)
     pair_wgrad = dot_tt(rows_one, pair_back)
-    normed_one_grad, query_came, output_deep = run(
+    normed_one_grad, query_came, output_deep, up_got = run(
         9,
         ScatterRows(
             (dot_tt(query_back, query_full) + dot_tt(pair_back, pair_proj)).astype(jnp.bfloat16)
         ),
         Swap(query_wgrad),
         Move(output_part, "zh", not_home),
+        Move(for_partner(up_part, up_deep), "c", at_home),
     )
     query_part = add_swapped(query_wgrad, query_came)
     input_back, gain_attn_grad = norm_back(normed_one_grad, inputs, inverse_one, gain_attn)
@@ -1012,11 +1067,13 @@
         ],
         axis=1,
     ).astype(jnp.bfloat16)
-    small_sums, query_deep = run(
+    small_sums, query_deep, output_got = run(
         10,
         Everyone(small_grads, lambda device: device, devices),
         Move(query_part, "zh", not_home),
-    )
+        Move(for_partner(output_part, output_deep), "c", at_home),
+    )
+    query_got = lax.ppermute(for_partner(query_part, query_deep), ("c", "zh"), TO_AWAY_CORE)
     small_sums = small_sums.astype(jnp.float32)
     pair_sums = (
         small_sums[:, :pair_rows]
@@ -1032,13 +1089,40 @@
         .reshape(pad_rows * 2 * HD)[: 2 * gain_cols]
         .reshape(2, gain_cols)
     )
-    query_sum = to_owners(query_part, query_deep)
-    output_sum = to_owners(output_part, output_deep)
-    gateup_sum = jnp.stack([to_owners(gate_part, gate_deep), to_owners(up_part, up_deep)])
-    down_sum = to_owners(down_part, down_deep)
     step_value = step_count[0].astype(jnp.float32)
-    query_new, query_mone, query_mtwo = adam_step(
-        query_weight, query_sum, query_first, query_second, D ** (-0.5), DECAY, step_value
+    fixes = jnp.stack(
+        [
+            1.0 - jnp.power(jnp.float32(BETA_ONE), step_value),
+            1.0 - jnp.power(jnp.float32(BETA_TWO), step_value),
+        ]
+    )
+
+    def adam(weight, first, second, rate, *grads):
+        shape = weight.shape
+        three = lambda a: a.reshape((-1,) + shape[-2:])
+        new = adam_shard(three(weight), three(first), three(second), grads, rate, fixes)
+        return tuple(a.reshape(shape) for a in new)
+
+    down_new, down_mone, down_mtwo = adam(
+        down_weight, down_first, down_second, FF ** (-0.5), (down_part, down_deep, down_got)
+    )
+    gateup_new, gateup_mone, gateup_mtwo = adam(
+        gateup_weight,
+        gateup_first,
+        gateup_second,
+        D ** (-0.5),
+        (gate_part, gate_deep, gate_got),
+        (up_part, up_deep, up_got),
+    )
+    output_new, output_mone, output_mtwo = adam(
+        output_weight,
+        output_first,
+        output_second,
+        (H * HD // 16) ** (-0.5),
+        (output_part, output_deep, output_got),
+    )
+    query_new, query_mone, query_mtwo = adam(
+        query_weight, query_first, query_second, D ** (-0.5), (query_part, query_deep, query_got)
     )
     pair_new, pair_mone, pair_mtwo = adam_step(
         keyvalue_weight,
@@ -1048,21 +1132,6 @@
         D ** (-0.5),
         DECAY,
         step_value,
-    )
-    output_new, output_mone, output_mtwo = adam_step(
-        output_weight,
-        output_sum,
-        output_first,
-        output_second,
-        (H * HD // 16) ** (-0.5),
-        DECAY,
-        step_value,
-    )
-    gateup_new, gateup_mone, gateup_mtwo = adam_step(
-        gateup_weight, gateup_sum, gateup_first, gateup_second, D ** (-0.5), DECAY, step_value
-    )
-    down_new, down_mone, down_mtwo = adam_step(
-        down_weight, down_sum, down_first, down_second, FF ** (-0.5), DECAY, step_value
     )
     gains_new, gains_mone, gains_mtwo = adam_step(
         norm_gains, gains_sum, gains_first, gains_second, GAIN_RATE, 0.0, step_value

time: 1030 us -> 992 us (0.963)
  other arithmetic: 91.9 us -> 64.5 us
  Pallas kernels: 647 us -> 630 us
    pallas_call x11, Pallas kernels: 608 us -> 571 us  [run(): pl.pallas_call(kernel, in_specs=in_specs, out_specs=out_specs, out_shape=...]
    sub x6 -> x2, other arithmetic: 20.9 us -> 1.39 us  [adam_step(): return (weight - rate * (update + decay * weight), first_new, second_new)]
    pallas_call x0 -> x4, Pallas kernels: none -> 19.4 us  [adam_shard(): pl.pallas_call(functools.partial(adam_kernel, rate, DECAY, groups), grid_...]
    unnamed x193 -> x217, local copies, waits for them, and re-layouts: 26.1 us -> 32.2 us
  transfers between devices with their start and end apart: 6 -> 2, of which waited for: 0 -> 0; matrix products, arithmetic and copies ran while one was open for 11% -> 8% of each run, Pallas kernels for 11% -> 12%
where the time goes in v2:
time: 992 us; the launch traced here: 978 us
  Pallas kernels  630 us (64%)
  matrix products  158 us (16%)
  local copies, waits for them, and re-layouts  121 us (12%)
  other arithmetic  64.5 us (7%)
    pallas_call x11, Pallas kernels, run(): pl.pallas_call(kernel, in_specs=in_specs, out_specs=out_specs, out_shape=...  571 us
    dot_general x4, matrix products, dot_nt(): lax.dot_general(left, right, (((1,), (1,)), ((), ())), preferred_element_...  48.3 us
    dot_general x6, matrix products, dot_tt(): lax.dot_general(left, right, (((0,), (1,)), ((), ())), preferred_element_...  43.9 us
    dot_general x4, matrix products, dot_nn(): lax.dot_general(left, right, (((1,), (0,)), ((), ())), preferred_element_...  35.9 us
    unnamed x217, local copies, waits for them, and re-layouts  32.2 us
    dot_general x4, matrix products, dot_tn(): lax.dot_general(left, right, (((0,), (0,)), ((), ())), preferred_element_...  29.9 us
    dot_general x2, local copies, waits for them, and re-layouts, dot_tn(): lax.dot_general(left, right, (((0,), (0,)), ((), ())), preferred_element_...  24.6 us
    pallas_call x1, Pallas kernels, attn_bwd(): pl.pallas_call(functools.partial(attn_bwd_kernel, heads), grid_spec=pltpu...  22.3 us
  transfers between devices with their start and end apart: 2, of which 0 were waited for; matrix products, arithmetic and copies ran while one was open for 8% of the time, Pallas kernels for 12%

profile of v2, /device:TPU:0, one launch (start us, length us, event | category | flops | bytes accessed | tf_op | source)
XLA Modules:
  0.0 978.1 jit_solution(3308062764613464962)
XLA Ops:
  5.6 27.9 %shard_map.365 = (bf16[32,80,128]{2,1,0:T(8,128)(2,1)}, bf16[4,1,512,256]{3,2,1,0:T(8,128)(2,1)}) custom-call(bf16[4,80,128]{2,1,0:T(8,128)(2,1)} %pad_maximum_fusion.4.refs_0_, bf16[1,512,256]{2,1,0:T(8,128)(2,1)} %convert_bitcast_fusion.2.refs_1_), custom_call_target="tpu_custom_call" | custom-call | tf_op jit(solution)/shard_map/pallas_call | solution.py:585
  42.8 71.7 %shard_map.366 = (bf16[8,256,2048]{2,1,0:T(8,128)(2,1)}, bf16[4,1,512,256]{3,2,1,0:T(8,128)(2,1)}, bf16[4,1,256,512]{3,2,1,0:T(8,128)(2,1)}, bf16[4,1,512,704]{3,2,1,0:T(8,128)(2,1)}) custom-call(bf16[256,2048]{1,0:T(8,128)(2,1)} %fusion.21.refs_0_, bf16[4,1,512,256]{3,2,1,0:T(8,128)(2,1)} %get-tuple-element.74.refs_1_, ...), custom_call_target="tpu_custom_call", output_to_operand_aliasing={{1}: (1, {})} | custom-call | tf_op jit(solution)/shard_map/pallas_call | solution.py:585
  114.6 6.3 fusion.69
  128.1 7.4 fusion.68
  139.4 12.0 %copy.155 = bf16[2048,2048]{1,0:T(8,128)(2,1)} copy(bf16[2048,2048]{0,1:T(8,128)(2,1)} %bitcast.246) | data formatting | bytes 16777216 | tf_op jit(solution)/shard_map/dot_general | solution.py:53
  151.3 3.5 copy.161.m_ref
  154.8 3.6 copy.162.v_ref
  164.5 59.8 %shard_map.367 = (bf16[8,256,2048]{2,1,0:T(8,128)(2,1)}, bf16[2,64,2048]{2,1,0:T(8,128)(2,1)}, bf16[4,1,256,512]{3,2,1,0:T(8,128)(2,1)}, bf16[4,1,512,704]{3,2,1,0:T(8,128)(2,1)}, bf16[4,1,512,704]{3,2,1,0:T(8,128)(2,1)}) custom-call(bf16[256,2048]{1,0:T(8,128)(2,1)} %refs_0_.1, ...), custom_call_target="tpu_custom_call", output_to_operand_aliasing={{2}: (2, {}), {3}: (3, {})} | custom-call | tf_op jit(solution)/shard_map/pallas_call | solution.py:585
  230.2 16.8 %shard_map.368 = (bf16[256,2048]{1,0:T(8,128)(2,1)S(1)}, f32[2,4,1024]{2,1,0:T(4,128)S(1)}) custom-call(s32[2,4]{1,0:T(2,128)S(1)} %slice.99.first_ref, s32[2,1,1024]{2,1,0:T(1,128)S(1)} %broadcast_in_dim.40.start_ref, bf16[256,2048]{1,0:T(8,128)(2,1)S(1)} %bitcast.233, bf16[2,64,2048]{2,1,0:T(8,128)(2,1)S(1)} %copy-done.17, bf16[2,64,2048]{2,1,0:T(8,128)(2,1)S(1)} %copy-done.15), custom_call_target="tpu_custom_call" | custom-call | tf_op jit(solution)/shard_map/pallas_call | solution.py:707
  247.0 5.7 convolution_convert_fusion.1.refs_0_
  252.8 66.8 %shard_map.369 = (f32[256,2048]{1,0:T(8,128)}, bf16[4,1,512,704]{3,2,1,0:T(8,128)(2,1)}, bf16[4,1,704,512]{3,2,1,0:T(8,128)(2,1)}) custom-call(bf16[2048,2048]{1,0:T(8,128)(2,1)} %convolution_convert_fusion.1.refs_0_, bf16[4,1,512,704]{3,2,1,0:T(8,128)(2,1)} %get-tuple-element.82.refs_1_, ...), custom_call_target="tpu_custom_call", output_to_operand_aliasing={{1}: (1, {})} | custom-call | tf_op jit(solution)/shard_map/pallas_call | solution.py:585
  324.0 41.3 %shard_map.370 = (bf16[8,256,2048]{2,1,0:T(8,128)(2,1)}, bf16[4,1,704,512]{3,2,1,0:T(8,128)(2,1)}) custom-call(bf16[256,2048]{1,0:T(8,128)(2,1)} %multiply_convert_fusion.3.refs_0_, bf16[4,1,704,512]{3,2,1,0:T(8,128)(2,1)} %get-tuple-element.84.refs_1_), custom_call_target="tpu_custom_call", output_to_operand_aliasing={{1}: (1, {})} | custom-call | tf_op jit(solution)/shard_map/pallas_call | solution.py:585
  365.3 11.4 %fusion.71 = f32[2048,704]{0,1:T(8,128)} fusion(bf16[2048,2048]{1,0:T(8,128)(2,1)} %bitcast.257, bf16[2048,704]{1,0:T(8,128)(2,1)S(1)} %bitcast.279), kind=kOutput, calls=%fused_computation.163 | convolution fusion | flops 5905580032 | bytes 17039360 | tf_op jit(solution)/shard_map/dot_general | solution.py:35
  376.7 8.3 fusion.70
  385.0 4.5 copy.190
  389.5 8.0 reshape.557
  397.6 12.3 %copy.148 = bf16[2048,2048]{1,0:T(8,128)(2,1)} copy(bf16[2048,2048]{0,1:T(8,128)(2,1)} %bitcast.255) | data formatting | bytes 16777216 | tf_op jit(solution)/shard_map/dot_general | solution.py:47
  409.9 15.7 %multiply_convert_fusion = (bf16[2048,704]{0,1:T(8,128)(2,1)}, bf16[2048,704]{0,1:T(8,128)(2,1)}, bf16[2048,704]{0,1:T(8,128)(2,1)S(1)}) fusion(f32[2048,704]{0,1:T(8,128)} %fusion.70, f32[2048,704]{0,1:T(8,128)} %fusion.71, bf16[2048,2048]{1,0:T(8,128)(2,1)} %bitcast.256, bf16[704,2048]{1,0:T(8,128)(2,1)} %reshape.557), kind=kOutput, calls=%fused_computation.4 | convolution fusion | flops 5927206912 | bytes 31457280 | tf_op jit(solution)/shard_map/dot_general | solution.py:41
  425.6 9.1 convolution_convert_fusion.refs_0_
  434.7 7.7 fusion.18
  442.4 12.3 %copy.149 = bf16[2048,2048]{1,0:T(8,128)(2,1)} copy(bf16[2048,2048]{0,1:T(8,128)(2,1)} %bitcast.258) | data formatting | bytes 16777216 | tf_op jit(solution)/shard_map/dot_general | solution.py:47
  454.6 13.1 %fusion.72 = f32[2048,2048]{1,0:T(8,128)} fusion(bf16[2048,704]{0,1:T(8,128)(2,1)} %get-tuple-element.246, bf16[2048,704]{1,0:T(8,128)(2,1)} %bitcast.277), kind=kOutput, calls=%fused_computation.164 | convolution fusion | flops 5905580032 | bytes 22544384 | tf_op jit(solution)/shard_map/dot_general | solution.py:41
  467.7 8.3 fusion.12.refs_1_
  476.0 8.2 fusion.15.refs_1_
  484.2 12.7 %add_convert_fusion.1.refs_0_ = bf16[2048,2048]{1,0:T(8,128)(2,1)} fusion(f32[2048,2048]{1,0:T(8,128)} %fusion.72, bf16[2048,704]{0,1:T(8,128)(2,1)S(1)} %copy-done.99, bf16[2048,704]{1,0:T(8,128)(2,1)S(1)} %bitcast.280), kind=kOutput, calls=%fused_computation.1 | convolution fusion | flops 5913968640 | bytes 30932992 | tf_op jit(solution)/shard_map/dot_general | solution.py:41
  496.9 44.7 %shard_map.371 = (f32[256,2048]{1,0:T(8,128)}, bf16[2,704,512]{2,1,0:T(8,128)(2,1)}) custom-call(bf16[2048,2048]{1,0:T(8,128)(2,1)} %convolution_convert_fusion.refs_0_, bf16[2,2,704,512]{3,2,1,0:T(8,128)(2,1)} %bitcast.266), custom_call_target="tpu_custom_call" | custom-call | tf_op jit(solution)/shard_map/pallas_call | solution.py:585
  541.6 2.9 fusion.5.refs_2_.refs_0_
  544.4 53.3 %shard_map.372 = (f32[256,2048]{1,0:T(8,128)}, bf16[2,512,704]{2,1,0:T(8,128)(2,1)}, bf16[2,704,512]{2,1,0:T(8,128)(2,1)}) custom-call(bf16[2048,2048]{1,0:T(8,128)(2,1)} %add_convert_fusion.1.refs_0_, bf16[2,2,512,704]{3,2,1,0:T(8,128)(2,1)} %fusion.12.refs_1_, bf16[2,704,512]{2,1,0:T(8,128)(2,1)} %fusion.5.refs_2_.refs_0_), custom_call_target="tpu_custom_call" | custom-call | tf_op jit(solution)/shard_map/pallas_call | solution.py:585
  597.8 3.1 fusion.2.refs_2_.refs_0_
  605.1 62.1 %shard_map.373 = (bf16[8,256,2048]{2,1,0:T(8,128)(2,1)}, bf16[2,512,704]{2,1,0:T(8,128)(2,1)}, bf16[2,512,704]{2,1,0:T(8,128)(2,1)}, bf16[704,512]{1,0:T(8,128)(2,1)}) custom-call(bf16[256,2048]{1,0:T(8,128)(2,1)} %fusion.63.refs_0_, bf16[2,2,512,704]{3,2,1,0:T(8,128)(2,1)} %fusion.15.refs_1_, bf16[2,512,704]{2,1,0:T(8,128)(2,1)} %fusion.2.refs_2_.refs_0_, ...), custom_call_target="tpu_custom_call" | custom-call | tf_op jit(solution)/shard_map/pallas_call | solution.py:585
  669.4 12.3 %copy.154 = bf16[2048,2048]{1,0:T(8,128)(2,1)} copy(bf16[2048,2048]{0,1:T(8,128)(2,1)} %bitcast.260) | data formatting | bytes 16777216 | tf_op jit(solution)/shard_map/dot_general | solution.py:35
  681.7 7.2 convolution_convert_fusion.4
  690.4 6.9 convolution_convert_fusion.2.do_ref
  697.3 22.3 %shard_map.374 = (f32[256,2048]{1,0:T(8,128)}, f32[2,64,2048]{2,1,0:T(8,128)S(1)}, f32[2,64,2048]{2,1,0:T(8,128)S(1)}) custom-call(s32[2,4]{1,0:T(2,128)S(1)} %slice.99.first_ref, s32[2,1,1024]{2,1,0:T(1,128)S(1)} %broadcast_in_dim.40.start_ref, bf16[256,2048]{1,0:T(8,128)(2,1)S(1)} %bitcast.234, bf16[256,2048]{1,0:T(8,128)(2,1)S(1)} %copy-done.13, ...), custom_call_target="tpu_custom_call" | custom-call | tf_op jit(solution)/shard_map/pallas_call | solution.py:740
  723.6 63.8 %shard_map.375 = (bf16[2,64,2,1024]{3,2,1,0:T(2,128)(2,1)}, bf16[2,512,704]{2,1,0:T(8,128)(2,1)}, bf16[2,256,512]{2,1,0:T(8,128)(2,1)}, bf16[512,704]{1,0:T(8,128)(2,1)}) custom-call(bf16[2,64,2,1024]{3,2,1,0:T(2,128)(2,1)} %slice.184.refs_0_, bf16[2,512,704]{2,1,0:T(8,128)(2,1)} %fusion.1.refs_1_.refs_3_, bf16[2,2,256,512]{3,2,1,0:T(8,128)(2,1)} %bitcast.281, ...), custom_call_target="tpu_custom_call" | custom-call | tf_op jit(solution)/shard_map/pallas_call | solution.py:585
  795.4 2.7 fusion.49
  802.1 8.2 fusion.73
  810.4 11.6 %add_convert_fusion.refs_0_ = bf16[2048,2048]{1,0:T(8,128)(2,1)} fusion(f32[2048,2048]{1,0:T(8,128)} %fusion.73, bf16[128,2048]{1,0:T(8,128)(2,1)S(1)} %bitcast.283, bf16[2048,128]{1,0:T(8,128)(2,1)S(1)} %bitcast.268), kind=kOutput, calls=%fused_computation | convolution fusion | flops 1082130432 | bytes 26214400 | tf_op jit(solution)/shard_map/dot_general | solution.py:53
  822.1 4.6 convolution_convert_fusion.3.refs_1_
  826.7 41.8 %shard_map.376 = (f32[256,2048]{1,0:T(8,128)}, bf16[2,512,256]{2,1,0:T(8,128)(2,1)}, bf16[2,256,512]{2,1,0:T(8,128)(2,1)}, bf16[512,704]{1,0:T(8,128)(2,1)}) custom-call(bf16[2048,2048]{1,0:T(8,128)(2,1)} %add_convert_fusion.refs_0_, bf16[2,2,512,256]{3,2,1,0:T(8,128)(2,1)} %convolution_convert_fusion.3.refs_1_, ...), custom_call_target="tpu_custom_call" | custom-call | tf_op jit(solution)/shard_map/pallas_call | solution.py:585
  874.9 5.8 convolution_convert_fusion.5
  881.6 38.2 %shard_map.377 = (bf16[32,80,128]{2,1,0:T(8,128)(2,1)}, bf16[2,512,256]{2,1,0:T(8,128)(2,1)}, bf16[256,512]{1,0:T(8,128)(2,1)}) custom-call(bf16[32,80,128]{2,1,0:T(8,128)(2,1)} %pad_maximum_fusion.1.refs_0_, bf16[2,512,256]{2,1,0:T(8,128)(2,1)} %fusion.30.refs_1_.refs_0_, bf16[256,512]{1,0:T(8,128)(2,1)} %fusion.52.refs_2_), custom_call_target="tpu_custom_call" | custom-call | tf_op jit(solution)/shard_map/pallas_call | solution.py:585
  924.3 7.3 fusion.25
  933.4 7.7 shard_map.380
  946.1 3.4 copy.163
  949.5 3.6 copy.164
  965.2 6.2 shard_map.381
  974.9 3.0 shard_map.378
  (315 shorter events, 98.2 us)
Async XLA Ops:
  0.7 36.0 %copy-start.45 = (bf16[256,2048]{1,0:T(8,128)(2,1)S(1)}, bf16[256,2048]{1,0:T(8,128)(2,1)}, u32[]{:S(2)}) copy-start(bf16[256,2048]{1,0:T(8,128)(2,1)} %param.22) | copy-start | bytes 3145732
  0.7 157.7 %collective-permute-start = (s32[1,2048]{1,0:T(1,128)}, s32[1,2048]{1,0:T(1,128)S(1)}, u32[]{:S(2)}, u32[]{:S(2)}) collective-permute-start(s32[1,2048]{1,0:T(1,128)} %param.24), channel_id=1, source_target_pairs={{0,8},{8,0},{1,9},{9,1},{2,10},{10,2},{3,11},{11,3},{4,12},{12,4},... | collective-permute-start | bytes 24584 | tf_op jit(solution)/shard_map/ppermute | solution.py:900
  36.4 124.2 %copy-start.95 = (f32[32]{0:T(128)}, f32[32]{0:T(128)S(1)}, u32[]{:S(2)}) copy-start(f32[32]{0:T(128)S(1)} %multiply_power_fusion) | copy-start | bytes 388
  40.8 73.8 %copy-start.59 = (bf16[32,64,128]{2,1,0:T(8,128)(2,1)S(1)}, bf16[32,64,128]{2,1,0:T(8,128)(2,1)}, u32[]{:S(2)}) copy-start(bf16[32,64,128]{2,1,0:T(8,128)(2,1)} %slice.106) | copy-start | bytes 1572868
  139.4 182.2 %copy-start.79 = (f32[2048]{0:T(1024)}, f32[2048]{0:T(1024)S(1)}, u32[]{:S(2)}) copy-start(f32[2048]{0:T(1024)S(1)} %reshape.589) | copy-start | bytes 24580
  158.8 65.6 %copy-start.83 = (f32[1,8,2,128]{3,1,2,0:T(8,128)}, f32[1,8,2,128]{3,1,2,0:T(8,128)S(1)}, u32[]{:S(2)}) copy-start(f32[1,8,2,128]{3,1,2,0:T(8,128)S(1)} %copy.197) | copy-start | bytes 24580
  164.5 60.0 %copy-start.75 = (bf16[1,64,2,1024]{3,1,2,0:T(8,128)(2,1)S(1)}, bf16[1,64,2,1024]{3,1,2,0:T(8,128)(2,1)}, u32[]{:S(2)}) copy-start(bf16[1,64,2,1024]{3,1,2,0:T(8,128)(2,1)} %copy.144) | copy-start | bytes 786436
  229.9 17.1 %copy-start.64 = (bf16[2,2,1,256,512]{3,4,1,0,2:T(8,128)(2,1)S(1)}, bf16[2,2,1,256,512]{3,4,1,0,2:T(8,128)(2,1)}, u32[]{:S(2)}) copy-start(bf16[2,2,1,256,512]{3,4,1,0,2:T(8,128)(2,1)} %copy.146) | copy-start | bytes 3145732
  230.2 22.6 %copy-start.6 = (bf16[4,64,2048]{2,1,0:T(8,128)(2,1)}, bf16[4,64,2048]{2,1,0:T(8,128)(2,1)S(1)}, u32[]{:S(2)}) copy-start(bf16[4,64,2048]{2,1,0:T(8,128)(2,1)S(1)} %maximum_multiply_fusion) | copy-start | bytes 3145732
  252.8 66.8 %copy-start.47 = (bf16[256,2048]{1,0:T(8,128)(2,1)S(1)}, bf16[256,2048]{1,0:T(8,128)(2,1)}, u32[]{:S(2)}) copy-start(bf16[256,2048]{1,0:T(8,128)(2,1)} %param.22) | copy-start | bytes 3145732
  321.5 43.8 %copy-start.86 = (f32[256]{0:T(256)}, f32[256]{0:T(256)S(1)}, u32[]{:S(2)}) copy-start(f32[256]{0:T(256)S(1)} %add_rsqrt_fusion) | copy-start | bytes 3076
  322.8 42.5 %copy-start.67 = (bf16[4,1,512,704]{3,2,1,0:T(8,128)(2,1)S(1)}, bf16[4,1,512,704]{3,2,1,0:T(8,128)(2,1)}, u32[]{:S(2)}) copy-start(bf16[4,1,512,704]{3,2,1,0:T(8,128)(2,1)} %get-tuple-element.87) | copy-start | bytes 8650756
  365.3 11.4 %copy-start.53 = (bf16[8,256,2048]{2,1,0:T(8,128)(2,1)S(1)}, bf16[8,256,2048]{2,1,0:T(8,128)(2,1)}, u32[]{:S(2)}) copy-start(bf16[8,256,2048]{2,1,0:T(8,128)(2,1)} %get-tuple-element.85) | copy-start | bytes 25165828
  365.3 11.4 %copy-start.66 = (bf16[4,1,512,704]{3,2,1,0:T(8,128)(2,1)S(1)}, bf16[4,1,512,704]{3,2,1,0:T(8,128)(2,1)}, u32[]{:S(2)}) copy-start(bf16[4,1,512,704]{3,2,1,0:T(8,128)(2,1)} %get-tuple-element.86) | copy-start | bytes 8650756
  376.7 8.3 copy-start.50
  409.9 15.7 %copy-start.69 = (bf16[704,2048]{1,0:T(8,128)(2,1)S(1)}, bf16[704,2048]{1,0:T(8,128)(2,1)}, u32[]{:S(2)}) copy-start(bf16[704,2048]{1,0:T(8,128)(2,1)} %reshape.557) | copy-start | bytes 8650756
  425.6 9.1 copy-start.54
  454.6 13.1 %copy-start.55 = (bf16[2048,2048]{1,0:T(8,128)(2,1)S(1)}, bf16[2048,2048]{1,0:T(8,128)(2,1)}, u32[]{:S(2)}) copy-start(bf16[2048,2048]{1,0:T(8,128)(2,1)} %copy.149) | copy-start | bytes 25165828
  454.6 13.1 %copy-start.100 = (bf16[2048,704]{0,1:T(8,128)(2,1)S(1)}, bf16[2048,704]{0,1:T(8,128)(2,1)}, u32[]{:S(2)}) copy-start(bf16[2048,704]{0,1:T(8,128)(2,1)} %get-tuple-element.246) | copy-start | bytes 8650756
  467.7 8.3 copy-start.99
  476.0 8.2 copy-start.68
  496.9 44.7 %copy-start.58 = (bf16[704,2,2,512]{3,0,2,1:T(8,128)(2,1)S(1)}, bf16[704,2,2,512]{3,0,2,1:T(8,128)(2,1)}, u32[]{:S(2)}) copy-start(bf16[704,2,2,512]{3,0,2,1:T(8,128)(2,1)} %fusion.18) | copy-start | bytes 8650756
  544.4 53.4 %copy-start.57 = (bf16[2,2,512,704]{3,2,1,0:T(8,128)(2,1)S(1)}, bf16[2,2,512,704]{3,2,1,0:T(8,128)(2,1)}, u32[]{:S(2)}) copy-start(bf16[2,2,512,704]{3,2,1,0:T(8,128)(2,1)} %fusion.12.refs_1_) | copy-start | bytes 8650756
  605.1 62.1 %copy-start = (bf16[2,512,704]{2,1,0:T(8,128)(2,1)S(1)}, bf16[2,512,704]{2,1,0:T(8,128)(2,1)}, u32[]{:S(2)}) copy-start(bf16[2,512,704]{2,1,0:T(8,128)(2,1)} %fusion.2.refs_2_.refs_0_) | copy-start | bytes 4325380
  791.1 8.9 copy-start.70
  802.0 8.3 copy-start.63
  802.0 8.3 copy-start.74
  802.1 8.3 copy-start.78
  802.1 8.3 copy-start.60
  802.1 20.0 %slice-start = ((s8[8388608]{0:T(1024)(128)(4,1)}), s8[4194304]{0:T(1024)(128)(4,1)S(1)}, s32[]{:S(2)}) async-start(s8[8388608]{0:T(1024)(128)(4,1)} %bitcast.252), calls=%async_computation | async-start | bytes 8388608
  810.4 11.6 %copy-start.72 = (bf16[2,64,2048]{2,1,0:T(8,128)(2,1)}, bf16[2,64,2048]{2,1,0:T(8,128)(2,1)S(1)}, u32[]{:S(2)}) copy-start(bf16[2,64,2048]{2,1,0:T(8,128)(2,1)S(1)} %pad_maximum_fusion.3) | copy-start | bytes 1572868
  810.4 11.6 %slice-start.1 = ((s8[8388608]{0:T(1024)(128)(4,1)}), s8[4194304]{0:T(1024)(128)(4,1)S(1)}, s32[]{:S(2)}) async-start(s8[8388608]{0:T(1024)(128)(4,1)} %bitcast.252), calls=%async_computation.1 | async-start | bytes 8388608
  826.6 41.9 %copy-start.10 = (bf16[2,256,512]{2,1,0:T(8,128)(2,1)S(1)}, bf16[2,256,512]{2,1,0:T(8,128)(2,1)}, u32[]{:S(2)}) copy-start(bf16[2,256,512]{2,1,0:T(8,128)(2,1)} %fusion.31.refs_2_.refs_0_) | copy-start | bytes 1572868
  826.6 43.6 %copy-start.48 = (bf16[256,2048]{1,0:T(8,128)(2,1)S(1)}, bf16[256,2048]{1,0:T(8,128)(2,1)}, u32[]{:S(2)}) copy-start(bf16[256,2048]{1,0:T(8,128)(2,1)} %param.22) | copy-start | bytes 3145732
  826.6 43.6 %copy-start.82 = (f32[2048]{0:T(1024)S(1)}, f32[2048]{0:T(1024)}, u32[]{:S(2)}) copy-start(f32[2048]{0:T(1024)} %copy-done.81) | copy-start | bytes 24580
  826.6 43.6 %copy-start.90 = (f32[256]{0:T(256)S(1)}, f32[256]{0:T(256)}, u32[]{:S(2)}) copy-start(f32[256]{0:T(256)} %copy-done.89) | copy-start | bytes 3076
  880.7 39.2 %copy-start.8 = (bf16[2,512,256]{2,1,0:T(8,128)(2,1)S(1)}, bf16[2,512,256]{2,1,0:T(8,128)(2,1)}, u32[]{:S(2)}) copy-start(bf16[2,512,256]{2,1,0:T(8,128)(2,1)} %fusion.30.refs_1_.refs_0_) | copy-start | bytes 1572868
  880.7 43.5 %copy-start.88 = (f32[256]{0:T(256)S(1)}, f32[256]{0:T(256)}, u32[]{:S(2)}) copy-start(f32[256]{0:T(256)} %copy-done.86) | copy-start | bytes 3076
  880.7 43.5 %copy-start.93 = (f32[256]{0:T(256)S(1)}, f32[256]{0:T(256)}, u32[]{:S(2)}) copy-start(f32[256]{0:T(256)} %copy-done.92) | copy-start | bytes 3076
  921.6 53.3 %collective-permute-start.1 = (bf16[512,256]{1,0:T(8,128)(2,1)}, bf16[512,256]{1,0:T(8,128)(2,1)S(1)}, u32[]{:S(2)}, u32[]{:S(2)}) collective-permute-start(bf16[512,256]{1,0:T(8,128)(2,1)} %fusion.53), channel_id=1, source_target_pairs={{0,8},{12,4},{1,9},{13,5},{2,10},{14,6},{3,11},{15,7},{16,24},{28,... | collective-permute-start | bytes 786440 | tf_op jit(solution)/shard_map/ppermute | solution.py:1076
  924.2 7.4 copy-start.96
  924.2 8.0 copy-start.61
  924.2 9.1 copy-start.3
  924.3 9.1 copy-start.19
  924.3 9.1 copy-start.21
  924.3 9.1 copy-start.35
  924.3 9.1 copy-start.36
  965.2 8.9 copy-start.85
  (57 other events, 214.6 us)

commit v3 on v2

--- a/solution.py
+++ b/solution.py
@@ -1,4 +1,5 @@
 import functools
+import types
 
 import jax
 import jax.numpy as jnp
@@ -49,12 +50,6 @@
     )
 
 
-def dot_tt(left, right):
-    return lax.dot_general(
-        left, right, (((0,), (1,)), ((), ())), preferred_element_type=jnp.float32
-    )
-
-
 TO_AWAY_CORE = [(0, 2), (3, 1)]
 
 
@@ -63,15 +58,18 @@
     return lax.all_gather(shard, "h", axis=0) if h_size > 1 else shard[None]
 
 
-def halves(grad, h_size):
-    grad = grad.astype(jnp.bfloat16)
-    if h_size > 1:
-        return lax.psum_scatter(grad, "h", scatter_dimension=2, tiled=False)
-    return grad[:, :, 0]
+def col_blocks(parts):
+    n, h, rows, cols = parts.shape
+    return parts.transpose(0, 2, 1, 3).reshape(n, rows, h * cols)
+
+
+def row_blocks(parts):
+    n, h, rows, cols = parts.shape
+    return parts.reshape(n, h * rows, cols)
 
 
 def add_swapped(grad, came):
-    keep = lax.dynamic_index_in_dim(grad, lax.axis_index("y"), 0, keepdims=False)
+    keep = lax.dynamic_slice_in_dim(grad, 2 * lax.axis_index("y"), 2, 0)
     return (keep.astype(jnp.float32) + came.astype(jnp.float32)).astype(jnp.bfloat16)
 
 
@@ -101,9 +99,7 @@
 
 def adam_shard(weight, first, second, grads, rate, fixes):
     groups, rows, cols = weight.shape
-    size = min(rows, 128)
-    while rows % size:
-        size //= 2
+    size = max(n for n in range(16, 257, 16) if rows % n == 0)
     steps = rows // size
     place = jnp.stack([lax.axis_index("c"), (lax.axis_index("c") == lax.axis_index("zh"))])
     state = pl.BlockSpec((1, size, cols), lambda g, i, s: (g, i, 0))
@@ -134,7 +130,6 @@
 
 
 MESH_ID = pl.DeviceIdType.MESH
-CHUNKS = 2
 ROW_STRIP = 32
 PARTNERS = (("c",), ("x",), ("zl",), ("y",), ("y", "c"), ("zh",), ("zh", "c"))
 
@@ -209,6 +204,36 @@
         far_copy(src, dst.at[0], send.at[2], recv.at[0], flipped("zh")).wait_send()
 
 
+class SpreadAll:
+    alias = {}
+
+    def __init__(self, shard):
+        self.first = Spread(shard)
+        self.inputs, self.outputs = self.first.inputs, self.first.outputs
+        self.sems = self.first.sems + [1, 1]
+
+    def begin(self, ins, outs, sems):
+        self.first.begin(ins, outs, sems[:2])
+
+    def copy(self, outs, sems, y_from):
+        (dst,), (send, recv) = outs, sems[2:]
+        part = dst.at[pl.ds(2 * y_from, 2)]
+        return far_copy(part, part, send.at[0], recv.at[0], flipped("y"))
+
+    def middle(self, ins, outs, sems):
+        self.first.finish(ins, outs, sems[:2])
+
+        @pl.when(not_home())
+        def _():
+            self.copy(outs, sems, lax.axis_index("y")).start()
+
+    def finish(self, ins, outs, sems):
+        @pl.when(not_home())
+        def _():
+            self.copy(outs, sems, lax.axis_index("y")).wait_send()
+            self.copy(outs, sems, 1 - lax.axis_index("y")).wait_recv()
+
+
 class Pass:
     def __init__(self, gathered):
         self.inputs = [gathered]
@@ -233,18 +258,21 @@
             self.copy(outs, sems, 1 - lax.axis_index("y")).wait_recv()
 
 
+def swap_copy(src, dst, send, recv):
+    part = src.at[pl.ds(2 * (1 - lax.axis_index("y")), 2)]
+    return far_copy(part, dst, send, recv, flipped("y"))
+
+
 class Swap:
     def __init__(self, grad):
         self.inputs = [grad]
-        self.outputs = [jax.ShapeDtypeStruct(grad.shape[1:], grad.dtype)]
+        self.outputs = [jax.ShapeDtypeStruct((2,) + grad.shape[1:], grad.dtype)]
         self.sems = [1, 1]
         self.alias = {}
 
     def copy(self, ins, outs, sems):
         (src,), (dst,), (send, recv) = ins, outs, sems
-        return far_copy(
-            src.at[1 - lax.axis_index("y")], dst, send.at[0], recv.at[0], flipped("y")
-        )
+        return swap_copy(src, dst, send.at[0], recv.at[0])
 
     def begin(self, ins, outs, sems):
         self.copy(ins, outs, sems).start()
@@ -292,43 +320,69 @@
     return (core * 2 + z_low) * 2 + x_at
 
 
-class GatherRows:
-    def __init__(self, block, along_x=False):
-        self.inputs = [block]
-        self.outputs = [jax.ShapeDtypeStruct((8,) + block.shape, block.dtype)]
-        self.sems = [(7, CHUNKS), (8, CHUNKS), 1]
-        self.alias = {}
-        self.along_x = along_x
-
-    def places(self):
-        return tuple(lax.axis_index(a) for a in ("c", "zl", "x"))
-
-    def part(self, ref, k):
-        rows = ref.shape[0] // CHUNKS
-        return ref.at[pl.ds(k * rows, rows)]
-
-    def begin(self, ins, outs, sems):
-        (src,), (dst,), (send, recv, local) = ins, outs, sems
-        core, z_low, x_at = self.places()
-        own = group_index(core, z_low, x_at)
-        for k in range(CHUNKS):
-            for way, axis in enumerate(("x", "zl", "c")):
-                far_copy(
-                    self.part(src, k),
-                    self.part(dst.at[own], k),
-                    send.at[way, k],
-                    recv.at[own, k],
-                    flipped(axis),
-                ).start()
+class Fused:
+    alias = {}
+
+    def name(self, given, streams, results, scratch, far):
+        self.given, self.streams = list(given), list(streams)
+        self.results, self.held, self.far = list(results), list(scratch), list(far)
+        self.inputs += list(given.values()) + list(streams.values())
+        self.in_spaces += [pltpu.VMEM] * len(given) + [pl.ANY] * len(streams)
+        self.outputs += list(results.values()) + list(far.values())
+        self.out_spaces += [pltpu.VMEM] * len(results) + [pl.ANY] * len(far)
+        self.scratch += list(scratch.values())
+
+    def bind(self, ins, outs, scratch):
+        names = self.given + self.streams + self.results + self.far + self.held
+        tail = lambda refs, n: list(refs)[len(refs) - n :] if n else []
+        refs = tail(ins, len(self.given) + len(self.streams))
+        refs += tail(outs, len(self.results) + len(self.far)) + tail(scratch, len(self.held))
+        return types.SimpleNamespace(**dict(zip(names, refs)))
+
+
+class GatherRows(Fused):
+    def __init__(
+        self,
+        block,
+        along_x=False,
+        keep=True,
+        given={},
+        results={},
+        scratch={},
+        before=None,
+        work=None,
+        after=None,
+    ):
+        gathered = (8,) + block.shape
+        self.inputs, self.in_spaces = [block], [pl.ANY]
+        self.outputs, self.out_spaces, self.scratch = [], [], []
+        self.keep, self.along_x = keep, along_x
+        self.before, self.work, self.after = before, work, after
+        if keep:
+            self.outputs = [jax.ShapeDtypeStruct(gathered, block.dtype)]
+            self.out_spaces = [pltpu.VMEM if work else pl.ANY]
+        else:
+            self.scratch = [pltpu.VMEM(gathered, block.dtype)]
+        self.sems = [7, 8, 1]
+        self.name(given, {}, results, scratch, {})
+
+    def where(self, outs, scratch):
+        return outs[0] if self.keep else scratch[0]
+
+    def begin(self, ins, outs, sems, scratch):
+        src, dst, (send, recv, local) = ins[0], self.where(outs, scratch), sems
+        own = group_index(*(lax.axis_index(a) for a in ("c", "zl", "x")))
+        for way, axis in enumerate(("x", "zl", "c")):
+            far_copy(src, dst.at[own], send.at[way], recv.at[own], flipped(axis)).start()
         pltpu.make_async_copy(src, dst.at[own], local.at[0]).start()
 
-    def finish(self, ins, outs, sems):
-        (src,), (dst,), (send, recv, local) = ins, outs, sems
-        core, z_low, x_at = self.places()
+    def finish(self, ins, outs, sems, scratch, middle):
+        src, dst, (send, recv, local) = ins[0], self.where(outs, scratch), sems
+        refs = self.bind(ins, outs, scratch)
+        core, z_low, x_at = (lax.axis_index(a) for a in ("c", "zl", "x"))
         own = group_index(core, z_low, x_at)
         beside = group_index(core, z_low, 1 - x_at)
         below = group_index(core, 1 - z_low, x_at)
-        across = group_index(core, 1 - z_low, 1 - x_at)
         by_x = True if self.along_x else core == 0
         turn = jnp.where(by_x, below, beside)
         onward = {
@@ -336,49 +390,93 @@
             "zl": jnp.where(by_x, z_low, 1 - z_low),
         }
 
-        def pass_on(block, k, way, device):
-            part = self.part(dst.at[block], k)
-            return far_copy(part, part, send.at[way, k], recv.at[block, k], device)
-
-        for k in range(CHUNKS):
-            pass_on(beside, k, 0, flipped("x")).wait_recv()
-            pass_on(below, k, 0, flipped("x")).wait_recv()
-            pass_on(turn, k, 3, onward).start()
-            pass_on(beside, k, 4, flipped("c")).start()
-            pass_on(below, k, 5, flipped("c")).start()
-        for k in range(CHUNKS):
-            pass_on(across, k, 0, flipped("x")).wait_recv()
-            pass_on(across, k, 6, flipped("c")).start()
-        for k in range(CHUNKS):
-            for z_of in (0, 1):
-                for x_of in (0, 1):
-                    block = group_index(1 - core, z_of, x_of)
-                    pass_on(block, k, 0, flipped("c")).wait_recv()
-            for way in range(7):
-                pass_on(own, k, way, flipped("c")).wait_send()
-        pltpu.make_async_copy(src, dst.at[own], local.at[0]).wait()
-
-
-class ScatterRows:
-    alias = {}
-
-    def __init__(self, partial):
-        self.inputs = [partial]
-        self.in_spaces = [pltpu.VMEM]
-        self.rows, cols = partial.shape[0] // 8, partial.shape[1]
-        block = (self.rows, cols)
+        def pass_on(block, way, device):
+            part = dst.at[block]
+            return far_copy(part, part, send.at[way], recv.at[block], device)
+
+        if self.before:
+            self.before(refs)
+
+        @pl.loop(0, 8)
+        def _(step):
+            flip_c = (step == 1) | (step == 4) | (step == 5) | (step == 7)
+            flip_z = (step == 3) | (step == 5) | (step >= 6)
+            flip_x = (step == 2) | (step == 4) | (step >= 6)
+            block = group_index(
+                jnp.where(flip_c, 1 - core, core),
+                jnp.where(flip_z, 1 - z_low, z_low),
+                jnp.where(flip_x, 1 - x_at, x_at),
+            )
+
+            @pl.when(step == 0)
+            def _():
+                pltpu.make_async_copy(src, dst.at[own], local.at[0]).wait()
+
+            @pl.when((step != 0) & (step != 3))
+            def _():
+                pass_on(block, 0, flipped("c")).wait_recv()
+
+            @pl.when(step == 2)
+            def _():
+                pass_on(below, 0, flipped("c")).wait_recv()
+                pass_on(turn, 3, onward).start()
+                pass_on(beside, 4, flipped("c")).start()
+                pass_on(below, 5, flipped("c")).start()
+
+            @pl.when(step == 6)
+            def _():
+                pass_on(block, 6, flipped("c")).start()
+                middle()
+
+            if self.work:
+                self.work(refs, dst.at[block], block)
+
+        if self.after:
+            self.after(refs)
+        for way in range(7):
+            pass_on(own, way, flipped("c")).wait_send()
+
+
+class ScatterRows(Fused):
+    def __init__(
+        self,
+        rows,
+        cols,
+        produce,
+        given={},
+        streams={},
+        results={},
+        scratch={},
+        far={},
+        extra_sems=0,
+        fill_one=None,
+        fill_two=None,
+        end=None,
+    ):
+        self.inputs, self.in_spaces = [], []
+        self.rows = rows
+        block, kind = (rows, cols), jnp.bfloat16
         self.outputs = [jax.ShapeDtypeStruct(block, jnp.float32)]
         self.out_spaces = [pltpu.VMEM]
-        self.sems = [(7, CHUNKS), (7, CHUNKS)]
-        kind = partial.dtype
-        self.scratch = [pltpu.VMEM((4,) + block, kind)] * 2 + [pltpu.VMEM(block, kind)] * 3
+        self.sems = [7, 7, 2] + ([extra_sems] if extra_sems else [])
+        self.scratch = [pltpu.VMEM((8,) + block, kind)]
+        self.scratch += [pltpu.VMEM((4,) + block, kind)] * 2 + [pltpu.VMEM(block, kind)] * 3
+        if streams:
+            self.scratch += [pltpu.VMEM((2,) + block, kind)]
+        self.produce, self.fill_one, self.fill_two, self.end = produce, fill_one, fill_two, end
+        self.name(given, streams, results, scratch, far)
 
     def begin(self, ins, outs, sems, scratch):
-        (partial,) = ins
-        came, sums, turned, direct_in, late_in = scratch
-        send, recv = sems
+        pass
+
+    def finish(self, ins, outs, sems, scratch, middle):
+        out = outs[0]
+        partial, came, sums, turned, direct_in, late_in = scratch[:6]
+        send, recv, local = sems[:3]
+        refs = self.bind(ins, outs, scratch)
+        refs.more = sems[3] if len(sems) > 3 else None
         core, z_low, x_at = (lax.axis_index(a) for a in ("c", "zl", "x"))
-        rows, size = self.rows, self.rows // CHUNKS
+        rows = self.rows
         own, beside, below, across = (
             2 * z_low + x_at,
             2 * z_low + 1 - x_at,
@@ -395,79 +493,99 @@
             "x": jnp.where(core == 0, x_at, 1 - x_at),
             "zl": jnp.where(core == 0, 1 - z_low, z_low),
         }
-        self.blocks = (across, direct, late, own)
-
-        def to_core(n, k):
-            block = self.blocks[n]
-            at = (4 * (1 - core) + block) * rows + k * size
+
+        def to_core(turn_at, block):
             return far_copy(
-                partial.at[pl.ds(pl.multiple_of(at, size), size)],
-                came.at[block, pl.ds(k * size, size)],
-                send.at[n, k],
-                recv.at[block, k],
+                partial.at[4 * (1 - core) + block],
+                came.at[block],
+                send.at[turn_at],
+                recv.at[block],
                 flipped("c"),
             )
 
-        def add(n, k, target, *others):
-            block = self.blocks[n]
-
-            @pl.loop(0, size // ROW_STRIP)
+        def add(block, target, *others):
+            @pl.loop(0, rows // ROW_STRIP)
             def _(strip):
-                inner = pl.multiple_of(k * size + strip * ROW_STRIP, ROW_STRIP)
-                at = pl.ds(inner, ROW_STRIP)
-                there = pl.multiple_of((4 * core + block) * rows + inner, ROW_STRIP)
-                total = partial[pl.ds(there, ROW_STRIP)].astype(jnp.float32)
+                at = pl.ds(pl.multiple_of(strip * ROW_STRIP, ROW_STRIP), ROW_STRIP)
+                total = partial[4 * core + block, at].astype(jnp.float32)
                 total += came[block, at].astype(jnp.float32)
                 for other in others:
                     total += other[at].astype(jnp.float32)
                 target[at] = total.astype(target.dtype)
 
-        def send_sum(n, way, k, target, device):
-            at = pl.ds(k * size, size)
-            return far_copy(
-                sums.at[self.blocks[n], at],
-                target.at[at],
-                send.at[way, k],
-                recv.at[way, k],
-                device,
+        def send_sum(block, way, target, device):
+            return far_copy(sums.at[block], target, send.at[way], recv.at[way], device)
+
+        turn = send_sum(across, 4, turned, direct_way)
+        straight = send_sum(direct, 5, direct_in, direct_way)
+        last = send_sum(late, 6, late_in, late_way)
+
+        def stream(name, body):
+            source, held = getattr(refs, name), scratch[6]
+
+            def fetch(n):
+                slot = lax.rem(n, 2)
+                return pltpu.make_async_copy(source.at[n], held.at[slot], local.at[slot])
+
+            fetch(0).start()
+
+            @pl.loop(0, 8)
+            def _(n):
+                @pl.when(n < 7)
+                def _():
+                    fetch(n + 1).start()
+
+                fetch(n).wait()
+                body(n, held.at[lax.rem(n, 2)])
+
+        refs.stream = stream
+
+        @pl.loop(0, 8)
+        def _(step):
+            pair, mine = step // 2, lax.rem(step, 2)
+            first = jnp.where(mine == 1, direct, late)
+            second = jnp.where(mine == 1, late, direct)
+            block = jnp.where(
+                pair == 0, across, jnp.where(pair == 1, first, jnp.where(pair == 2, second, own))
             )
-
-        self.to_core, self.add, self.send_sum = to_core, add, send_sum
-        self.turn = lambda k: send_sum(0, 4, k, turned, direct_way)
-        self.straight = lambda k: send_sum(1, 5, k, direct_in, direct_way)
-        self.last = lambda k: send_sum(2, 6, k, late_in, late_way)
-        for n in range(4):
-            for k in range(CHUNKS):
-                to_core(n, k).start()
-
-    def finish(self, ins, outs, sems, scratch):
-        (out,) = outs
-        came, sums, turned, direct_in, late_in = scratch
-        across, direct, late, own = self.blocks
-        for k in range(CHUNKS):
-            self.to_core(0, k).wait_recv()
-            self.add(0, k, sums.at[across])
-            self.turn(k).start()
-        for k in range(CHUNKS):
-            self.to_core(1, k).wait_recv()
-            self.add(1, k, sums.at[direct])
-            self.straight(k).start()
-        for k in range(CHUNKS):
-            self.to_core(2, k).wait_recv()
-            self.turn(k).wait_recv()
-            self.add(2, k, sums.at[late], turned)
-            self.last(k).start()
-        for k in range(CHUNKS):
-            self.to_core(3, k).wait_recv()
-            self.straight(k).wait_recv()
-            self.last(k).wait_recv()
-            self.add(3, k, out, direct_in, late_in)
-        for k in range(CHUNKS):
-            for n in range(4):
-                self.to_core(n, k).wait_send()
-            self.turn(k).wait_send()
-            self.straight(k).wait_send()
-            self.last(k).wait_send()
+            index = 4 * jnp.where(mine == 1, core, 1 - core) + block
+            self.produce(refs, index, partial.at[index])
+
+            @pl.when(mine == 0)
+            def _():
+                to_core(pair, block).start()
+
+            @pl.when(step == 1)
+            def _():
+                to_core(0, across).wait_recv()
+                add(across, sums.at[across])
+                turn.start()
+
+            @pl.when(step == 3)
+            def _():
+                to_core(1, direct).wait_recv()
+                add(direct, sums.at[direct])
+                straight.start()
+
+        if self.fill_one:
+            self.fill_one(refs)
+        to_core(2, late).wait_recv()
+        turn.wait_recv()
+        add(late, sums.at[late], turned)
+        last.start()
+        middle()
+        if self.fill_two:
+            self.fill_two(refs)
+        to_core(3, own).wait_recv()
+        straight.wait_recv()
+        last.wait_recv()
+        add(own, out, direct_in, late_in)
+        for n, block in enumerate((across, direct, late, own)):
+            to_core(n, block).wait_send()
+        for copy in (turn, straight, last):
+            copy.wait_send()
+        if self.end:
+            self.end(refs)
 
 
 class Everyone:
@@ -549,7 +667,7 @@
         extra = getattr(task, "scratch", None)
         kinds = [pltpu.SemaphoreType.DMA(s if isinstance(s, tuple) else (s,)) for s in task.sems]
         counts.append(
-            (len(task.inputs), len(task.outputs), len(kinds), len(extra) if extra else None)
+            (len(task.inputs), len(task.outputs), len(kinds), len(extra) if extra is not None else None)
         )
         arrays += task.inputs
         shapes += task.outputs
@@ -579,8 +697,19 @@
             bound.append(mine)
         for task, mine in zip(tasks, bound):
             task.begin(*mine)
+        parts = [(t, m) for t, m in zip(tasks, bound) if hasattr(t, "middle")]
+
+        def middle():
+            for task, mine in parts:
+                task.middle(*mine)
+
+        if not any(isinstance(t, Fused) for t in tasks):
+            middle()
         for task, mine in zip(tasks, bound):
-            task.finish(*mine)
+            if isinstance(task, Fused):
+                task.finish(*mine, middle)
+            else:
+                task.finish(*mine)
 
     results = pl.pallas_call(
         kernel,
@@ -590,7 +719,7 @@
         scratch_shapes=scratch,
         input_output_aliases=aliases,
         compiler_params=pltpu.CompilerParams(
-            collective_id=collective_id, has_side_effects=True, vmem_limit_bytes=56 * 2**20
+            collective_id=collective_id, has_side_effects=True, vmem_limit_bytes=60 * 2**20
         ),
     )(*arrays)
     grouped, at = [], 0
@@ -772,11 +901,175 @@
     )(first, start, query_t, out_t, grad_t, lse, keys_t, values_t)
 
 
-def rotate(values, cos_table, sin_table):
-    front, back = values[:, :HALF], values[:, HALF:]
-    return jnp.concatenate(
-        [front * cos_table - back * sin_table, back * cos_table + front * sin_table], axis=1
-    )
+def cols_at(ref, block, h_size):
+    width = ref.shape[-1] // (4 * h_size)
+    parts = [
+        ref[:, (h * 4 + block) * width : (h * 4 + block + 1) * width] for h in range(h_size)
+    ]
+    return parts[0] if h_size == 1 else jnp.concatenate(parts, axis=1)
+
+
+def put_cols(ref, block, value, h_size):
+    width = ref.shape[-1] // (4 * h_size)
+    for h in range(h_size):
+        at = (h * 4 + block) * width
+        ref[:, at : at + width] = value[:, h * width : (h + 1) * width].astype(ref.dtype)
+
+
+def flip(value):
+    return value.astype(jnp.float32).T
+
+
+def lanes_of(block, rows):
+    return pl.ds(pl.multiple_of(block * rows, rows), rows)
+
+
+def turned(values, cos_table, sin_table):
+    front, back = values[:HALF], values[HALF:]
+    return (front * cos_table - back * sin_table, back * cos_table + front * sin_table)
+
+
+def query_work(h_size, heads, refs, rows, block):
+    at = lanes_of(block, rows.shape[0])
+    query = pair = 0.0
+    for j in range(4):
+        part = cols_at(rows, j, h_size)
+        query += dot_nn(part, refs.wq[j])
+        pair += dot_nn(part, refs.wp[j])
+    query_t, pair_t = query.T, pair.T
+    cos_table, sin_table = refs.cos[:, at], refs.sin[:, at]
+    for head in range(heads):
+        here = head * HD
+        front, back = turned(query_t[here : here + HD], cos_table, sin_table)
+        refs.q[here : here + HALF, at] = (front * SCALE).astype(jnp.bfloat16)
+        refs.q[here + HALF : here + HD, at] = (back * SCALE).astype(jnp.bfloat16)
+    front, back = turned(pair_t[:HD], cos_table, sin_table)
+    refs.pair[:HALF, at] = front.astype(jnp.bfloat16)
+    refs.pair[HALF:HD, at] = back.astype(jnp.bfloat16)
+    refs.pair[HD:, at] = pair_t[HD:].astype(jnp.bfloat16)
+
+
+def output_produce(h_size, refs, block, target):
+    mixed = flip(refs.o[:, lanes_of(block, target.shape[0])]).astype(jnp.bfloat16)
+    for j in range(4):
+        put_cols(target, j, dot_nn(mixed, refs.wo[j]), h_size)
+
+
+def gateup_work(h_size, refs, rows, block):
+    gate = up = 0.0
+    for j in range(4):
+        part = cols_at(rows, j, h_size)
+        gate += dot_nt(part, refs.wg[j])
+        up += dot_nt(part, refs.wu[j])
+    share = jax.nn.sigmoid(gate)
+    silu = gate * share
+    refs.hid[block] = (silu * up).astype(jnp.bfloat16)
+    refs.by_gate[block] = (up * share * (1.0 + gate * (1.0 - share))).astype(jnp.bfloat16)
+    refs.by_up[block] = silu.astype(jnp.bfloat16)
+
+
+def down_produce(h_size, refs, block, target):
+    hidden = refs.hid[block]
+    for j in range(4):
+        put_cols(target, j, dot_nn(hidden, refs.wd[j]), h_size)
+
+
+def weight_grad(h_size, refs, name, left, total, result):
+    total[...] = jnp.zeros_like(total)
+
+    def add(n, rows):
+        left_t = flip(left[n]).astype(jnp.bfloat16)
+        for j in range(4):
+            total[j] += dot_nn(left_t, cols_at(rows, j, h_size))
+
+    refs.stream(name, add)
+    result[...] = total[...].astype(jnp.bfloat16)
+
+
+def down_fill_one(h_size, refs):
+    weight_grad(h_size, refs, "dy", refs.hid, refs.total, refs.gwd)
+    swap_copy(refs.gwd, refs.came, refs.more.at[0], refs.more.at[1]).start()
+
+
+def down_fill_two(h_size, refs):
+    def back(n, rows):
+        grad = 0.0
+        for j in range(4):
+            grad += dot_nt(cols_at(rows, j, h_size), refs.wd[j])
+        refs.dgate[n] = (grad * refs.by_gate[n].astype(jnp.float32)).astype(jnp.bfloat16)
+        refs.dup[n] = (grad * refs.by_up[n].astype(jnp.float32)).astype(jnp.bfloat16)
+
+    refs.stream("dy", back)
+
+
+def down_end(refs):
+    swap_copy(refs.gwd, refs.came, refs.more.at[0], refs.more.at[1]).wait()
+
+
+def gateup_produce(h_size, refs, block, target):
+    gate, up = refs.dgate[block], refs.dup[block]
+    for j in range(4):
+        put_cols(target, j, dot_nn(gate, refs.wg[j]) + dot_nn(up, refs.wu[j]), h_size)
+
+
+def gateup_fill_one(h_size, refs):
+    weight_grad(h_size, refs, "rows", refs.dgate, refs.total, refs.gwg)
+    swap_copy(refs.gwg, refs.came, refs.more.at[0], refs.more.at[1]).start()
+
+
+def gateup_fill_two(h_size, refs):
+    weight_grad(h_size, refs, "rows", refs.dup, refs.total, refs.gwu)
+
+
+def gateup_end(refs):
+    swap_copy(refs.gwg, refs.came, refs.more.at[0], refs.more.at[1]).wait()
+
+
+def output_before(refs):
+    refs.total[...] = jnp.zeros_like(refs.total)
+
+
+def output_work(h_size, refs, rows, block):
+    at = lanes_of(block, rows.shape[0])
+    mixed_t = refs.o[:, at]
+    grad = 0.0
+    for j in range(4):
+        part = cols_at(rows, j, h_size)
+        grad += dot_nt(part, refs.wo[j])
+        refs.total[j] += dot_nn(mixed_t, part)
+    refs.do[:, at] = grad.T.astype(jnp.bfloat16)
+
+
+def output_after(refs):
+    refs.gwo[...] = refs.total[...].astype(jnp.bfloat16)
+
+
+def query_produce(h_size, refs, block, target):
+    at = lanes_of(block, target.shape[0])
+    query = flip(refs.dq[:, at]).astype(jnp.bfloat16)
+    pair = flip(refs.dpair[:, at]).astype(jnp.bfloat16)
+    for j in range(4):
+        put_cols(target, j, dot_nt(query, refs.wq[j]) + dot_nt(pair, refs.wp[j]), h_size)
+
+
+def query_fill(h_size, refs):
+    refs.total[...] = jnp.zeros_like(refs.total)
+    refs.pair_total[...] = jnp.zeros_like(refs.pair_total)
+
+    def add(n, rows):
+        at = lanes_of(n, rows.shape[0])
+        refs.total[...] += dot_nn(refs.dq[:, at], rows[...])
+        refs.pair_total[...] += dot_nn(refs.dpair[:, at], rows[...])
+
+    refs.stream("rows", add)
+    for j in range(4):
+        refs.gwq[j] = cols_at(refs.total, j, h_size).T.astype(jnp.bfloat16)
+        refs.gwp[j] = cols_at(refs.pair_total, j, h_size).T.astype(jnp.bfloat16)
+    swap_copy(refs.gwq, refs.came, refs.more.at[0], refs.more.at[1]).start()
+
+
+def query_end(refs):
+    swap_copy(refs.gwq, refs.came, refs.more.at[0], refs.more.at[1]).wait()
 
 
 def rotate_back(grads, cos_table, sin_table):
@@ -804,30 +1097,26 @@
     return (weight - rate * (update + decay * weight), first_new, second_new)
 
 
-def rows_of(blocks):
-    _, h, rows, cols = blocks.shape
-    y = c = 2
-    blocks = blocks.reshape(y, c, h, rows, cols)
-    return blocks.transpose(2, 0, 1, 3, 4).reshape(h * y * c * rows, cols)
-
-
-def cols_of(blocks):
-    _, h, rows, cols = blocks.shape
-    y = c = 2
-    blocks = blocks.reshape(y, c, h, rows, cols)
-    return blocks.transpose(3, 2, 0, 1, 4).reshape(rows, h * y * c * cols)
-
-
-def as_row_blocks(whole, h_size):
-    rows, cols = whole.shape
-    parts = whole.reshape(h_size, 2, 2, rows // (4 * h_size), cols)
-    return parts.transpose(1, 2, 0, 3, 4)
-
-
-def as_col_blocks(whole, h_size):
-    rows, cols = whole.shape
-    parts = whole.reshape(rows, h_size, 2, 2, cols // (4 * h_size))
-    return parts.transpose(2, 3, 1, 0, 4)
+def own_sum(grads, h_size, by_cols):
+    part, deep, got = grads
+    at = lax.axis_index("c")
+    pick = lambda a: lax.dynamic_index_in_dim(a, at, 0, keepdims=False).astype(jnp.float32)
+    home = at == lax.axis_index("zh")
+    total = jnp.where(home, pick(part) + pick(deep), got.astype(jnp.float32))
+    rows, cols = total.shape
+    if by_cols:
+        parts = total.reshape(rows, h_size, cols // h_size).transpose(1, 0, 2)
+    else:
+        parts = total.reshape(h_size, rows // h_size, cols)
+    parts = parts.astype(jnp.bfloat16)
+    return lax.psum_scatter(parts, "h", scatter_dimension=0, tiled=False).astype(jnp.float32)
+
+
+def flat(results):
+    out = []
+    for result in results:
+        out += result if isinstance(result, (list, tuple)) else [result]
+    return out
 
 
 def body(
@@ -881,9 +1170,15 @@
         return lax.div((at_core * zl_size + low) * 2 * (H // tensor_size), H // KVH)
 
     small_all, query_parts = run(
-        0, Everyone(small, head_of, devices), Spread(own_shard(query_weight, h_size))
-    )
-    pair_proj = small_all[:, :pair_rows].reshape(devices * pair_rows, 2 * HD)
+        0, Everyone(small, head_of, devices), SpreadAll(own_shard(query_weight, h_size))
+    )
+    pair_proj = (
+        small_all[:, :pair_rows]
+        .reshape(h_size, 4, D // (4 * h_size), 2 * HD)
+        .transpose(1, 0, 2, 3)
+        .reshape(4, D // 4, 2 * HD)
+    )
+    query_full = row_blocks(query_parts)
     gains_full = (
         small_all[:, pair_rows:]
         .reshape(devices, pad_rows * 2 * HD)[:, : 2 * gain_cols]
@@ -893,7 +1188,6 @@
     )
     gain_attn = gains_full[0].astype(jnp.float32)
     gain_mlp = gains_full[1].astype(jnp.float32)
-
     heads_here = query_weight.shape[1] // HD
 
     seg_mine = segment_ids
@@ -919,37 +1213,38 @@
 
     inverse_one = lax.rsqrt(jnp.mean(inputs * inputs, axis=1, keepdims=True) + NORM_EPS)
     normed_one = (inputs * inverse_one * gain_attn).astype(jnp.bfloat16)
-    rows_one, query_parts, output_parts, gate_parts = run(
-        1,
-        GatherRows(normed_one, along_x=True),
-        Pass(query_parts),
-        Spread(own_shard(output_weight, h_size)),
-        Spread(own_shard(gateup_weight[0], h_size)),
-    )
-    block_rows = rows_one.shape[1]
+    block_rows = inputs.shape[0]
     group_rows = 8 * block_rows
-    rows_one = rows_one.reshape(group_rows, D)
-    query_full = rows_of(query_parts)
-    query_pre = dot_tt(query_full, rows_one).reshape(heads_here, HD, group_rows)
-    pair_pre = dot_tt(pair_proj, rows_one).reshape(2, HD, group_rows)
-    query_rot = (rotate(query_pre, cos_table, sin_table).astype(jnp.bfloat16) * SCALE).astype(
-        jnp.bfloat16
-    )
-    query_rot = query_rot.reshape(heads_here * HD, group_rows)
-    key_rot = rotate(pair_pre[:1], cos_table, sin_table).astype(jnp.bfloat16)
-    pair_rot = jnp.concatenate([key_rot, pair_pre[1:].astype(jnp.bfloat16)])
-    grad_rows, pair_back_half, output_parts, gate_parts, up_parts = run(
+    width = heads_here * HD
+    gateup_t = gateup_weight.swapaxes(1, 2)
+    units = gateup_t.shape[1]
+
+    def shape(*dims, kind=jnp.bfloat16):
+        return jax.ShapeDtypeStruct(dims, kind)
+
+    rows_one, query_rot, pair_rot, output_parts, gate_parts = flat(
+        run(
+            1,
+            GatherRows(
+                normed_one,
+                along_x=True,
+                given=dict(wq=query_full, wp=pair_proj, cos=cos_table, sin=sin_table),
+                results=dict(q=shape(width, group_rows), pair=shape(2 * HD, group_rows)),
+                work=functools.partial(query_work, h_size, heads_here),
+            ),
+            Spread(own_shard(output_weight, h_size)),
+            Spread(own_shard(gateup_t[0], h_size)),
+        )
+    )
+    grad_rows, pair_back_half, output_parts, gate_parts = run(
         2,
-        GatherRows(out_grad, along_x=True),
+        GatherRows(out_grad),
         Move(pair_rot, "zh", lambda: lax.axis_index("zh") == 0),
         Pass(output_parts),
         Pass(gate_parts),
-        Spread(own_shard(gateup_weight[1], h_size)),
-    )
-    grad_rows = grad_rows.reshape(group_rows, D)
+    )
+    output_full, gate_full = col_blocks(output_parts), col_blocks(gate_parts)
     pair_back_half = jnp.where(z_high == 1, pair_back_half, 0)
-    output_full = cols_of(output_parts)
-    gate_full = rows_of(gate_parts)
     pair_window = jnp.concatenate(
         [
             pair_back_half.reshape(2, HD, 2, half_rows),
@@ -959,80 +1254,118 @@
     ).transpose(0, 2, 1, 3)
     keys_t, values_t = pair_window[0], pair_window[1]
     attended_t, log_totals = attn_fwd(block_first, start, query_rot, keys_t, values_t)
-    attn_out, up_parts, down_parts = run(
+    attn_out, up_parts = run(
         3,
-        ScatterRows(dot_tn(attended_t, output_full).astype(jnp.bfloat16)),
-        Pass(up_parts),
-        Spread(own_shard(down_weight, h_size)),
-    )
+        ScatterRows(
+            block_rows,
+            D,
+            functools.partial(output_produce, h_size),
+            given=dict(o=attended_t, wo=output_full),
+        ),
+        SpreadAll(own_shard(gateup_t[1], h_size)),
+    )
+    up_full = col_blocks(up_parts)
 
     residual_mid = inputs + attn_out
     inverse_two = lax.rsqrt(jnp.mean(residual_mid * residual_mid, axis=1, keepdims=True) + NORM_EPS)
     normed_two = (residual_mid * inverse_two * gain_mlp).astype(jnp.bfloat16)
-    rows_two, down_parts = run(4, GatherRows(normed_two), Pass(down_parts))
-    rows_two = rows_two.reshape(group_rows, D)
-    up_full = rows_of(up_parts)
-    down_full = cols_of(down_parts)
-    gate_proj = dot_nn(rows_two, gate_full)
-    up_proj = dot_nn(rows_two, up_full)
-    sigmoid_gate = jax.nn.sigmoid(gate_proj)
-    silu_gate = gate_proj * sigmoid_gate
-    hidden_mlp = (silu_gate * up_proj).astype(jnp.bfloat16)
-
-    down_grad = halves(as_col_blocks(dot_tn(hidden_mlp, grad_rows), h_size), h_size)
-    mlp_out, down_came = run(
-        5,
-        ScatterRows(dot_nn(hidden_mlp, down_full).astype(jnp.bfloat16)),
-        Swap(down_grad),
+    hidden_shape = shape(8, block_rows, units)
+    rows_two, hidden_mlp, by_gate, by_up, down_parts = flat(
+        run(
+            4,
+            GatherRows(
+                normed_two,
+                along_x=True,
+                given=dict(wg=gate_full, wu=up_full),
+                results=dict(hid=hidden_shape, by_gate=hidden_shape, by_up=hidden_shape),
+                work=functools.partial(gateup_work, h_size),
+            ),
+            SpreadAll(own_shard(down_weight, h_size)),
+        )
+    )
+    down_full = col_blocks(down_parts)
+
+    sums = pltpu.VMEM((4, units, D // 4), jnp.float32)
+    whole_grad, half_grad = shape(4, units, D // 4), shape(2, units, D // 4)
+    mlp_out, gate_grad, up_grad, down_grad, down_came = flat(
+        run(
+            5,
+            ScatterRows(
+                block_rows,
+                D,
+                functools.partial(down_produce, h_size),
+                given=dict(hid=hidden_mlp, wd=down_full, by_gate=by_gate, by_up=by_up),
+                streams=dict(dy=grad_rows),
+                results=dict(dgate=hidden_shape, dup=hidden_shape, gwd=whole_grad),
+                scratch=dict(total=sums),
+                far=dict(came=half_grad),
+                extra_sems=2,
+                fill_one=functools.partial(down_fill_one, h_size),
+                fill_two=functools.partial(down_fill_two, h_size),
+                end=down_end,
+            ),
+        )
     )
     hidden_out = (residual_mid + mlp_out).astype(jnp.bfloat16)
     down_part = add_swapped(down_grad, down_came)
-    hidden_grad = dot_nt(grad_rows, down_full)
-    gate_grad = (
-        hidden_grad * up_proj * sigmoid_gate * (1.0 + gate_proj * (1.0 - sigmoid_gate))
-    ).astype(jnp.bfloat16)
-    up_grad = (hidden_grad * silu_gate).astype(jnp.bfloat16)
-    gate_wgrad = halves(as_row_blocks(dot_tn(rows_two, gate_grad), h_size), h_size)
-    up_wgrad = halves(as_row_blocks(dot_tn(rows_two, up_grad), h_size), h_size)
-    normed_two_grad, gate_came, down_deep = run(
-        6,
-        ScatterRows(
-            (dot_nt(gate_grad, gate_full) + dot_nt(up_grad, up_full)).astype(jnp.bfloat16)
-        ),
-        Swap(gate_wgrad),
-        Move(down_part, "zh", not_home),
+    normed_two_grad, gate_wgrad, up_wgrad, gate_came, down_deep = flat(
+        run(
+            6,
+            ScatterRows(
+                block_rows,
+                D,
+                functools.partial(gateup_produce, h_size),
+                given=dict(dgate=gate_grad, dup=up_grad, wg=gate_full, wu=up_full),
+                streams=dict(rows=rows_two),
+                results=dict(gwg=whole_grad, gwu=whole_grad),
+                scratch=dict(total=sums),
+                far=dict(came=half_grad),
+                extra_sems=2,
+                fill_one=functools.partial(gateup_fill_one, h_size),
+                fill_two=functools.partial(gateup_fill_two, h_size),
+                end=gateup_end,
+            ),
+            Move(down_part, "zh", not_home),
+        )
     )
     gate_part = add_swapped(gate_wgrad, gate_came)
     mid_back, gain_mlp_grad = norm_back(normed_two_grad, residual_mid, inverse_two, gain_mlp)
     mid_grad = out_grad.astype(jnp.float32) + mid_back
-    attn_grad_rows, up_came, gate_deep, down_got = run(
-        7,
-        GatherRows(mid_grad.astype(jnp.bfloat16)),
-        Swap(up_wgrad),
-        Move(gate_part, "zh", not_home),
-        Move(for_partner(down_part, down_deep), "c", at_home),
-    )
-    attn_grad_rows = attn_grad_rows.reshape(group_rows, D)
+    attended_grad, output_grad, up_came, gate_deep, down_got = flat(
+        run(
+            7,
+            GatherRows(
+                mid_grad.astype(jnp.bfloat16),
+                keep=False,
+                given=dict(o=attended_t, wo=output_full),
+                results=dict(do=shape(width, group_rows), gwo=shape(*output_full.shape)),
+                scratch=dict(total=pltpu.VMEM(output_full.shape, jnp.float32)),
+                before=output_before,
+                work=functools.partial(output_work, h_size),
+                after=output_after,
+            ),
+            Swap(up_wgrad),
+            Move(gate_part, "zh", not_home),
+            Move(for_partner(down_part, down_deep), "c", at_home),
+        )
+    )
     up_part = add_swapped(up_wgrad, up_came)
-    output_grad = halves(as_col_blocks(dot_nn(attended_t, attn_grad_rows), h_size), h_size)
-    attended_grad = dot_nt(output_full, attn_grad_rows).astype(jnp.bfloat16)
     query_grads, key_grads, value_grads = attn_bwd(
         block_first, start, query_rot, attended_t, attended_grad, log_totals, keys_t, values_t
     )
     query_back = (
         rotate_back(query_grads.reshape(heads_here, HD, group_rows), cos_table, sin_table)
         .astype(jnp.bfloat16)
-        .reshape(heads_here * HD, group_rows)
+        .reshape(width, group_rows)
     )
     pair_grads = jnp.stack([key_grads, value_grads]).transpose(0, 2, 1, 3)
-    pair_later, up_deep, output_came, gate_got = run(
+    pair_later, output_came, gate_got = run(
         8,
         Move(
             pair_grads[..., :KEYS_BACK].astype(jnp.bfloat16),
             "zh",
             lambda: lax.axis_index("zh") == 1,
         ),
-        Move(up_part, "zh", not_home),
         Swap(output_grad),
         Move(for_partner(gate_part, gate_deep), "c", at_home),
     )
@@ -1043,35 +1376,50 @@
         [rotate_back(pair_sum[:1], cos_table, sin_table), pair_sum[1:]]
     ).astype(jnp.bfloat16)
     pair_back = pair_back.reshape(2 * HD, group_rows)
-    query_wgrad = halves(as_row_blocks(dot_tt(rows_one, query_back), h_size), h_size)
-    pair_wgrad = dot_tt(rows_one, pair_back)
-    normed_one_grad, query_came, output_deep, up_got = run(
-        9,
-        ScatterRows(
-            (dot_tt(query_back, query_full) + dot_tt(pair_back, pair_proj)).astype(jnp.bfloat16)
-        ),
-        Swap(query_wgrad),
-        Move(output_part, "zh", not_home),
-        Move(for_partner(up_part, up_deep), "c", at_home),
+    quarter = D // 4
+    normed_one_grad, query_wgrad, pair_wgrad, query_came, up_deep, output_deep = flat(
+        run(
+            9,
+            ScatterRows(
+                block_rows,
+                D,
+                functools.partial(query_produce, h_size),
+                given=dict(dq=query_back, dpair=pair_back, wq=query_full, wp=pair_proj),
+                streams=dict(rows=rows_one),
+                results=dict(gwq=shape(4, quarter, width), gwp=shape(4, quarter, 2 * HD)),
+                scratch=dict(
+                    total=pltpu.VMEM((width, D), jnp.float32),
+                    pair_total=pltpu.VMEM((2 * HD, D), jnp.float32),
+                ),
+                far=dict(came=shape(2, quarter, width)),
+                extra_sems=2,
+                fill_one=functools.partial(query_fill, h_size),
+                end=query_end,
+            ),
+            Move(up_part, "zh", not_home),
+            Move(output_part, "zh", not_home),
+        )
     )
     query_part = add_swapped(query_wgrad, query_came)
+    pair_wgrad = (
+        pair_wgrad.reshape(4, h_size, quarter // h_size, 2 * HD)
+        .transpose(1, 0, 2, 3)
+        .reshape(devices, pair_rows, 2 * HD)
+    )
     input_back, gain_attn_grad = norm_back(normed_one_grad, inputs, inverse_one, gain_attn)
     input_grad = mid_grad + input_back
     gains_grad = jnp.stack([gain_attn_grad, gain_mlp_grad]).reshape(2, devices, gain_cols)
     gains_grad = gains_grad.transpose(1, 0, 2).reshape(devices, 2 * gain_cols)
     gains_grad = jnp.pad(gains_grad, ((0, 0), (0, pad_rows * 2 * HD - 2 * gain_cols)))
     small_grads = jnp.concatenate(
-        [
-            pair_wgrad.reshape(devices, pair_rows, 2 * HD),
-            gains_grad.reshape(devices, pad_rows, 2 * HD),
-        ],
-        axis=1,
-    ).astype(jnp.bfloat16)
-    small_sums, query_deep, output_got = run(
+        [pair_wgrad, gains_grad.reshape(devices, pad_rows, 2 * HD).astype(jnp.bfloat16)], axis=1
+    )
+    small_sums, query_deep, output_got, up_got = run(
         10,
         Everyone(small_grads, lambda device: device, devices),
         Move(query_part, "zh", not_home),
         Move(for_partner(output_part, output_deep), "c", at_home),
+        Move(for_partner(up_part, up_deep), "c", at_home),
     )
     query_got = lax.ppermute(for_partner(query_part, query_deep), ("c", "zh"), TO_AWAY_CORE)
     small_sums = small_sums.astype(jnp.float32)
@@ -1097,20 +1445,31 @@
         ]
     )
 
-    def adam(weight, first, second, rate, *grads):
-        shape = weight.shape
-        three = lambda a: a.reshape((-1,) + shape[-2:])
-        new = adam_shard(three(weight), three(first), three(second), grads, rate, fixes)
-        return tuple(a.reshape(shape) for a in new)
+    def adam(weight, first, second, rate, by_cols, *grads):
+        dims = weight.shape
+        three = lambda a: a.reshape((-1,) + dims[-2:])
+        if h_size == 1:
+            new = adam_shard(three(weight), three(first), three(second), grads, rate, fixes)
+            return tuple(a.reshape(dims) for a in new)
+        return adam_step(
+            weight,
+            jnp.stack([own_sum(g, h_size, by_cols) for g in grads]).reshape(dims),
+            first,
+            second,
+            rate,
+            DECAY,
+            step_value,
+        )
 
     down_new, down_mone, down_mtwo = adam(
-        down_weight, down_first, down_second, FF ** (-0.5), (down_part, down_deep, down_got)
+        down_weight, down_first, down_second, FF ** (-0.5), True, (down_part, down_deep, down_got)
     )
     gateup_new, gateup_mone, gateup_mtwo = adam(
-        gateup_weight,
-        gateup_first,
-        gateup_second,
+        gateup_t,
+        gateup_first.swapaxes(1, 2),
+        gateup_second.swapaxes(1, 2),
         D ** (-0.5),
+        True,
         (gate_part, gate_deep, gate_got),
         (up_part, up_deep, up_got),
     )
@@ -1119,10 +1478,16 @@
         output_first,
         output_second,
         (H * HD // 16) ** (-0.5),
+        True,
         (output_part, output_deep, output_got),
     )
     query_new, query_mone, query_mtwo = adam(
-        query_weight, query_first, query_second, D ** (-0.5), (query_part, query_deep, query_got)
+        query_weight,
+        query_first,
+        query_second,
+        D ** (-0.5),
+        False,
+        (query_part, query_deep, query_got),
     )
     pair_new, pair_mone, pair_mtwo = adam_step(
         keyvalue_weight,
@@ -1142,19 +1507,19 @@
         query_new,
         pair_new,
         output_new,
-        gateup_new,
+        gateup_new.swapaxes(1, 2),
         down_new,
         gains_new,
         query_mone,
         pair_mone,
         output_mone,
-        gateup_mone,
+        gateup_mone.swapaxes(1, 2),
         down_mone,
         gains_mone,
         query_mtwo,
         pair_mtwo,
         output_mtwo,
-        gateup_mtwo,
+        gateup_mtwo.swapaxes(1, 2),
         down_mtwo,
         gains_mtwo,
     )

time: 992 us -> 820 us (0.83); the launches traced: 978 us -> 816 us
  matrix products: 158 us -> 0 us
  local copies, waits for them, and re-layouts: 121 us -> 37.1 us
  Pallas kernels: 630 us -> 709 us
    dot_general x18 -> x0, matrix products: 158 us -> none  [the longest x4 48.3 us: dot_nt(): lax.dot_general(left, right, (((1,), (1,)), ((), ())), preferred_element_...]
    pallas_call x11, Pallas kernels: 571 us -> 651 us  [run(): pl.pallas_call(kernel, in_specs=in_specs, out_specs=out_specs, out_shape=...]
    dot_general x5 -> x0, local copies, waits for them, and re-layouts: 51.1 us -> none  [the longest x2 24.6 us: dot_tn(): lax.dot_general(left, right, (((0,), (0,)), ((), ())), preferred_element_...]
    reshape x3 -> x2, local copies, waits for them, and re-layouts: 14.8 us -> 1.54 us  [body(): pair_rot.reshape(2, HD, 2, half_rows)]
    unnamed x217 -> x147, local copies, waits for them, and re-layouts: 32.2 us -> 21.4 us
  transfers between devices with their start and end apart: 2 -> 2, of which waited for: 0 -> 0; matrix products, arithmetic and copies ran while one was open for 8% -> 4% of each run, Pallas kernels for 12% -> 5%
where the time goes in v3:
time: 820 us; the launch traced here: 816 us
  Pallas kernels  709 us (86%)
  other arithmetic  64.7 us (8%)
  local copies, waits for them, and re-layouts  37.1 us (5%)
    pallas_call x11, Pallas kernels, run(): pl.pallas_call(kernel, in_specs=in_specs, out_specs=out_specs, out_shape=...  651 us
    pallas_call x1, Pallas kernels, attn_bwd(): pl.pallas_call(functools.partial(attn_bwd_kernel, heads), grid_spec=pltpu...  23.3 us
    unnamed x147, local copies, waits for them, and re-layouts  21.4 us
    pallas_call x1, Pallas kernels, attn_fwd(): pl.pallas_call(functools.partial(attn_fwd_kernel, heads), grid_spec=pltpu...  17.9 us
    pallas_call x4, Pallas kernels, adam_shard(): pl.pallas_call(functools.partial(adam_kernel, rate, DECAY, groups), grid_...  16.6 us
  transfers between devices with their start and end apart: 2, of which 0 were waited for; matrix products, arithmetic and copies ran while one was open for 4% of the time, Pallas kernels for 5%

profile of v3, /device:TPU:0, one launch (start us, length us, event | category | flops | bytes accessed | tf_op | source)
XLA Modules:
  0.0 816.3 jit_solution(11319673968879772396)
XLA Ops:
  3.6 1.8 convert_bitcast_fusion.2.refs_1_
  6.0 27.7 %shard_map.365 = (bf16[32,80,128]{2,1,0:T(8,128)(2,1)}, bf16[4,1,512,256]{3,2,1,0:T(8,128)(2,1)}) custom-call(bf16[4,80,128]{2,1,0:T(8,128)(2,1)} %pad_maximum_fusion.3.refs_0_, bf16[1,512,256]{2,1,0:T(8,128)(2,1)} %convert_bitcast_fusion.2.refs_1_), custom_call_target="tpu_custom_call" | custom-call | tf_op jit(solution)/shard_map/pallas_call | solution.py:714
  35.0 1.5 fusion.7
  43.2 1.8 multiply_sine_fusion.1
  45.0 92.8 %shard_map.366 = (bf16[8,256,2048]{2,1,0:T(8,128)(2,1)}, bf16[256,2048]{1,0:T(8,128)(2,1)}, bf16[128,2048]{1,0:T(8,128)(2,1)}, bf16[4,1,256,512]{3,2,1,0:T(8,128)(2,1)}, bf16[4,1,704,512]{3,2,1,0:T(8,128)(2,1)}) custom-call(bf16[256,2048]{1,0:T(8,128)(2,1)} %fusion.2.refs_0_, bf16[4,512,256]{2,1,0:T(8,128)(2,1)} %bitcast.114, ...), custom_call_target="tpu_custom_call" | custom-call | tf_op jit(solution)/shard_map/pallas_call | solution.py:714
  137.9 1.4 reshape.373
  139.3 52.4 %shard_map.367 = (bf16[8,256,2048]{2,1,0:T(8,128)(2,1)}, bf16[128,2048]{1,0:T(8,128)(2,1)}, bf16[4,1,256,512]{3,2,1,0:T(8,128)(2,1)}, bf16[4,1,704,512]{3,2,1,0:T(8,128)(2,1)}) custom-call(bf16[256,2048]{1,0:T(8,128)(2,1)} %refs_0_.1, bf16[128,2048]{1,0:T(8,128)(2,1)} %get-tuple-element.86.refs_1_, ...), custom_call_target="tpu_custom_call", output_to_operand_aliasing={{2}: (2, {}), {3}: (3, {})} | custom-call | tf_op jit(solution)/shard_map/pallas_call | solution.py:714
  193.7 17.9 %shard_map.368 = (bf16[256,2048]{1,0:T(8,128)(2,1)S(1)}, f32[2,4,1024]{2,1,0:T(4,128)S(1)}) custom-call(s32[2,4]{1,0:T(2,128)S(1)} %slice.76.first_ref, s32[2,1,1024]{2,1,0:T(1,128)S(1)} %broadcast_in_dim.41.start_ref, bf16[256,2048]{1,0:T(8,128)(2,1)S(1)} %copy-done.13, bf16[2,64,2048]{2,1,0:T(8,128)(2,1)S(1)} %get-tuple-element.172.kt_ref, ...), custom_call_target="tpu_custom_call" | custom-call | tf_op jit(solution)/shard_map/pallas_call | solution.py:836
  212.6 62.0 %shard_map.369 = (f32[256,2048]{1,0:T(8,128)}, bf16[4,1,704,512]{3,2,1,0:T(8,128)(2,1)}) custom-call(bf16[256,2048]{1,0:T(8,128)(2,1)} %copy-done.6, bf16[4,256,512]{2,1,0:T(8,128)(2,1)} %bitcast.109, bf16[1,704,512]{2,1,0:T(8,128)(2,1)} %get-tuple-element.169.refs_2_), custom_call_target="tpu_custom_call" | custom-call | tf_op jit(solution)/shard_map/pallas_call | solution.py:714
  274.6 2.0 multiply_reduce_fusion.2
  279.1 81.5 %shard_map.370 = (bf16[8,256,2048]{2,1,0:T(8,128)(2,1)}, bf16[8,256,704]{2,1,0:T(8,128)(2,1)}, bf16[8,256,704]{2,1,0:T(8,128)(2,1)}, bf16[8,256,704]{2,1,0:T(8,128)(2,1)}, bf16[4,1,704,512]{3,2,1,0:T(8,128)(2,1)}) custom-call(bf16[256,2048]{1,0:T(8,128)(2,1)} %multiply_convert_fusion.refs_0_, bf16[4,704,512]{2,1,0:T(8,128)(2,1)} %bitcast.105, ...), custom_call_target="tpu_custom_call" | custom-call | tf_op jit(solution)/shard_map/pallas_call | solution.py:714
  360.6 78.1 %shard_map.371 = (f32[256,2048]{1,0:T(8,128)}, bf16[8,256,704]{2,1,0:T(8,128)(2,1)}, bf16[8,256,704]{2,1,0:T(8,128)(2,1)}, bf16[4,704,512]{2,1,0:T(8,128)(2,1)}, bf16[2,704,512]{2,1,0:T(8,128)(2,1)}) custom-call(bf16[8,256,704]{2,1,0:T(8,128)(2,1)} %get-tuple-element.95.refs_0_, bf16[4,704,512]{2,1,0:T(8,128)(2,1)} %bitcast.117, ...), custom_call_target="tpu_custom_call" | custom-call | tf_op jit(solution)/shard_map/pallas_call | solution.py:714
  438.6 3.3 add_convert_fusion.2.refs_5_.refs_0_
  441.9 69.1 %shard_map.372 = (f32[256,2048]{1,0:T(8,128)}, bf16[4,704,512]{2,1,0:T(8,128)(2,1)}, bf16[4,704,512]{2,1,0:T(8,128)(2,1)}, bf16[2,704,512]{2,1,0:T(8,128)(2,1)}, bf16[2,704,512]{2,1,0:T(8,128)(2,1)}) custom-call(bf16[8,256,704]{2,1,0:T(8,128)(2,1)} %get-tuple-element.101.refs_0_, bf16[8,256,704]{2,1,0:T(8,128)(2,1)} %get-tuple-element.102.refs_1_, ...), custom_call_target="tpu_custom_call" | custom-call | tf_op jit(solution)/shard_map/pallas_call | solution.py:714
  511.0 3.5 multiply_reduce_fusion
  514.6 1.8 fusion.33.refs_0_
  518.5 1.5 add_convert_fusion.1.refs_4_.refs_0_
  520.0 63.5 %shard_map.373 = (bf16[256,2048]{1,0:T(8,128)(2,1)}, bf16[4,256,512]{2,1,0:T(8,128)(2,1)}, bf16[2,704,512]{2,1,0:T(8,128)(2,1)}, bf16[2,704,512]{2,1,0:T(8,128)(2,1)}, bf16[704,512]{1,0:T(8,128)(2,1)}) custom-call(bf16[256,2048]{1,0:T(8,128)(2,1)} %fusion.33.refs_0_, bf16[256,2048]{1,0:T(8,128)(2,1)} %copy-done.6, bf16[4,256,512]{2,1,0:T(8,128)(2,1)} %bitcast.110, ...), custom_call_target="tpu_custom_call" | custom-call | tf_op jit(solution)/shard_map/pallas_call | solution.py:714
  583.6 2.3 fusion.12.refs_2_
  585.9 23.3 %shard_map.374 = (f32[256,2048]{1,0:T(8,128)}, f32[2,64,2048]{2,1,0:T(8,128)S(1)}, f32[2,64,2048]{2,1,0:T(8,128)S(1)}) custom-call(s32[2,4]{1,0:T(2,128)S(1)} %slice.76.first_ref, s32[2,1,1024]{2,1,0:T(1,128)S(1)} %broadcast_in_dim.41.start_ref, bf16[256,2048]{1,0:T(8,128)(2,1)S(1)} %copy-done.14, bf16[256,2048]{1,0:T(8,128)(2,1)S(1)} %copy-done.7, ...), custom_call_target="tpu_custom_call" | custom-call | tf_op jit(solution)/shard_map/pallas_call | solution.py:869
  609.2 1.6 copy_bitcast_fusion
  613.2 27.6 %shard_map.375 = (bf16[2,64,2,1024]{3,2,1,0:T(2,128)(2,1)}, bf16[2,256,512]{2,1,0:T(8,128)(2,1)}, bf16[704,512]{1,0:T(8,128)(2,1)}) custom-call(bf16[2,64,2,1024]{3,2,1,0:T(2,128)(2,1)} %slice.138.refs_0_, bf16[4,256,512]{2,1,0:T(8,128)(2,1)} %get-tuple-element.116.refs_1_, bf16[704,512]{1,0:T(8,128)(2,1)} %fusion.12.refs_2_), custom_call_target="tpu_custom_call" | custom-call | tf_op jit(solution)/shard_map/pallas_call | solution.py:714
  640.9 1.9 slice_add_fusion
  644.0 2.1 add_convert_fusion.8.refs_6_.refs_0_
  646.0 1.5 add_convert_fusion.refs_5_.refs_3_
  648.0 1.9 fusion.19
  650.1 1.8 add_convert_fusion.9
  653.8 61.7 %shard_map.376 = (f32[256,2048]{1,0:T(8,128)}, bf16[4,512,256]{2,1,0:T(8,128)(2,1)}, bf16[4,512,128]{2,1,0:T(8,128)(2,1)}, bf16[2,512,256]{2,1,0:T(8,128)(2,1)},...) custom-call(bf16[256,2048]{1,0:T(8,128)(2,1)} %bitcast.113, bf16[128,2048]{1,0:T(8,128)(2,1)} %bitcast.119, ...), custom_call_target="tpu_custom_call" | custom-call | tf_op jit(solution)/shard_map/pallas_call | solution.py:714
  715.6 2.3 fusion.13.refs_3_
  718.7 2.2 fusion.10
  721.2 1.9 pad_maximum_fusion.1.refs_0_
  723.1 2.1 add_convert_fusion.7.refs_1_.refs_0_
  725.2 34.9 %shard_map.377 = (bf16[32,80,128]{2,1,0:T(8,128)(2,1)}, bf16[2,512,256]{2,1,0:T(8,128)(2,1)}, bf16[256,512]{1,0:T(8,128)(2,1)}, bf16[704,512]{1,0:T(8,128)(2,1)}) custom-call(bf16[32,80,128]{2,1,0:T(8,128)(2,1)} %pad_maximum_fusion.1.refs_0_, bf16[2,512,256]{2,1,0:T(8,128)(2,1)} %add_convert_fusion.7.refs_1_.refs_0_, bf16[256,512]{1,0:T(8,128)(2,1)} %fusion.22.refs_2_, ...), custom_call_target="tpu_custom_call" | custom-call | tf_op jit(solution)/shard_map/pallas_call | solution.py:714
  760.2 1.7 fusion.23
  761.9 2.2 collective-permute-start.1
  765.5 7.2 fusion.6
  774.4 2.0 reduce_sum.107
  776.4 2.1 reshape.381
  778.5 2.2 reduce_sum.108
  783.6 1.4 copy-done.12
  785.0 1.4 copy-done.16
  786.4 1.4 copy-done.24
  787.7 1.4 copy-done.25
  790.2 4.1 shard_map.381
  798.6 2.5 shard_map.379
  801.1 1.8 copy-done.20
  805.2 7.1 shard_map.380
  813.1 2.9 shard_map.378
  (211 shorter events, 39.6 us)
Async XLA Ops:
  0.7 35.8 %copy-start.4 = (f32[2,512,704]{1,2,0:T(8,128)S(1)}, f32[2,512,704]{1,2,0:T(8,128)}, u32[]{:S(2)}) copy-start(f32[2,512,704]{1,2,0:T(8,128)} %param.29) | copy-start | bytes 8650756
  0.7 42.2 %collective-permute-start = (s32[1,2048]{1,0:T(1,128)}, s32[1,2048]{1,0:T(1,128)S(1)}, u32[]{:S(2)}, u32[]{:S(2)}) collective-permute-start(s32[1,2048]{1,0:T(1,128)} %param.24), channel_id=1, source_target_pairs={{0,8},{8,0},{1,9},{9,1},{2,10},{10,2},{3,11},{11,3},{4,12},{12,4},... | collective-permute-start | bytes 24584 | tf_op jit(solution)/shard_map/ppermute | solution.py:1194
  1.2 42.0 %copy-start.67 = (f32[32]{0:T(128)}, f32[32]{0:T(128)S(1)}, u32[]{:S(2)}) copy-start(f32[32]{0:T(128)S(1)} %multiply_power_fusion) | copy-start | bytes 388
  34.9 5.5 copy-start.54
  36.5 4.0 copy-start.61
  37.9 2.6 copy-start.39
  38.8 3.2 copy-start.52
  39.7 3.1 copy-start.66
  43.2 94.7 %copy-start.58 = (f32[1,8,2,128]{3,1,2,0:T(8,128)}, f32[1,8,2,128]{3,1,2,0:T(8,128)S(1)}, u32[]{:S(2)}) copy-start(f32[1,8,2,128]{3,1,2,0:T(8,128)S(1)} %copy.85) | copy-start | bytes 24580
  276.5 238.0 %copy-start.59 = (f32[256]{0:T(256)}, f32[256]{0:T(256)S(1)}, u32[]{:S(2)}) copy-start(f32[256]{0:T(256)S(1)} %add_rsqrt_fusion) | copy-start | bytes 3076
  441.9 72.6 %copy-start.42 = (bf16[256,2048]{1,0:T(8,128)(2,1)S(1)}, bf16[256,2048]{1,0:T(8,128)(2,1)}, u32[]{:S(2)}) copy-start(bf16[256,2048]{1,0:T(8,128)(2,1)} %refs_0_.1) | copy-start | bytes 3145732
  511.0 3.6 copy-start.38
  511.0 3.6 copy-start.41
  514.6 3.1 copy-start.51
  520.0 63.6 %copy-start.2 = (bf16[2,704,512]{2,1,0:T(8,128)(2,1)S(1)}, bf16[2,704,512]{2,1,0:T(8,128)(2,1)}, u32[]{:S(2)}) copy-start(bf16[2,704,512]{2,1,0:T(8,128)(2,1)} %add_convert_fusion.1.refs_4_.refs_0_) | copy-start | bytes 4325380
  640.8 3.1 copy-start.48
  640.8 5.2 copy-start.49
  642.8 3.2 copy-start.43
  647.5 2.5 copy-start.46
  647.5 2.6 copy-start.47
  653.8 61.8 %copy-start = (bf16[2,704,512]{2,1,0:T(8,128)(2,1)S(1)}, bf16[2,704,512]{2,1,0:T(8,128)(2,1)}, u32[]{:S(2)}) copy-start(bf16[2,704,512]{2,1,0:T(8,128)(2,1)} %add_convert_fusion.refs_5_.refs_3_) | copy-start | bytes 4325380
  715.5 2.4 copy-start.8
  715.5 3.1 copy-start.40
  715.5 3.1 copy-start.55
  715.5 3.1 copy-start.62
  717.9 3.0 copy-start.63
  725.2 34.9 %copy-start.9 = (bf16[2,512,256]{2,1,0:T(8,128)(2,1)S(1)}, bf16[2,512,256]{2,1,0:T(8,128)(2,1)}, u32[]{:S(2)}) copy-start(bf16[2,512,256]{2,1,0:T(8,128)(2,1)} %add_convert_fusion.7.refs_1_.refs_0_) | copy-start | bytes 1572868
  725.2 40.2 %copy-start.60 = (f32[256]{0:T(256)S(1)}, f32[256]{0:T(256)}, u32[]{:S(2)}) copy-start(f32[256]{0:T(256)} %copy-done.59) | copy-start | bytes 3076
  725.2 40.2 %copy-start.65 = (f32[256]{0:T(256)S(1)}, f32[256]{0:T(256)}, u32[]{:S(2)}) copy-start(f32[256]{0:T(256)} %copy-done.64) | copy-start | bytes 3076
  761.9 51.2 %collective-permute-start.1 = (bf16[512,256]{1,0:T(8,128)(2,1)}, bf16[512,256]{1,0:T(8,128)(2,1)}, u32[]{:S(2)}, u32[]{:S(2)}) collective-permute-start(bf16[512,256]{1,0:T(8,128)(2,1)} %fusion.23), channel_id=1, source_target_pairs={{0,8},{12,4},{1,9},{13,5},{2,10},{14,6},{3,11},{15,7},{16,24},{28,... | collective-permute-start | bytes 786440 | tf_op jit(solution)/shard_map/ppermute | solution.py:1424
  765.4 7.3 copy-start.68
  765.5 7.3 copy-start.69
  765.5 7.3 copy-start.70
  765.5 7.9 copy-start.44
  790.2 4.2 copy-start.22
  790.2 10.9 %copy-start.5 = (f32[2,512,704]{1,2,0:T(8,128)S(1)}, f32[2,512,704]{1,2,0:T(8,128)}, u32[]{:S(2)}) copy-start(f32[2,512,704]{1,2,0:T(8,128)} %param.29) | copy-start | bytes 8650756
  790.2 10.9 %copy-start.18 = (bf16[2,704,512]{2,1,0:T(8,128)(2,1)S(1)}, bf16[2,704,512]{2,1,0:T(8,128)(2,1)}, u32[]{:S(2)}) copy-start(bf16[2,704,512]{2,1,0:T(8,128)(2,1)} %get-tuple-element.127.refs_4_) | copy-start | bytes 4325380
  790.2 10.9 %copy-start.19 = (f32[2,512,704]{1,2,0:T(8,128)S(1)}, f32[2,512,704]{1,2,0:T(8,128)}, u32[]{:S(2)}) copy-start(f32[2,512,704]{1,2,0:T(8,128)} %param.35) | copy-start | bytes 8650756
  794.3 6.7 copy-start.3
  794.3 6.7 copy-start.17
  805.1 7.2 copy-start.53
  805.1 7.2 copy-start.56
  805.1 7.2 copy-start.57
  805.1 8.0 copy-start.10
  805.1 8.0 copy-start.23
  805.2 8.0 copy-start.28
  805.2 8.0 copy-start.34
  805.2 8.0 copy-start.35
  (26 other events, 38.7 us)

commit v4 on v3

--- a/solution.py
+++ b/solution.py
@@ -323,21 +323,66 @@
 class Fused:
     alias = {}
 
-    def name(self, given, streams, results, scratch, far):
+    def name(self, given, streams, results, scratch, far, by_block):
         self.given, self.streams = list(given), list(streams)
         self.results, self.held, self.far = list(results), list(scratch), list(far)
+        self.by_block = by_block
         self.inputs += list(given.values()) + list(streams.values())
-        self.in_spaces += [pltpu.VMEM] * len(given) + [pl.ANY] * len(streams)
         self.outputs += list(results.values()) + list(far.values())
-        self.out_spaces += [pltpu.VMEM] * len(results) + [pl.ANY] * len(far)
+        self.sems += [max(1, len(given)), (max(1, len(results)), 8)]
+        self.scratch += [pltpu.VMEM(a.shape, a.dtype) for a in given.values()]
+        self.scratch += [pltpu.VMEM(a.shape, a.dtype) for a in results.values()]
         self.scratch += list(scratch.values())
 
-    def bind(self, ins, outs, scratch):
-        names = self.given + self.streams + self.results + self.far + self.held
+    def bind(self, ins, outs, sems, scratch):
         tail = lambda refs, n: list(refs)[len(refs) - n :] if n else []
-        refs = tail(ins, len(self.given) + len(self.streams))
-        refs += tail(outs, len(self.results) + len(self.far)) + tail(scratch, len(self.held))
-        return types.SimpleNamespace(**dict(zip(names, refs)))
+        moved = tail(ins, len(self.given) + len(self.streams))
+        back = tail(outs, len(self.results) + len(self.far))
+        held = tail(scratch, len(self.given) + len(self.results) + len(self.held))
+        refs = types.SimpleNamespace(**dict(zip(self.given + self.results + self.held, held)))
+        for key, ref in zip(self.streams, moved[len(self.given) :]):
+            setattr(refs, key, ref)
+        for key, ref in zip(self.far, back[len(self.results) :]):
+            setattr(refs, key, ref)
+        fetch_sem, flush_sem = sems[-2], sems[-1]
+        at_given = {key: n for n, key in enumerate(self.given)}
+        at_result = {key: n for n, key in enumerate(self.results)}
+
+        def fetch(key):
+            n = at_given[key]
+            return pltpu.make_async_copy(moved[n], held[n], fetch_sem.at[n])
+
+        def flush(key, block=None):
+            n = at_result[key]
+            here, there = held[len(self.given) + n], back[n]
+            if block is None:
+                return pltpu.make_async_copy(here, there, flush_sem.at[n, 0])
+            return pltpu.make_async_copy(here.at[block], there.at[block], flush_sem.at[n, block])
+
+        refs.fetch, refs.flush = fetch, flush
+        return refs
+
+    def fetch_all(self, refs):
+        for key in self.given:
+            refs.fetch(key).start()
+
+    def ready(self, refs, keys):
+        for key in keys:
+            refs.fetch(key).wait()
+
+    def flush_block(self, refs, block):
+        for key in self.by_block:
+            refs.flush(key, block).start()
+
+    def flushed(self, refs):
+        for key in self.results:
+            if key in self.by_block:
+
+                @pl.loop(0, 8)
+                def _(block):
+                    refs.flush(key, block).wait()
+            else:
+                refs.flush(key).wait()
 
 
 class GatherRows(Fused):
@@ -348,37 +393,42 @@
         keep=True,
         given={},
         results={},
+        by_block=(),
         scratch={},
         before=None,
         work=None,
         after=None,
     ):
         gathered = (8,) + block.shape
-        self.inputs, self.in_spaces = [block], [pl.ANY]
-        self.outputs, self.out_spaces, self.scratch = [], [], []
-        self.keep, self.along_x = keep, along_x
+        self.inputs, self.outputs, self.scratch = [block], [], []
+        self.in_vmem = work is not None
+        self.along_x = along_x
         self.before, self.work, self.after = before, work, after
-        if keep:
+        self.sems = [7, 8, 1]
+        if self.in_vmem:
+            self.scratch = [pltpu.VMEM(gathered, block.dtype)]
+        else:
             self.outputs = [jax.ShapeDtypeStruct(gathered, block.dtype)]
-            self.out_spaces = [pltpu.VMEM if work else pl.ANY]
-        else:
-            self.scratch = [pltpu.VMEM(gathered, block.dtype)]
-        self.sems = [7, 8, 1]
-        self.name(given, {}, results, scratch, {})
+        self.keep = keep and self.in_vmem
+        if self.keep:
+            self.outputs = [jax.ShapeDtypeStruct(gathered, block.dtype)]
+            self.sems += [8]
+        self.name(given, {}, results, scratch, {}, by_block)
 
     def where(self, outs, scratch):
-        return outs[0] if self.keep else scratch[0]
+        return scratch[0] if self.in_vmem else outs[0]
 
     def begin(self, ins, outs, sems, scratch):
-        src, dst, (send, recv, local) = ins[0], self.where(outs, scratch), sems
+        src, dst, (send, recv, local) = ins[0], self.where(outs, scratch), sems[:3]
         own = group_index(*(lax.axis_index(a) for a in ("c", "zl", "x")))
-        for way, axis in enumerate(("x", "zl", "c")):
+        for way, axis in enumerate(("zl", "x", "c")):
             far_copy(src, dst.at[own], send.at[way], recv.at[own], flipped(axis)).start()
         pltpu.make_async_copy(src, dst.at[own], local.at[0]).start()
-
-    def finish(self, ins, outs, sems, scratch, middle):
-        src, dst, (send, recv, local) = ins[0], self.where(outs, scratch), sems
-        refs = self.bind(ins, outs, scratch)
+        self.fetch_all(self.bind(ins, outs, sems, scratch))
+
+    def finish(self, ins, outs, sems, scratch, late, middle):
+        src, dst, (send, recv, local) = ins[0], self.where(outs, scratch), sems[:3]
+        refs = self.bind(ins, outs, sems, scratch)
         core, z_low, x_at = (lax.axis_index(a) for a in ("c", "zl", "x"))
         own = group_index(core, z_low, x_at)
         beside = group_index(core, z_low, 1 - x_at)
@@ -394,6 +444,10 @@
             part = dst.at[block]
             return far_copy(part, part, send.at[way], recv.at[block], device)
 
+        def kept(block):
+            return pltpu.make_async_copy(dst.at[block], outs[0].at[block], sems[3].at[block])
+
+        self.ready(refs, self.given)
         if self.before:
             self.before(refs)
 
@@ -422,19 +476,30 @@
                 pass_on(turn, 3, onward).start()
                 pass_on(beside, 4, flipped("c")).start()
                 pass_on(below, 5, flipped("c")).start()
+                late()
 
             @pl.when(step == 6)
             def _():
                 pass_on(block, 6, flipped("c")).start()
                 middle()
 
+            if self.keep:
+                kept(block).start()
             if self.work:
                 self.work(refs, dst.at[block], block)
+                self.flush_block(refs, block)
 
         if self.after:
             self.after(refs)
         for way in range(7):
             pass_on(own, way, flipped("c")).wait_send()
+        if self.keep:
+
+            @pl.loop(0, 8)
+            def _(block):
+                kept(block).wait()
+
+        self.flushed(refs)
 
 
 class ScatterRows(Fused):
@@ -443,38 +508,40 @@
         rows,
         cols,
         produce,
+        along_x=False,
+        first=(),
         given={},
         streams={},
         results={},
+        by_block=(),
         scratch={},
         far={},
-        extra_sems=0,
+        extra_sems=1,
         fill_one=None,
         fill_two=None,
         end=None,
     ):
-        self.inputs, self.in_spaces = [], []
-        self.rows = rows
+        self.inputs = []
+        self.rows, self.first, self.along_x = rows, first, along_x
         block, kind = (rows, cols), jnp.bfloat16
         self.outputs = [jax.ShapeDtypeStruct(block, jnp.float32)]
-        self.out_spaces = [pltpu.VMEM]
-        self.sems = [7, 7, 2] + ([extra_sems] if extra_sems else [])
+        self.sems = [7, 7, 2, 1, extra_sems]
         self.scratch = [pltpu.VMEM((8,) + block, kind)]
         self.scratch += [pltpu.VMEM((4,) + block, kind)] * 2 + [pltpu.VMEM(block, kind)] * 3
+        self.scratch += [pltpu.VMEM(block, jnp.float32)]
         if streams:
             self.scratch += [pltpu.VMEM((2,) + block, kind)]
         self.produce, self.fill_one, self.fill_two, self.end = produce, fill_one, fill_two, end
-        self.name(given, streams, results, scratch, far)
+        self.name(given, streams, results, scratch, far, by_block)
 
     def begin(self, ins, outs, sems, scratch):
-        pass
-
-    def finish(self, ins, outs, sems, scratch, middle):
-        out = outs[0]
-        partial, came, sums, turned, direct_in, late_in = scratch[:6]
+        self.fetch_all(self.bind(ins, outs, sems, scratch))
+
+    def finish(self, ins, outs, sems, scratch, late, middle):
+        partial, came, sums, turned, direct_in, late_in, out = scratch[:7]
         send, recv, local = sems[:3]
-        refs = self.bind(ins, outs, scratch)
-        refs.more = sems[3] if len(sems) > 3 else None
+        refs = self.bind(ins, outs, sems, scratch)
+        refs.more = sems[4]
         core, z_low, x_at = (lax.axis_index(a) for a in ("c", "zl", "x"))
         rows = self.rows
         own, beside, below, across = (
@@ -483,15 +550,16 @@
             2 * (1 - z_low) + x_at,
             2 * (1 - z_low) + 1 - x_at,
         )
-        direct = jnp.where(core == 0, beside, below)
-        late = jnp.where(core == 0, below, beside)
+        by_x = True if self.along_x else core == 0
+        direct = jnp.where(by_x, beside, below)
+        after = jnp.where(by_x, below, beside)
         direct_way = {
-            "x": jnp.where(core == 0, 1 - x_at, x_at),
-            "zl": jnp.where(core == 0, z_low, 1 - z_low),
+            "x": jnp.where(by_x, 1 - x_at, x_at),
+            "zl": jnp.where(by_x, z_low, 1 - z_low),
         }
-        late_way = {
-            "x": jnp.where(core == 0, x_at, 1 - x_at),
-            "zl": jnp.where(core == 0, 1 - z_low, z_low),
+        after_way = {
+            "x": jnp.where(by_x, x_at, 1 - x_at),
+            "zl": jnp.where(by_x, 1 - z_low, z_low),
         }
 
         def to_core(turn_at, block):
@@ -518,10 +586,10 @@
 
         turn = send_sum(across, 4, turned, direct_way)
         straight = send_sum(direct, 5, direct_in, direct_way)
-        last = send_sum(late, 6, late_in, late_way)
+        last = send_sum(after, 6, late_in, after_way)
 
         def stream(name, body):
-            source, held = getattr(refs, name), scratch[6]
+            source, held = getattr(refs, name), scratch[7]
 
             def fetch(n):
                 slot = lax.rem(n, 2)
@@ -539,12 +607,16 @@
                 body(n, held.at[lax.rem(n, 2)])
 
         refs.stream = stream
+        self.ready(refs, self.first)
 
         @pl.loop(0, 8)
         def _(step):
             pair, mine = step // 2, lax.rem(step, 2)
-            first = jnp.where(mine == 1, direct, late)
-            second = jnp.where(mine == 1, late, direct)
+            if self.along_x:
+                first, second = direct, after
+            else:
+                first = jnp.where(mine == 1, direct, after)
+                second = jnp.where(mine == 1, after, direct)
             block = jnp.where(
                 pair == 0, across, jnp.where(pair == 1, first, jnp.where(pair == 2, second, own))
             )
@@ -565,14 +637,19 @@
             def _():
                 to_core(1, direct).wait_recv()
                 add(direct, sums.at[direct])
-                straight.start()
-
+                if not self.along_x:
+                    straight.start()
+
+        self.ready(refs, [key for key in self.given if key not in self.first])
         if self.fill_one:
             self.fill_one(refs)
-        to_core(2, late).wait_recv()
+        to_core(2, after).wait_recv()
         turn.wait_recv()
-        add(late, sums.at[late], turned)
+        if self.along_x:
+            straight.start()
+        add(after, sums.at[after], turned)
         last.start()
+        late()
         middle()
         if self.fill_two:
             self.fill_two(refs)
@@ -580,12 +657,15 @@
         straight.wait_recv()
         last.wait_recv()
         add(own, out, direct_in, late_in)
-        for n, block in enumerate((across, direct, late, own)):
+        pltpu.make_async_copy(out, outs[0], sems[3].at[0]).start()
+        for n, block in enumerate((across, direct, after, own)):
             to_core(n, block).wait_send()
         for copy in (turn, straight, last):
             copy.wait_send()
         if self.end:
             self.end(refs)
+        pltpu.make_async_copy(out, outs[0], sems[3].at[0]).wait()
+        self.flushed(refs)
 
 
 class Everyone:
@@ -656,6 +736,11 @@
         )
 
     pl.semaphore_wait(barrier, devices - 1)
+
+
+def later(task):
+    task.later = True
+    return task
 
 
 def run(collective_id, *tasks):
@@ -695,19 +780,26 @@
                 mine.append(rest[:e])
                 rest = rest[e:]
             bound.append(mine)
+        later = [(t, m) for t, m in zip(tasks, bound) if getattr(t, "later", False)]
         for task, mine in zip(tasks, bound):
-            task.begin(*mine)
+            if not getattr(task, "later", False):
+                task.begin(*mine)
         parts = [(t, m) for t, m in zip(tasks, bound) if hasattr(t, "middle")]
+
+        def late():
+            for task, mine in later:
+                task.begin(*mine)
 
         def middle():
             for task, mine in parts:
                 task.middle(*mine)
 
         if not any(isinstance(t, Fused) for t in tasks):
+            late()
             middle()
         for task, mine in zip(tasks, bound):
             if isinstance(task, Fused):
-                task.finish(*mine, middle)
+                task.finish(*mine, late, middle)
             else:
                 task.finish(*mine)
 
@@ -974,7 +1066,8 @@
         put_cols(target, j, dot_nn(hidden, refs.wd[j]), h_size)
 
 
-def weight_grad(h_size, refs, name, left, total, result):
+def weight_grad(h_size, refs, name, left, total, key):
+    result = getattr(refs, key)
     total[...] = jnp.zeros_like(total)
 
     def add(n, rows):
@@ -984,10 +1077,11 @@
 
     refs.stream(name, add)
     result[...] = total[...].astype(jnp.bfloat16)
+    refs.flush(key).start()
 
 
 def down_fill_one(h_size, refs):
-    weight_grad(h_size, refs, "dy", refs.hid, refs.total, refs.gwd)
+    weight_grad(h_size, refs, "dy", refs.hid, refs.total, "gwd")
     swap_copy(refs.gwd, refs.came, refs.more.at[0], refs.more.at[1]).start()
 
 
@@ -998,6 +1092,8 @@
             grad += dot_nt(cols_at(rows, j, h_size), refs.wd[j])
         refs.dgate[n] = (grad * refs.by_gate[n].astype(jnp.float32)).astype(jnp.bfloat16)
         refs.dup[n] = (grad * refs.by_up[n].astype(jnp.float32)).astype(jnp.bfloat16)
+        refs.flush("dgate", n).start()
+        refs.flush("dup", n).start()
 
     refs.stream("dy", back)
 
@@ -1013,12 +1109,12 @@
 
 
 def gateup_fill_one(h_size, refs):
-    weight_grad(h_size, refs, "rows", refs.dgate, refs.total, refs.gwg)
+    weight_grad(h_size, refs, "rows", refs.dgate, refs.total, "gwg")
     swap_copy(refs.gwg, refs.came, refs.more.at[0], refs.more.at[1]).start()
 
 
 def gateup_fill_two(h_size, refs):
-    weight_grad(h_size, refs, "rows", refs.dup, refs.total, refs.gwu)
+    weight_grad(h_size, refs, "rows", refs.dup, refs.total, "gwu")
 
 
 def gateup_end(refs):
@@ -1042,6 +1138,13 @@
 
 def output_after(refs):
     refs.gwo[...] = refs.total[...].astype(jnp.bfloat16)
+    refs.flush("gwo").start()
+    refs.flush("do").start()
+
+
+def query_after(refs):
+    refs.flush("q").start()
+    refs.flush("pair").start()
 
 
 def query_produce(h_size, refs, block, target):
@@ -1065,6 +1168,8 @@
     for j in range(4):
         refs.gwq[j] = cols_at(refs.total, j, h_size).T.astype(jnp.bfloat16)
         refs.gwp[j] = cols_at(refs.pair_total, j, h_size).T.astype(jnp.bfloat16)
+    refs.flush("gwq").start()
+    refs.flush("gwp").start()
     swap_copy(refs.gwq, refs.came, refs.more.at[0], refs.more.at[1]).start()
 
 
@@ -1169,8 +1274,11 @@
         at_core = lax.rem(lax.div(device, tensor_size), 2)
         return lax.div((at_core * zl_size + low) * 2 * (H // tensor_size), H // KVH)
 
-    small_all, query_parts = run(
-        0, Everyone(small, head_of, devices), SpreadAll(own_shard(query_weight, h_size))
+    small_all, query_parts, output_parts = run(
+        0,
+        Everyone(small, head_of, devices),
+        SpreadAll(own_shard(query_weight, h_size)),
+        SpreadAll(own_shard(output_weight, h_size)),
     )
     pair_proj = (
         small_all[:, :pair_rows]
@@ -1222,7 +1330,7 @@
     def shape(*dims, kind=jnp.bfloat16):
         return jax.ShapeDtypeStruct(dims, kind)
 
-    rows_one, query_rot, pair_rot, output_parts, gate_parts = flat(
+    rows_one, query_rot, pair_rot, gate_parts = flat(
         run(
             1,
             GatherRows(
@@ -1231,17 +1339,17 @@
                 given=dict(wq=query_full, wp=pair_proj, cos=cos_table, sin=sin_table),
                 results=dict(q=shape(width, group_rows), pair=shape(2 * HD, group_rows)),
                 work=functools.partial(query_work, h_size, heads_here),
+                after=query_after,
             ),
-            Spread(own_shard(output_weight, h_size)),
-            Spread(own_shard(gateup_t[0], h_size)),
+            later(Spread(own_shard(gateup_t[0], h_size))),
         )
     )
-    grad_rows, pair_back_half, output_parts, gate_parts = run(
+    grad_rows, pair_back_half, gate_parts, up_parts = run(
         2,
-        GatherRows(out_grad),
+        GatherRows(out_grad, along_x=True),
         Move(pair_rot, "zh", lambda: lax.axis_index("zh") == 0),
-        Pass(output_parts),
         Pass(gate_parts),
+        later(Spread(own_shard(gateup_t[1], h_size))),
     )
     output_full, gate_full = col_blocks(output_parts), col_blocks(gate_parts)
     pair_back_half = jnp.where(z_high == 1, pair_back_half, 0)
@@ -1254,15 +1362,18 @@
     ).transpose(0, 2, 1, 3)
     keys_t, values_t = pair_window[0], pair_window[1]
     attended_t, log_totals = attn_fwd(block_first, start, query_rot, keys_t, values_t)
-    attn_out, up_parts = run(
+    attn_out, up_parts, down_parts = run(
         3,
         ScatterRows(
             block_rows,
             D,
             functools.partial(output_produce, h_size),
+            along_x=True,
+            first=("o", "wo"),
             given=dict(o=attended_t, wo=output_full),
         ),
-        SpreadAll(own_shard(gateup_t[1], h_size)),
+        Pass(up_parts),
+        SpreadAll(own_shard(down_weight, h_size)),
     )
     up_full = col_blocks(up_parts)
 
@@ -1270,17 +1381,16 @@
     inverse_two = lax.rsqrt(jnp.mean(residual_mid * residual_mid, axis=1, keepdims=True) + NORM_EPS)
     normed_two = (residual_mid * inverse_two * gain_mlp).astype(jnp.bfloat16)
     hidden_shape = shape(8, block_rows, units)
-    rows_two, hidden_mlp, by_gate, by_up, down_parts = flat(
+    rows_two, hidden_mlp, by_gate, by_up = flat(
         run(
             4,
             GatherRows(
                 normed_two,
-                along_x=True,
                 given=dict(wg=gate_full, wu=up_full),
                 results=dict(hid=hidden_shape, by_gate=hidden_shape, by_up=hidden_shape),
+                by_block=("hid", "by_gate", "by_up"),
                 work=functools.partial(gateup_work, h_size),
             ),
-            SpreadAll(own_shard(down_weight, h_size)),
         )
     )
     down_full = col_blocks(down_parts)
@@ -1294,6 +1404,8 @@
                 block_rows,
                 D,
                 functools.partial(down_produce, h_size),
+                first=("hid", "wd"),
+                by_block=("dgate", "dup"),
                 given=dict(hid=hidden_mlp, wd=down_full, by_gate=by_gate, by_up=by_up),
                 streams=dict(dy=grad_rows),
                 results=dict(dgate=hidden_shape, dup=hidden_shape, gwd=whole_grad),
@@ -1315,6 +1427,8 @@
                 block_rows,
                 D,
                 functools.partial(gateup_produce, h_size),
+                along_x=True,
+                first=("dgate", "dup", "wg", "wu"),
                 given=dict(dgate=gate_grad, dup=up_grad, wg=gate_full, wu=up_full),
                 streams=dict(rows=rows_two),
                 results=dict(gwg=whole_grad, gwu=whole_grad),
@@ -1336,6 +1450,7 @@
             7,
             GatherRows(
                 mid_grad.astype(jnp.bfloat16),
+                along_x=True,
                 keep=False,
                 given=dict(o=attended_t, wo=output_full),
                 results=dict(do=shape(width, group_rows), gwo=shape(*output_full.shape)),
@@ -1345,7 +1460,7 @@
                 after=output_after,
             ),
             Swap(up_wgrad),
-            Move(gate_part, "zh", not_home),
+            later(Move(gate_part, "zh", not_home)),
             Move(for_partner(down_part, down_deep), "c", at_home),
         )
     )
@@ -1384,6 +1499,8 @@
                 block_rows,
                 D,
                 functools.partial(query_produce, h_size),
+                along_x=True,
+                first=("dq", "dpair", "wq", "wp"),
                 given=dict(dq=query_back, dpair=pair_back, wq=query_full, wp=pair_proj),
                 streams=dict(rows=rows_one),
                 results=dict(gwq=shape(4, quarter, width), gwp=shape(4, quarter, 2 * HD)),

time: 820 us -> 776 us (0.946)
  Pallas kernels: 709 us -> 660 us
    pallas_call x11, Pallas kernels: 651 us -> 607 us  [run(): pl.pallas_call(kernel, in_specs=in_specs, out_specs=out_specs, out_shape=...]
    unnamed x147 -> x145, local copies, waits for them, and re-layouts: 21.4 us -> 21.9 us
  transfers between devices with their start and end apart: 2 -> 2, of which waited for: 0 -> 0; matrix products, arithmetic and copies ran while one was open for 4% -> 4% of each run, Pallas kernels for 5% -> 6%
where the time goes in v4:
time: 776 us; the launch traced here: 769 us
  Pallas kernels  660 us (85%)
  other arithmetic  65.4 us (8%)
  local copies, waits for them, and re-layouts  37.8 us (5%)
    pallas_call x11, Pallas kernels, run(): pl.pallas_call(kernel, in_specs=in_specs, out_specs=out_specs, out_shape=...  607 us
    unnamed x145, local copies, waits for them, and re-layouts  21.9 us
    pallas_call x1, Pallas kernels, attn_bwd(): pl.pallas_call(functools.partial(attn_bwd_kernel, heads), grid_spec=pltpu...  20.8 us
    pallas_call x4, Pallas kernels, adam_shard(): pl.pallas_call(functools.partial(adam_kernel, rate, DECAY, groups), grid_...  16.6 us
    pallas_call x1, Pallas kernels, attn_fwd(): pl.pallas_call(functools.partial(attn_fwd_kernel, heads), grid_spec=pltpu...  15.7 us
  transfers between devices with their start and end apart: 2, of which 0 were waited for; matrix products, arithmetic and copies ran while one was open for 4% of the time, Pallas kernels for 6%

profile of v4, /device:TPU:0, one launch (start us, length us, event | category | flops | bytes accessed | tf_op | source)
XLA Modules:
  0.0 768.7 jit_solution(8716055176746650773)
XLA Ops:
  3.4 1.8 convert_bitcast_fusion.1.refs_2_
  5.2 1.8 convert_bitcast_fusion.2.refs_1_
  7.6 33.6 %shard_map.365 = (bf16[32,80,128]{2,1,0:T(8,128)(2,1)}, bf16[4,1,512,256]{3,2,1,0:T(8,128)(2,1)}, bf16[4,1,256,512]{3,2,1,0:T(8,128)(2,1)}) custom-call(bf16[4,80,128]{2,1,0:T(8,128)(2,1)} %pad_maximum_fusion.3.refs_0_, bf16[1,512,256]{2,1,0:T(8,128)(2,1)} %convert_bitcast_fusion.2.refs_1_, bf16[1,256,512]{2,1,0:T(8,128)(2,1)} %convert_bitcast_fusion.1.refs_2_), custom_call_target="tpu_custom_call" | custom-call | tf_op jit(solution)/shard_map/pallas_call | solution.py:806
  42.4 1.5 fusion.7
  50.6 1.8 multiply_sine_fusion.1
  52.4 74.5 %shard_map.366 = (bf16[8,256,2048]{2,1,0:T(8,128)(2,1)}, bf16[256,2048]{1,0:T(8,128)(2,1)}, bf16[128,2048]{1,0:T(8,128)(2,1)}, bf16[4,1,704,512]{3,2,1,0:T(8,128)(2,1)}) custom-call(bf16[256,2048]{1,0:T(8,128)(2,1)} %fusion.2.refs_0_, bf16[4,512,256]{2,1,0:T(8,128)(2,1)} %bitcast.112, bf16[4,512,128]{2,1,0:T(8,128)(2,1)} %bitcast.109, ...), custom_call_target="tpu_custom_call" | custom-call | tf_op jit(solution)/shard_map/pallas_call | solution.py:806
  126.9 1.4 reshape.373
  128.3 66.6 %shard_map.367 = (bf16[8,256,2048]{2,1,0:T(8,128)(2,1)}, bf16[128,2048]{1,0:T(8,128)(2,1)}, bf16[4,1,704,512]{3,2,1,0:T(8,128)(2,1)}, bf16[4,1,704,512]{3,2,1,0:T(8,128)(2,1)}) custom-call(bf16[256,2048]{1,0:T(8,128)(2,1)} %refs_0_.1, bf16[128,2048]{1,0:T(8,128)(2,1)} %get-tuple-element.86.refs_1_, ...), custom_call_target="tpu_custom_call", output_to_operand_aliasing={{2}: (2, {})} | custom-call | tf_op jit(solution)/shard_map/pallas_call | solution.py:806
  196.9 15.7 %shard_map.368 = (bf16[256,2048]{1,0:T(8,128)(2,1)S(1)}, f32[2,4,1024]{2,1,0:T(4,128)S(1)}) custom-call(s32[2,4]{1,0:T(2,128)S(1)} %slice.76.first_ref, s32[2,1,1024]{2,1,0:T(1,128)S(1)} %broadcast_in_dim.41.start_ref, bf16[256,2048]{1,0:T(8,128)(2,1)S(1)} %copy-done.13, bf16[2,64,2048]{2,1,0:T(8,128)(2,1)S(1)} %get-tuple-element.172.kt_ref, ...), custom_call_target="tpu_custom_call" | custom-call | tf_op jit(solution)/shard_map/pallas_call | solution.py:928
  213.5 71.0 %shard_map.369 = (f32[256,2048]{1,0:T(8,128)}, bf16[4,1,704,512]{3,2,1,0:T(8,128)(2,1)}, bf16[4,1,704,512]{3,2,1,0:T(8,128)(2,1)}) custom-call(bf16[256,2048]{1,0:T(8,128)(2,1)} %copy-done.6, bf16[4,256,512]{2,1,0:T(8,128)(2,1)} %bitcast.115, bf16[4,1,704,512]{3,2,1,0:T(8,128)(2,1)} %get-tuple-element.91.refs_2_, ...), custom_call_target="tpu_custom_call", output_to_operand_aliasing={{1}: (2, {})} | custom-call | tf_op jit(solution)/shard_map/pallas_call | solution.py:806
  284.5 2.0 multiply_reduce_fusion.2
  289.0 45.1 %shard_map.370 = (bf16[8,256,2048]{2,1,0:T(8,128)(2,1)}, bf16[8,256,704]{2,1,0:T(8,128)(2,1)}, bf16[8,256,704]{2,1,0:T(8,128)(2,1)}, bf16[8,256,704]{2,1,0:T(8,128)(2,1)}) custom-call(bf16[256,2048]{1,0:T(8,128)(2,1)} %multiply_convert_fusion.refs_0_, bf16[4,704,512]{2,1,0:T(8,128)(2,1)} %bitcast.107, bf16[4,704,512]{2,1,0:T(8,128)(2,1)} %bitcast.105), custom_call_target="tpu_custom_call" | custom-call | tf_op jit(solution)/shard_map/pallas_call | solution.py:806
  334.2 59.3 %shard_map.371 = (f32[256,2048]{1,0:T(8,128)}, bf16[8,256,704]{2,1,0:T(8,128)(2,1)}, bf16[8,256,704]{2,1,0:T(8,128)(2,1)}, bf16[4,704,512]{2,1,0:T(8,128)(2,1)}, bf16[2,704,512]{2,1,0:T(8,128)(2,1)}) custom-call(bf16[8,256,704]{2,1,0:T(8,128)(2,1)} %get-tuple-element.95.refs_0_, bf16[4,704,512]{2,1,0:T(8,128)(2,1)} %bitcast.117, ...), custom_call_target="tpu_custom_call" | custom-call | tf_op jit(solution)/shard_map/pallas_call | solution.py:806
  393.5 3.3 add_convert_fusion.2.refs_5_.refs_0_
  396.8 66.0 %shard_map.372 = (f32[256,2048]{1,0:T(8,128)}, bf16[4,704,512]{2,1,0:T(8,128)(2,1)}, bf16[4,704,512]{2,1,0:T(8,128)(2,1)}, bf16[2,704,512]{2,1,0:T(8,128)(2,1)}, bf16[2,704,512]{2,1,0:T(8,128)(2,1)}) custom-call(bf16[8,256,704]{2,1,0:T(8,128)(2,1)} %get-tuple-element.101.refs_0_, bf16[8,256,704]{2,1,0:T(8,128)(2,1)} %get-tuple-element.102.refs_1_, ...), custom_call_target="tpu_custom_call" | custom-call | tf_op jit(solution)/shard_map/pallas_call | solution.py:806
  462.8 3.5 multiply_reduce_fusion
  466.4 1.8 fusion.33.refs_0_
  470.2 1.5 add_convert_fusion.1.refs_4_.refs_0_
  471.8 61.2 %shard_map.373 = (bf16[256,2048]{1,0:T(8,128)(2,1)}, bf16[4,256,512]{2,1,0:T(8,128)(2,1)}, bf16[2,704,512]{2,1,0:T(8,128)(2,1)}, bf16[2,704,512]{2,1,0:T(8,128)(2,1)}, bf16[704,512]{1,0:T(8,128)(2,1)}) custom-call(bf16[256,2048]{1,0:T(8,128)(2,1)} %fusion.33.refs_0_, bf16[256,2048]{1,0:T(8,128)(2,1)} %copy-done.6, bf16[4,256,512]{2,1,0:T(8,128)(2,1)} %bitcast.116, ...), custom_call_target="tpu_custom_call" | custom-call | tf_op jit(solution)/shard_map/pallas_call | solution.py:806
  533.1 2.3 fusion.12.refs_2_
  535.4 20.8 %shard_map.374 = (f32[256,2048]{1,0:T(8,128)}, f32[2,64,2048]{2,1,0:T(8,128)S(1)}, f32[2,64,2048]{2,1,0:T(8,128)S(1)}) custom-call(s32[2,4]{1,0:T(2,128)S(1)} %slice.76.first_ref, s32[2,1,1024]{2,1,0:T(1,128)S(1)} %broadcast_in_dim.41.start_ref, bf16[256,2048]{1,0:T(8,128)(2,1)S(1)} %copy-done.14, bf16[256,2048]{1,0:T(8,128)(2,1)S(1)} %copy-done.7, ...), custom_call_target="tpu_custom_call" | custom-call | tf_op jit(solution)/shard_map/pallas_call | solution.py:961
  556.2 1.6 copy_bitcast_fusion
  560.2 29.5 %shard_map.375 = (bf16[2,64,2,1024]{3,2,1,0:T(2,128)(2,1)}, bf16[2,256,512]{2,1,0:T(8,128)(2,1)}, bf16[704,512]{1,0:T(8,128)(2,1)}) custom-call(bf16[2,64,2,1024]{3,2,1,0:T(2,128)(2,1)} %slice.138.refs_0_, bf16[4,256,512]{2,1,0:T(8,128)(2,1)} %get-tuple-element.116.refs_1_, bf16[704,512]{1,0:T(8,128)(2,1)} %fusion.12.refs_2_), custom_call_target="tpu_custom_call" | custom-call | tf_op jit(solution)/shard_map/pallas_call | solution.py:806
  589.7 1.9 slice_add_fusion
  592.8 2.1 add_convert_fusion.8.refs_6_.refs_0_
  594.9 1.5 add_convert_fusion.refs_5_.refs_3_
  596.9 1.9 fusion.19
  599.0 1.8 add_convert_fusion.9
  602.7 68.4 %shard_map.376 = (f32[256,2048]{1,0:T(8,128)}, bf16[4,512,256]{2,1,0:T(8,128)(2,1)}, bf16[4,512,128]{2,1,0:T(8,128)(2,1)}, bf16[2,512,256]{2,1,0:T(8,128)(2,1)},...) custom-call(bf16[256,2048]{1,0:T(8,128)(2,1)} %bitcast.111, bf16[128,2048]{1,0:T(8,128)(2,1)} %bitcast.119, ...), custom_call_target="tpu_custom_call" | custom-call | tf_op jit(solution)/shard_map/pallas_call | solution.py:806
  671.1 2.3 fusion.13.refs_3_
  674.2 2.2 fusion.10
  676.7 1.9 pad_maximum_fusion.1.refs_0_
  678.7 2.1 add_convert_fusion.7.refs_1_.refs_0_
  680.8 31.8 %shard_map.377 = (bf16[32,80,128]{2,1,0:T(8,128)(2,1)}, bf16[2,512,256]{2,1,0:T(8,128)(2,1)}, bf16[256,512]{1,0:T(8,128)(2,1)}, bf16[704,512]{1,0:T(8,128)(2,1)}) custom-call(bf16[32,80,128]{2,1,0:T(8,128)(2,1)} %pad_maximum_fusion.1.refs_0_, bf16[2,512,256]{2,1,0:T(8,128)(2,1)} %add_convert_fusion.7.refs_1_.refs_0_, bf16[256,512]{1,0:T(8,128)(2,1)} %fusion.22.refs_2_, ...), custom_call_target="tpu_custom_call" | custom-call | tf_op jit(solution)/shard_map/pallas_call | solution.py:806
  712.6 1.7 fusion.23
  714.3 2.2 collective-permute-start.1
  717.9 7.2 fusion.6
  726.8 2.0 reduce_sum.107
  728.9 2.1 reshape.381
  730.9 2.2 reduce_sum.108
  737.4 1.4 copy-done.16
  738.8 1.4 copy-done.23
  740.1 1.4 copy-done.24
  742.6 4.1 shard_map.381
  751.0 2.5 shard_map.379
  753.5 1.8 copy-done.20
  757.6 7.1 shard_map.380
  765.6 2.9 shard_map.378
  (209 shorter events, 40.6 us)
Async XLA Ops:
  0.7 49.5 %collective-permute-start = (s32[1,2048]{1,0:T(1,128)}, s32[1,2048]{1,0:T(1,128)S(1)}, u32[]{:S(2)}, u32[]{:S(2)}) collective-permute-start(s32[1,2048]{1,0:T(1,128)} %param.24), channel_id=1, source_target_pairs={{0,8},{8,0},{1,9},{9,1},{2,10},{10,2},{3,11},{11,3},{4,12},{12,4},... | collective-permute-start | bytes 24584 | tf_op jit(solution)/shard_map/ppermute | solution.py:1302
  1.2 49.4 %copy-start.66 = (f32[32]{0:T(128)}, f32[32]{0:T(128)S(1)}, u32[]{:S(2)}) copy-start(f32[32]{0:T(128)S(1)} %multiply_power_fusion) | copy-start | bytes 388
  2.4 41.6 %copy-start.4 = (f32[2,512,704]{1,2,0:T(8,128)S(1)}, f32[2,512,704]{1,2,0:T(8,128)}, u32[]{:S(2)}) copy-start(f32[2,512,704]{1,2,0:T(8,128)} %param.29) | copy-start | bytes 8650756
  42.4 5.3 copy-start.53
  44.0 3.8 copy-start.60
  44.2 3.6 copy-start.38
  46.1 3.2 copy-start.51
  47.0 3.1 copy-start.65
  50.6 76.4 %copy-start.57 = (f32[1,8,2,128]{3,1,2,0:T(8,128)}, f32[1,8,2,128]{3,1,2,0:T(8,128)S(1)}, u32[]{:S(2)}) copy-start(f32[1,8,2,128]{3,1,2,0:T(8,128)S(1)} %copy.85) | copy-start | bytes 24580
  286.5 179.8 %copy-start.58 = (f32[256]{0:T(256)}, f32[256]{0:T(256)S(1)}, u32[]{:S(2)}) copy-start(f32[256]{0:T(256)S(1)} %add_rsqrt_fusion) | copy-start | bytes 3076
  396.8 69.6 %copy-start.41 = (bf16[256,2048]{1,0:T(8,128)(2,1)S(1)}, bf16[256,2048]{1,0:T(8,128)(2,1)}, u32[]{:S(2)}) copy-start(bf16[256,2048]{1,0:T(8,128)(2,1)} %refs_0_.1) | copy-start | bytes 3145732
  462.8 3.6 copy-start.37
  462.8 3.6 copy-start.40
  466.4 3.1 copy-start.50
  471.8 61.3 %copy-start.2 = (bf16[2,704,512]{2,1,0:T(8,128)(2,1)S(1)}, bf16[2,704,512]{2,1,0:T(8,128)(2,1)}, u32[]{:S(2)}) copy-start(bf16[2,704,512]{2,1,0:T(8,128)(2,1)} %add_convert_fusion.1.refs_4_.refs_0_) | copy-start | bytes 4325380
  589.7 3.1 copy-start.45
  589.7 5.2 copy-start.48
  591.7 3.2 copy-start.42
  596.4 2.5 copy-start.46
  596.4 2.6 copy-start.47
  602.7 68.5 %copy-start = (bf16[2,704,512]{2,1,0:T(8,128)(2,1)S(1)}, bf16[2,704,512]{2,1,0:T(8,128)(2,1)}, u32[]{:S(2)}) copy-start(bf16[2,704,512]{2,1,0:T(8,128)(2,1)} %add_convert_fusion.refs_5_.refs_3_) | copy-start | bytes 4325380
  671.1 2.4 copy-start.8
  671.1 3.1 copy-start.39
  671.1 3.1 copy-start.54
  671.1 3.1 copy-start.61
  673.4 3.0 copy-start.62
  680.8 31.8 %copy-start.9 = (bf16[2,512,256]{2,1,0:T(8,128)(2,1)S(1)}, bf16[2,512,256]{2,1,0:T(8,128)(2,1)}, u32[]{:S(2)}) copy-start(bf16[2,512,256]{2,1,0:T(8,128)(2,1)} %add_convert_fusion.7.refs_1_.refs_0_) | copy-start | bytes 1572868
  680.8 37.1 %copy-start.59 = (f32[256]{0:T(256)S(1)}, f32[256]{0:T(256)}, u32[]{:S(2)}) copy-start(f32[256]{0:T(256)} %copy-done.58) | copy-start | bytes 3076
  680.8 37.1 %copy-start.64 = (f32[256]{0:T(256)S(1)}, f32[256]{0:T(256)}, u32[]{:S(2)}) copy-start(f32[256]{0:T(256)} %copy-done.63) | copy-start | bytes 3076
  714.3 51.2 %collective-permute-start.1 = (bf16[512,256]{1,0:T(8,128)(2,1)}, bf16[512,256]{1,0:T(8,128)(2,1)}, u32[]{:S(2)}, u32[]{:S(2)}) collective-permute-start(bf16[512,256]{1,0:T(8,128)(2,1)} %fusion.23), channel_id=1, source_target_pairs={{0,8},{12,4},{1,9},{13,5},{2,10},{14,6},{3,11},{15,7},{16,24},{28,... | collective-permute-start | bytes 786440 | tf_op jit(solution)/shard_map/ppermute | solution.py:1541
  717.9 7.3 copy-start.67
  717.9 7.3 copy-start.68
  717.9 7.3 copy-start.69
  717.9 7.9 %copy-start.43 = (bf16[32,80,128]{2,1,0:T(8,128)(2,1)S(1)}, bf16[32,80,128]{2,1,0:T(8,128)(2,1)}, u32[]{:S(2)}) copy-start(bf16[32,80,128]{2,1,0:T(8,128)(2,1)} %get-tuple-element.130) | copy-start | bytes 1966084
  742.6 4.2 copy-start.21
  742.6 10.9 %copy-start.5 = (f32[2,512,704]{1,2,0:T(8,128)S(1)}, f32[2,512,704]{1,2,0:T(8,128)}, u32[]{:S(2)}) copy-start(f32[2,512,704]{1,2,0:T(8,128)} %param.29) | copy-start | bytes 8650756
  742.6 10.9 %copy-start.18 = (bf16[2,704,512]{2,1,0:T(8,128)(2,1)S(1)}, bf16[2,704,512]{2,1,0:T(8,128)(2,1)}, u32[]{:S(2)}) copy-start(bf16[2,704,512]{2,1,0:T(8,128)(2,1)} %get-tuple-element.127.refs_4_) | copy-start | bytes 4325380
  742.6 10.9 %copy-start.19 = (f32[2,512,704]{1,2,0:T(8,128)S(1)}, f32[2,512,704]{1,2,0:T(8,128)}, u32[]{:S(2)}) copy-start(f32[2,512,704]{1,2,0:T(8,128)} %param.35) | copy-start | bytes 8650756
  746.8 6.7 copy-start.3
  746.8 6.7 copy-start.17
  757.6 7.2 copy-start.52
  757.6 7.2 copy-start.55
  757.6 7.2 copy-start.56
  757.6 8.0 %copy-start.10 = (bf16[2,512,256]{2,1,0:T(8,128)(2,1)S(1)}, bf16[2,512,256]{2,1,0:T(8,128)(2,1)}, u32[]{:S(2)}) copy-start(bf16[2,512,256]{2,1,0:T(8,128)(2,1)} %add_convert_fusion.7.refs_1_.refs_0_) | copy-start | bytes 1572868
  757.6 8.0 %copy-start.22 = (f32[512,256]{1,0:T(8,128)S(1)}, f32[512,256]{1,0:T(8,128)}, u32[]{:S(2)}) copy-start(f32[512,256]{1,0:T(8,128)} %param.26) | copy-start | bytes 1572868
  757.6 8.0 %copy-start.27 = (bf16[2,512,256]{2,1,0:T(8,128)(2,1)S(1)}, bf16[2,512,256]{2,1,0:T(8,128)(2,1)}, u32[]{:S(2)}) copy-start(bf16[2,512,256]{2,1,0:T(8,128)(2,1)} %get-tuple-element.128.refs_1_) | copy-start | bytes 1572868
  757.6 8.0 %copy-start.33 = (f32[512,256]{1,0:T(8,128)S(1)}, f32[512,256]{1,0:T(8,128)}, u32[]{:S(2)}) copy-start(f32[512,256]{1,0:T(8,128)} %param.32) | copy-start | bytes 1572868
  757.6 8.0 %copy-start.34 = (f32[512,256]{1,0:T(8,128)S(1)}, f32[512,256]{1,0:T(8,128)}, u32[]{:S(2)}) copy-start(f32[512,256]{1,0:T(8,128)} %param.38) | copy-start | bytes 1572868
  (25 other events, 37.3 us)

commit v5 on v4

--- a/solution.py
+++ b/solution.py
@@ -390,6 +390,7 @@
         self,
         block,
         along_x=False,
+        onward_first=False,
         keep=True,
         given={},
         results={},
@@ -402,7 +403,7 @@
         gathered = (8,) + block.shape
         self.inputs, self.outputs, self.scratch = [block], [], []
         self.in_vmem = work is not None
-        self.along_x = along_x
+        self.along_x, self.onward_first = along_x, onward_first
         self.before, self.work, self.after = before, work, after
         self.sems = [7, 8, 1]
         if self.in_vmem:
@@ -426,7 +427,7 @@
         pltpu.make_async_copy(src, dst.at[own], local.at[0]).start()
         self.fetch_all(self.bind(ins, outs, sems, scratch))
 
-    def finish(self, ins, outs, sems, scratch, late, middle):
+    def finish(self, ins, outs, sems, scratch, early, late, middle):
         src, dst, (send, recv, local) = ins[0], self.where(outs, scratch), sems[:3]
         refs = self.bind(ins, outs, sems, scratch)
         core, z_low, x_at = (lax.axis_index(a) for a in ("c", "zl", "x"))
@@ -447,6 +448,17 @@
         def kept(block):
             return pltpu.make_async_copy(dst.at[block], outs[0].at[block], sems[3].at[block])
 
+        def onwards():
+            pass_on(beside, 0, flipped("c")).wait_recv()
+            pass_on(below, 0, flipped("c")).wait_recv()
+            pass_on(turn, 3, onward).start()
+            pass_on(beside, 4, flipped("c")).start()
+            pass_on(below, 5, flipped("c")).start()
+            late()
+
+        if self.onward_first:
+            onwards()
+        early()
         self.ready(refs, self.given)
         if self.before:
             self.before(refs)
@@ -466,17 +478,12 @@
             def _():
                 pltpu.make_async_copy(src, dst.at[own], local.at[0]).wait()
 
-            @pl.when((step != 0) & (step != 3))
+            @pl.when((step != 0) & (step != 2) & (step != 3))
             def _():
                 pass_on(block, 0, flipped("c")).wait_recv()
 
-            @pl.when(step == 2)
-            def _():
-                pass_on(below, 0, flipped("c")).wait_recv()
-                pass_on(turn, 3, onward).start()
-                pass_on(beside, 4, flipped("c")).start()
-                pass_on(below, 5, flipped("c")).start()
-                late()
+            if not self.onward_first:
+                pl.when(step == 2)(onwards)
 
             @pl.when(step == 6)
             def _():
@@ -537,7 +544,7 @@
     def begin(self, ins, outs, sems, scratch):
         self.fetch_all(self.bind(ins, outs, sems, scratch))
 
-    def finish(self, ins, outs, sems, scratch, late, middle):
+    def finish(self, ins, outs, sems, scratch, early, late, middle):
         partial, came, sums, turned, direct_in, late_in, out = scratch[:7]
         send, recv, local = sems[:3]
         refs = self.bind(ins, outs, sems, scratch)
@@ -607,6 +614,7 @@
                 body(n, held.at[lax.rem(n, 2)])
 
         refs.stream = stream
+        early()
         self.ready(refs, self.first)
 
         @pl.loop(0, 8)
@@ -781,10 +789,24 @@
                 rest = rest[e:]
             bound.append(mine)
         later = [(t, m) for t, m in zip(tasks, bound) if getattr(t, "later", False)]
+        mains = [n for n, t in enumerate(tasks) if isinstance(t, Fused)]
+        main_at = mains[0] if mains else 0
         for task, mine in zip(tasks, bound):
-            if not getattr(task, "later", False):
-                task.begin(*mine)
-        parts = [(t, m) for t, m in zip(tasks, bound) if hasattr(t, "middle")]
+            task.live = mine
+        for n in sorted(range(len(tasks)), key=lambda n: n != main_at):
+            if not getattr(tasks[n], "later", False):
+                tasks[n].begin(*bound[n])
+        parts = [
+            (t, m)
+            for n, (t, m) in enumerate(zip(tasks, bound))
+            if hasattr(t, "middle") and n >= main_at
+        ]
+
+        def early():
+            for task, mine in zip(tasks[:main_at], bound):
+                if hasattr(task, "middle"):
+                    task.middle(*mine)
+                task.finish(*mine)
 
         def late():
             for task, mine in later:
@@ -797,10 +819,10 @@
         if not any(isinstance(t, Fused) for t in tasks):
             late()
             middle()
-        for task, mine in zip(tasks, bound):
+        for n, (task, mine) in enumerate(zip(tasks, bound)):
             if isinstance(task, Fused):
-                task.finish(*mine, late, middle)
-            else:
+                task.finish(*mine, early, late, middle)
+            elif n >= main_at:
                 task.finish(*mine)
 
     results = pl.pallas_call(
@@ -996,7 +1018,8 @@
 def cols_at(ref, block, h_size):
     width = ref.shape[-1] // (4 * h_size)
     parts = [
-        ref[:, (h * 4 + block) * width : (h * 4 + block + 1) * width] for h in range(h_size)
+        ref[:, pl.ds(pl.multiple_of((h * 4 + block) * width, width), width)]
+        for h in range(h_size)
     ]
     return parts[0] if h_size == 1 else jnp.concatenate(parts, axis=1)
 
@@ -1021,13 +1044,39 @@
     return (front * cos_table - back * sin_table, back * cos_table + front * sin_table)
 
 
-def query_work(h_size, heads, refs, rows, block):
+def query_before(query_task, small_task, pair_rows, gain_cols, refs):
+    small = small_task.live[1][0]
+    pltpu.sync_copy(query_task.live[1][0], refs.wq)
+    pltpu.sync_copy(small, refs.small)
+    shared = 128 // gain_cols
+    for tile in range(D // 128):
+        total = 0.0
+        for n in range(shared):
+            total += refs.small[tile * shared + n, pair_rows : pair_rows + 16].astype(jnp.float32)
+        refs.gains[:, tile * 128 : (tile + 1) * 128] = total
+    refs.flush("gains").start()
+
+
+def query_work(h_size, heads, pair_rows, refs, rows, block):
     at = lanes_of(block, rows.shape[0])
+
+    @pl.loop(0, rows.shape[0] // ROW_STRIP)
+    def _(strip):
+        here = pl.ds(pl.multiple_of(strip * ROW_STRIP, ROW_STRIP), ROW_STRIP)
+        x = rows[here].astype(jnp.float32)
+        inverse = lax.rsqrt(jnp.mean(x * x, axis=1, keepdims=True) + NORM_EPS)
+        refs.rows[block, here] = (x * inverse * refs.gains[0:1]).astype(jnp.bfloat16)
+
+    normed = refs.rows.at[block]
     query = pair = 0.0
+    width = D // (4 * h_size)
     for j in range(4):
-        part = cols_at(rows, j, h_size)
-        query += dot_nn(part, refs.wq[j])
-        pair += dot_nn(part, refs.wp[j])
+        for h in range(h_size):
+            first = (h * 4 + j) * width
+            part = normed[:, first : first + width]
+            query += dot_nn(part, refs.wq[j, h])
+            senders = refs.small[first // pair_rows : (first + width) // pair_rows, :pair_rows]
+            pair += dot_nn(part, senders.reshape(width, 2 * HD))
     query_t, pair_t = query.T, pair.T
     cos_table, sin_table = refs.cos[:, at], refs.sin[:, at]
     for head in range(heads):
@@ -1066,23 +1115,29 @@
         put_cols(target, j, dot_nn(hidden, refs.wd[j]), h_size)
 
 
-def weight_grad(h_size, refs, name, left, total, key):
+def weight_grad(h_size, refs, name, left, total, key, between=None):
     result = getattr(refs, key)
-    total[...] = jnp.zeros_like(total)
-
-    def add(n, rows):
-        left_t = flip(left[n]).astype(jnp.bfloat16)
-        for j in range(4):
-            total[j] += dot_nn(left_t, cols_at(rows, j, h_size))
-
-    refs.stream(name, add)
-    result[...] = total[...].astype(jnp.bfloat16)
+    y_at = lax.axis_index("y")
+    for y_of in (1 - y_at, y_at):
+        total[...] = jnp.zeros_like(total)
+
+        def add(n, rows):
+            left_t = flip(left[n]).astype(jnp.bfloat16)
+            for j in range(2):
+                total[j] += dot_nn(left_t, cols_at(rows, 2 * y_of + j, h_size))
+
+        refs.stream(name, add)
+        for j in range(2):
+            result[2 * y_of + j] = total[j].astype(jnp.bfloat16)
+        if between is not None:
+            between()
+            between = None
     refs.flush(key).start()
 
 
 def down_fill_one(h_size, refs):
-    weight_grad(h_size, refs, "dy", refs.hid, refs.total, "gwd")
-    swap_copy(refs.gwd, refs.came, refs.more.at[0], refs.more.at[1]).start()
+    swap = lambda: swap_copy(refs.gwd, refs.came, refs.more.at[0], refs.more.at[1]).start()
+    weight_grad(h_size, refs, "dy", refs.hid, refs.total, "gwd", swap)
 
 
 def down_fill_two(h_size, refs):
@@ -1109,8 +1164,8 @@
 
 
 def gateup_fill_one(h_size, refs):
-    weight_grad(h_size, refs, "rows", refs.dgate, refs.total, "gwg")
-    swap_copy(refs.gwg, refs.came, refs.more.at[0], refs.more.at[1]).start()
+    swap = lambda: swap_copy(refs.gwg, refs.came, refs.more.at[0], refs.more.at[1]).start()
+    weight_grad(h_size, refs, "rows", refs.dgate, refs.total, "gwg", swap)
 
 
 def gateup_fill_two(h_size, refs):
@@ -1258,44 +1313,25 @@
 
     pair_rows = keyvalue_weight.shape[0]
     gain_cols = norm_gains.shape[1]
-    small_rows = -(-(2 * gain_cols) // (2 * HD))
-    pad_rows = 16 * (-(-small_rows // 16))
+    pad_rows = 16
     by_head = (
         keyvalue_weight.reshape(pair_rows, 2, KVH, HD)
         .transpose(2, 0, 1, 3)
         .reshape(KVH, pair_rows, 2 * HD)
     )
-    flat_gains = jnp.pad(norm_gains.reshape(-1), (0, pad_rows * 2 * HD - 2 * gain_cols))
-    flat_gains = jnp.broadcast_to(flat_gains.reshape(1, pad_rows, 2 * HD), (KVH, pad_rows, 2 * HD))
-    small = jnp.concatenate([by_head, flat_gains], axis=1).astype(jnp.bfloat16)
+    me = my_number()
+    lane = lax.rem(me * gain_cols, 128)
+    placed = lax.dynamic_update_slice(
+        jnp.zeros((pad_rows, 2 * HD), jnp.float32), norm_gains, (jnp.int32(0), lane)
+    )
+    placed = jnp.broadcast_to(placed[None], (KVH, pad_rows, 2 * HD))
+    small = jnp.concatenate([by_head, placed], axis=1).astype(jnp.bfloat16)
 
     def head_of(device):
         low = lax.rem(lax.div(device, 2), zl_size)
         at_core = lax.rem(lax.div(device, tensor_size), 2)
         return lax.div((at_core * zl_size + low) * 2 * (H // tensor_size), H // KVH)
 
-    small_all, query_parts, output_parts = run(
-        0,
-        Everyone(small, head_of, devices),
-        SpreadAll(own_shard(query_weight, h_size)),
-        SpreadAll(own_shard(output_weight, h_size)),
-    )
-    pair_proj = (
-        small_all[:, :pair_rows]
-        .reshape(h_size, 4, D // (4 * h_size), 2 * HD)
-        .transpose(1, 0, 2, 3)
-        .reshape(4, D // 4, 2 * HD)
-    )
-    query_full = row_blocks(query_parts)
-    gains_full = (
-        small_all[:, pair_rows:]
-        .reshape(devices, pad_rows * 2 * HD)[:, : 2 * gain_cols]
-        .reshape(devices, 2, gain_cols)
-        .transpose(1, 0, 2)
-        .reshape(2, devices * gain_cols)
-    )
-    gain_attn = gains_full[0].astype(jnp.float32)
-    gain_mlp = gains_full[1].astype(jnp.float32)
     heads_here = query_weight.shape[1] // HD
 
     seg_mine = segment_ids
@@ -1319,8 +1355,6 @@
     block_first = start[:, ::QUERY_BLOCK]
     start = start[:, None, :]
 
-    inverse_one = lax.rsqrt(jnp.mean(inputs * inputs, axis=1, keepdims=True) + NORM_EPS)
-    normed_one = (inputs * inverse_one * gain_attn).astype(jnp.bfloat16)
     block_rows = inputs.shape[0]
     group_rows = 8 * block_rows
     width = heads_here * HD
@@ -1330,24 +1364,55 @@
     def shape(*dims, kind=jnp.bfloat16):
         return jax.ShapeDtypeStruct(dims, kind)
 
-    rows_one, query_rot, pair_rot, gate_parts = flat(
+    small_task = Everyone(small, head_of, devices)
+    query_task = SpreadAll(own_shard(query_weight, h_size))
+    small_kind, query_kind = small_task.outputs[0], query_task.outputs[0]
+    small_all, query_parts, gains_all, rows_one, query_rot, pair_rot, output_parts, gate_parts = flat(
         run(
             1,
+            small_task,
+            query_task,
             GatherRows(
-                normed_one,
+                hidden_in,
                 along_x=True,
-                given=dict(wq=query_full, wp=pair_proj, cos=cos_table, sin=sin_table),
-                results=dict(q=shape(width, group_rows), pair=shape(2 * HD, group_rows)),
-                work=functools.partial(query_work, h_size, heads_here),
+                onward_first=True,
+                keep=False,
+                given=dict(cos=cos_table, sin=sin_table),
+                results=dict(
+                    gains=shape(pad_rows, D, kind=jnp.float32),
+                    rows=shape(8, block_rows, D),
+                    q=shape(width, group_rows),
+                    pair=shape(2 * HD, group_rows),
+                ),
+                by_block=("rows",),
+                scratch=dict(
+                    wq=pltpu.VMEM(query_kind.shape, query_kind.dtype),
+                    small=pltpu.VMEM(small_kind.shape, small_kind.dtype),
+                ),
+                before=functools.partial(
+                    query_before, query_task, small_task, pair_rows, gain_cols
+                ),
+                work=functools.partial(query_work, h_size, heads_here, pair_rows),
                 after=query_after,
             ),
+            later(Spread(own_shard(output_weight, h_size))),
             later(Spread(own_shard(gateup_t[0], h_size))),
         )
     )
-    grad_rows, pair_back_half, gate_parts, up_parts = run(
+    pair_proj = (
+        small_all[:, :pair_rows]
+        .reshape(h_size, 4, D // (4 * h_size), 2 * HD)
+        .transpose(1, 0, 2, 3)
+        .reshape(4, D // 4, 2 * HD)
+    )
+    query_full = row_blocks(query_parts)
+    gain_attn, gain_mlp = gains_all[0], gains_all[1]
+    inverse_one = lax.rsqrt(jnp.mean(inputs * inputs, axis=1, keepdims=True) + NORM_EPS)
+    grad_rows, pair_back_half, output_parts, gate_parts, up_parts = run(
         2,
         GatherRows(out_grad, along_x=True),
         Move(pair_rot, "zh", lambda: lax.axis_index("zh") == 0),
+        Pass(output_parts),
         Pass(gate_parts),
         later(Spread(own_shard(gateup_t[1], h_size))),
     )
@@ -1395,7 +1460,7 @@
     )
     down_full = col_blocks(down_parts)
 
-    sums = pltpu.VMEM((4, units, D // 4), jnp.float32)
+    sums = pltpu.VMEM((2, units, D // 4), jnp.float32)
     whole_grad, half_grad = shape(4, units, D // 4), shape(2, units, D // 4)
     mlp_out, gate_grad, up_grad, down_grad, down_came = flat(
         run(

time: 776 us -> 756 us (0.974)
  Pallas kernels: 660 us -> 644 us
    pallas_call x11 -> x10, Pallas kernels: 607 us -> 586 us  [run(): pl.pallas_call(kernel, in_specs=in_specs, out_specs=out_specs, out_shape=...]
    unnamed x145 -> x128, local copies, waits for them, and re-layouts: 21.9 us -> 22.8 us
  transfers between devices with their start and end apart: 2 -> 2, of which waited for: 0 -> 0; matrix products, arithmetic and copies ran while one was open for 4% -> 4% of each run, Pallas kernels for 6% -> 2%
where the time goes in v5:
time: 756 us; the launch traced here: 751 us
  Pallas kernels  644 us (85%)
  other arithmetic  63.2 us (8%)
  local copies, waits for them, and re-layouts  39.3 us (5%)
    pallas_call x10, Pallas kernels, run(): pl.pallas_call(kernel, in_specs=in_specs, out_specs=out_specs, out_shape=...  586 us
    pallas_call x1, Pallas kernels, attn_bwd(): pl.pallas_call(functools.partial(attn_bwd_kernel, heads), grid_spec=pltpu...  23.3 us
    unnamed x128, local copies, waits for them, and re-layouts  22.8 us
    pallas_call x1, Pallas kernels, attn_fwd(): pl.pallas_call(functools.partial(attn_fwd_kernel, heads), grid_spec=pltpu...  17.9 us
    pallas_call x4, Pallas kernels, adam_shard(): pl.pallas_call(functools.partial(adam_kernel, rate, DECAY, groups), grid_...  16.6 us
  transfers between devices with their start and end apart: 2, of which 0 were waited for; matrix products, arithmetic and copies ran while one was open for 4% of the time, Pallas kernels for 2%

profile of v5, /device:TPU:0, one launch (start us, length us, event | category | flops | bytes accessed | tf_op | source)
XLA Modules:
  0.0 751.3 jit_solution(9249631037604841354)
XLA Ops:
  3.2 1.9 convert_bitcast_fusion.2.refs_1_
  5.2 1.8 convert_bitcast_fusion.1.refs_5_
  6.9 2.3 convert_bitcast_fusion.refs_3_
  12.1 1.8 multiply_sine_fusion.1
  13.9 98.1 %shard_map.365 = (bf16[32,80,128]{2,1,0:T(8,128)(2,1)}, bf16[4,1,512,256]{3,2,1,0:T(8,128)(2,1)}, f32[16,2048]{1,0:T(8,128)}, bf16[8,256,2048]{2,1,0:T(8,128)(2,...) custom-call(bf16[4,80,128]{2,1,0:T(8,128)(2,1)} %pad_maximum_fusion., ...), custom_call_target="tpu_custom_call" | custom-call | tf_op jit(solution)/shard_map/pallas_call | solution.py:828
  112.9 1.4 reshape.344
  114.5 62.1 %shard_map.366 = (bf16[8,256,2048]{2,1,0:T(8,128)(2,1)}, bf16[128,2048]{1,0:T(8,128)(2,1)}, bf16[4,1,256,512]{3,2,1,0:T(8,128)(2,1)}, bf16[4,1,704,512]{3,2,1,0:T(8,128)(2,1)}, bf16[4,1,704,512]{3,2,1,0:T(8,128)(2,1)}) custom-call(bf16[256,2048]{1,0:T(8,128)(2,1)} %refs_0_.1, ...), custom_call_target="tpu_custom_call", output_to_operand_aliasing={{2}: (2, {}), {3}: (3, {})} | custom-call | tf_op jit(solution)/shard_map/pallas_call | solution.py:828
  178.3 17.9 %shard_map.367 = (bf16[256,2048]{1,0:T(8,128)(2,1)S(1)}, f32[2,4,1024]{2,1,0:T(4,128)S(1)}) custom-call(s32[2,4]{1,0:T(2,128)S(1)} %slice.68.first_ref, s32[2,1,1024]{2,1,0:T(1,128)S(1)} %broadcast_in_dim.69.start_ref, bf16[256,2048]{1,0:T(8,128)(2,1)S(1)} %copy-done.12, bf16[2,64,2048]{2,1,0:T(8,128)(2,1)S(1)} %get-tuple-element.175.kt_ref, ...), custom_call_target="tpu_custom_call" | custom-call | tf_op jit(solution)/shard_map/pallas_call | solution.py:950
  197.2 68.5 %shard_map.368 = (f32[256,2048]{1,0:T(8,128)}, bf16[4,1,704,512]{3,2,1,0:T(8,128)(2,1)}, bf16[4,1,704,512]{3,2,1,0:T(8,128)(2,1)}) custom-call(bf16[256,2048]{1,0:T(8,128)(2,1)} %copy-done.6, bf16[4,256,512]{2,1,0:T(8,128)(2,1)} %bitcast.106, bf16[4,1,704,512]{3,2,1,0:T(8,128)(2,1)} %get-tuple-element.92.refs_2_, ...), custom_call_target="tpu_custom_call", output_to_operand_aliasing={{1}: (2, {})} | custom-call | tf_op jit(solution)/shard_map/pallas_call | solution.py:828
  265.7 2.1 multiply_reduce_fusion.2
  267.8 1.3 copy-done.34
  270.4 44.7 %shard_map.369 = (bf16[8,256,2048]{2,1,0:T(8,128)(2,1)}, bf16[8,256,704]{2,1,0:T(8,128)(2,1)}, bf16[8,256,704]{2,1,0:T(8,128)(2,1)}, bf16[8,256,704]{2,1,0:T(8,128)(2,1)}) custom-call(bf16[256,2048]{1,0:T(8,128)(2,1)} %multiply_convert_fusion.refs_0_, bf16[4,704,512]{2,1,0:T(8,128)(2,1)} %bitcast.104, bf16[4,704,512]{2,1,0:T(8,128)(2,1)} %bitcast.102), custom_call_target="tpu_custom_call" | custom-call | tf_op jit(solution)/shard_map/pallas_call | solution.py:828
  315.0 58.0 %shard_map.370 = (f32[256,2048]{1,0:T(8,128)}, bf16[8,256,704]{2,1,0:T(8,128)(2,1)}, bf16[8,256,704]{2,1,0:T(8,128)(2,1)}, bf16[4,704,512]{2,1,0:T(8,128)(2,1)}, bf16[2,704,512]{2,1,0:T(8,128)(2,1)}) custom-call(bf16[8,256,704]{2,1,0:T(8,128)(2,1)} %get-tuple-element.97.refs_0_, bf16[4,704,512]{2,1,0:T(8,128)(2,1)} %bitcast.112, ...), custom_call_target="tpu_custom_call" | custom-call | tf_op jit(solution)/shard_map/pallas_call | solution.py:828
  373.1 3.3 add_convert_fusion.2.refs_5_.refs_0_
  376.4 65.7 %shard_map.371 = (f32[256,2048]{1,0:T(8,128)}, bf16[4,704,512]{2,1,0:T(8,128)(2,1)}, bf16[4,704,512]{2,1,0:T(8,128)(2,1)}, bf16[2,704,512]{2,1,0:T(8,128)(2,1)}, bf16[2,704,512]{2,1,0:T(8,128)(2,1)}) custom-call(bf16[8,256,704]{2,1,0:T(8,128)(2,1)} %get-tuple-element.103.refs_0_, bf16[8,256,704]{2,1,0:T(8,128)(2,1)} %get-tuple-element.104.refs_1_, ...), custom_call_target="tpu_custom_call" | custom-call | tf_op jit(solution)/shard_map/pallas_call | solution.py:828
  442.1 2.9 multiply_reduce_fusion
  445.5 1.8 fusion.28.refs_0_
  448.2 1.6 add_convert_fusion.1.refs_4_.refs_0_
  451.5 60.7 %shard_map.372 = (bf16[256,2048]{1,0:T(8,128)(2,1)}, bf16[4,256,512]{2,1,0:T(8,128)(2,1)}, bf16[2,704,512]{2,1,0:T(8,128)(2,1)}, bf16[2,704,512]{2,1,0:T(8,128)(2,1)}, bf16[704,512]{1,0:T(8,128)(2,1)}) custom-call(bf16[256,2048]{1,0:T(8,128)(2,1)} %fusion.28.refs_0_, bf16[256,2048]{1,0:T(8,128)(2,1)} %copy-done.6, bf16[4,256,512]{2,1,0:T(8,128)(2,1)} %bitcast.107, ...), custom_call_target="tpu_custom_call" | custom-call | tf_op jit(solution)/shard_map/pallas_call | solution.py:828
  512.3 2.3 fusion.10.refs_2_
  514.6 23.3 %shard_map.373 = (f32[256,2048]{1,0:T(8,128)}, f32[2,64,2048]{2,1,0:T(8,128)S(1)}, f32[2,64,2048]{2,1,0:T(8,128)S(1)}) custom-call(s32[2,4]{1,0:T(2,128)S(1)} %slice.68.first_ref, s32[2,1,1024]{2,1,0:T(1,128)S(1)} %broadcast_in_dim.69.start_ref, bf16[256,2048]{1,0:T(8,128)(2,1)S(1)} %copy-done.13, bf16[256,2048]{1,0:T(8,128)(2,1)S(1)} %copy-done.7, ...), custom_call_target="tpu_custom_call" | custom-call | tf_op jit(solution)/shard_map/pallas_call | solution.py:983
  540.7 1.3 copy-done.39
  542.0 1.3 slice.119.refs_0_
  543.3 27.3 %shard_map.374 = (bf16[2,64,2,1024]{3,2,1,0:T(2,128)(2,1)}, bf16[2,256,512]{2,1,0:T(8,128)(2,1)}, bf16[704,512]{1,0:T(8,128)(2,1)}) custom-call(bf16[2,64,2,1024]{3,2,1,0:T(2,128)(2,1)} %slice.119.refs_0_, bf16[4,256,512]{2,1,0:T(8,128)(2,1)} %get-tuple-element.118.refs_1_, bf16[704,512]{1,0:T(8,128)(2,1)} %fusion.10.refs_2_), custom_call_target="tpu_custom_call" | custom-call | tf_op jit(solution)/shard_map/pallas_call | solution.py:828
  570.6 2.1 slice_add_fusion
  574.0 3.5 add_convert_fusion.refs_5_.refs_3_
  579.9 1.2 slice.80
  581.2 2.1 fusion.17
  585.3 69.5 %shard_map.375 = (f32[256,2048]{1,0:T(8,128)}, bf16[4,512,256]{2,1,0:T(8,128)(2,1)}, bf16[4,512,128]{2,1,0:T(8,128)(2,1)}, bf16[2,512,256]{2,1,0:T(8,128)(2,1)},...) custom-call(bf16[256,2048]{1,0:T(8,128)(2,1)} %bitcast.108, bf16[128,2048]{1,0:T(8,128)(2,1)} %bitcast.115, ...), custom_call_target="tpu_custom_call" | custom-call | tf_op jit(solution)/shard_map/pallas_call | solution.py:828
  654.8 2.5 fusion.8
  657.7 1.9 fusion.20.refs_2_
  659.5 2.2 fusion.11.refs_3_
  663.5 31.4 %shard_map.376 = (bf16[32,80,128]{2,1,0:T(8,128)(2,1)}, bf16[2,512,256]{2,1,0:T(8,128)(2,1)}, bf16[256,512]{1,0:T(8,128)(2,1)}, bf16[704,512]{1,0:T(8,128)(2,1)}) custom-call(bf16[32,80,128]{2,1,0:T(8,128)(2,1)} %pad_maximum_fusion.1.refs_0_, bf16[2,512,256]{2,1,0:T(8,128)(2,1)} %add_convert_fusion.7.refs_1_.refs_0_, bf16[256,512]{1,0:T(8,128)(2,1)} %fusion.20.refs_2_, ...), custom_call_target="tpu_custom_call" | custom-call | tf_op jit(solution)/shard_map/pallas_call | solution.py:828
  694.9 1.7 fusion.21
  696.6 2.2 collective-permute-start.1
  700.2 7.2 fusion.5
  709.1 2.0 reduce_sum.107
  711.1 2.1 reshape.353
  713.2 2.2 reduce_sum.108
  717.2 1.8 reshape.354
  724.3 2.5 shard_map.378
  726.8 1.4 copy-done.22
  728.1 1.4 copy-done.23
  730.6 4.1 shard_map.380
  735.4 1.8 copy-done.18
  737.2 1.8 copy-done.19
  740.2 7.1 shard_map.379
  748.2 2.9 shard_map.377
  (184 shorter events, 37.1 us)
Async XLA Ops:
  0.7 11.1 %collective-permute-start = (s32[1,2048]{1,0:T(1,128)}, s32[1,2048]{1,0:T(1,128)S(1)}, u32[]{:S(2)}, u32[]{:S(2)}) collective-permute-start(s32[1,2048]{1,0:T(1,128)} %param.24), channel_id=1, source_target_pairs={{0,8},{8,0},{1,9},{9,1},{2,10},{10,2},{3,11},{11,3},{4,12},{12,4},... | collective-permute-start | bytes 24584 | tf_op jit(solution)/shard_map/ppermute | solution.py:1338
  3.0 6.2 copy-start.4
  9.5 2.3 copy-start.58
  197.2 68.5 %copy-start.37 = (bf16[256,2048]{1,0:T(8,128)(2,1)S(1)}, bf16[256,2048]{1,0:T(8,128)(2,1)}, u32[]{:S(2)}) copy-start(bf16[256,2048]{1,0:T(8,128)(2,1)} %refs_2_.1) | copy-start | bytes 3145732
  376.4 68.6 %copy-start.38 = (bf16[256,2048]{1,0:T(8,128)(2,1)S(1)}, bf16[256,2048]{1,0:T(8,128)(2,1)}, u32[]{:S(2)}) copy-start(bf16[256,2048]{1,0:T(8,128)(2,1)} %refs_0_.1) | copy-start | bytes 3145732
  442.0 3.0 copy-start.35
  442.1 3.5 copy-start.36
  445.5 1.8 copy-start.47
  445.5 2.6 copy-start.48
  448.2 2.3 copy-start.14
  451.5 60.8 %copy-start.2 = (bf16[2,704,512]{2,1,0:T(8,128)(2,1)S(1)}, bf16[2,704,512]{2,1,0:T(8,128)(2,1)}, u32[]{:S(2)}) copy-start(bf16[2,704,512]{2,1,0:T(8,128)(2,1)} %add_convert_fusion.1.refs_4_.refs_0_) | copy-start | bytes 4325380
  512.3 2.3 copy-start.7
  512.3 2.3 copy-start.13
  570.6 2.4 copy-start.54
  572.7 4.7 copy-start.41
  574.0 3.5 copy-start.42
  574.0 3.5 copy-start.43
  574.0 3.5 copy-start.45
  577.5 2.5 slice-start
  578.6 4.9 copy-start.46
  654.8 2.8 copy-start.8
  654.8 4.7 copy-start
  657.6 4.1 copy-start.50
  657.6 4.1 copy-start.55
  657.7 5.0 copy-start.49
  662.6 32.3 %copy-start.9 = (bf16[2,512,256]{2,1,0:T(8,128)(2,1)S(1)}, bf16[2,512,256]{2,1,0:T(8,128)(2,1)}, u32[]{:S(2)}) copy-start(bf16[2,512,256]{2,1,0:T(8,128)(2,1)} %add_convert_fusion.7.refs_1_.refs_0_) | copy-start | bytes 1572868
  696.6 51.5 %collective-permute-start.1 = (bf16[512,256]{1,0:T(8,128)(2,1)}, bf16[512,256]{1,0:T(8,128)(2,1)}, u32[]{:S(2)}, u32[]{:S(2)}) collective-permute-start(bf16[512,256]{1,0:T(8,128)(2,1)} %fusion.21), channel_id=1, source_target_pairs={{0,8},{12,4},{1,9},{13,5},{2,10},{14,6},{3,11},{15,7},{16,24},{28,... | collective-permute-start | bytes 786440 | tf_op jit(solution)/shard_map/ppermute | solution.py:1606
  700.2 7.2 copy-start.60
  700.2 7.2 copy-start.61
  700.2 7.8 %copy-start.40 = (bf16[32,80,128]{2,1,0:T(8,128)(2,1)S(1)}, bf16[32,80,128]{2,1,0:T(8,128)(2,1)}, u32[]{:S(2)}) copy-start(bf16[32,80,128]{2,1,0:T(8,128)(2,1)} %get-tuple-element.134) | copy-start | bytes 1966084
  719.0 7.7 %copy-start.11 = (f32[704,512]{1,0:T(8,128)S(1)}, f32[704,512]{1,0:T(8,128)}, u32[]{:S(2)}) copy-start(f32[704,512]{1,0:T(8,128)} %param.30) | copy-start | bytes 4325380
  719.0 7.8 %copy-start.15 = (bf16[2,704,512]{2,1,0:T(8,128)(2,1)S(1)}, bf16[2,704,512]{2,1,0:T(8,128)(2,1)}, u32[]{:S(2)}) copy-start(bf16[2,704,512]{2,1,0:T(8,128)(2,1)} %get-tuple-element.112.refs_1_) | copy-start | bytes 4325380
  730.6 4.2 copy-start.3
  730.6 4.2 copy-start.5
  730.6 4.2 copy-start.16
  730.6 4.2 copy-start.17
  730.6 4.8 copy-start.26
  735.4 1.8 copy-start.18
  737.2 1.8 copy-start.19
  740.1 7.2 copy-start.52
  740.1 7.2 copy-start.53
  740.1 7.2 copy-start.56
  740.1 7.2 copy-start.57
  740.1 8.0 %copy-start.10 = (bf16[2,512,256]{2,1,0:T(8,128)(2,1)S(1)}, bf16[2,512,256]{2,1,0:T(8,128)(2,1)}, u32[]{:S(2)}) copy-start(bf16[2,512,256]{2,1,0:T(8,128)(2,1)} %add_convert_fusion.7.refs_1_.refs_0_) | copy-start | bytes 1572868
  740.2 8.0 %copy-start.21 = (f32[512,256]{1,0:T(8,128)S(1)}, f32[512,256]{1,0:T(8,128)}, u32[]{:S(2)}) copy-start(f32[512,256]{1,0:T(8,128)} %param.26) | copy-start | bytes 1572868
  740.2 8.0 %copy-start.25 = (bf16[2,512,256]{2,1,0:T(8,128)(2,1)S(1)}, bf16[2,512,256]{2,1,0:T(8,128)(2,1)}, u32[]{:S(2)}) copy-start(bf16[2,512,256]{2,1,0:T(8,128)(2,1)} %get-tuple-element.132.refs_1_) | copy-start | bytes 1572868
  740.2 8.0 %copy-start.31 = (f32[512,256]{1,0:T(8,128)S(1)}, f32[512,256]{1,0:T(8,128)}, u32[]{:S(2)}) copy-start(f32[512,256]{1,0:T(8,128)} %param.32) | copy-start | bytes 1572868
  740.2 8.0 %copy-start.32 = (f32[512,256]{1,0:T(8,128)S(1)}, f32[512,256]{1,0:T(8,128)}, u32[]{:S(2)}) copy-start(f32[512,256]{1,0:T(8,128)} %param.38) | copy-start | bytes 1572868
  (17 other events, 20.7 us)

commit v6 on v5

--- a/solution.py
+++ b/solution.py
@@ -80,13 +80,17 @@
 
 
 def adam_kernel(rate, decay, groups, place_ref, fix_ref, w_ref, m_ref, v_ref, *refs):
-    grads, (w_out, m_out, v_out) = refs[: 3 * groups], refs[3 * groups :]
+    grads, (w_out, m_out, v_out) = refs[:-3], refs[-3:]
     home = place_ref[1] == 1
+    each = len(grads) // groups
     grad = None
     for n in range(groups):
-        part, deep, got = grads[3 * n : 3 * n + 3]
-        mine = part[0].astype(jnp.float32) + deep[0].astype(jnp.float32)
-        found = jnp.where(home, mine, got[...].astype(jnp.float32))
+        if each == 1:
+            found = grads[n][...].astype(jnp.float32)
+        else:
+            part, deep, got = grads[3 * n : 3 * n + 3]
+            mine = part[0].astype(jnp.float32) + deep[0].astype(jnp.float32)
+            found = jnp.where(home, mine, got[...].astype(jnp.float32))
         grad = found if n == 0 else jnp.where(pl.program_id(0) == n, found, grad)
     first_new = BETA_ONE * m_ref[0] + (1.0 - BETA_ONE) * grad
     second_new = BETA_TWO * v_ref[0] + (1.0 - BETA_TWO) * grad * grad
@@ -110,11 +114,12 @@
         return lambda g, i: jnp.where(g == n, i, jnp.where(g < n, 0, steps - 1))
 
     specs, arrays = [], []
-    for n, (part, deep, got) in enumerate(grads):
+    for n, arrays_of in enumerate(grads):
         where = at(n)
         half = pl.BlockSpec((1, size, cols), lambda g, i, s, f=where: (s[0], f(g, i), 0))
-        specs += [half, half, pl.BlockSpec((size, cols), lambda g, i, s, f=where: (f(g, i), 0))]
-        arrays += [part, deep, got]
+        whole = pl.BlockSpec((size, cols), lambda g, i, s, f=where: (f(g, i), 0))
+        specs += [half, half, whole][3 - len(arrays_of) :]
+        arrays += list(arrays_of)
     kind = jax.ShapeDtypeStruct(weight.shape, jnp.float32)
     return pl.pallas_call(
         functools.partial(adam_kernel, rate, DECAY, groups),
@@ -125,7 +130,7 @@
             out_specs=[state] * 3,
         ),
         out_shape=[kind] * 3,
-        compiler_params=pltpu.CompilerParams(vmem_limit_bytes=32 * 2**20),
+        compiler_params=pltpu.CompilerParams(vmem_limit_bytes=60 * 2**20),
     )(place.astype(jnp.int32), fixes, weight, first, second, *arrays)
 
 
@@ -524,6 +529,9 @@
         scratch={},
         far={},
         extra_sems=1,
+        keep=True,
+        summed=None,
+        everyone=0,
         fill_one=None,
         fill_two=None,
         end=None,
@@ -531,7 +539,9 @@
         self.inputs = []
         self.rows, self.first, self.along_x = rows, first, along_x
         block, kind = (rows, cols), jnp.bfloat16
-        self.outputs = [jax.ShapeDtypeStruct(block, jnp.float32)]
+        self.outputs = [jax.ShapeDtypeStruct(block, jnp.float32)] if keep else []
+        self.keep, self.summed = keep, summed
+        self.everyone, self.devices = everyone > 0, everyone
         self.sems = [7, 7, 2, 1, extra_sems]
         self.scratch = [pltpu.VMEM((8,) + block, kind)]
         self.scratch += [pltpu.VMEM((4,) + block, kind)] * 2 + [pltpu.VMEM(block, kind)] * 3
@@ -665,14 +675,18 @@
         straight.wait_recv()
         last.wait_recv()
         add(own, out, direct_in, late_in)
-        pltpu.make_async_copy(out, outs[0], sems[3].at[0]).start()
+        if self.summed:
+            self.summed(refs, out)
+        if self.keep:
+            pltpu.make_async_copy(out, outs[0], sems[3].at[0]).start()
         for n, block in enumerate((across, direct, after, own)):
             to_core(n, block).wait_send()
         for copy in (turn, straight, last):
             copy.wait_send()
         if self.end:
             self.end(refs)
-        pltpu.make_async_copy(out, outs[0], sems[3].at[0]).wait()
+        if self.keep:
+            pltpu.make_async_copy(out, outs[0], sems[3].at[0]).wait()
         self.flushed(refs)
 
 
@@ -968,7 +982,7 @@
             jax.ShapeDtypeStruct(query_t.shape, jnp.bfloat16),
             jax.ShapeDtypeStruct((packs, heads, rows), jnp.float32),
         ],
-        compiler_params=pltpu.CompilerParams(vmem_limit_bytes=48 * 2**20),
+        compiler_params=pltpu.CompilerParams(vmem_limit_bytes=60 * 2**20),
     )(first, start, query_t, keys_t, values_t)
 
 
@@ -1011,7 +1025,7 @@
             jax.ShapeDtypeStruct((packs, HD, window), jnp.float32),
             jax.ShapeDtypeStruct((packs, HD, window), jnp.float32),
         ],
-        compiler_params=pltpu.CompilerParams(vmem_limit_bytes=48 * 2**20),
+        compiler_params=pltpu.CompilerParams(vmem_limit_bytes=60 * 2**20),
     )(first, start, query_t, out_t, grad_t, lse, keys_t, values_t)
 
 
@@ -1210,41 +1224,240 @@
         put_cols(target, j, dot_nt(query, refs.wq[j]) + dot_nt(pair, refs.wp[j]), h_size)
 
 
-def query_fill(h_size, refs):
-    refs.total[...] = jnp.zeros_like(refs.total)
-    refs.pair_total[...] = jnp.zeros_like(refs.pair_total)
-
-    def add(n, rows):
-        at = lanes_of(n, rows.shape[0])
-        refs.total[...] += dot_nn(refs.dq[:, at], rows[...])
-        refs.pair_total[...] += dot_nn(refs.dpair[:, at], rows[...])
-
-    refs.stream("rows", add)
-    for j in range(4):
-        refs.gwq[j] = cols_at(refs.total, j, h_size).T.astype(jnp.bfloat16)
-        refs.gwp[j] = cols_at(refs.pair_total, j, h_size).T.astype(jnp.bfloat16)
-    refs.flush("gwq").start()
-    refs.flush("gwp").start()
-    swap_copy(refs.gwq, refs.came, refs.more.at[0], refs.more.at[1]).start()
-
-
-def query_end(refs):
-    swap_copy(refs.gwq, refs.came, refs.more.at[0], refs.more.at[1]).wait()
+NORM_STRIP = 16
+
+
+def strips(rows, body):
+    @pl.loop(0, rows // NORM_STRIP)
+    def _(strip):
+        body(pl.ds(pl.multiple_of(strip * NORM_STRIP, NORM_STRIP), NORM_STRIP))
+
+
+def inverse_of(values):
+    return lax.rsqrt(jnp.mean(values * values, axis=1, keepdims=True) + NORM_EPS)
+
+
+def attn_summed(refs, out):
+    def body(at):
+        middle = refs.x[at].astype(jnp.float32) + out[at]
+        out[at] = middle
+        refs.normed[at] = (middle * inverse_of(middle) * refs.gains[1:2]).astype(jnp.bfloat16)
+
+    strips(out.shape[0], body)
+    refs.flush("normed").start()
+
+
+def mlp_summed(refs, out):
+    def body(at):
+        refs.hidden_out[at] = (refs.middle[at] + out[at]).astype(jnp.bfloat16)
+
+    strips(out.shape[0], body)
+    refs.flush("hidden_out").start()
+
+
+def norm_back_strip(upstream, inputs, gain):
+    inverse = inverse_of(inputs)
+    scaled = gain * upstream
+    inner = jnp.mean(scaled * inputs, axis=1, keepdims=True)
+    back = inverse * scaled - inputs * inverse * inverse * inverse * inner
+    by_gain = upstream * inputs * inverse
+    return back, by_gain[:8] + by_gain[8:]
+
+
+def mlp_norm_summed(refs, out):
+    refs.gain_sums[...] = jnp.zeros_like(refs.gain_sums)
+
+    def body(at):
+        back, sums = norm_back_strip(out[at], refs.middle[at], refs.gains[1:2])
+        grad = refs.dy_own[at].astype(jnp.float32) + back
+        out[at] = grad
+        refs.dat[at] = grad.astype(jnp.bfloat16)
+        refs.gain_sums[...] += sums
+
+    strips(out.shape[0], body)
+    refs.flush("dat").start()
+    refs.flush("gain_sums").start()
+
+
+def to_device(src, dst, send, recv, device):
+    return pltpu.make_async_remote_copy(
+        src_ref=src,
+        dst_ref=dst,
+        send_sem=send,
+        recv_sem=recv,
+        device_id=device,
+        device_id_type=pl.DeviceIdType.LOGICAL,
+    )
+
+
+class Last:
+    def __init__(self, h_size, devices, pair_rows, gain_cols, head_of):
+        self.h_size, self.devices, self.pair_rows = h_size, devices, pair_rows
+        self.gain_cols, self.head_of = gain_cols, head_of
+        self.sems = 6 + 4 * devices
+
+    def pair_part(self, refs, device):
+        width = D // (4 * self.h_size)
+        row = device * self.pair_rows
+        block = lax.rem(row // width, 4)
+        at = (row // (4 * width)) * width + lax.rem(row, width)
+        return refs.gwp.at[block, pl.ds(pl.multiple_of(at, self.pair_rows), self.pair_rows)]
+
+    def gain_part(self, refs, device):
+        tile = (device * self.gain_cols) // 128
+        return refs.gain_send.at[:, pl.ds(pl.multiple_of(tile * 128, 128), 128)]
+
+    def send(self, refs, kind, step):
+        me = my_number()
+        to = lax.rem(me + step, self.devices)
+        base = 6 + 2 * kind * self.devices
+        part = self.pair_part if kind == 0 else self.gain_part
+        held = refs.pair_in if kind == 0 else refs.gain_in
+        return to_device(
+            part(refs, to),
+            held.at[me],
+            refs.more.at[base + step],
+            refs.more.at[base + self.devices + me],
+            to,
+        )
+
+    def arrive(self, refs, kind, step):
+        me = my_number()
+        origin = lax.rem(me + step, self.devices)
+        base = 6 + 2 * kind * self.devices
+        part = self.pair_part if kind == 0 else self.gain_part
+        held = refs.pair_in if kind == 0 else refs.gain_in
+        to_device(
+            part(refs, me),
+            held.at[origin],
+            refs.more.at[base + step],
+            refs.more.at[base + self.devices + origin],
+            origin,
+        ).wait_recv()
+
+    def swap(self, refs):
+        return swap_copy(refs.gwq, refs.q_came, refs.more.at[0], refs.more.at[1])
+
+    def deep(self, refs):
+        return far_copy(
+            refs.q_part, refs.q_deep, refs.more.at[2], refs.more.at[3], flipped("zh")
+        )
+
+    def across(self, refs):
+        return far_copy(refs.q_send, refs.q_got, refs.more.at[4], refs.more.at[5], flipped("c"))
+
+    def fill_one(self, refs):
+        refs.total[...] = jnp.zeros_like(refs.total)
+        refs.pair_total[...] = jnp.zeros_like(refs.pair_total)
+
+        def add(n, rows):
+            at = lanes_of(n, rows.shape[0])
+            refs.total[...] += dot_nn(refs.dq[:, at], rows[...])
+            refs.pair_total[...] += dot_nn(refs.dpair[:, at], rows[...])
+
+        refs.stream("rows", add)
+        for j in range(4):
+            refs.gwq[j] = cols_at(refs.total, j, self.h_size).T.astype(jnp.bfloat16)
+            refs.gwp[j] = cols_at(refs.pair_total, j, self.h_size).T.astype(jnp.bfloat16)
+        self.swap(refs).start()
+
+        @pl.loop(1, self.devices)
+        def _(step):
+            self.send(refs, 0, step).start()
+
+        pltpu.sync_copy(self.pair_part(refs, my_number()), refs.pair_in.at[my_number()])
+
+    def fill_two(self, refs):
+        self.swap(refs).wait_recv()
+        mine = 2 * lax.axis_index("y")
+        for n in range(2):
+            kept = refs.gwq[mine + n].astype(jnp.float32)
+            refs.q_part[n] = (kept + refs.q_came[n].astype(jnp.float32)).astype(jnp.bfloat16)
+
+        @pl.when(not_home())
+        def _():
+            self.deep(refs).start()
+
+        refs.pair_sum[...] = jnp.zeros_like(refs.pair_sum)
+        refs.pair_sum[self.head_of(my_number())] += refs.pair_in[my_number()].astype(jnp.float32)
+
+        @pl.loop(1, self.devices)
+        def _(step):
+            self.arrive(refs, 0, step)
+            origin = lax.rem(my_number() + step, self.devices)
+            refs.pair_sum[self.head_of(origin)] += refs.pair_in[origin].astype(jnp.float32)
+
+        refs.flush("pair_sum").start()
+
+    def summed(self, refs, out):
+        refs.sums[...] = jnp.zeros_like(refs.sums)
+
+        def body(at):
+            x = refs.x[at].astype(jnp.float32)
+            back, sums = norm_back_strip(out[at], x, refs.gains[0:1])
+            out[at] = refs.mid[at] + back
+            refs.sums[...] += sums
+
+        strips(out.shape[0], body)
+        attn = jnp.sum(refs.sums[...], axis=0, keepdims=True)
+        mlp = jnp.sum(refs.mlp_sums[...], axis=0, keepdims=True)
+        row = lax.broadcasted_iota(jnp.int32, refs.gain_send.shape, 0)
+        both = jnp.where(row == 0, attn, jnp.where(row == 1, mlp, 0.0))
+        refs.gain_send[...] = both.astype(jnp.bfloat16)
+
+        @pl.loop(1, self.devices)
+        def _(step):
+            self.send(refs, 1, step).start()
+
+        pltpu.sync_copy(self.gain_part(refs, my_number()), refs.gain_in.at[my_number()])
+
+    def end(self, refs):
+        core = lax.axis_index("c")
+
+        @pl.when(at_home())
+        def _():
+            self.deep(refs).wait_recv()
+            pick = lambda n: refs.q_part[n].astype(jnp.float32) + refs.q_deep[n].astype(jnp.float32)
+            refs.q_send[...] = pick(1 - core).astype(jnp.bfloat16)
+            self.across(refs).start()
+            refs.gq[...] = pick(core).astype(jnp.bfloat16)
+
+        @pl.when(not_home())
+        def _():
+            self.across(refs).wait_recv()
+            refs.gq[...] = refs.q_got[...]
+
+        refs.flush("gq").start()
+        total = refs.gain_in[my_number()].astype(jnp.float32)
+        refs.gain_sum[...] = total
+
+        @pl.loop(1, self.devices)
+        def _(step):
+            self.arrive(refs, 1, step)
+            origin = lax.rem(my_number() + step, self.devices)
+            refs.gain_sum[...] += refs.gain_in[origin].astype(jnp.float32)
+
+        refs.flush("gain_sum").start()
+        self.swap(refs).wait_send()
+
+        @pl.when(at_home())
+        def _():
+            self.across(refs).wait_send()
+
+        @pl.when(not_home())
+        def _():
+            self.deep(refs).wait_send()
+
+        @pl.loop(1, self.devices)
+        def _(step):
+            self.send(refs, 0, step).wait_send()
+            self.send(refs, 1, step).wait_send()
 
 
 def rotate_back(grads, cos_table, sin_table):
     front, back = grads[:, :HALF], grads[:, HALF:]
     return jnp.concatenate(
         [front * cos_table + back * sin_table, back * cos_table - front * sin_table], axis=1
-    )
-
-
-def norm_back(upstream, inputs, inverse, gain):
-    scaled = gain * upstream
-    inner = jnp.mean(scaled * inputs, axis=1, keepdims=True)
-    return (
-        inverse * scaled - inputs * inverse * inverse * inverse * inner,
-        jnp.sum(upstream * inputs * inverse, axis=0),
     )
 
 
@@ -1258,11 +1471,12 @@
 
 
 def own_sum(grads, h_size, by_cols):
-    part, deep, got = grads
-    at = lax.axis_index("c")
-    pick = lambda a: lax.dynamic_index_in_dim(a, at, 0, keepdims=False).astype(jnp.float32)
-    home = at == lax.axis_index("zh")
-    total = jnp.where(home, pick(part) + pick(deep), got.astype(jnp.float32))
+    total = grads[-1].astype(jnp.float32)
+    if len(grads) == 3:
+        part, deep, _ = grads
+        at = lax.axis_index("c")
+        pick = lambda a: lax.dynamic_index_in_dim(a, at, 0, keepdims=False).astype(jnp.float32)
+        total = jnp.where(at == lax.axis_index("zh"), pick(part) + pick(deep), total)
     rows, cols = total.shape
     if by_cols:
         parts = total.reshape(rows, h_size, cols // h_size).transpose(1, 0, 2)
@@ -1308,7 +1522,6 @@
     zl_size = tensor_size // 4
     core, z_high = lax.axis_index("c"), lax.axis_index("zh")
     z_low, x_at = lax.axis_index("zl"), lax.axis_index("x")
-    inputs = hidden_in.astype(jnp.float32)
     devices = h_size * 4 * tensor_size
 
     pair_rows = keyvalue_weight.shape[0]
@@ -1355,7 +1568,7 @@
     block_first = start[:, ::QUERY_BLOCK]
     start = start[:, None, :]
 
-    block_rows = inputs.shape[0]
+    block_rows = hidden_in.shape[0]
     group_rows = 8 * block_rows
     width = heads_here * HD
     gateup_t = gateup_weight.swapaxes(1, 2)
@@ -1374,7 +1587,6 @@
             query_task,
             GatherRows(
                 hidden_in,
-                along_x=True,
                 onward_first=True,
                 keep=False,
                 given=dict(cos=cos_table, sin=sin_table),
@@ -1406,15 +1618,13 @@
         .reshape(4, D // 4, 2 * HD)
     )
     query_full = row_blocks(query_parts)
-    gain_attn, gain_mlp = gains_all[0], gains_all[1]
-    inverse_one = lax.rsqrt(jnp.mean(inputs * inputs, axis=1, keepdims=True) + NORM_EPS)
     grad_rows, pair_back_half, output_parts, gate_parts, up_parts = run(
         2,
-        GatherRows(out_grad, along_x=True),
+        GatherRows(out_grad),
         Move(pair_rot, "zh", lambda: lax.axis_index("zh") == 0),
         Pass(output_parts),
         Pass(gate_parts),
-        later(Spread(own_shard(gateup_t[1], h_size))),
+        Spread(own_shard(gateup_t[1], h_size)),
     )
     output_full, gate_full = col_blocks(output_parts), col_blocks(gate_parts)
     pair_back_half = jnp.where(z_high == 1, pair_back_half, 0)
@@ -1427,24 +1637,24 @@
     ).transpose(0, 2, 1, 3)
     keys_t, values_t = pair_window[0], pair_window[1]
     attended_t, log_totals = attn_fwd(block_first, start, query_rot, keys_t, values_t)
-    attn_out, up_parts, down_parts = run(
-        3,
-        ScatterRows(
-            block_rows,
-            D,
-            functools.partial(output_produce, h_size),
-            along_x=True,
-            first=("o", "wo"),
-            given=dict(o=attended_t, wo=output_full),
-        ),
-        Pass(up_parts),
-        SpreadAll(own_shard(down_weight, h_size)),
+    residual_mid, normed_two, up_parts, down_parts = flat(
+        run(
+            3,
+            ScatterRows(
+                block_rows,
+                D,
+                functools.partial(output_produce, h_size),
+                first=("o", "wo"),
+                given=dict(o=attended_t, wo=output_full, x=hidden_in, gains=gains_all),
+                results=dict(normed=shape(block_rows, D)),
+                summed=attn_summed,
+            ),
+            Pass(up_parts),
+            SpreadAll(own_shard(down_weight, h_size)),
+        )
     )
     up_full = col_blocks(up_parts)
 
-    residual_mid = inputs + attn_out
-    inverse_two = lax.rsqrt(jnp.mean(residual_mid * residual_mid, axis=1, keepdims=True) + NORM_EPS)
-    normed_two = (residual_mid * inverse_two * gain_mlp).astype(jnp.bfloat16)
     hidden_shape = shape(8, block_rows, units)
     rows_two, hidden_mlp, by_gate, by_up = flat(
         run(
@@ -1462,7 +1672,7 @@
 
     sums = pltpu.VMEM((2, units, D // 4), jnp.float32)
     whole_grad, half_grad = shape(4, units, D // 4), shape(2, units, D // 4)
-    mlp_out, gate_grad, up_grad, down_grad, down_came = flat(
+    gate_grad, up_grad, down_grad, hidden_out, down_came = flat(
         run(
             5,
             ScatterRows(
@@ -1471,9 +1681,18 @@
                 functools.partial(down_produce, h_size),
                 first=("hid", "wd"),
                 by_block=("dgate", "dup"),
-                given=dict(hid=hidden_mlp, wd=down_full, by_gate=by_gate, by_up=by_up),
+                given=dict(
+                    hid=hidden_mlp, wd=down_full, by_gate=by_gate, by_up=by_up, middle=residual_mid
+                ),
                 streams=dict(dy=grad_rows),
-                results=dict(dgate=hidden_shape, dup=hidden_shape, gwd=whole_grad),
+                results=dict(
+                    dgate=hidden_shape,
+                    dup=hidden_shape,
+                    gwd=whole_grad,
+                    hidden_out=shape(block_rows, D),
+                ),
+                keep=False,
+                summed=mlp_summed,
                 scratch=dict(total=sums),
                 far=dict(came=half_grad),
                 extra_sems=2,
@@ -1483,20 +1702,32 @@
             ),
         )
     )
-    hidden_out = (residual_mid + mlp_out).astype(jnp.bfloat16)
     down_part = add_swapped(down_grad, down_came)
-    normed_two_grad, gate_wgrad, up_wgrad, gate_came, down_deep = flat(
+    mid_grad, gate_wgrad, up_wgrad, mid_rounded, mlp_sums, gate_came, down_deep = flat(
         run(
             6,
             ScatterRows(
                 block_rows,
                 D,
                 functools.partial(gateup_produce, h_size),
-                along_x=True,
                 first=("dgate", "dup", "wg", "wu"),
-                given=dict(dgate=gate_grad, dup=up_grad, wg=gate_full, wu=up_full),
+                given=dict(
+                    dgate=gate_grad,
+                    dup=up_grad,
+                    wg=gate_full,
+                    wu=up_full,
+                    middle=residual_mid,
+                    dy_own=out_grad,
+                    gains=gains_all,
+                ),
                 streams=dict(rows=rows_two),
-                results=dict(gwg=whole_grad, gwu=whole_grad),
+                results=dict(
+                    gwg=whole_grad,
+                    gwu=whole_grad,
+                    dat=shape(block_rows, D),
+                    gain_sums=shape(8, D, kind=jnp.float32),
+                ),
+                summed=mlp_norm_summed,
                 scratch=dict(total=sums),
                 far=dict(came=half_grad),
                 extra_sems=2,
@@ -1508,14 +1739,11 @@
         )
     )
     gate_part = add_swapped(gate_wgrad, gate_came)
-    mid_back, gain_mlp_grad = norm_back(normed_two_grad, residual_mid, inverse_two, gain_mlp)
-    mid_grad = out_grad.astype(jnp.float32) + mid_back
     attended_grad, output_grad, up_came, gate_deep, down_got = flat(
         run(
             7,
             GatherRows(
-                mid_grad.astype(jnp.bfloat16),
-                along_x=True,
+                mid_rounded,
                 keep=False,
                 given=dict(o=attended_t, wo=output_full),
                 results=dict(do=shape(width, group_rows), gwo=shape(*output_full.shape)),
@@ -1525,7 +1753,7 @@
                 after=output_after,
             ),
             Swap(up_wgrad),
-            later(Move(gate_part, "zh", not_home)),
+            Move(gate_part, "zh", not_home),
             Move(for_partner(down_part, down_deep), "c", at_home),
         )
     )
@@ -1557,68 +1785,68 @@
     ).astype(jnp.bfloat16)
     pair_back = pair_back.reshape(2 * HD, group_rows)
     quarter = D // 4
-    normed_one_grad, query_wgrad, pair_wgrad, query_came, up_deep, output_deep = flat(
+    last = Last(h_size, devices, pair_rows, gain_cols, head_of)
+    half_q = pltpu.VMEM((2, quarter, width), jnp.bfloat16)
+    whole_q = pltpu.VMEM((quarter, width), jnp.bfloat16)
+    input_grad, query_grad, pair_sums, gain_sums, up_deep, output_deep = flat(
         run(
             9,
             ScatterRows(
                 block_rows,
                 D,
                 functools.partial(query_produce, h_size),
-                along_x=True,
                 first=("dq", "dpair", "wq", "wp"),
-                given=dict(dq=query_back, dpair=pair_back, wq=query_full, wp=pair_proj),
+                given=dict(
+                    dq=query_back,
+                    dpair=pair_back,
+                    wq=query_full,
+                    wp=pair_proj,
+                    x=hidden_in,
+                    mid=mid_grad,
+                    gains=gains_all,
+                    mlp_sums=mlp_sums,
+                ),
                 streams=dict(rows=rows_one),
-                results=dict(gwq=shape(4, quarter, width), gwp=shape(4, quarter, 2 * HD)),
+                results=dict(
+                    gq=shape(quarter, width),
+                    pair_sum=shape(KVH, pair_rows, 2 * HD, kind=jnp.float32),
+                    gain_sum=shape(pad_rows, 128, kind=jnp.float32),
+                ),
                 scratch=dict(
                     total=pltpu.VMEM((width, D), jnp.float32),
                     pair_total=pltpu.VMEM((2 * HD, D), jnp.float32),
+                    gwq=pltpu.VMEM((4, quarter, width), jnp.bfloat16),
+                    gwp=pltpu.VMEM((4, quarter, 2 * HD), jnp.bfloat16),
+                    q_came=half_q,
+                    q_part=half_q,
+                    q_deep=half_q,
+                    q_send=whole_q,
+                    q_got=whole_q,
+                    sums=pltpu.VMEM((8, D), jnp.float32),
+                    gain_send=pltpu.VMEM((pad_rows, D), jnp.bfloat16),
+                    pair_in=pltpu.VMEM((devices, pair_rows, 2 * HD), jnp.bfloat16),
+                    gain_in=pltpu.VMEM((devices, pad_rows, 128), jnp.bfloat16),
                 ),
-                far=dict(came=shape(2, quarter, width)),
-                extra_sems=2,
-                fill_one=functools.partial(query_fill, h_size),
-                end=query_end,
+                extra_sems=last.sems,
+                everyone=devices,
+                fill_one=last.fill_one,
+                fill_two=last.fill_two,
+                summed=last.summed,
+                end=last.end,
             ),
             Move(up_part, "zh", not_home),
             Move(output_part, "zh", not_home),
         )
     )
-    query_part = add_swapped(query_wgrad, query_came)
-    pair_wgrad = (
-        pair_wgrad.reshape(4, h_size, quarter // h_size, 2 * HD)
-        .transpose(1, 0, 2, 3)
-        .reshape(devices, pair_rows, 2 * HD)
-    )
-    input_back, gain_attn_grad = norm_back(normed_one_grad, inputs, inverse_one, gain_attn)
-    input_grad = mid_grad + input_back
-    gains_grad = jnp.stack([gain_attn_grad, gain_mlp_grad]).reshape(2, devices, gain_cols)
-    gains_grad = gains_grad.transpose(1, 0, 2).reshape(devices, 2 * gain_cols)
-    gains_grad = jnp.pad(gains_grad, ((0, 0), (0, pad_rows * 2 * HD - 2 * gain_cols)))
-    small_grads = jnp.concatenate(
-        [pair_wgrad, gains_grad.reshape(devices, pad_rows, 2 * HD).astype(jnp.bfloat16)], axis=1
-    )
-    small_sums, query_deep, output_got, up_got = run(
-        10,
-        Everyone(small_grads, lambda device: device, devices),
-        Move(query_part, "zh", not_home),
-        Move(for_partner(output_part, output_deep), "c", at_home),
-        Move(for_partner(up_part, up_deep), "c", at_home),
-    )
-    query_got = lax.ppermute(for_partner(query_part, query_deep), ("c", "zh"), TO_AWAY_CORE)
-    small_sums = small_sums.astype(jnp.float32)
-    pair_sums = (
-        small_sums[:, :pair_rows]
-        .reshape(h_size * 2, 2, 2, zl_size * 2, pair_rows, 2 * HD)
-        .sum(axis=(0, 2))
-        .reshape(KVH, tensor_size // KVH, pair_rows, 2, HD)
-        .sum(axis=1)
-    )
-    keyvalue_sum = pair_sums.transpose(1, 2, 0, 3).reshape(pair_rows, 2 * KVH * HD)
-    gains_sum = (
-        small_sums[:, pair_rows:]
-        .sum(axis=0)
-        .reshape(pad_rows * 2 * HD)[: 2 * gain_cols]
-        .reshape(2, gain_cols)
-    )
+    cores = lambda a: lax.ppermute(a, ("c", "zh"), TO_AWAY_CORE)
+    up_got = cores(for_partner(up_part, up_deep))
+    output_got = cores(for_partner(output_part, output_deep))
+    keyvalue_sum = (
+        pair_sums.reshape(KVH, pair_rows, 2, HD)
+        .transpose(1, 2, 0, 3)
+        .reshape(pair_rows, 2 * KVH * HD)
+    )
+    gains_sum = lax.dynamic_slice(gain_sums, (jnp.int32(0), lane), (2, gain_cols))
     step_value = step_count[0].astype(jnp.float32)
     fixes = jnp.stack(
         [
@@ -1669,7 +1897,7 @@
         query_second,
         D ** (-0.5),
         False,
-        (query_part, query_deep, query_got),
+        (query_grad,),
     )
     pair_new, pair_mone, pair_mtwo = adam_step(
         keyvalue_weight,

time: 756 us -> 713 us (0.943)
  other arithmetic: 63.2 us -> 34.2 us
  local copies, waits for them, and re-layouts: 39.3 us -> 19.9 us
    unnamed x128 -> x57, local copies, waits for them, and re-layouts: 22.8 us -> 6.14 us
    reduce_sum x6 -> x0, other arithmetic: 11.8 us -> none  [the longest x2 5.49 us: norm_back(): jnp.sum(upstream * inputs * inverse, axis=0)]
    pallas_call x4, Pallas kernels: 16.6 us -> 25.1 us  [adam_shard(): pl.pallas_call(functools.partial(adam_kernel, rate, DECAY, groups), grid_...]
    pallas_call x10 -> x9, Pallas kernels: 586 us -> 580 us  [run(): pl.pallas_call(kernel, in_specs=in_specs, out_specs=out_specs, out_shape=...]
  transfers between devices with their start and end apart: 2 -> 3, of which waited for: 0 -> 0; matrix products, arithmetic and copies ran while one was open for 4% -> 2% of each run, Pallas kernels for 2% -> 2%
where the time goes in v6:
time: 713 us; the launch traced here: 707 us
  Pallas kernels  647 us (91%)
  other arithmetic  34.2 us (5%)
  local copies, waits for them, and re-layouts  19.9 us (3%)
    pallas_call x9, Pallas kernels, run(): pl.pallas_call(kernel, in_specs=in_specs, out_specs=out_specs, out_shape=...  580 us
    pallas_call x4, Pallas kernels, adam_shard(): pl.pallas_call(functools.partial(adam_kernel, rate, DECAY, groups), grid_...  25.1 us
    pallas_call x1, Pallas kernels, attn_bwd(): pl.pallas_call(functools.partial(attn_bwd_kernel, heads), grid_spec=pltpu...  23.2 us
    pallas_call x1, Pallas kernels, attn_fwd(): pl.pallas_call(functools.partial(attn_fwd_kernel, heads), grid_spec=pltpu...  19.1 us
  transfers between devices with their start and end apart: 3, of which 0 were waited for; matrix products, arithmetic and copies ran while one was open for 2% of the time, Pallas kernels for 2%

profile of v6, /device:TPU:0, one launch (start us, length us, event | category | flops | bytes accessed | tf_op | source)
XLA Modules:
  0.0 706.6 jit_solution(12740056178592127022)
XLA Ops:
  1.2 0.9 convert.36
  2.5 1.9 convert_bitcast_fusion.2.refs_1_
  4.4 1.8 convert_bitcast_fusion.1.refs_5_
  6.2 2.3 convert_bitcast_fusion.refs_5_
  8.7 1.2 fusion.21
  12.4 1.8 multiply_sine_fusion.1
  14.2 98.0 %shard_map.365 = (bf16[32,80,128]{2,1,0:T(8,128)(2,1)}, bf16[4,1,512,256]{3,2,1,0:T(8,128)(2,1)}, f32[16,2048]{1,0:T(8,128)}, bf16[8,256,2048]{2,1,0:T(8,128)(2,...) custom-call(bf16[4,80,128]{2,1,0:T(8,128)(2,1)} %pad_maximum_fusion., ...), custom_call_target="tpu_custom_call" | custom-call | tf_op jit(solution)/shard_map/pallas_call | solution.py:842
  112.2 1.4 reshape.294
  113.8 58.5 %shard_map.366 = (bf16[8,256,2048]{2,1,0:T(8,128)(2,1)}, bf16[128,2048]{1,0:T(8,128)(2,1)}, bf16[4,1,256,512]{3,2,1,0:T(8,128)(2,1)}, bf16[4,1,704,512]{3,2,1,0:T(8,128)(2,1)}, bf16[4,1,704,512]{3,2,1,0:T(8,128)(2,1)}) custom-call(bf16[256,2048]{1,0:T(8,128)(2,1)} %refs_5_.1, ...), custom_call_target="tpu_custom_call", output_to_operand_aliasing={{2}: (2, {}), {3}: (3, {})} | custom-call | tf_op jit(solution)/shard_map/pallas_call | solution.py:842
  172.9 1.1 slice_bitcast_fusion
  174.0 19.1 %shard_map.367 = (bf16[256,2048]{1,0:T(8,128)(2,1)}, f32[2,4,1024]{2,1,0:T(4,128)}) custom-call(s32[2,4]{1,0:T(2,128)} %slice.52.first_ref, s32[2,1,1024]{2,1,0:T(1,128)} %broadcast_in_dim.65.start_ref, bf16[256,2048]{1,0:T(8,128)(2,1)} %get-tuple-element.84.q_ref, bf16[2,64,2048]{2,1,0:T(8,128)(2,1)} %get-tuple-element.164.kt_ref, ...), custom_call_target="tpu_custom_call" | custom-call | tf_op jit(solution)/shard_map/pallas_call | solution.py:964
  193.1 72.1 %shard_map.368 = (f32[256,2048]{1,0:T(8,128)}, bf16[256,2048]{1,0:T(8,128)(2,1)}, bf16[4,1,704,512]{3,2,1,0:T(8,128)(2,1)}, bf16[4,1,704,512]{3,2,1,0:T(8,128)(2,1)}) custom-call(bf16[256,2048]{1,0:T(8,128)(2,1)} %get-tuple-element.89.refs_0_.refs_1_.o_ref, bf16[4,256,512]{2,1,0:T(8,128)(2,1)} %bitcast.78, ...), custom_call_target="tpu_custom_call", output_to_operand_aliasing={{2}: (4, {})} | custom-call | tf_op jit(solution)/shard_map/pallas_call | solution.py:842
  265.2 46.9 %shard_map.369 = (bf16[8,256,2048]{2,1,0:T(8,128)(2,1)}, bf16[8,256,704]{2,1,0:T(8,128)(2,1)}, bf16[8,256,704]{2,1,0:T(8,128)(2,1)}, bf16[8,256,704]{2,1,0:T(8,128)(2,1)}) custom-call(bf16[256,2048]{1,0:T(8,128)(2,1)} %get-tuple-element.93.refs_0_, bf16[4,704,512]{2,1,0:T(8,128)(2,1)} %bitcast.75, bf16[4,704,512]{2,1,0:T(8,128)(2,1)} %bitcast.73), custom_call_target="tpu_custom_call" | custom-call | tf_op jit(solution)/shard_map/pallas_call | solution.py:842
  312.1 58.4 %shard_map.370 = (bf16[8,256,704]{2,1,0:T(8,128)(2,1)}, bf16[8,256,704]{2,1,0:T(8,128)(2,1)}, bf16[4,704,512]{2,1,0:T(8,128)(2,1)}, bf16[256,2048]{1,0:T(8,128)(2,1)}, bf16[2,704,512]{2,1,0:T(8,128)(2,1)}) custom-call(bf16[8,256,704]{2,1,0:T(8,128)(2,1)} %get-tuple-element.96.refs_0_, bf16[4,704,512]{2,1,0:T(8,128)(2,1)} %bitcast.82, ...), custom_call_target="tpu_custom_call" | custom-call | tf_op jit(solution)/shard_map/pallas_call | solution.py:842
  370.5 3.3 add_convert_fusion.2.refs_8_.refs_0_
  373.8 66.7 %shard_map.371 = (f32[256,2048]{1,0:T(8,128)}, bf16[4,704,512]{2,1,0:T(8,128)(2,1)}, bf16[4,704,512]{2,1,0:T(8,128)(2,1)}, bf16[256,2048]{1,0:T(8,128)(2,1)}, f3...) custom-call(bf16[8,256,704]{2,1,0:T(8,128)(2,1)} %get-tuple-element.103.refs_0_, ...), custom_call_target="tpu_custom_call" | custom-call | tf_op jit(solution)/shard_map/pallas_call | solution.py:842
  440.6 2.3 fusion.refs_5_
  442.8 2.9 add_convert_fusion.1.refs_4_.refs_0_
  445.7 58.8 %shard_map.372 = (bf16[256,2048]{1,0:T(8,128)(2,1)}, bf16[4,256,512]{2,1,0:T(8,128)(2,1)}, bf16[2,704,512]{2,1,0:T(8,128)(2,1)}, bf16[2,704,512]{2,1,0:T(8,128)(2,1)}, bf16[704,512]{1,0:T(8,128)(2,1)}) custom-call(bf16[256,2048]{1,0:T(8,128)(2,1)} %get-tuple-element.108.refs_0_, bf16[256,2048]{1,0:T(8,128)(2,1)} %get-tuple-element.89.refs_0_.refs_1_.o_ref, ...), custom_call_target="tpu_custom_call" | custom-call | tf_op jit(solution)/shard_map/pallas_call | solution.py:842
  504.5 2.2 fusion.1.refs_2_
  506.7 23.2 %shard_map.373 = (f32[256,2048]{1,0:T(8,128)}, f32[2,64,2048]{2,1,0:T(8,128)}, f32[2,64,2048]{2,1,0:T(8,128)}) custom-call(s32[2,4]{1,0:T(2,128)} %slice.52.first_ref, s32[2,1,1024]{2,1,0:T(1,128)} %broadcast_in_dim.65.start_ref, bf16[256,2048]{1,0:T(8,128)(2,1)} %get-tuple-element.84.q_ref, bf16[256,2048]{1,0:T(8,128)(2,1)} %get-tuple-element.89.refs_0_.refs_1_.o_ref, ...), custom_call_target="tpu_custom_call" | custom-call | tf_op jit(solution)/shard_map/pallas_call | solution.py:997
  529.9 3.2 copy_bitcast_fusion
  533.1 1.1 maximum_bitcast_fusion
  534.2 1.3 slice.93.refs_0_
  535.4 29.3 %shard_map.374 = (bf16[2,64,2,1024]{3,2,1,0:T(2,128)(2,1)}, bf16[2,256,512]{2,1,0:T(8,128)(2,1)}, bf16[704,512]{1,0:T(8,128)(2,1)}) custom-call(bf16[2,64,2,1024]{3,2,1,0:T(2,128)(2,1)} %slice.93.refs_0_, bf16[4,256,512]{2,1,0:T(8,128)(2,1)} %get-tuple-element.118.refs_1_, bf16[704,512]{1,0:T(8,128)(2,1)} %fusion.1.refs_2_), custom_call_target="tpu_custom_call" | custom-call | tf_op jit(solution)/shard_map/pallas_call | solution.py:842
  564.8 1.9 slice_add_fusion
  566.9 0.9 slice.67
  567.9 1.6 add_convert_fusion.refs_9_.refs_3_
  571.0 0.9 add_convert_fusion.6.refs_10_.refs_0_
  572.3 1.2 fusion.8
  573.7 1.0 pad_maximum_fusion
  574.7 0.8 pad_maximum_fusion.1
  575.6 90.7 %shard_map.375 = (f32[256,2048]{1,0:T(8,128)}, bf16[512,256]{1,0:T(8,128)(2,1)}, f32[4,64,128]{2,1,0:T(8,128)}, f32[16,128]{1,0:T(8,128)}, bf16[2,704,512]{2,1,0:T(8,128)(2,1)}, /*index=5*/bf16[2,256,512]{2,1,0:T(8,128)(2,1)}) custom-call(bf16[256,2048]{1,0:T(8,128)(2,1)} %bitcast.81, bf16[128,2048]{1,0:T(8,128)(2,1)} %bitcast.88, ...), custom_call_target="tpu_custom_call" | custom-call | tf_op jit(solution)/shard_map/pallas_call | solution.py:842
  666.3 1.4 fusion.2
  667.7 1.7 collective-permute-start.2
  671.4 1.3 collective-permute-start.1
  672.8 1.3 add_subtract_fusion
  674.1 1.1 reshape.301
  675.6 6.5 shard_map.379
  682.1 3.2 shard_map.376
  685.3 0.8 multiply_subtract_fusion
  686.1 0.7 copy-done.20
  686.8 3.6 shard_map.377
  690.5 0.9 copy-done.16
  691.3 11.8 %shard_map.378 = (f32[2,704,512]{2,1,0:T(8,128)}, f32[2,704,512]{2,1,0:T(8,128)}, f32[2,704,512]{2,1,0:T(8,128)}) custom-call(s32[2]{0:T(128)} %pad_add_fusion.place_ref, f32[2]{0:T(128)} %pad_maximum_fusion.3.fix_ref, f32[2,704,512]{2,1,0:T(8,128)} %bitcast.77, f32[2,704,512]{2,1,0:T(8,128)} %bitcast.83, f32[2,704,512]{2,1,0:T(8,128)} %bitcast.84, ...), custom_call_target="tpu_custom_call" | custom-call | tf_op jit(solution)/shard_map/pallas_call | solution.py:124
  703.1 1.0 copy.69
  704.1 1.0 copy-done.11
  705.1 1.3 copy.70
  (88 shorter events, 8.3 us)
Async XLA Ops:
  0.7 10.2 %collective-permute-start = (s32[1,2048]{1,0:T(1,128)}, s32[1,2048]{1,0:T(1,128)S(1)}, u32[]{:S(2)}, u32[]{:S(2)}) collective-permute-start(s32[1,2048]{1,0:T(1,128)} %param.24), channel_id=1, source_target_pairs={{0,8},{8,0},{1,9},{9,1},{2,10},{10,2},{3,11},{11,3},{4,12},{12,4},... | collective-permute-start | bytes 24584 | tf_op jit(solution)/shard_map/ppermute | solution.py:1551
  2.2 6.2 copy-start.3
  8.7 1.2 copy-start.24
  8.7 2.1 copy-start.23
  373.8 66.7 %copy-start = (bf16[2,704,512]{2,1,0:T(8,128)(2,1)S(1)}, bf16[2,704,512]{2,1,0:T(8,128)(2,1)}, u32[]{:S(2)}) copy-start(bf16[2,704,512]{2,1,0:T(8,128)(2,1)} %add_convert_fusion.2.refs_8_.refs_0_) | copy-start | bytes 4325380
  440.6 2.3 copy-start.13
  445.7 58.8 %copy-start.1 = (bf16[2,704,512]{2,1,0:T(8,128)(2,1)S(1)}, bf16[2,704,512]{2,1,0:T(8,128)(2,1)}, u32[]{:S(2)}) copy-start(bf16[2,704,512]{2,1,0:T(8,128)(2,1)} %add_convert_fusion.1.refs_4_.refs_0_) | copy-start | bytes 4325380
  535.4 31.5 %copy-start.19 = (bf16[32,80,128]{2,1,0:T(8,128)(2,1)S(1)}, bf16[32,80,128]{2,1,0:T(8,128)(2,1)}, u32[]{:S(2)}) copy-start(bf16[32,80,128]{2,1,0:T(8,128)(2,1)} %get-tuple-element.122) | copy-start | bytes 1966084
  564.8 3.1 copy-start.4
  564.8 3.1 copy-start.12
  566.7 2.7 copy-start.6
  567.9 1.6 copy-start.7
  567.9 1.6 copy-start.8
  567.9 2.3 copy-start.10
  569.4 1.4 copy-start.9
  569.4 1.5 copy-start.17
  570.1 1.7 slice-start
  575.6 90.7 %copy-start.2 = (bf16[2,704,512]{2,1,0:T(8,128)(2,1)S(1)}, bf16[2,704,512]{2,1,0:T(8,128)(2,1)}, u32[]{:S(2)}) copy-start(bf16[2,704,512]{2,1,0:T(8,128)(2,1)} %add_convert_fusion.refs_9_.refs_3_) | copy-start | bytes 4325380
  666.3 5.1 copy-start.5
  666.3 5.1 copy-start.14
  666.3 6.5 copy-start.25
  666.3 6.5 copy-start.26
  667.7 22.8 %collective-permute-start.2 = (bf16[704,512]{1,0:T(8,128)(2,1)S(1)}, bf16[704,512]{1,0:T(8,128)(2,1)S(1)}, u32[]{:S(2)}, u32[]{:S(2)}) collective-permute-start(bf16[704,512]{1,0:T(8,128)(2,1)S(1)} %fusion.2), channel_id=1, source_target_pairs={{0,8},{12,4},{1,9},{13,5},{2,10},{14,6},{3,11},{15,7},{16,24},{28,... | collective-permute-start | bytes 2162696 | tf_op jit(solution)/shard_map/ppermute | solution.py:1841
  671.4 14.7 %collective-permute-start.1 = (bf16[256,512]{1,0:T(8,128)(2,1)S(1)}, bf16[256,512]{1,0:T(8,128)(2,1)S(1)}, u32[]{:S(2)}, u32[]{:S(2)}) collective-permute-start(bf16[256,512]{1,0:T(8,128)(2,1)S(1)} %fusion.11), channel_id=1, source_target_pairs={{0,8},{12,4},{1,9},{13,5},{2,10},{14,6},{3,11},{15,7},{16,24},{28,... | collective-permute-start | bytes 786440 | tf_op jit(solution)/shard_map/ppermute | solution.py:1841
  675.6 9.7 %copy-start.18 = (f32[64,512]{1,0:T(8,128)S(1)}, f32[64,512]{1,0:T(8,128)}, u32[]{:S(2)}) copy-start(f32[64,512]{1,0:T(8,128)} %param.27) | copy-start | bytes 393220
  675.6 9.7 %copy-start.21 = (f32[64,512]{1,0:T(8,128)S(1)}, f32[64,512]{1,0:T(8,128)}, u32[]{:S(2)}) copy-start(f32[64,512]{1,0:T(8,128)} %param.39) | copy-start | bytes 393220
  675.6 9.7 %copy-start.22 = (f32[64,512]{1,0:T(8,128)S(1)}, f32[64,512]{1,0:T(8,128)}, u32[]{:S(2)}) copy-start(f32[64,512]{1,0:T(8,128)} %param.33) | copy-start | bytes 393220
  686.1 0.7 copy-start.20
  690.5 0.9 copy-start.16
  691.3 11.8 %copy-start.15 = (bf16[256,2048]{1,0:T(8,128)(2,1)S(1)}, bf16[256,2048]{1,0:T(8,128)(2,1)}, u32[]{:S(2)}) copy-start(bf16[256,2048]{1,0:T(8,128)(2,1)} %get-tuple-element.191) | copy-start | bytes 3145732
  703.1 2.0 copy-start.11

commit v7 on v6

--- a/solution.py
+++ b/solution.py
@@ -394,7 +394,7 @@
     def __init__(
         self,
         block,
-        along_x=False,
+        by_x=4,
         onward_first=False,
         keep=True,
         given={},
@@ -408,9 +408,10 @@
         gathered = (8,) + block.shape
         self.inputs, self.outputs, self.scratch = [block], [], []
         self.in_vmem = work is not None
-        self.along_x, self.onward_first = along_x, onward_first
+        self.x_rows = block.shape[0] * by_x // 8
+        self.onward_first = onward_first
         self.before, self.work, self.after = before, work, after
-        self.sems = [7, 8, 1]
+        self.sems = [8, 9, 1]
         if self.in_vmem:
             self.scratch = [pltpu.VMEM(gathered, block.dtype)]
         else:
@@ -439,12 +440,12 @@
         own = group_index(core, z_low, x_at)
         beside = group_index(core, z_low, 1 - x_at)
         below = group_index(core, 1 - z_low, x_at)
-        by_x = True if self.along_x else core == 0
-        turn = jnp.where(by_x, below, beside)
-        onward = {
-            "x": jnp.where(by_x, 1 - x_at, x_at),
-            "zl": jnp.where(by_x, z_low, 1 - z_low),
-        }
+        across = group_index(core, 1 - z_low, 1 - x_at)
+        x_part, z_part = pl.ds(0, self.x_rows), pl.ds(self.x_rows, src.shape[0] - self.x_rows)
+
+        def turn(block, rows, way, arrive, axis):
+            part = dst.at[block, rows]
+            return far_copy(part, part, send.at[way], recv.at[arrive], flipped(axis))
 
         def pass_on(block, way, device):
             part = dst.at[block]
@@ -456,7 +457,8 @@
         def onwards():
             pass_on(beside, 0, flipped("c")).wait_recv()
             pass_on(below, 0, flipped("c")).wait_recv()
-            pass_on(turn, 3, onward).start()
+            turn(below, x_part, 3, below, "x").start()
+            turn(beside, z_part, 7, 8, "zl").start()
             pass_on(beside, 4, flipped("c")).start()
             pass_on(below, 5, flipped("c")).start()
             late()
@@ -483,7 +485,7 @@
             def _():
                 pltpu.make_async_copy(src, dst.at[own], local.at[0]).wait()
 
-            @pl.when((step != 0) & (step != 2) & (step != 3))
+            @pl.when((step != 0) & (step != 2) & (step != 3) & (step != 6))
             def _():
                 pass_on(block, 0, flipped("c")).wait_recv()
 
@@ -492,19 +494,24 @@
 
             @pl.when(step == 6)
             def _():
-                pass_on(block, 6, flipped("c")).start()
+                turn(across, x_part, 3, across, "x").wait_recv()
+                turn(across, z_part, 7, 8, "zl").wait_recv()
+                pass_on(across, 6, flipped("c")).start()
                 middle()
 
             if self.keep:
                 kept(block).start()
             if self.work:
+                refs.step = step
                 self.work(refs, dst.at[block], block)
                 self.flush_block(refs, block)
 
         if self.after:
             self.after(refs)
-        for way in range(7):
+        for way in (0, 1, 2, 4, 5, 6):
             pass_on(own, way, flipped("c")).wait_send()
+        turn(below, x_part, 3, below, "x").wait_send()
+        turn(beside, z_part, 7, 8, "zl").wait_send()
         if self.keep:
 
             @pl.loop(0, 8)
@@ -520,7 +527,7 @@
         rows,
         cols,
         produce,
-        along_x=False,
+        by_x=4,
         first=(),
         given={},
         streams={},
@@ -537,12 +544,12 @@
         end=None,
     ):
         self.inputs = []
-        self.rows, self.first, self.along_x = rows, first, along_x
+        self.rows, self.first, self.x_rows = rows, first, rows * by_x // 8
         block, kind = (rows, cols), jnp.bfloat16
         self.outputs = [jax.ShapeDtypeStruct(block, jnp.float32)] if keep else []
         self.keep, self.summed = keep, summed
         self.everyone, self.devices = everyone > 0, everyone
-        self.sems = [7, 7, 2, 1, extra_sems]
+        self.sems = [10, 10, 2, 1, extra_sems]
         self.scratch = [pltpu.VMEM((8,) + block, kind)]
         self.scratch += [pltpu.VMEM((4,) + block, kind)] * 2 + [pltpu.VMEM(block, kind)] * 3
         self.scratch += [pltpu.VMEM(block, jnp.float32)]
@@ -555,7 +562,7 @@
         self.fetch_all(self.bind(ins, outs, sems, scratch))
 
     def finish(self, ins, outs, sems, scratch, early, late, middle):
-        partial, came, sums, turned, direct_in, late_in, out = scratch[:7]
+        partial, came, sums, turned, beside_in, below_in, out = scratch[:7]
         send, recv, local = sems[:3]
         refs = self.bind(ins, outs, sems, scratch)
         refs.more = sems[4]
@@ -567,17 +574,8 @@
             2 * (1 - z_low) + x_at,
             2 * (1 - z_low) + 1 - x_at,
         )
-        by_x = True if self.along_x else core == 0
-        direct = jnp.where(by_x, beside, below)
-        after = jnp.where(by_x, below, beside)
-        direct_way = {
-            "x": jnp.where(by_x, 1 - x_at, x_at),
-            "zl": jnp.where(by_x, z_low, 1 - z_low),
-        }
-        after_way = {
-            "x": jnp.where(by_x, x_at, 1 - x_at),
-            "zl": jnp.where(by_x, 1 - z_low, z_low),
-        }
+        size = self.x_rows
+        x_part, z_part = pl.ds(0, size), pl.ds(size, rows - size)
 
         def to_core(turn_at, block):
             return far_copy(
@@ -588,22 +586,31 @@
                 flipped("c"),
             )
 
-        def add(block, target, *others):
-            @pl.loop(0, rows // ROW_STRIP)
+        def add(block, target, begin, count, *others):
+            @pl.loop(0, count // ROW_STRIP)
             def _(strip):
-                at = pl.ds(pl.multiple_of(strip * ROW_STRIP, ROW_STRIP), ROW_STRIP)
+                at = pl.ds(pl.multiple_of(begin + strip * ROW_STRIP, ROW_STRIP), ROW_STRIP)
                 total = partial[4 * core + block, at].astype(jnp.float32)
                 total += came[block, at].astype(jnp.float32)
                 for other in others:
                     total += other[at].astype(jnp.float32)
                 target[at] = total.astype(target.dtype)
 
-        def send_sum(block, way, target, device):
-            return far_copy(sums.at[block], target, send.at[way], recv.at[way], device)
-
-        turn = send_sum(across, 4, turned, direct_way)
-        straight = send_sum(direct, 5, direct_in, direct_way)
-        last = send_sum(after, 6, late_in, after_way)
+        def send_sum(block, part, way, target, axis):
+            return far_copy(
+                sums.at[block, part],
+                target.at[part],
+                send.at[way],
+                recv.at[way],
+                flipped(axis),
+            )
+
+        turn_x = send_sum(across, x_part, 4, turned, "x")
+        turn_z = send_sum(across, z_part, 5, turned, "zl")
+        free_x = send_sum(beside, x_part, 6, beside_in, "x")
+        free_z = send_sum(below, z_part, 7, below_in, "zl")
+        last_x = send_sum(beside, z_part, 8, beside_in, "x")
+        last_z = send_sum(below, x_part, 9, below_in, "zl")
 
         def stream(name, body):
             source, held = getattr(refs, name), scratch[7]
@@ -630,13 +637,8 @@
         @pl.loop(0, 8)
         def _(step):
             pair, mine = step // 2, lax.rem(step, 2)
-            if self.along_x:
-                first, second = direct, after
-            else:
-                first = jnp.where(mine == 1, direct, after)
-                second = jnp.where(mine == 1, after, direct)
             block = jnp.where(
-                pair == 0, across, jnp.where(pair == 1, first, jnp.where(pair == 2, second, own))
+                pair == 0, across, jnp.where(pair == 1, beside, jnp.where(pair == 2, below, own))
             )
             index = 4 * jnp.where(mine == 1, core, 1 - core) + block
             self.produce(refs, index, partial.at[index])
@@ -648,40 +650,46 @@
             @pl.when(step == 1)
             def _():
                 to_core(0, across).wait_recv()
-                add(across, sums.at[across])
-                turn.start()
+                add(across, sums.at[across], 0, rows)
+                turn_x.start()
+                turn_z.start()
 
             @pl.when(step == 3)
             def _():
-                to_core(1, direct).wait_recv()
-                add(direct, sums.at[direct])
-                if not self.along_x:
-                    straight.start()
+                to_core(1, beside).wait_recv()
+                add(beside, sums.at[beside], 0, size)
+                free_x.start()
+
+            @pl.when(step == 5)
+            def _():
+                to_core(2, below).wait_recv()
+                add(below, sums.at[below], size, rows - size)
+                free_z.start()
 
         self.ready(refs, [key for key in self.given if key not in self.first])
         if self.fill_one:
             self.fill_one(refs)
-        to_core(2, after).wait_recv()
-        turn.wait_recv()
-        if self.along_x:
-            straight.start()
-        add(after, sums.at[after], turned)
-        last.start()
+        turn_x.wait_recv()
+        add(below, sums.at[below], 0, size, turned)
+        last_z.start()
+        turn_z.wait_recv()
+        add(beside, sums.at[beside], size, rows - size, turned)
+        last_x.start()
         late()
         middle()
         if self.fill_two:
             self.fill_two(refs)
         to_core(3, own).wait_recv()
-        straight.wait_recv()
-        last.wait_recv()
-        add(own, out, direct_in, late_in)
+        for copy in (free_x, free_z, last_x, last_z):
+            copy.wait_recv()
+        add(own, out, 0, rows, beside_in, below_in)
         if self.summed:
             self.summed(refs, out)
         if self.keep:
             pltpu.make_async_copy(out, outs[0], sems[3].at[0]).start()
-        for n, block in enumerate((across, direct, after, own)):
+        for n, block in enumerate((across, beside, below, own)):
             to_core(n, block).wait_send()
-        for copy in (turn, straight, last):
+        for copy in (turn_x, turn_z, free_x, free_z, last_x, last_z):
             copy.wait_send()
         if self.end:
             self.end(refs)
@@ -866,167 +874,69 @@
     return (keys >= start_row) & (keys <= rows)
 
 
-def attn_fwd_kernel(heads, first_ref, start_ref, q_ref, kt_ref, vt_ref, o_ref, lse_ref, k_s):
-    pack, block = pl.program_id(0), pl.program_id(1)
-
-    @pl.when(block == 0)
-    def _():
-        k_s[...] = kt_ref[0].astype(jnp.float32).T.astype(jnp.bfloat16)
-
-    needed = block + 5 - first_ref[pack, block] // QUERY_BLOCK
+def windows(block, body):
+    later_half = lax.axis_index("zh") == 1
     for count in range(1, 6):
+        needed = jnp.where(later_half, 5, block + 1)
 
         @pl.when(needed == count)
         def _():
-            key_at = pl.multiple_of((block + 5 - count) * QUERY_BLOCK, QUERY_BLOCK)
-            window = pl.ds(key_at, count * QUERY_BLOCK)
-            allowed = attn_mask(start_ref[0], block, count)
-            keys = k_s[window, :]
-            values_t = vt_ref[0, :, window]
-            for head in range(heads):
-                scores = dot_nn(keys, q_ref[head * HD : (head + 1) * HD, :])
-                scores = jnp.where(allowed, scores, NEG_FILL)
-                top = jnp.max(scores, axis=0, keepdims=True)
-                weights = jnp.exp(scores - top)
-                total = jnp.sum(weights, axis=0, keepdims=True)
-                mixed = dot_nn(values_t, weights.astype(jnp.bfloat16))
-                o_ref[head * HD : (head + 1) * HD, :] = (mixed / total).astype(jnp.bfloat16)
-                lse_ref[0, head : head + 1, :] = top + jnp.log(total)
-
-
-def attn_bwd_kernel(
-    heads,
-    first_ref,
-    start_ref,
-    q_ref,
-    o_ref,
-    do_ref,
-    lse_ref,
-    kt_ref,
-    vt_ref,
-    dq_ref,
-    dk_ref,
-    dv_ref,
-    k_s,
-    v_s,
-    dk_s,
-    dv_s,
-):
-    pack, block = pl.program_id(0), pl.program_id(1)
-
-    @pl.when(block == 0)
+            body(count, pl.multiple_of((block + 5 - count) * QUERY_BLOCK, QUERY_BLOCK))
+
+
+def attn_before(move_task, refs):
+    half = refs.pair.shape[1] // 2
+    later_half = lax.axis_index("zh") == 1
+
+    def place(pair, at):
+        for pack in range(2):
+            cols = slice(pack * half, (pack + 1) * half)
+            refs.kt[pack, :, at] = pair[:HD, cols]
+            refs.vt[pack, :, at] = pair[HD:, cols]
+            refs.k_s[pack, at] = flip(pair[:HD, cols]).astype(jnp.bfloat16)
+
+    place(refs.pair, slice(KEYS_BACK, KEYS_BACK + half))
+
+    @pl.when(later_half)
     def _():
-        k_s[...] = kt_ref[0].astype(jnp.float32).T.astype(jnp.bfloat16)
-        v_s[...] = vt_ref[0].astype(jnp.float32).T.astype(jnp.bfloat16)
-        dk_s[...] = jnp.zeros_like(dk_s)
-        dv_s[...] = jnp.zeros_like(dv_s)
-
-    needed = block + 5 - first_ref[pack, block] // QUERY_BLOCK
-    for count in range(1, 6):
-
-        @pl.when(needed == count)
-        def _():
-            key_at = pl.multiple_of((block + 5 - count) * QUERY_BLOCK, QUERY_BLOCK)
-            window = pl.ds(key_at, count * QUERY_BLOCK)
-            allowed = attn_mask(start_ref[0], block, count)
-            keys = k_s[window, :]
-            values = v_s[window, :]
-            keys_t = kt_ref[0, :, window]
-            for head in range(heads):
-                here = slice(head * HD, (head + 1) * HD)
-                query_t = q_ref[here, :]
-                grad_t = do_ref[here, :]
-                grad_f = grad_t.astype(jnp.float32)
-                delta = jnp.sum(grad_f * o_ref[here, :].astype(jnp.float32), axis=0, keepdims=True)
-                scores = jnp.where(allowed, dot_nn(keys, query_t), NEG_FILL)
-                weights = jnp.exp(scores - lse_ref[0, head : head + 1, :])
-                weights_grad = dot_nn(values, grad_t)
-                scores_grad = (weights * (weights_grad - delta)).astype(jnp.bfloat16)
-                dq_ref[here, :] = dot_nn(keys_t, scores_grad) * SCALE
-                query = query_t.astype(jnp.float32).T.astype(jnp.bfloat16)
-                grad = grad_f.T.astype(jnp.bfloat16)
-                dk_s[window, :] += dot_nn(scores_grad, query)
-                dv_s[window, :] += dot_nn(weights.astype(jnp.bfloat16), grad)
-
-    @pl.when(block == pl.num_programs(1) - 1)
+        pltpu.sync_copy(move_task.live[1][0], refs.before)
+        place(refs.before, slice(0, KEYS_BACK))
+
+    @pl.when(jnp.logical_not(later_half))
     def _():
-        dk_ref[0] = dk_s[...].T
-        dv_ref[0] = dv_s[...].T
-
-
-def attn_fwd(first, start, query_t, keys_t, values_t):
-    packs, _, window = keys_t.shape
-    rows = query_t.shape[1] // packs
-    blocks = rows // QUERY_BLOCK
-    heads = query_t.shape[0] // HD
-    width = query_t.shape[0]
-    col = lambda p, b, s: (0, p * blocks + b)
-    return pl.pallas_call(
-        functools.partial(attn_fwd_kernel, heads),
-        grid_spec=pltpu.PrefetchScalarGridSpec(
-            num_scalar_prefetch=1,
-            grid=(packs, blocks),
-            in_specs=[
-                pl.BlockSpec((1, 1, QUERY_BLOCK), lambda p, b, s: (p, 0, b)),
-                pl.BlockSpec((width, QUERY_BLOCK), col),
-                pl.BlockSpec((1, HD, window), lambda p, b, s: (p, 0, 0)),
-                pl.BlockSpec((1, HD, window), lambda p, b, s: (p, 0, 0)),
-            ],
-            out_specs=[
-                pl.BlockSpec((width, QUERY_BLOCK), col),
-                pl.BlockSpec((1, heads, QUERY_BLOCK), lambda p, b, s: (p, 0, b)),
-            ],
-            scratch_shapes=[pltpu.VMEM((window, HD), jnp.bfloat16)],
-        ),
-        out_shape=[
-            jax.ShapeDtypeStruct(query_t.shape, jnp.bfloat16),
-            jax.ShapeDtypeStruct((packs, heads, rows), jnp.float32),
-        ],
-        compiler_params=pltpu.CompilerParams(vmem_limit_bytes=60 * 2**20),
-    )(first, start, query_t, keys_t, values_t)
-
-
-def attn_bwd(first, start, query_t, out_t, grad_t, lse, keys_t, values_t):
-    packs, _, window = keys_t.shape
-    rows = query_t.shape[1] // packs
-    blocks = rows // QUERY_BLOCK
-    heads = query_t.shape[0] // HD
-    width = query_t.shape[0]
-    col = lambda p, b, s: (0, p * blocks + b)
-    whole = lambda p, b, s: (p, 0, 0)
-    return pl.pallas_call(
-        functools.partial(attn_bwd_kernel, heads),
-        grid_spec=pltpu.PrefetchScalarGridSpec(
-            num_scalar_prefetch=1,
-            grid=(packs, blocks),
-            in_specs=[
-                pl.BlockSpec((1, 1, QUERY_BLOCK), lambda p, b, s: (p, 0, b)),
-                pl.BlockSpec((width, QUERY_BLOCK), col),
-                pl.BlockSpec((width, QUERY_BLOCK), col),
-                pl.BlockSpec((width, QUERY_BLOCK), col),
-                pl.BlockSpec((1, heads, QUERY_BLOCK), lambda p, b, s: (p, 0, b)),
-                pl.BlockSpec((1, HD, window), whole),
-                pl.BlockSpec((1, HD, window), whole),
-            ],
-            out_specs=[
-                pl.BlockSpec((width, QUERY_BLOCK), col),
-                pl.BlockSpec((1, HD, window), whole),
-                pl.BlockSpec((1, HD, window), whole),
-            ],
-            scratch_shapes=[
-                pltpu.VMEM((window, HD), jnp.bfloat16),
-                pltpu.VMEM((window, HD), jnp.bfloat16),
-                pltpu.VMEM((window, HD), jnp.float32),
-                pltpu.VMEM((window, HD), jnp.float32),
-            ],
-        ),
-        out_shape=[
-            jax.ShapeDtypeStruct(query_t.shape, jnp.float32),
-            jax.ShapeDtypeStruct((packs, HD, window), jnp.float32),
-            jax.ShapeDtypeStruct((packs, HD, window), jnp.float32),
-        ],
-        compiler_params=pltpu.CompilerParams(vmem_limit_bytes=60 * 2**20),
-    )(first, start, query_t, out_t, grad_t, lse, keys_t, values_t)
+        refs.kt[:, :, :KEYS_BACK] = jnp.zeros((2, HD, KEYS_BACK), jnp.bfloat16)
+        refs.vt[:, :, :KEYS_BACK] = jnp.zeros((2, HD, KEYS_BACK), jnp.bfloat16)
+
+    refs.flush("kt").start()
+    refs.flush("vt").start()
+
+
+def attn_step(heads, refs, rows, block_of):
+    blocks = refs.q.shape[1] // (2 * QUERY_BLOCK)
+    pack, block = refs.step // blocks, lax.rem(refs.step, blocks)
+    at, inner = lanes_of(refs.step, QUERY_BLOCK), lanes_of(block, QUERY_BLOCK)
+
+    def attend(count, key_at):
+        window = pl.ds(key_at, count * QUERY_BLOCK)
+        allowed = attn_mask(refs.start[:, at], block, count)
+        keys = refs.k_s[pack, window, :]
+        values_t = refs.vt[pack, :, window]
+        for head in range(heads):
+            here = slice(head * HD, (head + 1) * HD)
+            scores = jnp.where(allowed, dot_nn(keys, refs.q[here, at]), NEG_FILL)
+            top = jnp.max(scores, axis=0, keepdims=True)
+            weights = jnp.exp(scores - top)
+            total = jnp.sum(weights, axis=0, keepdims=True)
+            mixed = dot_nn(values_t, weights.astype(jnp.bfloat16))
+            refs.o[here, at] = (mixed / total).astype(jnp.bfloat16)
+            refs.lse[pack, head : head + 1, inner] = top + jnp.log(total)
+
+    windows(block, attend)
+
+
+def attn_after(refs):
+    refs.flush("o").start()
+    refs.flush("lse").start()
 
 
 def cols_at(ref, block, h_size):
@@ -1454,11 +1364,133 @@
             self.send(refs, 1, step).wait_send()
 
 
-def rotate_back(grads, cos_table, sin_table):
-    front, back = grads[:, :HALF], grads[:, HALF:]
-    return jnp.concatenate(
-        [front * cos_table + back * sin_table, back * cos_table - front * sin_table], axis=1
-    )
+def turned_back(grads, cos_table, sin_table):
+    front, back = grads[:HALF], grads[HALF:]
+    return (front * cos_table + back * sin_table, back * cos_table - front * sin_table)
+
+
+class AttentionBack(Fused):
+    def __init__(self, heads, given, results):
+        self.inputs, self.outputs = [], []
+        self.heads = heads
+        packed = given["kt"].shape
+        rows = (packed[0], packed[2], HD)
+        part = (2, 2, 2 * HD, KEYS_BACK // 2)
+        self.sems = [2, 2]
+        self.scratch = []
+        scratch = dict(
+            k_s=pltpu.VMEM(rows, jnp.bfloat16),
+            v_s=pltpu.VMEM(rows, jnp.bfloat16),
+            dk_s=pltpu.VMEM(rows, jnp.float32),
+            dv_s=pltpu.VMEM(rows, jnp.float32),
+            early=pltpu.VMEM(part, jnp.bfloat16),
+            came=pltpu.VMEM(part, jnp.bfloat16),
+        )
+        self.name(given, {}, results, scratch, {}, ())
+
+    def begin(self, ins, outs, sems, scratch):
+        self.fetch_all(self.bind(ins, outs, sems, scratch))
+
+    def step(self, refs, pack, block):
+        blocks = refs.q.shape[1] // (2 * QUERY_BLOCK)
+        at, inner = lanes_of(pack * blocks + block, QUERY_BLOCK), lanes_of(block, QUERY_BLOCK)
+        cos_table, sin_table = refs.cos[:, at], refs.sin[:, at]
+
+        def back(count, key_at):
+            window = pl.ds(key_at, count * QUERY_BLOCK)
+            allowed = attn_mask(refs.start[:, at], block, count)
+            keys = refs.k_s[pack, window, :]
+            values = refs.v_s[pack, window, :]
+            keys_t = refs.kt[pack, :, window]
+            for head in range(self.heads):
+                here = head * HD
+                span = slice(here, here + HD)
+                query_t, grad_t = refs.q[span, at], refs.do[span, at]
+                grad_f = grad_t.astype(jnp.float32)
+                delta = jnp.sum(
+                    grad_f * refs.o[span, at].astype(jnp.float32), axis=0, keepdims=True
+                )
+                scores = jnp.where(allowed, dot_nn(keys, query_t), NEG_FILL)
+                weights = jnp.exp(scores - refs.lse[pack, head : head + 1, inner])
+                weights_grad = dot_nn(values, grad_t)
+                scores_grad = (weights * (weights_grad - delta)).astype(jnp.bfloat16)
+                query_grad = dot_nn(keys_t, scores_grad) * SCALE
+                front, rear = turned_back(query_grad, cos_table, sin_table)
+                refs.dq[here : here + HALF, at] = front.astype(jnp.bfloat16)
+                refs.dq[here + HALF : here + HD, at] = rear.astype(jnp.bfloat16)
+                refs.dk_s[pack, window, :] += dot_nn(
+                    scores_grad, flip(query_t).astype(jnp.bfloat16)
+                )
+                refs.dv_s[pack, window, :] += dot_nn(
+                    weights.astype(jnp.bfloat16), grad_f.T.astype(jnp.bfloat16)
+                )
+
+        windows(block, back)
+
+    def finish(self, ins, outs, sems, scratch, early, late, middle):
+        refs = self.bind(ins, outs, sems, scratch)
+        send, recv = sems[:2]
+        z_high = lax.axis_index("zh")
+        half = KEYS_BACK // 2
+        early()
+        self.ready(refs, self.given)
+        for pack in range(2):
+            refs.k_s[pack] = flip(refs.kt[pack]).astype(jnp.bfloat16)
+            refs.v_s[pack] = flip(refs.vt[pack]).astype(jnp.bfloat16)
+        refs.dk_s[...] = jnp.zeros_like(refs.dk_s)
+        refs.dv_s[...] = jnp.zeros_like(refs.dv_s)
+        late()
+
+        def share(n):
+            return far_copy(
+                refs.early.at[n], refs.came.at[n], send.at[n], recv.at[n], flipped("zh")
+            )
+
+        def give(n):
+            rows = slice(n * half, (n + 1) * half)
+            for pack in range(2):
+                refs.early[n, pack, :HD] = refs.dk_s[pack, rows].T.astype(jnp.bfloat16)
+                refs.early[n, pack, HD:] = refs.dv_s[pack, rows].T.astype(jnp.bfloat16)
+            share(n).start()
+
+        @pl.loop(0, 8)
+        def _(step):
+            self.step(refs, lax.rem(step, 2), step // 2)
+            for n, done in enumerate((3, 7)):
+
+                @pl.when((step == done) & (z_high == 1))
+                def _():
+                    give(n)
+
+        refs.flush("dq").start()
+        middle()
+        for pack in range(2):
+            for n in range(2):
+                rows = slice(KEYS_BACK + n * half, KEYS_BACK + (n + 1) * half)
+                first = pack * KEYS_BACK + n * half
+                at = slice(first, first + half)
+                if pack == 0:
+
+                    @pl.when(z_high == 0)
+                    def _():
+                        share(n).wait_recv()
+
+                key_grad, value_grad = refs.dk_s[pack, rows].T, refs.dv_s[pack, rows].T
+                take = lambda part: jnp.where(z_high == 0, part.astype(jnp.float32), 0.0)
+                key_grad += take(refs.came[n, pack, :HD])
+                value_grad += take(refs.came[n, pack, HD:])
+                front, rear = turned_back(key_grad, refs.cos[:, at], refs.sin[:, at])
+                refs.dpair[:HALF, at] = front.astype(jnp.bfloat16)
+                refs.dpair[HALF:HD, at] = rear.astype(jnp.bfloat16)
+                refs.dpair[HD:, at] = value_grad.astype(jnp.bfloat16)
+        refs.flush("dpair").start()
+
+        @pl.when(z_high == 1)
+        def _():
+            share(0).wait_send()
+            share(1).wait_send()
+
+        self.flushed(refs)
 
 
 def adam_step(weight, grad, first_old, second_old, rate, decay, step_value):
@@ -1565,7 +1597,6 @@
     frequency = jnp.power(ROPE_BASE, -2.0 * jnp.arange(HALF, dtype=jnp.float32) / HD)
     angles = frequency[:, None] * position.reshape(1, 2 * half_rows).astype(jnp.float32)
     cos_table, sin_table = jnp.cos(angles), jnp.sin(angles)
-    block_first = start[:, ::QUERY_BLOCK]
     start = start[:, None, :]
 
     block_rows = hidden_in.shape[0]
@@ -1618,25 +1649,37 @@
         .reshape(4, D // 4, 2 * HD)
     )
     query_full = row_blocks(query_parts)
-    grad_rows, pair_back_half, output_parts, gate_parts, up_parts = run(
-        2,
-        GatherRows(out_grad),
-        Move(pair_rot, "zh", lambda: lax.axis_index("zh") == 0),
-        Pass(output_parts),
-        Pass(gate_parts),
-        Spread(own_shard(gateup_t[1], h_size)),
-    )
+    pair_task = Move(pair_rot, "zh", lambda: lax.axis_index("zh") == 0)
+    packed = shape(2, HD, KEYS_BACK + half_rows)
+    _, grad_rows, attended_t, log_totals, keys_t, values_t, output_parts, gate_parts, up_parts = flat(
+        run(
+            2,
+            pair_task,
+            GatherRows(
+                out_grad,
+                onward_first=True,
+                given=dict(q=query_rot, pair=pair_rot, start=start.reshape(1, group_rows)),
+                results=dict(
+                    o=shape(width, group_rows),
+                    lse=shape(2, heads_here, half_rows, kind=jnp.float32),
+                    kt=packed,
+                    vt=packed,
+                ),
+                scratch=dict(
+                    before=pltpu.VMEM((2 * HD, group_rows), jnp.bfloat16),
+                    k_s=pltpu.VMEM((2, KEYS_BACK + half_rows, HD), jnp.bfloat16),
+                ),
+                before=functools.partial(attn_before, pair_task),
+                work=functools.partial(attn_step, heads_here),
+                after=attn_after,
+            ),
+            Pass(output_parts),
+            Pass(gate_parts),
+            Spread(own_shard(gateup_t[1], h_size)),
+        )
+    )
+    grad_rows = grad_rows.reshape(8, block_rows, D)
     output_full, gate_full = col_blocks(output_parts), col_blocks(gate_parts)
-    pair_back_half = jnp.where(z_high == 1, pair_back_half, 0)
-    pair_window = jnp.concatenate(
-        [
-            pair_back_half.reshape(2, HD, 2, half_rows),
-            pair_rot.reshape(2, HD, 2, half_rows),
-        ],
-        axis=3,
-    ).transpose(0, 2, 1, 3)
-    keys_t, values_t = pair_window[0], pair_window[1]
-    attended_t, log_totals = attn_fwd(block_first, start, query_rot, keys_t, values_t)
     residual_mid, normed_two, up_parts, down_parts = flat(
         run(
             3,
@@ -1644,6 +1687,7 @@
                 block_rows,
                 D,
                 functools.partial(output_produce, h_size),
+                by_x=6,
                 first=("o", "wo"),
                 given=dict(o=attended_t, wo=output_full, x=hidden_in, gains=gains_all),
                 results=dict(normed=shape(block_rows, D)),
@@ -1710,6 +1754,7 @@
                 block_rows,
                 D,
                 functools.partial(gateup_produce, h_size),
+                by_x=6,
                 first=("dgate", "dup", "wg", "wu"),
                 given=dict(
                     dgate=gate_grad,
@@ -1758,32 +1803,29 @@
         )
     )
     up_part = add_swapped(up_wgrad, up_came)
-    query_grads, key_grads, value_grads = attn_bwd(
-        block_first, start, query_rot, attended_t, attended_grad, log_totals, keys_t, values_t
-    )
-    query_back = (
-        rotate_back(query_grads.reshape(heads_here, HD, group_rows), cos_table, sin_table)
-        .astype(jnp.bfloat16)
-        .reshape(width, group_rows)
-    )
-    pair_grads = jnp.stack([key_grads, value_grads]).transpose(0, 2, 1, 3)
-    pair_later, output_came, gate_got = run(
-        8,
-        Move(
-            pair_grads[..., :KEYS_BACK].astype(jnp.bfloat16),
-            "zh",
-            lambda: lax.axis_index("zh") == 1,
-        ),
-        Swap(output_grad),
-        Move(for_partner(gate_part, gate_deep), "c", at_home),
+    query_back, pair_back, output_came, gate_got = flat(
+        run(
+            8,
+            AttentionBack(
+                heads_here,
+                given=dict(
+                    q=query_rot,
+                    o=attended_t,
+                    do=attended_grad,
+                    kt=keys_t,
+                    vt=values_t,
+                    start=start.reshape(1, group_rows),
+                    lse=log_totals,
+                    cos=cos_table,
+                    sin=sin_table,
+                ),
+                results=dict(dq=shape(width, group_rows), dpair=shape(2 * HD, group_rows)),
+            ),
+            Swap(output_grad),
+            Move(for_partner(gate_part, gate_deep), "c", at_home),
+        )
     )
     output_part = add_swapped(output_grad, output_came)
-    pair_later = jnp.where(z_high == 0, pair_later, 0).astype(jnp.float32)
-    pair_sum = (pair_grads[..., KEYS_BACK:] + pair_later).reshape(2, HD, group_rows)
-    pair_back = jnp.concatenate(
-        [rotate_back(pair_sum[:1], cos_table, sin_table), pair_sum[1:]]
-    ).astype(jnp.bfloat16)
-    pair_back = pair_back.reshape(2 * HD, group_rows)
     quarter = D // 4
     last = Last(h_size, devices, pair_rows, gain_cols, head_of)
     half_q = pltpu.VMEM((2, quarter, width), jnp.bfloat16)
@@ -1795,6 +1837,7 @@
                 block_rows,
                 D,
                 functools.partial(query_produce, h_size),
+                by_x=6,
                 first=("dq", "dpair", "wq", "wp"),
                 given=dict(
                     dq=query_back,

time: 713 us -> 673 us (0.944)
  Pallas kernels: 647 us -> 625 us
  local copies, waits for them, and re-layouts: 19.9 us -> 9.74 us
    pallas_call x2 -> x0, Pallas kernels: 42.3 us -> none  [the longest x1 23.2 us: attn_bwd(): pl.pallas_call(functools.partial(attn_bwd_kernel, heads), grid_spec=pltpu...]
    pallas_call x9, Pallas kernels: 580 us -> 599 us  [run(): pl.pallas_call(kernel, in_specs=in_specs, out_specs=out_specs, out_shape=...]
where the time goes in v7:
time: 673 us; the launch traced here: 667 us
  Pallas kernels  625 us (93%)
  other arithmetic  27.7 us (4%)
  local copies, waits for them, and re-layouts  9.74 us (1%)
    pallas_call x9, Pallas kernels, run(): pl.pallas_call(kernel, in_specs=in_specs, out_specs=out_specs, out_shape=...  599 us
    pallas_call x4, Pallas kernels, adam_shard(): pl.pallas_call(functools.partial(adam_kernel, rate, DECAY, groups), grid_...  25.1 us
  transfers between devices with their start and end apart: 3, of which 0 were waited for; matrix products, arithmetic and copies ran while one was open for 2% of the time, Pallas kernels for 2%

profile of v7, /device:TPU:0, one launch (start us, length us, event | category | flops | bytes accessed | tf_op | source)
XLA Modules:
  0.0 667.3 jit_solution(1334805428704006)
XLA Ops:
  0.7 0.5 collective-permute-start
  1.2 0.9 convert.15
  2.1 0.1 reshape.169
  2.5 1.8 convert_bitcast_fusion.2.refs_1_
  4.2 1.9 convert_bitcast_fusion.1.refs_5_
  6.2 0.9 convert_bitcast_fusion.refs_5_
  7.1 0.2 bitcast_convert_fusion
  7.3 1.2 fusion.13
  8.5 0.3 dynamic_update_slice.5
  8.8 0.6 pad_maximum_fusion.refs_0_
  9.5 0.2 fusion.5
  9.7 0.6 copy.48
  10.4 1.8 multiply_sine_fusion
  12.2 98.2 %shard_map.365 = (bf16[32,80,128]{2,1,0:T(8,128)(2,1)}, bf16[4,1,512,256]{3,2,1,0:T(8,128)(2,1)}, f32[16,2048]{1,0:T(8,128)}, bf16[8,256,2048]{2,1,0:T(8,128)(2,...) custom-call(bf16[4,80,128]{2,1,0:T(8,128)(2,1)} %pad_maximum_fusion., ...), custom_call_target="tpu_custom_call" | custom-call | tf_op jit(solution)/shard_map/pallas_call | solution.py:850
  110.4 1.9 slice.13
  112.2 63.0 %shard_map.366 = (bf16[128,2048]{1,0:T(8,128)(2,1)}, bf16[8,256,2048]{2,1,0:T(8,128)(2,1)}, bf16[256,2048]{1,0:T(8,128)(2,1)}, f32[2,4,1024]{2,1,0:T(4,128)}, bf...) custom-call(bf16[128,2048]{1,0:T(8,128)(2,1)} %get-tuple-element.83., ...), custom_call_target="tpu_custom_call", output_to_operand_aliasing={{6}: (5, {}), {7}: (6, {})} | custom-call | tf_op jit(solution)/shard_map/pallas_call | solution.py:850
  175.2 73.2 %shard_map.367 = (f32[256,2048]{1,0:T(8,128)}, bf16[256,2048]{1,0:T(8,128)(2,1)}, bf16[4,1,704,512]{3,2,1,0:T(8,128)(2,1)}, bf16[4,1,704,512]{3,2,1,0:T(8,128)(2,1)}) custom-call(bf16[256,2048]{1,0:T(8,128)(2,1)} %get-tuple-element.87.refs_0_.refs_1_, bf16[4,256,512]{2,1,0:T(8,128)(2,1)} %bitcast.67, ...), custom_call_target="tpu_custom_call", output_to_operand_aliasing={{2}: (4, {})} | custom-call | tf_op jit(solution)/shard_map/pallas_call | solution.py:850
  248.5 44.6 %shard_map.368 = (bf16[8,256,2048]{2,1,0:T(8,128)(2,1)}, bf16[8,256,704]{2,1,0:T(8,128)(2,1)}, bf16[8,256,704]{2,1,0:T(8,128)(2,1)}, bf16[8,256,704]{2,1,0:T(8,128)(2,1)}) custom-call(bf16[256,2048]{1,0:T(8,128)(2,1)} %get-tuple-element.91.refs_0_, bf16[4,704,512]{2,1,0:T(8,128)(2,1)} %bitcast.62, bf16[4,704,512]{2,1,0:T(8,128)(2,1)} %bitcast.64), custom_call_target="tpu_custom_call" | custom-call | tf_op jit(solution)/shard_map/pallas_call | solution.py:850
  293.1 60.4 %shard_map.369 = (bf16[8,256,704]{2,1,0:T(8,128)(2,1)}, bf16[8,256,704]{2,1,0:T(8,128)(2,1)}, bf16[4,704,512]{2,1,0:T(8,128)(2,1)}, bf16[256,2048]{1,0:T(8,128)(2,1)}, bf16[2,704,512]{2,1,0:T(8,128)(2,1)}) custom-call(bf16[8,256,704]{2,1,0:T(8,128)(2,1)} %get-tuple-element.94.refs_0_, bf16[4,704,512]{2,1,0:T(8,128)(2,1)} %bitcast.70, ...), custom_call_target="tpu_custom_call" | custom-call | tf_op jit(solution)/shard_map/pallas_call | solution.py:850
  353.5 3.3 add_convert_fusion.2.refs_8_.refs_0_
  356.8 64.3 %shard_map.370 = (f32[256,2048]{1,0:T(8,128)}, bf16[4,704,512]{2,1,0:T(8,128)(2,1)}, bf16[4,704,512]{2,1,0:T(8,128)(2,1)}, bf16[256,2048]{1,0:T(8,128)(2,1)}, f3...) custom-call(bf16[8,256,704]{2,1,0:T(8,128)(2,1)} %get-tuple-element.101.refs_0_, ...), custom_call_target="tpu_custom_call" | custom-call | tf_op jit(solution)/shard_map/pallas_call | solution.py:850
  421.1 2.3 fusion.refs_5_
  423.4 2.9 add_convert_fusion.1.refs_4_.refs_0_
  426.3 57.6 %shard_map.371 = (bf16[256,2048]{1,0:T(8,128)(2,1)}, bf16[4,256,512]{2,1,0:T(8,128)(2,1)}, bf16[2,704,512]{2,1,0:T(8,128)(2,1)}, bf16[2,704,512]{2,1,0:T(8,128)(2,1)}, bf16[704,512]{1,0:T(8,128)(2,1)}) custom-call(bf16[256,2048]{1,0:T(8,128)(2,1)} %get-tuple-element.106.refs_0_, bf16[256,2048]{1,0:T(8,128)(2,1)} %get-tuple-element.87.refs_0_.refs_1_, ...), custom_call_target="tpu_custom_call" | custom-call | tf_op jit(solution)/shard_map/pallas_call | solution.py:850
  484.0 3.0 add_convert_fusion.refs_9_.refs_3_
  487.0 1.0 fusion.1.refs_10_
  488.1 53.1 %shard_map.372 = (bf16[256,2048]{1,0:T(8,128)(2,1)}, bf16[128,2048]{1,0:T(8,128)(2,1)}, bf16[2,256,512]{2,1,0:T(8,128)(2,1)}, bf16[704,512]{1,0:T(8,128)(2,1)}) custom-call(bf16[256,2048]{1,0:T(8,128)(2,1)} %get-tuple-element.84.refs_2_.refs_0_, bf16[256,2048]{1,0:T(8,128)(2,1)} %get-tuple-element.87.refs_0_.refs_1_, ...), custom_call_target="tpu_custom_call" | custom-call | tf_op jit(solution)/shard_map/pallas_call | solution.py:850
  541.2 2.0 add_convert_fusion.6.refs_10_.refs_0_
  543.2 85.0 %shard_map.373 = (f32[256,2048]{1,0:T(8,128)}, bf16[512,256]{1,0:T(8,128)(2,1)}, f32[4,64,128]{2,1,0:T(8,128)}, f32[16,128]{1,0:T(8,128)}, bf16[2,704,512]{2,1,0:T(8,128)(2,1)}, /*index=5*/bf16[2,256,512]{2,1,0:T(8,128)(2,1)}) custom-call(bf16[256,2048]{1,0:T(8,128)(2,1)} %get-tuple-element.117.refs_0_, bf16[128,2048]{1,0:T(8,128)(2,1)} %get-tuple-element.118.refs_1_, ...), custom_call_target="tpu_custom_call" | custom-call | tf_op jit(solution)/shard_map/pallas_call | solution.py:850
  628.2 1.4 fusion.2
  629.6 1.4 collective-permute-start.2
  631.0 0.6 pad_add_fusion.place_ref
  632.4 0.6 pad_maximum_fusion.1.fix_ref
  633.0 1.3 collective-permute-start.1
  634.4 1.3 add_subtract_fusion
  635.7 0.2 reshape.176
  635.9 0.2 copy.46
  636.1 0.2 reshape.177
  636.2 6.4 shard_map.377
  642.7 3.3 shard_map.374
  646.0 0.8 multiply_subtract_fusion
  646.8 0.7 copy-done.15
  647.5 3.6 shard_map.375
  651.2 0.9 copy-done.13
  652.0 11.8 %shard_map.376 = (f32[2,704,512]{2,1,0:T(8,128)}, f32[2,704,512]{2,1,0:T(8,128)}, f32[2,704,512]{2,1,0:T(8,128)}) custom-call(s32[2]{0:T(128)} %pad_add_fusion.place_ref, f32[2]{0:T(128)} %pad_maximum_fusion.1.fix_ref, f32[2,704,512]{2,1,0:T(8,128)} %bitcast.66, f32[2,704,512]{2,1,0:T(8,128)} %bitcast.71, f32[2,704,512]{2,1,0:T(8,128)} %bitcast.72, ...), custom_call_target="tpu_custom_call" | custom-call | tf_op jit(solution)/shard_map/pallas_call | solution.py:124
  663.8 1.0 copy.60
  664.8 1.0 copy-done.9
  665.8 1.3 copy.61
  (56 shorter events, 0.5 us)
Async XLA Ops:
  0.7 5.5 copy-start.6
  0.7 8.8 %collective-permute-start = (s32[1,2048]{1,0:T(1,128)}, s32[1,2048]{1,0:T(1,128)S(1)}, u32[]{:S(2)}, u32[]{:S(2)}) collective-permute-start(s32[1,2048]{1,0:T(1,128)} %param.24), channel_id=1, source_target_pairs={{0,8},{8,0},{1,9},{9,1},{2,10},{10,2},{3,11},{11,3},{4,12},{12,4},... | collective-permute-start | bytes 24584 | tf_op jit(solution)/shard_map/ppermute | solution.py:1583
  4.2 2.9 copy-start.3
  7.3 1.2 copy-start.20
  7.3 2.1 copy-start.19
  356.8 64.3 %copy-start = (bf16[2,704,512]{2,1,0:T(8,128)(2,1)S(1)}, bf16[2,704,512]{2,1,0:T(8,128)(2,1)}, u32[]{:S(2)}) copy-start(bf16[2,704,512]{2,1,0:T(8,128)(2,1)} %add_convert_fusion.2.refs_8_.refs_0_) | copy-start | bytes 4325380
  421.1 2.3 copy-start.10
  426.3 57.6 %copy-start.4 = (bf16[4,704,512]{2,1,0:T(8,128)(2,1)S(1)}, bf16[4,704,512]{2,1,0:T(8,128)(2,1)}, u32[]{:S(2)}) copy-start(bf16[4,704,512]{2,1,0:T(8,128)(2,1)} %get-tuple-element.107.refs_3_) | copy-start | bytes 8650756
  483.9 3.1 copy-start.1
  484.0 3.0 copy-start.7
  488.1 53.1 %copy-start.8 = (bf16[4,256,512]{2,1,0:T(8,128)(2,1)S(1)}, bf16[4,256,512]{2,1,0:T(8,128)(2,1)}, u32[]{:S(2)}) copy-start(bf16[4,256,512]{2,1,0:T(8,128)(2,1)} %get-tuple-element.115.refs_9_) | copy-start | bytes 3145732
  543.2 85.0 %copy-start.2 = (bf16[2,704,512]{2,1,0:T(8,128)(2,1)S(1)}, bf16[2,704,512]{2,1,0:T(8,128)(2,1)}, u32[]{:S(2)}) copy-start(bf16[2,704,512]{2,1,0:T(8,128)(2,1)} %add_convert_fusion.refs_9_.refs_3_) | copy-start | bytes 4325380
  628.1 4.8 copy-start.5
  628.2 4.8 copy-start.11
  628.2 6.2 copy-start.21
  628.2 6.2 copy-start.22
  628.2 7.5 %copy-start.16 = (f32[4,64,128]{2,1,0:T(8,128)S(1)}, f32[4,64,128]{2,1,0:T(8,128)}, u32[]{:S(2)}) copy-start(f32[4,64,128]{2,1,0:T(8,128)} %get-tuple-element.129) | copy-start | bytes 393220
  629.6 21.5 %collective-permute-start.2 = (bf16[704,512]{1,0:T(8,128)(2,1)S(1)}, bf16[704,512]{1,0:T(8,128)(2,1)S(1)}, u32[]{:S(2)}, u32[]{:S(2)}) collective-permute-start(bf16[704,512]{1,0:T(8,128)(2,1)S(1)} %fusion.2), channel_id=1, source_target_pairs={{0,8},{12,4},{1,9},{13,5},{2,10},{14,6},{3,11},{15,7},{16,24},{28,... | collective-permute-start | bytes 2162696 | tf_op jit(solution)/shard_map/ppermute | solution.py:1884
  633.0 13.8 %collective-permute-start.1 = (bf16[256,512]{1,0:T(8,128)(2,1)S(1)}, bf16[256,512]{1,0:T(8,128)(2,1)S(1)}, u32[]{:S(2)}, u32[]{:S(2)}) collective-permute-start(bf16[256,512]{1,0:T(8,128)(2,1)S(1)} %fusion.3), channel_id=1, source_target_pairs={{0,8},{12,4},{1,9},{13,5},{2,10},{14,6},{3,11},{15,7},{16,24},{28,... | collective-permute-start | bytes 786440 | tf_op jit(solution)/shard_map/ppermute | solution.py:1884
  642.6 3.3 copy-start.14
  642.6 3.3 copy-start.17
  642.7 3.3 copy-start.18
  646.8 0.7 copy-start.15
  651.1 0.9 copy-start.13
  652.0 11.8 %copy-start.12 = (bf16[256,2048]{1,0:T(8,128)(2,1)S(1)}, bf16[256,2048]{1,0:T(8,128)(2,1)}, u32[]{:S(2)}) copy-start(bf16[256,2048]{1,0:T(8,128)(2,1)} %get-tuple-element.183) | copy-start | bytes 3145732
  663.8 2.0 copy-start.9

commit v8 on v7

--- a/solution.py
+++ b/solution.py
@@ -94,7 +94,7 @@
         grad = found if n == 0 else jnp.where(pl.program_id(0) == n, found, grad)
     first_new = BETA_ONE * m_ref[0] + (1.0 - BETA_ONE) * grad
     second_new = BETA_TWO * v_ref[0] + (1.0 - BETA_TWO) * grad * grad
-    update = first_new / fix_ref[0] / (jnp.sqrt(second_new / fix_ref[1]) + ADAM_EPS)
+    update = first_new * fix_ref[0] / (jnp.sqrt(second_new * fix_ref[1]) + ADAM_EPS)
     weight = w_ref[0]
     w_out[0] = weight - rate * (update + decay * weight)
     m_out[0] = first_new
@@ -1039,29 +1039,22 @@
         put_cols(target, j, dot_nn(hidden, refs.wd[j]), h_size)
 
 
-def weight_grad(h_size, refs, name, left, total, key, between=None):
-    result = getattr(refs, key)
-    y_at = lax.axis_index("y")
-    for y_of in (1 - y_at, y_at):
-        total[...] = jnp.zeros_like(total)
-
-        def add(n, rows):
-            left_t = flip(left[n]).astype(jnp.bfloat16)
-            for j in range(2):
-                total[j] += dot_nn(left_t, cols_at(rows, 2 * y_of + j, h_size))
-
-        refs.stream(name, add)
-        for j in range(2):
-            result[2 * y_of + j] = total[j].astype(jnp.bfloat16)
-        if between is not None:
-            between()
-            between = None
+def weight_grad(h_size, refs, name, left, key):
+    total, result = refs.total, getattr(refs, key)
+    total[...] = jnp.zeros_like(total)
+
+    def add(n, rows):
+        left_t = flip(left[n]).astype(jnp.bfloat16)
+        for j in range(4):
+            total[j] += dot_nn(left_t, cols_at(rows, j, h_size))
+
+    refs.stream(name, add)
+    result[...] = total[...].astype(jnp.bfloat16)
     refs.flush(key).start()
 
 
 def down_fill_one(h_size, refs):
-    swap = lambda: swap_copy(refs.gwd, refs.came, refs.more.at[0], refs.more.at[1]).start()
-    weight_grad(h_size, refs, "dy", refs.hid, refs.total, "gwd", swap)
+    weight_grad(h_size, refs, "dy", refs.hid, "gwd")
 
 
 def down_fill_two(h_size, refs):
@@ -1077,10 +1070,6 @@
     refs.stream("dy", back)
 
 
-def down_end(refs):
-    swap_copy(refs.gwd, refs.came, refs.more.at[0], refs.more.at[1]).wait()
-
-
 def gateup_produce(h_size, refs, block, target):
     gate, up = refs.dgate[block], refs.dup[block]
     for j in range(4):
@@ -1088,16 +1077,11 @@
 
 
 def gateup_fill_one(h_size, refs):
-    swap = lambda: swap_copy(refs.gwg, refs.came, refs.more.at[0], refs.more.at[1]).start()
-    weight_grad(h_size, refs, "rows", refs.dgate, refs.total, "gwg", swap)
+    weight_grad(h_size, refs, "rows", refs.dgate, "gwg")
 
 
 def gateup_fill_two(h_size, refs):
-    weight_grad(h_size, refs, "rows", refs.dup, refs.total, "gwu")
-
-
-def gateup_end(refs):
-    swap_copy(refs.gwg, refs.came, refs.more.at[0], refs.more.at[1]).wait()
+    weight_grad(h_size, refs, "rows", refs.dup, "gwu")
 
 
 def output_before(refs):
@@ -1675,7 +1659,7 @@
             ),
             Pass(output_parts),
             Pass(gate_parts),
-            Spread(own_shard(gateup_t[1], h_size)),
+            later(Spread(own_shard(gateup_t[1], h_size))),
         )
     )
     grad_rows = grad_rows.reshape(8, block_rows, D)
@@ -1714,9 +1698,9 @@
     )
     down_full = col_blocks(down_parts)
 
-    sums = pltpu.VMEM((2, units, D // 4), jnp.float32)
-    whole_grad, half_grad = shape(4, units, D // 4), shape(2, units, D // 4)
-    gate_grad, up_grad, down_grad, hidden_out, down_came = flat(
+    sums = pltpu.VMEM((4, units, D // 4), jnp.float32)
+    whole_grad = shape(4, units, D // 4)
+    gate_grad, up_grad, down_grad, hidden_out = flat(
         run(
             5,
             ScatterRows(
@@ -1738,23 +1722,18 @@
                 keep=False,
                 summed=mlp_summed,
                 scratch=dict(total=sums),
-                far=dict(came=half_grad),
-                extra_sems=2,
                 fill_one=functools.partial(down_fill_one, h_size),
                 fill_two=functools.partial(down_fill_two, h_size),
-                end=down_end,
             ),
         )
     )
-    down_part = add_swapped(down_grad, down_came)
-    mid_grad, gate_wgrad, up_wgrad, mid_rounded, mlp_sums, gate_came, down_deep = flat(
+    mid_grad, gate_wgrad, up_wgrad, mid_rounded, mlp_sums, down_came = flat(
         run(
             6,
             ScatterRows(
                 block_rows,
                 D,
                 functools.partial(gateup_produce, h_size),
-                by_x=6,
                 first=("dgate", "dup", "wg", "wu"),
                 given=dict(
                     dgate=gate_grad,
@@ -1774,17 +1753,14 @@
                 ),
                 summed=mlp_norm_summed,
                 scratch=dict(total=sums),
-                far=dict(came=half_grad),
-                extra_sems=2,
                 fill_one=functools.partial(gateup_fill_one, h_size),
                 fill_two=functools.partial(gateup_fill_two, h_size),
-                end=gateup_end,
             ),
-            Move(down_part, "zh", not_home),
+            Swap(down_grad),
         )
     )
-    gate_part = add_swapped(gate_wgrad, gate_came)
-    attended_grad, output_grad, up_came, gate_deep, down_got = flat(
+    down_part = add_swapped(down_grad, down_came)
+    attended_grad, output_grad, gate_came, down_deep = flat(
         run(
             7,
             GatherRows(
@@ -1797,13 +1773,12 @@
                 work=functools.partial(output_work, h_size),
                 after=output_after,
             ),
-            Swap(up_wgrad),
-            Move(gate_part, "zh", not_home),
-            Move(for_partner(down_part, down_deep), "c", at_home),
+            Swap(gate_wgrad),
+            Move(down_part, "zh", not_home),
         )
     )
-    up_part = add_swapped(up_wgrad, up_came)
-    query_back, pair_back, output_came, gate_got = flat(
+    gate_part = add_swapped(gate_wgrad, gate_came)
+    query_back, pair_back, output_came, up_came, gate_deep, down_got = flat(
         run(
             8,
             AttentionBack(
@@ -1822,15 +1797,18 @@
                 results=dict(dq=shape(width, group_rows), dpair=shape(2 * HD, group_rows)),
             ),
             Swap(output_grad),
-            Move(for_partner(gate_part, gate_deep), "c", at_home),
+            Swap(up_wgrad),
+            Move(gate_part, "zh", not_home),
+            Move(for_partner(down_part, down_deep), "c", at_home),
         )
     )
     output_part = add_swapped(output_grad, output_came)
+    up_part = add_swapped(up_wgrad, up_came)
     quarter = D // 4
     last = Last(h_size, devices, pair_rows, gain_cols, head_of)
     half_q = pltpu.VMEM((2, quarter, width), jnp.bfloat16)
     whole_q = pltpu.VMEM((quarter, width), jnp.bfloat16)
-    input_grad, query_grad, pair_sums, gain_sums, up_deep, output_deep = flat(
+    input_grad, query_grad, pair_sums, gain_sums, up_deep, output_deep, gate_got = flat(
         run(
             9,
             ScatterRows(
@@ -1879,6 +1857,7 @@
             ),
             Move(up_part, "zh", not_home),
             Move(output_part, "zh", not_home),
+            Move(for_partner(gate_part, gate_deep), "c", at_home),
         )
     )
     cores = lambda a: lax.ppermute(a, ("c", "zh"), TO_AWAY_CORE)
@@ -1891,7 +1870,7 @@
     )
     gains_sum = lax.dynamic_slice(gain_sums, (jnp.int32(0), lane), (2, gain_cols))
     step_value = step_count[0].astype(jnp.float32)
-    fixes = jnp.stack(
+    fixes = 1.0 / jnp.stack(
         [
             1.0 - jnp.power(jnp.float32(BETA_ONE), step_value),
             1.0 - jnp.power(jnp.float32(BETA_TWO), step_value),

time: 673 us -> 643 us (0.955)
  Pallas kernels: 625 us -> 596 us
    pallas_call x9, Pallas kernels: 599 us -> 571 us  [run(): pl.pallas_call(kernel, in_specs=in_specs, out_specs=out_specs, out_shape=...]
where the time goes in v8:
time: 643 us; the launch traced here: 637 us
  Pallas kernels  596 us (93%)
  other arithmetic  25 us (4%)
  local copies, waits for them, and re-layouts  10.5 us (2%)
    pallas_call x9, Pallas kernels, run(): pl.pallas_call(kernel, in_specs=in_specs, out_specs=out_specs, out_shape=...  571 us
    pallas_call x4, Pallas kernels, adam_shard(): pl.pallas_call(functools.partial(adam_kernel, rate, DECAY, groups), grid_...  25.1 us
  transfers between devices with their start and end apart: 3, of which 0 were waited for; matrix products, arithmetic and copies ran while one was open for 2% of the time, Pallas kernels for 2%

profile of v8, /device:TPU:0, one launch (start us, length us, event | category | flops | bytes accessed | tf_op | source)
XLA Modules:
  0.0 637.3 jit_solution(2211860262612109373)
XLA Ops:
  0.7 0.5 collective-permute-start
  1.2 0.9 convert.15
  2.5 1.8 convert_bitcast_fusion.2.refs_1_
  4.2 1.9 convert_bitcast_fusion.1.refs_5_
  6.2 0.9 convert_bitcast_fusion.refs_5_
  7.1 0.2 bitcast_convert_fusion
  7.3 1.2 fusion.13
  8.5 0.3 dynamic_update_slice.5
  8.8 0.6 pad_maximum_fusion.refs_0_
  9.5 0.2 fusion.5
  9.7 0.6 copy.48
  10.4 1.8 multiply_sine_fusion
  12.2 98.2 %shard_map.365 = (bf16[32,80,128]{2,1,0:T(8,128)(2,1)}, bf16[4,1,512,256]{3,2,1,0:T(8,128)(2,1)}, f32[16,2048]{1,0:T(8,128)}, bf16[8,256,2048]{2,1,0:T(8,128)(2,...) custom-call(bf16[4,80,128]{2,1,0:T(8,128)(2,1)} %pad_maximum_fusion., ...), custom_call_target="tpu_custom_call" | custom-call | tf_op jit(solution)/shard_map/pallas_call | solution.py:850
  110.4 1.9 slice.13
  112.3 63.1 %shard_map.366 = (bf16[128,2048]{1,0:T(8,128)(2,1)}, bf16[8,256,2048]{2,1,0:T(8,128)(2,1)}, bf16[256,2048]{1,0:T(8,128)(2,1)}, f32[2,4,1024]{2,1,0:T(4,128)}, bf...) custom-call(bf16[128,2048]{1,0:T(8,128)(2,1)} %get-tuple-element.83., ...), custom_call_target="tpu_custom_call", output_to_operand_aliasing={{6}: (5, {}), {7}: (6, {})} | custom-call | tf_op jit(solution)/shard_map/pallas_call | solution.py:850
  175.4 62.8 %shard_map.367 = (f32[256,2048]{1,0:T(8,128)}, bf16[256,2048]{1,0:T(8,128)(2,1)}, bf16[4,1,704,512]{3,2,1,0:T(8,128)(2,1)}, bf16[4,1,704,512]{3,2,1,0:T(8,128)(2,1)}) custom-call(bf16[256,2048]{1,0:T(8,128)(2,1)} %get-tuple-element.87.refs_0_.refs_1_, bf16[4,256,512]{2,1,0:T(8,128)(2,1)} %bitcast.67, ...), custom_call_target="tpu_custom_call", output_to_operand_aliasing={{2}: (4, {})} | custom-call | tf_op jit(solution)/shard_map/pallas_call | solution.py:850
  238.2 44.7 %shard_map.368 = (bf16[8,256,2048]{2,1,0:T(8,128)(2,1)}, bf16[8,256,704]{2,1,0:T(8,128)(2,1)}, bf16[8,256,704]{2,1,0:T(8,128)(2,1)}, bf16[8,256,704]{2,1,0:T(8,128)(2,1)}) custom-call(bf16[256,2048]{1,0:T(8,128)(2,1)} %get-tuple-element.91.refs_0_, bf16[4,704,512]{2,1,0:T(8,128)(2,1)} %bitcast.62, bf16[4,704,512]{2,1,0:T(8,128)(2,1)} %bitcast.64), custom_call_target="tpu_custom_call" | custom-call | tf_op jit(solution)/shard_map/pallas_call | solution.py:850
  282.9 46.5 %shard_map.369 = (bf16[8,256,704]{2,1,0:T(8,128)(2,1)}, bf16[8,256,704]{2,1,0:T(8,128)(2,1)}, bf16[4,704,512]{2,1,0:T(8,128)(2,1)}, bf16[256,2048]{1,0:T(8,128)(2,1)}) custom-call(bf16[8,256,704]{2,1,0:T(8,128)(2,1)} %get-tuple-element.94.refs_0_, bf16[4,704,512]{2,1,0:T(8,128)(2,1)} %bitcast.70, bf16[8,256,704]{2,1,0:T(8,128)(2,1)} %get-tuple-element.96.refs_2_, ...), custom_call_target="tpu_custom_call" | custom-call | tf_op jit(solution)/shard_map/pallas_call | solution.py:850
  329.4 52.7 %shard_map.370 = (f32[256,2048]{1,0:T(8,128)}, bf16[4,704,512]{2,1,0:T(8,128)(2,1)}, bf16[4,704,512]{2,1,0:T(8,128)(2,1)}, bf16[256,2048]{1,0:T(8,128)(2,1)}, f3...) custom-call(bf16[8,256,704]{2,1,0:T(8,128)(2,1)} %get-tuple-element.101.refs_0_, ...), custom_call_target="tpu_custom_call" | custom-call | tf_op jit(solution)/shard_map/pallas_call | solution.py:850
  382.1 2.9 add_convert_fusion.2.refs_4_.refs_0_
  384.9 57.4 %shard_map.371 = (bf16[256,2048]{1,0:T(8,128)(2,1)}, bf16[4,256,512]{2,1,0:T(8,128)(2,1)}, bf16[2,704,512]{2,1,0:T(8,128)(2,1)}, bf16[2,704,512]{2,1,0:T(8,128)(2,1)}) custom-call(bf16[256,2048]{1,0:T(8,128)(2,1)} %get-tuple-element.105.refs_0_, bf16[256,2048]{1,0:T(8,128)(2,1)} %get-tuple-element.87.refs_0_.refs_1_, bf16[4,256,512]{2,1,0:T(8,128)(2,1)} %bitcast.68, ...), custom_call_target="tpu_custom_call" | custom-call | tf_op jit(solution)/shard_map/pallas_call | solution.py:850
  442.4 3.1 add_convert_fusion.1.refs_11_.refs_0_
  445.5 1.0 fusion.refs_12_
  446.6 61.1 %shard_map.372 = (bf16[256,2048]{1,0:T(8,128)(2,1)}, bf16[128,2048]{1,0:T(8,128)(2,1)}, bf16[2,256,512]{2,1,0:T(8,128)(2,1)}, bf16[2,704,512]{2,1,0:T(8,128)(2,1...) custom-call(bf16[256,2048]{1,0:T(8,128)(2,1)} %get-tuple-element.84.refs_2_.refs_0_, ...), custom_call_target="tpu_custom_call" | custom-call | tf_op jit(solution)/shard_map/pallas_call | solution.py:850
  507.7 2.1 add_convert_fusion.6.refs_10_.refs_0_
  509.8 1.5 add_convert_fusion.refs_9_.refs_3_
  511.3 0.8 copy-done.10
  512.1 1.0 fusion.1.refs_11_
  513.2 84.8 %shard_map.373 = (f32[256,2048]{1,0:T(8,128)}, bf16[512,256]{1,0:T(8,128)(2,1)}, f32[4,64,128]{2,1,0:T(8,128)}, f32[16,128]{1,0:T(8,128)}, bf16[2,704,512]{2,1,0...) custom-call(bf16[256,2048]{1,0:T(8,128)(2,1)} %get-tuple-element.116.refs_0_, ...), custom_call_target="tpu_custom_call" | custom-call | tf_op jit(solution)/shard_map/pallas_call | solution.py:850
  598.0 1.4 fusion.2
  599.4 1.6 collective-permute-start.2
  601.0 0.6 pad_add_fusion.place_ref
  602.3 0.6 maximum_divide_fusion.fix_ref
  603.0 1.3 collective-permute-start.1
  604.3 1.3 add_subtract_fusion
  605.7 0.2 reshape.176
  605.9 0.2 copy.46
  606.1 0.2 reshape.177
  606.2 6.4 %shard_map.377 = (f32[1,704,512]{2,1,0:T(8,128)}, f32[1,704,512]{2,1,0:T(8,128)}, f32[1,704,512]{2,1,0:T(8,128)}) custom-call(s32[2]{0:T(128)} %pad_add_fusion.place_ref, f32[2]{0:T(128)} %maximum_divide_fusion.fix_ref, f32[1,704,512]{2,1,0:T(8,128)} %bitcast.69, f32[1,704,512]{2,1,0:T(8,128)} %bitcast.76, f32[1,704,512]{2,1,0:T(8,128)} %bitcast.77, ...), custom_call_target="tpu_custom_call" | custom-call | tf_op jit(solution)/shard_map/pallas_call | solution.py:124
  612.7 3.3 shard_map.374
  616.0 0.8 multiply_subtract_fusion
  616.8 0.7 copy-done.18
  617.5 3.6 shard_map.375
  621.1 0.9 copy-done.16
  622.0 11.8 %shard_map.376 = (f32[2,704,512]{2,1,0:T(8,128)}, f32[2,704,512]{2,1,0:T(8,128)}, f32[2,704,512]{2,1,0:T(8,128)}) custom-call(s32[2]{0:T(128)} %pad_add_fusion.place_ref, f32[2]{0:T(128)} %maximum_divide_fusion.fix_ref, f32[2,704,512]{2,1,0:T(8,128)} %bitcast.66, f32[2,704,512]{2,1,0:T(8,128)} %bitcast.71, f32[2,704,512]{2,1,0:T(8,128)} %bitcast.72, ...), custom_call_target="tpu_custom_call" | custom-call | tf_op jit(solution)/shard_map/pallas_call | solution.py:124
  633.8 1.0 copy.60
  634.8 1.0 copy-done.12
  635.8 1.3 copy.61
  (62 shorter events, 0.6 us)
Async XLA Ops:
  0.7 5.5 copy-start.8
  0.7 8.8 %collective-permute-start = (s32[1,2048]{1,0:T(1,128)}, s32[1,2048]{1,0:T(1,128)S(1)}, u32[]{:S(2)}, u32[]{:S(2)}) collective-permute-start(s32[1,2048]{1,0:T(1,128)} %param.24), channel_id=1, source_target_pairs={{0,8},{8,0},{1,9},{9,1},{2,10},{10,2},{3,11},{11,3},{4,12},{12,4},... | collective-permute-start | bytes 24584 | tf_op jit(solution)/shard_map/ppermute | solution.py:1567
  4.2 2.9 copy-start.3
  7.3 1.2 copy-start.23
  7.3 2.1 copy-start.22
  329.4 52.7 %copy-start.4 = (bf16[4,704,512]{2,1,0:T(8,128)(2,1)S(1)}, bf16[4,704,512]{2,1,0:T(8,128)(2,1)}, u32[]{:S(2)}) copy-start(bf16[4,704,512]{2,1,0:T(8,128)(2,1)} %get-tuple-element.104.refs_8_) | copy-start | bytes 8650756
  384.9 57.4 %copy-start.5 = (bf16[4,704,512]{2,1,0:T(8,128)(2,1)S(1)}, bf16[4,704,512]{2,1,0:T(8,128)(2,1)}, u32[]{:S(2)}) copy-start(bf16[4,704,512]{2,1,0:T(8,128)(2,1)} %get-tuple-element.106.refs_3_) | copy-start | bytes 8650756
  442.4 3.1 copy-start
  442.4 3.1 copy-start.9
  446.6 61.1 %copy-start.11 = (bf16[4,256,512]{2,1,0:T(8,128)(2,1)S(1)}, bf16[4,256,512]{2,1,0:T(8,128)(2,1)}, u32[]{:S(2)}) copy-start(bf16[4,256,512]{2,1,0:T(8,128)(2,1)} %get-tuple-element.112.refs_9_) | copy-start | bytes 3145732
  446.6 63.2 %copy-start.6 = (bf16[4,704,512]{2,1,0:T(8,128)(2,1)S(1)}, bf16[4,704,512]{2,1,0:T(8,128)(2,1)}, u32[]{:S(2)}) copy-start(bf16[4,704,512]{2,1,0:T(8,128)(2,1)} %get-tuple-element.113.refs_10_) | copy-start | bytes 8650756
  507.7 2.1 copy-start.13
  509.8 1.5 copy-start.1
  509.8 2.3 copy-start.10
  513.2 84.8 %copy-start.2 = (bf16[2,704,512]{2,1,0:T(8,128)(2,1)S(1)}, bf16[2,704,512]{2,1,0:T(8,128)(2,1)}, u32[]{:S(2)}) copy-start(bf16[2,704,512]{2,1,0:T(8,128)(2,1)} %add_convert_fusion.refs_9_.refs_3_) | copy-start | bytes 4325380
  597.9 5.0 copy-start.7
  598.0 5.0 copy-start.14
  598.0 6.4 copy-start.24
  598.0 6.4 copy-start.25
  598.0 7.7 %copy-start.19 = (f32[4,64,128]{2,1,0:T(8,128)S(1)}, f32[4,64,128]{2,1,0:T(8,128)}, u32[]{:S(2)}) copy-start(f32[4,64,128]{2,1,0:T(8,128)} %get-tuple-element.129) | copy-start | bytes 393220
  599.4 21.7 %collective-permute-start.2 = (bf16[704,512]{1,0:T(8,128)(2,1)S(1)}, bf16[704,512]{1,0:T(8,128)(2,1)S(1)}, u32[]{:S(2)}, u32[]{:S(2)}) collective-permute-start(bf16[704,512]{1,0:T(8,128)(2,1)S(1)} %fusion.2), channel_id=1, source_target_pairs={{0,8},{12,4},{1,9},{13,5},{2,10},{14,6},{3,11},{15,7},{16,24},{28,... | collective-permute-start | bytes 2162696 | tf_op jit(solution)/shard_map/ppermute | solution.py:1863
  603.0 13.8 %collective-permute-start.1 = (bf16[256,512]{1,0:T(8,128)(2,1)S(1)}, bf16[256,512]{1,0:T(8,128)(2,1)S(1)}, u32[]{:S(2)}, u32[]{:S(2)}) collective-permute-start(bf16[256,512]{1,0:T(8,128)(2,1)S(1)} %fusion.3), channel_id=1, source_target_pairs={{0,8},{12,4},{1,9},{13,5},{2,10},{14,6},{3,11},{15,7},{16,24},{28,... | collective-permute-start | bytes 786440 | tf_op jit(solution)/shard_map/ppermute | solution.py:1863
  612.6 3.3 copy-start.17
  612.6 3.3 copy-start.20
  612.7 3.3 copy-start.21
  616.8 0.7 copy-start.18
  621.1 0.9 copy-start.16
  622.0 11.8 %copy-start.15 = (bf16[256,2048]{1,0:T(8,128)(2,1)S(1)}, bf16[256,2048]{1,0:T(8,128)(2,1)}, u32[]{:S(2)}) copy-start(bf16[256,2048]{1,0:T(8,128)(2,1)} %get-tuple-element.183) | copy-start | bytes 3145732
  633.8 2.0 copy-start.12

commit v9 on v8

--- a/solution.py
+++ b/solution.py
@@ -103,7 +103,7 @@
 
 def adam_shard(weight, first, second, grads, rate, fixes):
     groups, rows, cols = weight.shape
-    size = max(n for n in range(16, 257, 16) if rows % n == 0)
+    size = max(n for n in range(16, 353, 16) if rows % n == 0)
     steps = rows // size
     place = jnp.stack([lax.axis_index("c"), (lax.axis_index("c") == lax.axis_index("zh"))])
     state = pl.BlockSpec((1, size, cols), lambda g, i, s: (g, i, 0))
@@ -1255,13 +1255,12 @@
             refs.gwp[j] = cols_at(refs.pair_total, j, self.h_size).T.astype(jnp.bfloat16)
         self.swap(refs).start()
 
+    def fill_two(self, refs):
         @pl.loop(1, self.devices)
         def _(step):
             self.send(refs, 0, step).start()
 
         pltpu.sync_copy(self.pair_part(refs, my_number()), refs.pair_in.at[my_number()])
-
-    def fill_two(self, refs):
         self.swap(refs).wait_recv()
         mine = 2 * lax.axis_index("y")
         for n in range(2):
@@ -1271,17 +1270,6 @@
         @pl.when(not_home())
         def _():
             self.deep(refs).start()
-
-        refs.pair_sum[...] = jnp.zeros_like(refs.pair_sum)
-        refs.pair_sum[self.head_of(my_number())] += refs.pair_in[my_number()].astype(jnp.float32)
-
-        @pl.loop(1, self.devices)
-        def _(step):
-            self.arrive(refs, 0, step)
-            origin = lax.rem(my_number() + step, self.devices)
-            refs.pair_sum[self.head_of(origin)] += refs.pair_in[origin].astype(jnp.float32)
-
-        refs.flush("pair_sum").start()
 
     def summed(self, refs, out):
         refs.sums[...] = jnp.zeros_like(refs.sums)
@@ -1322,6 +1310,16 @@
             refs.gq[...] = refs.q_got[...]
 
         refs.flush("gq").start()
+        refs.pair_sum[...] = jnp.zeros_like(refs.pair_sum)
+        refs.pair_sum[self.head_of(my_number())] += refs.pair_in[my_number()].astype(jnp.float32)
+
+        @pl.loop(1, self.devices)
+        def _(step):
+            self.arrive(refs, 0, step)
+            origin = lax.rem(my_number() + step, self.devices)
+            refs.pair_sum[self.head_of(origin)] += refs.pair_in[origin].astype(jnp.float32)
+
+        refs.flush("pair_sum").start()
         total = refs.gain_in[my_number()].astype(jnp.float32)
         refs.gain_sum[...] = total
 
@@ -1359,8 +1357,8 @@
         self.heads = heads
         packed = given["kt"].shape
         rows = (packed[0], packed[2], HD)
-        part = (2, 2, 2 * HD, KEYS_BACK // 2)
-        self.sems = [2, 2]
+        part = (4, 2, 2 * HD, KEYS_BACK // 4)
+        self.sems = [4, 4]
         self.scratch = []
         scratch = dict(
             k_s=pltpu.VMEM(rows, jnp.bfloat16),
@@ -1415,7 +1413,7 @@
         refs = self.bind(ins, outs, sems, scratch)
         send, recv = sems[:2]
         z_high = lax.axis_index("zh")
-        half = KEYS_BACK // 2
+        half = KEYS_BACK // 4
         early()
         self.ready(refs, self.given)
         for pack in range(2):
@@ -1440,16 +1438,16 @@
         @pl.loop(0, 8)
         def _(step):
             self.step(refs, lax.rem(step, 2), step // 2)
-            for n, done in enumerate((3, 7)):
-
-                @pl.when((step == done) & (z_high == 1))
+            for n in range(4):
+
+                @pl.when((step == 2 * n + 1) & (z_high == 1))
                 def _():
                     give(n)
 
         refs.flush("dq").start()
         middle()
         for pack in range(2):
-            for n in range(2):
+            for n in range(4):
                 rows = slice(KEYS_BACK + n * half, KEYS_BACK + (n + 1) * half)
                 first = pack * KEYS_BACK + n * half
                 at = slice(first, first + half)
@@ -1471,8 +1469,8 @@
 
         @pl.when(z_high == 1)
         def _():
-            share(0).wait_send()
-            share(1).wait_send()
+            for n in range(4):
+                share(n).wait_send()
 
         self.flushed(refs)
 
@@ -1622,8 +1620,8 @@
                 work=functools.partial(query_work, h_size, heads_here, pair_rows),
                 after=query_after,
             ),
-            later(Spread(own_shard(output_weight, h_size))),
-            later(Spread(own_shard(gateup_t[0], h_size))),
+            Spread(own_shard(output_weight, h_size)),
+            Spread(own_shard(gateup_t[0], h_size)),
         )
     )
     pair_proj = (

time: 643 us -> 640 us (level)
  no operation moved by 1% of the time
where the time goes in v9:
time: 640 us; the launch traced here: 635 us
  Pallas kernels  594 us (93%)
  other arithmetic  25 us (4%)
  local copies, waits for them, and re-layouts  10.5 us (2%)
    pallas_call x9, Pallas kernels, run(): pl.pallas_call(kernel, in_specs=in_specs, out_specs=out_specs, out_shape=...  571 us
    pallas_call x4, Pallas kernels, adam_shard(): pl.pallas_call(functools.partial(adam_kernel, rate, DECAY, groups), grid_...  22.2 us
  transfers between devices with their start and end apart: 3, of which 0 were waited for; matrix products, arithmetic and copies ran while one was open for 2% of the time, Pallas kernels for 2%

profile of v9, /device:TPU:0, one launch (start us, length us, event | category | flops | bytes accessed | tf_op | source)
XLA Modules:
  0.0 635.1 jit_solution(1695568186814106506)
XLA Ops:
  0.7 0.5 collective-permute-start
  1.2 0.9 convert.15
  2.5 1.8 convert_bitcast_fusion.2.refs_1_
  4.2 1.9 convert_bitcast_fusion.1.refs_5_
  6.2 0.9 convert_bitcast_fusion.refs_5_
  7.1 0.2 bitcast_convert_fusion
  7.3 1.2 fusion.13
  8.5 0.3 dynamic_update_slice.5
  8.8 0.6 pad_maximum_fusion.refs_0_
  9.5 0.2 fusion.5
  9.7 0.6 copy.48
  10.4 1.8 multiply_sine_fusion
  12.2 88.2 %shard_map.365 = (bf16[32,80,128]{2,1,0:T(8,128)(2,1)}, bf16[4,1,512,256]{3,2,1,0:T(8,128)(2,1)}, f32[16,2048]{1,0:T(8,128)}, bf16[8,256,2048]{2,1,0:T(8,128)(2,...) custom-call(bf16[4,80,128]{2,1,0:T(8,128)(2,1)} %pad_maximum_fusion., ...), custom_call_target="tpu_custom_call" | custom-call | tf_op jit(solution)/shard_map/pallas_call | solution.py:850
  100.4 1.9 slice.13
  102.3 63.7 %shard_map.366 = (bf16[128,2048]{1,0:T(8,128)(2,1)}, bf16[8,256,2048]{2,1,0:T(8,128)(2,1)}, bf16[256,2048]{1,0:T(8,128)(2,1)}, f32[2,4,1024]{2,1,0:T(4,128)}, bf...) custom-call(bf16[128,2048]{1,0:T(8,128)(2,1)} %get-tuple-element.83., ...), custom_call_target="tpu_custom_call", output_to_operand_aliasing={{6}: (5, {}), {7}: (6, {})} | custom-call | tf_op jit(solution)/shard_map/pallas_call | solution.py:850
  166.0 66.6 %shard_map.367 = (f32[256,2048]{1,0:T(8,128)}, bf16[256,2048]{1,0:T(8,128)(2,1)}, bf16[4,1,704,512]{3,2,1,0:T(8,128)(2,1)}, bf16[4,1,704,512]{3,2,1,0:T(8,128)(2,1)}) custom-call(bf16[256,2048]{1,0:T(8,128)(2,1)} %get-tuple-element.87.refs_0_.refs_1_, bf16[4,256,512]{2,1,0:T(8,128)(2,1)} %bitcast.67, ...), custom_call_target="tpu_custom_call", output_to_operand_aliasing={{2}: (4, {})} | custom-call | tf_op jit(solution)/shard_map/pallas_call | solution.py:850
  232.6 50.3 %shard_map.368 = (bf16[8,256,2048]{2,1,0:T(8,128)(2,1)}, bf16[8,256,704]{2,1,0:T(8,128)(2,1)}, bf16[8,256,704]{2,1,0:T(8,128)(2,1)}, bf16[8,256,704]{2,1,0:T(8,128)(2,1)}) custom-call(bf16[256,2048]{1,0:T(8,128)(2,1)} %get-tuple-element.91.refs_0_, bf16[4,704,512]{2,1,0:T(8,128)(2,1)} %bitcast.62, bf16[4,704,512]{2,1,0:T(8,128)(2,1)} %bitcast.64), custom_call_target="tpu_custom_call" | custom-call | tf_op jit(solution)/shard_map/pallas_call | solution.py:850
  282.9 47.4 %shard_map.369 = (bf16[8,256,704]{2,1,0:T(8,128)(2,1)}, bf16[8,256,704]{2,1,0:T(8,128)(2,1)}, bf16[4,704,512]{2,1,0:T(8,128)(2,1)}, bf16[256,2048]{1,0:T(8,128)(2,1)}) custom-call(bf16[8,256,704]{2,1,0:T(8,128)(2,1)} %get-tuple-element.94.refs_0_, bf16[4,704,512]{2,1,0:T(8,128)(2,1)} %bitcast.70, bf16[8,256,704]{2,1,0:T(8,128)(2,1)} %get-tuple-element.96.refs_2_, ...), custom_call_target="tpu_custom_call" | custom-call | tf_op jit(solution)/shard_map/pallas_call | solution.py:850
  330.3 51.7 %shard_map.370 = (f32[256,2048]{1,0:T(8,128)}, bf16[4,704,512]{2,1,0:T(8,128)(2,1)}, bf16[4,704,512]{2,1,0:T(8,128)(2,1)}, bf16[256,2048]{1,0:T(8,128)(2,1)}, f3...) custom-call(bf16[8,256,704]{2,1,0:T(8,128)(2,1)} %get-tuple-element.101.refs_0_, ...), custom_call_target="tpu_custom_call" | custom-call | tf_op jit(solution)/shard_map/pallas_call | solution.py:850
  382.0 2.9 add_convert_fusion.2.refs_4_.refs_0_
  384.9 57.7 %shard_map.371 = (bf16[256,2048]{1,0:T(8,128)(2,1)}, bf16[4,256,512]{2,1,0:T(8,128)(2,1)}, bf16[2,704,512]{2,1,0:T(8,128)(2,1)}, bf16[2,704,512]{2,1,0:T(8,128)(2,1)}) custom-call(bf16[256,2048]{1,0:T(8,128)(2,1)} %get-tuple-element.105.refs_0_, bf16[256,2048]{1,0:T(8,128)(2,1)} %get-tuple-element.87.refs_0_.refs_1_, bf16[4,256,512]{2,1,0:T(8,128)(2,1)} %bitcast.68, ...), custom_call_target="tpu_custom_call" | custom-call | tf_op jit(solution)/shard_map/pallas_call | solution.py:850
  442.6 3.1 add_convert_fusion.1.refs_11_.refs_0_
  445.7 1.0 fusion.refs_12_
  446.8 61.0 %shard_map.372 = (bf16[256,2048]{1,0:T(8,128)(2,1)}, bf16[128,2048]{1,0:T(8,128)(2,1)}, bf16[2,256,512]{2,1,0:T(8,128)(2,1)}, bf16[2,704,512]{2,1,0:T(8,128)(2,1...) custom-call(bf16[256,2048]{1,0:T(8,128)(2,1)} %get-tuple-element.84.refs_2_.refs_0_, ...), custom_call_target="tpu_custom_call" | custom-call | tf_op jit(solution)/shard_map/pallas_call | solution.py:850
  507.8 2.1 add_convert_fusion.6.refs_10_.refs_0_
  509.9 1.5 add_convert_fusion.refs_9_.refs_3_
  511.4 0.8 copy-done.10
  512.2 1.0 fusion.1.refs_11_
  513.2 84.8 %shard_map.373 = (f32[256,2048]{1,0:T(8,128)}, bf16[512,256]{1,0:T(8,128)(2,1)}, f32[4,64,128]{2,1,0:T(8,128)}, f32[16,128]{1,0:T(8,128)}, bf16[2,704,512]{2,1,0...) custom-call(bf16[256,2048]{1,0:T(8,128)(2,1)} %get-tuple-element.116.refs_0_, ...), custom_call_target="tpu_custom_call" | custom-call | tf_op jit(solution)/shard_map/pallas_call | solution.py:850
  598.1 1.4 fusion.2
  599.5 2.1 collective-permute-start.2
  601.7 0.6 pad_add_fusion.place_ref
  603.0 0.6 maximum_divide_fusion.fix_ref
  603.7 1.3 collective-permute-start.1
  605.0 1.3 add_subtract_fusion
  606.4 0.2 reshape.176
  606.6 0.2 copy.46
  606.8 0.2 reshape.177
  606.9 5.4 shard_map.377
  612.4 3.3 shard_map.374
  615.7 0.8 multiply_subtract_fusion
  616.5 0.7 copy-done.18
  617.2 3.6 shard_map.375
  620.9 0.9 copy-done.16
  621.7 9.9 %shard_map.376 = (f32[2,704,512]{2,1,0:T(8,128)}, f32[2,704,512]{2,1,0:T(8,128)}, f32[2,704,512]{2,1,0:T(8,128)}) custom-call(s32[2]{0:T(128)} %pad_add_fusion.place_ref, f32[2]{0:T(128)} %maximum_divide_fusion.fix_ref, f32[2,704,512]{2,1,0:T(8,128)} %bitcast.66, f32[2,704,512]{2,1,0:T(8,128)} %bitcast.71, f32[2,704,512]{2,1,0:T(8,128)} %bitcast.72, ...), custom_call_target="tpu_custom_call" | custom-call | tf_op jit(solution)/shard_map/pallas_call | solution.py:124
  631.6 1.0 copy.60
  632.6 1.0 copy-done.12
  633.6 1.3 copy.61
  (62 shorter events, 0.6 us)
Async XLA Ops:
  0.7 5.5 copy-start.8
  0.7 8.8 %collective-permute-start = (s32[1,2048]{1,0:T(1,128)}, s32[1,2048]{1,0:T(1,128)S(1)}, u32[]{:S(2)}, u32[]{:S(2)}) collective-permute-start(s32[1,2048]{1,0:T(1,128)} %param.24), channel_id=1, source_target_pairs={{0,8},{8,0},{1,9},{9,1},{2,10},{10,2},{3,11},{11,3},{4,12},{12,4},... | collective-permute-start | bytes 24584 | tf_op jit(solution)/shard_map/ppermute | solution.py:1565
  4.2 2.9 copy-start.3
  7.3 1.2 copy-start.23
  7.3 2.1 copy-start.22
  330.3 51.8 %copy-start.4 = (bf16[4,704,512]{2,1,0:T(8,128)(2,1)S(1)}, bf16[4,704,512]{2,1,0:T(8,128)(2,1)}, u32[]{:S(2)}) copy-start(bf16[4,704,512]{2,1,0:T(8,128)(2,1)} %get-tuple-element.104.refs_8_) | copy-start | bytes 8650756
  384.9 57.7 %copy-start.5 = (bf16[4,704,512]{2,1,0:T(8,128)(2,1)S(1)}, bf16[4,704,512]{2,1,0:T(8,128)(2,1)}, u32[]{:S(2)}) copy-start(bf16[4,704,512]{2,1,0:T(8,128)(2,1)} %get-tuple-element.106.refs_3_) | copy-start | bytes 8650756
  442.6 3.1 copy-start
  442.6 3.1 copy-start.9
  446.8 61.0 %copy-start.11 = (bf16[4,256,512]{2,1,0:T(8,128)(2,1)S(1)}, bf16[4,256,512]{2,1,0:T(8,128)(2,1)}, u32[]{:S(2)}) copy-start(bf16[4,256,512]{2,1,0:T(8,128)(2,1)} %get-tuple-element.112.refs_9_) | copy-start | bytes 3145732
  446.8 63.1 %copy-start.6 = (bf16[4,704,512]{2,1,0:T(8,128)(2,1)S(1)}, bf16[4,704,512]{2,1,0:T(8,128)(2,1)}, u32[]{:S(2)}) copy-start(bf16[4,704,512]{2,1,0:T(8,128)(2,1)} %get-tuple-element.113.refs_10_) | copy-start | bytes 8650756
  507.8 2.1 copy-start.13
  509.9 1.5 copy-start.1
  509.9 2.3 copy-start.10
  513.2 84.8 %copy-start.2 = (bf16[2,704,512]{2,1,0:T(8,128)(2,1)S(1)}, bf16[2,704,512]{2,1,0:T(8,128)(2,1)}, u32[]{:S(2)}) copy-start(bf16[2,704,512]{2,1,0:T(8,128)(2,1)} %add_convert_fusion.refs_9_.refs_3_) | copy-start | bytes 4325380
  598.1 5.6 copy-start.7
  598.1 5.6 copy-start.14
  598.1 6.9 %copy-start.24 = (f32[2,64]{1,0:T(2,128)S(1)}, f32[2,64]{1,0:T(2,128)}, u32[]{:S(2)}) copy-start(f32[2,64]{1,0:T(2,128)} %param.43) | copy-start | bytes 1540
  598.1 6.9 %copy-start.25 = (f32[2,64]{1,0:T(2,128)S(1)}, f32[2,64]{1,0:T(2,128)}, u32[]{:S(2)}) copy-start(f32[2,64]{1,0:T(2,128)} %param.37) | copy-start | bytes 1540
  598.1 8.3 %copy-start.19 = (f32[4,64,128]{2,1,0:T(8,128)S(1)}, f32[4,64,128]{2,1,0:T(8,128)}, u32[]{:S(2)}) copy-start(f32[4,64,128]{2,1,0:T(8,128)} %get-tuple-element.129) | copy-start | bytes 393220
  599.5 21.3 %collective-permute-start.2 = (bf16[704,512]{1,0:T(8,128)(2,1)S(1)}, bf16[704,512]{1,0:T(8,128)(2,1)S(1)}, u32[]{:S(2)}, u32[]{:S(2)}) collective-permute-start(bf16[704,512]{1,0:T(8,128)(2,1)S(1)} %fusion.2), channel_id=1, source_target_pairs={{0,8},{12,4},{1,9},{13,5},{2,10},{14,6},{3,11},{15,7},{16,24},{28,... | collective-permute-start | bytes 2162696 | tf_op jit(solution)/shard_map/ppermute | solution.py:1861
  603.7 12.8 %collective-permute-start.1 = (bf16[256,512]{1,0:T(8,128)(2,1)S(1)}, bf16[256,512]{1,0:T(8,128)(2,1)S(1)}, u32[]{:S(2)}, u32[]{:S(2)}) collective-permute-start(bf16[256,512]{1,0:T(8,128)(2,1)S(1)} %fusion.3), channel_id=1, source_target_pairs={{0,8},{12,4},{1,9},{13,5},{2,10},{14,6},{3,11},{15,7},{16,24},{28,... | collective-permute-start | bytes 786440 | tf_op jit(solution)/shard_map/ppermute | solution.py:1861
  612.3 3.3 copy-start.17
  612.4 3.3 copy-start.20
  612.4 3.3 copy-start.21
  616.5 0.7 copy-start.18
  620.9 0.9 copy-start.16
  621.7 9.9 %copy-start.15 = (bf16[256,2048]{1,0:T(8,128)(2,1)S(1)}, bf16[256,2048]{1,0:T(8,128)(2,1)}, u32[]{:S(2)}) copy-start(bf16[256,2048]{1,0:T(8,128)(2,1)} %get-tuple-element.183) | copy-start | bytes 3145732
  631.6 2.0 copy-start.12

commit v10 on v9

--- a/solution.py
+++ b/solution.py
@@ -66,11 +66,6 @@
 def row_blocks(parts):
     n, h, rows, cols = parts.shape
     return parts.reshape(n, h * rows, cols)
-
-
-def add_swapped(grad, came):
-    keep = lax.dynamic_slice_in_dim(grad, 2 * lax.axis_index("y"), 2, 0)
-    return (keep.astype(jnp.float32) + came.astype(jnp.float32)).astype(jnp.bfloat16)
 
 
 def for_partner(part, deep):
@@ -269,21 +264,45 @@
 
 
 class Swap:
+    alias = {}
+
     def __init__(self, grad):
+        half = (2,) + grad.shape[1:]
         self.inputs = [grad]
-        self.outputs = [jax.ShapeDtypeStruct((2,) + grad.shape[1:], grad.dtype)]
-        self.sems = [1, 1]
-        self.alias = {}
-
-    def copy(self, ins, outs, sems):
-        (src,), (dst,), (send, recv) = ins, outs, sems
-        return swap_copy(src, dst, send.at[0], recv.at[0])
-
-    def begin(self, ins, outs, sems):
-        self.copy(ins, outs, sems).start()
-
-    def finish(self, ins, outs, sems):
-        self.copy(ins, outs, sems).wait()
+        self.outputs = [jax.ShapeDtypeStruct(half, grad.dtype)]
+        self.sems = [4]
+        self.scratch = [pltpu.VMEM(half, grad.dtype)] * 2
+
+    def copies(self, ins, outs, sems, scratch):
+        (grad,), (out,), (sem,), (came, kept) = ins, outs, sems, scratch
+        mine = grad.at[pl.ds(2 * lax.axis_index("y"), 2)]
+        return (
+            swap_copy(grad, came, sem.at[0], sem.at[1]),
+            pltpu.make_async_copy(mine, kept, sem.at[2]),
+            pltpu.make_async_copy(kept, out, sem.at[3]),
+        )
+
+    def begin(self, *refs):
+        swap, keep, _ = self.copies(*refs)
+        swap.start()
+        keep.start()
+
+    def finish(self, *refs):
+        came, kept = refs[3]
+        swap, keep, back = self.copies(*refs)
+        keep.wait()
+        swap.wait_recv()
+        for n in range(2):
+
+            @pl.loop(0, kept.shape[1] // 64)
+            def _(strip):
+                at = pl.ds(pl.multiple_of(strip * 64, 64), 64)
+                total = kept[n, at].astype(jnp.float32) + came[n, at].astype(jnp.float32)
+                kept[n, at] = total.astype(kept.dtype)
+
+        back.start()
+        swap.wait_send()
+        back.wait()
 
 
 class Move:
@@ -1357,15 +1376,17 @@
         self.heads = heads
         packed = given["kt"].shape
         rows = (packed[0], packed[2], HD)
-        part = (4, 2, 2 * HD, KEYS_BACK // 4)
-        self.sems = [4, 4]
+        part = (4, 2, HD, KEYS_BACK // 4)
+        self.sems = [4, 4, 4, 4]
         self.scratch = []
         scratch = dict(
             k_s=pltpu.VMEM(rows, jnp.bfloat16),
             v_s=pltpu.VMEM(rows, jnp.bfloat16),
             dk_s=pltpu.VMEM(rows, jnp.float32),
             dv_s=pltpu.VMEM(rows, jnp.float32),
-            early=pltpu.VMEM(part, jnp.bfloat16),
+            early=pltpu.VMEM((2,) + part, jnp.bfloat16),
+            mate=pltpu.VMEM(part, jnp.bfloat16),
+            joint=pltpu.VMEM(part, jnp.bfloat16),
             came=pltpu.VMEM(part, jnp.bfloat16),
         )
         self.name(given, {}, results, scratch, {}, ())
@@ -1411,8 +1432,8 @@
 
     def finish(self, ins, outs, sems, scratch, early, late, middle):
         refs = self.bind(ins, outs, sems, scratch)
-        send, recv = sems[:2]
-        z_high = lax.axis_index("zh")
+        send, recv, x_send, x_recv = sems[:4]
+        z_high, x_at = lax.axis_index("zh"), lax.axis_index("x")
         half = KEYS_BACK // 4
         early()
         self.ready(refs, self.given)
@@ -1425,14 +1446,29 @@
 
         def share(n):
             return far_copy(
-                refs.early.at[n], refs.came.at[n], send.at[n], recv.at[n], flipped("zh")
+                refs.joint.at[n], refs.came.at[n], send.at[n], recv.at[n], flipped("zh")
+            )
+
+        def pool(n):
+            return far_copy(
+                refs.early.at[1 - x_at, n],
+                refs.mate.at[n],
+                x_send.at[n],
+                x_recv.at[n],
+                flipped("x"),
             )
 
         def give(n):
             rows = slice(n * half, (n + 1) * half)
             for pack in range(2):
-                refs.early[n, pack, :HD] = refs.dk_s[pack, rows].T.astype(jnp.bfloat16)
-                refs.early[n, pack, HD:] = refs.dv_s[pack, rows].T.astype(jnp.bfloat16)
+                refs.early[0, n, pack] = refs.dk_s[pack, rows].T.astype(jnp.bfloat16)
+                refs.early[1, n, pack] = refs.dv_s[pack, rows].T.astype(jnp.bfloat16)
+            pool(n).start()
+
+        def hand_on(n):
+            pool(n).wait_recv()
+            mine = refs.early[x_at, n].astype(jnp.float32)
+            refs.joint[n] = (mine + refs.mate[n].astype(jnp.float32)).astype(jnp.bfloat16)
             share(n).start()
 
         @pl.loop(0, 8)
@@ -1444,7 +1480,18 @@
                 def _():
                     give(n)
 
+            for n in range(3):
+
+                @pl.when((step == 2 * n + 2) & (z_high == 1))
+                def _():
+                    hand_on(n)
+
         refs.flush("dq").start()
+
+        @pl.when(z_high == 1)
+        def _():
+            hand_on(3)
+
         middle()
         for pack in range(2):
             for n in range(4):
@@ -1458,9 +1505,9 @@
                         share(n).wait_recv()
 
                 key_grad, value_grad = refs.dk_s[pack, rows].T, refs.dv_s[pack, rows].T
-                take = lambda part: jnp.where(z_high == 0, part.astype(jnp.float32), 0.0)
-                key_grad += take(refs.came[n, pack, :HD])
-                value_grad += take(refs.came[n, pack, HD:])
+                extra = refs.came[n, pack].astype(jnp.float32)
+                key_grad += jnp.where((z_high == 0) & (x_at == 0), extra, 0.0)
+                value_grad += jnp.where((z_high == 0) & (x_at == 1), extra, 0.0)
                 front, rear = turned_back(key_grad, refs.cos[:, at], refs.sin[:, at])
                 refs.dpair[:HALF, at] = front.astype(jnp.bfloat16)
                 refs.dpair[HALF:HD, at] = rear.astype(jnp.bfloat16)
@@ -1470,6 +1517,7 @@
         @pl.when(z_high == 1)
         def _():
             for n in range(4):
+                pool(n).wait_send()
                 share(n).wait_send()
 
         self.flushed(refs)
@@ -1725,7 +1773,7 @@
             ),
         )
     )
-    mid_grad, gate_wgrad, up_wgrad, mid_rounded, mlp_sums, down_came = flat(
+    mid_grad, gate_wgrad, up_wgrad, mid_rounded, mlp_sums, down_part = flat(
         run(
             6,
             ScatterRows(
@@ -1757,8 +1805,7 @@
             Swap(down_grad),
         )
     )
-    down_part = add_swapped(down_grad, down_came)
-    attended_grad, output_grad, gate_came, down_deep = flat(
+    attended_grad, output_grad, gate_part, down_deep = flat(
         run(
             7,
             GatherRows(
@@ -1775,8 +1822,7 @@
             Move(down_part, "zh", not_home),
         )
     )
-    gate_part = add_swapped(gate_wgrad, gate_came)
-    query_back, pair_back, output_came, up_came, gate_deep, down_got = flat(
+    query_back, pair_back, output_part, up_part, gate_deep, down_got = flat(
         run(
             8,
             AttentionBack(
@@ -1800,8 +1846,6 @@
             Move(for_partner(down_part, down_deep), "c", at_home),
         )
     )
-    output_part = add_swapped(output_grad, output_came)
-    up_part = add_swapped(up_wgrad, up_came)
     quarter = D // 4
     last = Last(h_size, devices, pair_rows, gain_cols, head_of)
     half_q = pltpu.VMEM((2, quarter, width), jnp.bfloat16)

time: 640 us -> 627 us (0.980)
  other arithmetic: 25 us -> 17.6 us
    convert_element_type x4 -> x0, other arithmetic: 9.58 us -> none  [add_swapped(): (keep.astype(jnp.float32) + came.astype(jnp.float32)).astype(jnp.bfloat16)]
where the time goes in v10:
time: 627 us; the launch traced here: 622 us
  Pallas kernels  589 us (94%)
  other arithmetic  17.6 us (3%)
  local copies, waits for them, and re-layouts  9.72 us (2%)
    pallas_call x9, Pallas kernels, run(): pl.pallas_call(kernel, in_specs=in_specs, out_specs=out_specs, out_shape=...  567 us
    pallas_call x4, Pallas kernels, adam_shard(): pl.pallas_call(functools.partial(adam_kernel, rate, DECAY, groups), grid_...  22.3 us
  transfers between devices with their start and end apart: 3, of which 0 were waited for; matrix products, arithmetic and copies ran while one was open for 2% of the time, Pallas kernels for 2%

profile of v10, /device:TPU:0, one launch (start us, length us, event | category | flops | bytes accessed | tf_op | source)
XLA Modules:
  0.0 622.1 jit_solution(3246700541355570005)
XLA Ops:
  0.7 0.5 collective-permute-start
  1.2 0.9 convert.15
  2.1 0.1 reshape.169
  2.2 0.1 copy.51
  2.3 0.1 reshape.170
  2.5 1.8 convert_bitcast_fusion.2.refs_1_
  4.2 1.9 convert_bitcast_fusion.1.refs_5_
  6.2 0.9 convert_bitcast_fusion.refs_5_
  7.1 0.2 bitcast_convert_fusion
  7.3 1.2 fusion.13
  8.5 0.3 dynamic_update_slice.5
  8.8 0.6 pad_maximum_fusion.refs_0_
  9.5 0.2 fusion.5
  9.7 0.1 subtract_bitcast_fusion
  9.7 0.6 copy.48
  10.4 1.8 multiply_sine_fusion
  12.2 88.2 %shard_map.365 = (bf16[32,80,128]{2,1,0:T(8,128)(2,1)}, bf16[4,1,512,256]{3,2,1,0:T(8,128)(2,1)}, f32[16,2048]{1,0:T(8,128)}, bf16[8,256,2048]{2,1,0:T(8,128)(2,...) custom-call(bf16[4,80,128]{2,1,0:T(8,128)(2,1)} %pad_maximum_fusion., ...), custom_call_target="tpu_custom_call" | custom-call | tf_op jit(solution)/shard_map/pallas_call | solution.py:869
  100.4 1.9 slice.13
  102.3 63.7 %shard_map.366 = (bf16[128,2048]{1,0:T(8,128)(2,1)}, bf16[8,256,2048]{2,1,0:T(8,128)(2,1)}, bf16[256,2048]{1,0:T(8,128)(2,1)}, f32[2,4,1024]{2,1,0:T(4,128)}, bf...) custom-call(bf16[128,2048]{1,0:T(8,128)(2,1)} %get-tuple-element.83., ...), custom_call_target="tpu_custom_call", output_to_operand_aliasing={{6}: (5, {}), {7}: (6, {})} | custom-call | tf_op jit(solution)/shard_map/pallas_call | solution.py:869
  166.0 66.8 %shard_map.367 = (f32[256,2048]{1,0:T(8,128)}, bf16[256,2048]{1,0:T(8,128)(2,1)}, bf16[4,1,704,512]{3,2,1,0:T(8,128)(2,1)}, bf16[4,1,704,512]{3,2,1,0:T(8,128)(2,1)}) custom-call(bf16[256,2048]{1,0:T(8,128)(2,1)} %get-tuple-element.87.refs_0_.refs_1_, bf16[4,256,512]{2,1,0:T(8,128)(2,1)} %bitcast.67, ...), custom_call_target="tpu_custom_call", output_to_operand_aliasing={{2}: (4, {})} | custom-call | tf_op jit(solution)/shard_map/pallas_call | solution.py:869
  232.8 50.3 %shard_map.368 = (bf16[8,256,2048]{2,1,0:T(8,128)(2,1)}, bf16[8,256,704]{2,1,0:T(8,128)(2,1)}, bf16[8,256,704]{2,1,0:T(8,128)(2,1)}, bf16[8,256,704]{2,1,0:T(8,128)(2,1)}) custom-call(bf16[256,2048]{1,0:T(8,128)(2,1)} %get-tuple-element.91.refs_0_, bf16[4,704,512]{2,1,0:T(8,128)(2,1)} %bitcast.62, bf16[4,704,512]{2,1,0:T(8,128)(2,1)} %bitcast.64), custom_call_target="tpu_custom_call" | custom-call | tf_op jit(solution)/shard_map/pallas_call | solution.py:869
  283.1 47.5 %shard_map.369 = (bf16[8,256,704]{2,1,0:T(8,128)(2,1)}, bf16[8,256,704]{2,1,0:T(8,128)(2,1)}, bf16[4,704,512]{2,1,0:T(8,128)(2,1)}, bf16[256,2048]{1,0:T(8,128)(2,1)}) custom-call(bf16[8,256,704]{2,1,0:T(8,128)(2,1)} %get-tuple-element.94.refs_0_, bf16[4,704,512]{2,1,0:T(8,128)(2,1)} %bitcast.70, bf16[8,256,704]{2,1,0:T(8,128)(2,1)} %get-tuple-element.96.refs_2_, ...), custom_call_target="tpu_custom_call" | custom-call | tf_op jit(solution)/shard_map/pallas_call | solution.py:869
  330.5 53.4 %shard_map.370 = (f32[256,2048]{1,0:T(8,128)}, bf16[4,704,512]{2,1,0:T(8,128)(2,1)}, bf16[4,704,512]{2,1,0:T(8,128)(2,1)}, bf16[256,2048]{1,0:T(8,128)(2,1)}, f3...) custom-call(bf16[8,256,704]{2,1,0:T(8,128)(2,1)} %get-tuple-element.101.refs_0_, ...), custom_call_target="tpu_custom_call" | custom-call | tf_op jit(solution)/shard_map/pallas_call | solution.py:869
  384.0 59.3 %shard_map.371 = (bf16[256,2048]{1,0:T(8,128)(2,1)}, bf16[4,256,512]{2,1,0:T(8,128)(2,1)}, bf16[2,704,512]{2,1,0:T(8,128)(2,1)}, bf16[2,704,512]{2,1,0:T(8,128)(2,1)}) custom-call(bf16[256,2048]{1,0:T(8,128)(2,1)} %get-tuple-element.105.refs_0_, bf16[256,2048]{1,0:T(8,128)(2,1)} %get-tuple-element.87.refs_0_.refs_1_, bf16[4,256,512]{2,1,0:T(8,128)(2,1)} %bitcast.68, ...), custom_call_target="tpu_custom_call" | custom-call | tf_op jit(solution)/shard_map/pallas_call | solution.py:869
  443.3 2.2 fusion.refs_12_
  445.5 52.5 %shard_map.372 = (bf16[256,2048]{1,0:T(8,128)(2,1)}, bf16[128,2048]{1,0:T(8,128)(2,1)}, bf16[2,256,512]{2,1,0:T(8,128)(2,1)}, bf16[2,704,512]{2,1,0:T(8,128)(2,1...) custom-call(bf16[256,2048]{1,0:T(8,128)(2,1)} %get-tuple-element.84.refs_2_.refs_0_, ...), custom_call_target="tpu_custom_call" | custom-call | tf_op jit(solution)/shard_map/pallas_call | solution.py:869
  498.0 2.2 fusion.1.refs_11_
  500.2 84.8 %shard_map.373 = (f32[256,2048]{1,0:T(8,128)}, bf16[512,256]{1,0:T(8,128)(2,1)}, f32[4,64,128]{2,1,0:T(8,128)}, f32[16,128]{1,0:T(8,128)}, bf16[2,704,512]{2,1,0...) custom-call(bf16[256,2048]{1,0:T(8,128)(2,1)} %get-tuple-element.116.refs_0_, ...), custom_call_target="tpu_custom_call" | custom-call | tf_op jit(solution)/shard_map/pallas_call | solution.py:869
  585.0 1.4 fusion.2
  586.4 2.2 collective-permute-start.2
  588.6 0.6 pad_add_fusion.place_ref
  589.9 0.6 maximum_divide_fusion.fix_ref
  590.6 0.1 fusion.3
  590.6 1.3 collective-permute-start.1
  592.0 1.3 add_subtract_fusion
  593.3 0.2 reshape.176
  593.5 0.2 copy.46
  593.7 0.2 reshape.177
  593.8 5.4 shard_map.377
  599.3 3.3 shard_map.374
  602.7 0.8 multiply_subtract_fusion
  603.5 0.7 copy-done.11
  604.2 3.6 shard_map.375
  607.8 0.9 copy-done.9
  608.7 9.9 %shard_map.376 = (f32[2,704,512]{2,1,0:T(8,128)}, f32[2,704,512]{2,1,0:T(8,128)}, f32[2,704,512]{2,1,0:T(8,128)}) custom-call(s32[2]{0:T(128)} %pad_add_fusion.place_ref, f32[2]{0:T(128)} %maximum_divide_fusion.fix_ref, f32[2,704,512]{2,1,0:T(8,128)} %bitcast.66, f32[2,704,512]{2,1,0:T(8,128)} %bitcast.71, f32[2,704,512]{2,1,0:T(8,128)} %bitcast.72, ...), custom_call_target="tpu_custom_call" | custom-call | tf_op jit(solution)/shard_map/pallas_call | solution.py:119
  618.6 1.0 copy.60
  619.5 1.0 copy-done.6
  620.5 1.3 copy.61
  (44 shorter events, 0.1 us)
Async XLA Ops:
  0.7 5.5 copy-start.4
  0.7 8.8 %collective-permute-start = (s32[1,2048]{1,0:T(1,128)}, s32[1,2048]{1,0:T(1,128)S(1)}, u32[]{:S(2)}, u32[]{:S(2)}) collective-permute-start(s32[1,2048]{1,0:T(1,128)} %param.24), channel_id=1, source_target_pairs={{0,8},{8,0},{1,9},{9,1},{2,10},{10,2},{3,11},{11,3},{4,12},{12,4},... | collective-permute-start | bytes 24584 | tf_op jit(solution)/shard_map/ppermute | solution.py:1613
  4.2 2.9 copy-start
  7.3 1.2 copy-start.16
  7.3 2.1 copy-start.15
  384.0 59.3 %copy-start.1 = (bf16[2,704,512]{2,1,0:T(8,128)(2,1)S(1)}, bf16[2,704,512]{2,1,0:T(8,128)(2,1)}, u32[]{:S(2)}) copy-start(bf16[2,704,512]{2,1,0:T(8,128)(2,1)} %get-tuple-element.107.refs_4_.refs_0_) | copy-start | bytes 4325380
  445.5 52.5 %copy-start.2 = (bf16[2,704,512]{2,1,0:T(8,128)(2,1)S(1)}, bf16[2,704,512]{2,1,0:T(8,128)(2,1)}, u32[]{:S(2)}) copy-start(bf16[2,704,512]{2,1,0:T(8,128)(2,1)} %get-tuple-element.114.refs_11_.refs_0_) | copy-start | bytes 4325380
  500.2 84.8 %copy-start.3 = (bf16[2,704,512]{2,1,0:T(8,128)(2,1)S(1)}, bf16[2,704,512]{2,1,0:T(8,128)(2,1)}, u32[]{:S(2)}) copy-start(bf16[2,704,512]{2,1,0:T(8,128)(2,1)} %get-tuple-element.123.refs_9_.refs_3_) | copy-start | bytes 4325380
  585.0 5.6 copy-start.5
  585.0 5.6 copy-start.7
  585.0 6.9 %copy-start.17 = (f32[2,64]{1,0:T(2,128)S(1)}, f32[2,64]{1,0:T(2,128)}, u32[]{:S(2)}) copy-start(f32[2,64]{1,0:T(2,128)} %param.43) | copy-start | bytes 1540
  585.0 6.9 %copy-start.18 = (f32[2,64]{1,0:T(2,128)S(1)}, f32[2,64]{1,0:T(2,128)}, u32[]{:S(2)}) copy-start(f32[2,64]{1,0:T(2,128)} %param.37) | copy-start | bytes 1540
  585.0 8.3 %copy-start.12 = (f32[4,64,128]{2,1,0:T(8,128)S(1)}, f32[4,64,128]{2,1,0:T(8,128)}, u32[]{:S(2)}) copy-start(f32[4,64,128]{2,1,0:T(8,128)} %get-tuple-element.129) | copy-start | bytes 393220
  586.4 21.4 %collective-permute-start.2 = (bf16[704,512]{1,0:T(8,128)(2,1)S(1)}, bf16[704,512]{1,0:T(8,128)(2,1)S(1)}, u32[]{:S(2)}, u32[]{:S(2)}) collective-permute-start(bf16[704,512]{1,0:T(8,128)(2,1)S(1)} %fusion.2), channel_id=1, source_target_pairs={{0,8},{12,4},{1,9},{13,5},{2,10},{14,6},{3,11},{15,7},{16,24},{28,... | collective-permute-start | bytes 2162696 | tf_op jit(solution)/shard_map/ppermute | solution.py:1905
  590.6 12.8 %collective-permute-start.1 = (bf16[256,512]{1,0:T(8,128)(2,1)S(1)}, bf16[256,512]{1,0:T(8,128)(2,1)S(1)}, u32[]{:S(2)}, u32[]{:S(2)}) collective-permute-start(bf16[256,512]{1,0:T(8,128)(2,1)S(1)} %fusion.3), channel_id=1, source_target_pairs={{0,8},{12,4},{1,9},{13,5},{2,10},{14,6},{3,11},{15,7},{16,24},{28,... | collective-permute-start | bytes 786440 | tf_op jit(solution)/shard_map/ppermute | solution.py:1905
  599.3 3.3 copy-start.10
  599.3 3.3 copy-start.13
  599.3 3.3 copy-start.14
  603.5 0.7 copy-start.11
  607.8 0.9 copy-start.9
  608.7 9.9 %copy-start.8 = (bf16[256,2048]{1,0:T(8,128)(2,1)S(1)}, bf16[256,2048]{1,0:T(8,128)(2,1)}, u32[]{:S(2)}) copy-start(bf16[256,2048]{1,0:T(8,128)(2,1)} %get-tuple-element.183) | copy-start | bytes 3145732
  618.5 2.0 copy-start.6

commit v11 on v10

--- a/solution.py
+++ b/solution.py
@@ -417,6 +417,7 @@
         onward_first=False,
         keep=True,
         given={},
+        streams={},
         results={},
         by_block=(),
         scratch={},
@@ -439,7 +440,8 @@
         if self.keep:
             self.outputs = [jax.ShapeDtypeStruct(gathered, block.dtype)]
             self.sems += [8]
-        self.name(given, {}, results, scratch, {}, by_block)
+        self.sems += [2]
+        self.name(given, streams, results, scratch, {}, by_block)
 
     def where(self, outs, scratch):
         return scratch[0] if self.in_vmem else outs[0]
@@ -455,6 +457,7 @@
     def finish(self, ins, outs, sems, scratch, early, late, middle):
         src, dst, (send, recv, local) = ins[0], self.where(outs, scratch), sems[:3]
         refs = self.bind(ins, outs, sems, scratch)
+        refs.stream_sems = sems[-3]
         core, z_low, x_at = (lax.axis_index(a) for a in ("c", "zl", "x"))
         own = group_index(core, z_low, x_at)
         beside = group_index(core, z_low, 1 - x_at)
@@ -1099,12 +1102,29 @@
     weight_grad(h_size, refs, "rows", refs.dgate, "gwg")
 
 
-def gateup_fill_two(h_size, refs):
-    weight_grad(h_size, refs, "rows", refs.dup, "gwu")
+def rows_fetch(refs, n):
+    slot = lax.rem(n, 2)
+    return pltpu.make_async_copy(refs.stream_rows.at[n], refs.held.at[slot], refs.stream_sems.at[slot])
 
 
 def output_before(refs):
+    rows_fetch(refs, 0).start()
     refs.total[...] = jnp.zeros_like(refs.total)
+    refs.up_total[...] = jnp.zeros_like(refs.up_total)
+
+
+def up_step(h_size, refs):
+    n = refs.step
+
+    @pl.when(n < 7)
+    def _():
+        rows_fetch(refs, n + 1).start()
+
+    left_t = flip(refs.dup[n]).astype(jnp.bfloat16)
+    rows_fetch(refs, n).wait()
+    rows = refs.held.at[lax.rem(n, 2)]
+    for j in range(4):
+        refs.up_total[j] += dot_nn(left_t, cols_at(rows, j, h_size))
 
 
 def output_work(h_size, refs, rows, block):
@@ -1116,12 +1136,15 @@
         grad += dot_nt(part, refs.wo[j])
         refs.total[j] += dot_nn(mixed_t, part)
     refs.do[:, at] = grad.T.astype(jnp.bfloat16)
+    up_step(h_size, refs)
 
 
 def output_after(refs):
     refs.gwo[...] = refs.total[...].astype(jnp.bfloat16)
     refs.flush("gwo").start()
     refs.flush("do").start()
+    refs.gwu[...] = refs.up_total[...].astype(jnp.bfloat16)
+    refs.flush("gwu").start()
 
 
 def query_after(refs):
@@ -1724,13 +1747,13 @@
                 summed=attn_summed,
             ),
             Pass(up_parts),
-            SpreadAll(own_shard(down_weight, h_size)),
+            Spread(own_shard(down_weight, h_size)),
         )
     )
     up_full = col_blocks(up_parts)
 
     hidden_shape = shape(8, block_rows, units)
-    rows_two, hidden_mlp, by_gate, by_up = flat(
+    rows_two, hidden_mlp, by_gate, by_up, down_parts = flat(
         run(
             4,
             GatherRows(
@@ -1740,6 +1763,7 @@
                 by_block=("hid", "by_gate", "by_up"),
                 work=functools.partial(gateup_work, h_size),
             ),
+            Pass(down_parts),
         )
     )
     down_full = col_blocks(down_parts)
@@ -1773,7 +1797,7 @@
             ),
         )
     )
-    mid_grad, gate_wgrad, up_wgrad, mid_rounded, mlp_sums, down_part = flat(
+    mid_grad, gate_wgrad, mid_rounded, mlp_sums, down_part = flat(
         run(
             6,
             ScatterRows(
@@ -1793,27 +1817,32 @@
                 streams=dict(rows=rows_two),
                 results=dict(
                     gwg=whole_grad,
-                    gwu=whole_grad,
                     dat=shape(block_rows, D),
                     gain_sums=shape(8, D, kind=jnp.float32),
                 ),
                 summed=mlp_norm_summed,
                 scratch=dict(total=sums),
                 fill_one=functools.partial(gateup_fill_one, h_size),
-                fill_two=functools.partial(gateup_fill_two, h_size),
             ),
             Swap(down_grad),
         )
     )
-    attended_grad, output_grad, gate_part, down_deep = flat(
+    attended_grad, output_grad, up_wgrad, gate_part, down_deep = flat(
         run(
             7,
             GatherRows(
                 mid_rounded,
                 keep=False,
-                given=dict(o=attended_t, wo=output_full),
-                results=dict(do=shape(width, group_rows), gwo=shape(*output_full.shape)),
-                scratch=dict(total=pltpu.VMEM(output_full.shape, jnp.float32)),
+                given=dict(o=attended_t, wo=output_full, dup=up_grad),
+                streams=dict(stream_rows=rows_two),
+                results=dict(
+                    do=shape(width, group_rows), gwo=shape(*output_full.shape), gwu=whole_grad
+                ),
+                scratch=dict(
+                    total=pltpu.VMEM(output_full.shape, jnp.float32),
+                    up_total=sums,
+                    held=pltpu.VMEM((2, block_rows, D), jnp.bfloat16),
+                ),
                 before=output_before,
                 work=functools.partial(output_work, h_size),
                 after=output_after,

time: 627 us -> 628 us (level)
  no operation moved by 1% of the time
where the time goes in v11:
time: 628 us; the launch traced here: 624 us
  Pallas kernels  591 us (94%)
  other arithmetic  17.6 us (3%)
  local copies, waits for them, and re-layouts  9.72 us (2%)
    pallas_call x9, Pallas kernels, run(): pl.pallas_call(kernel, in_specs=in_specs, out_specs=out_specs, out_shape=...  568 us
    pallas_call x4, Pallas kernels, adam_shard(): pl.pallas_call(functools.partial(adam_kernel, rate, DECAY, groups), grid_...  22.2 us
  transfers between devices with their start and end apart: 3, of which 0 were waited for; matrix products, arithmetic and copies ran while one was open for 2% of the time, Pallas kernels for 2%

profile of v11, /device:TPU:0, one launch (start us, length us, event | category | flops | bytes accessed | tf_op | source)
XLA Modules:
  0.0 623.9 jit_solution(581857277151541627)
XLA Ops:
  0.7 0.5 collective-permute-start
  1.2 0.9 convert.15
  2.1 0.1 reshape.169
  2.2 0.1 copy.52
  2.3 0.1 reshape.170
  2.5 1.8 convert_bitcast_fusion.2.refs_1_
  4.2 1.9 convert_bitcast_fusion.1.refs_5_
  6.2 0.9 convert_bitcast_fusion.refs_5_
  7.1 0.2 bitcast_convert_fusion
  7.3 1.2 fusion.13
  8.5 0.3 dynamic_update_slice.5
  8.8 0.6 pad_maximum_fusion.refs_0_
  9.5 0.2 fusion.5
  9.7 0.1 subtract_bitcast_fusion
  9.7 0.6 copy.49
  10.4 1.8 multiply_sine_fusion
  12.2 88.2 %shard_map.365 = (bf16[32,80,128]{2,1,0:T(8,128)(2,1)}, bf16[4,1,512,256]{3,2,1,0:T(8,128)(2,1)}, f32[16,2048]{1,0:T(8,128)}, bf16[8,256,2048]{2,1,0:T(8,128)(2,...) custom-call(bf16[4,80,128]{2,1,0:T(8,128)(2,1)} %pad_maximum_fusion., ...), custom_call_target="tpu_custom_call" | custom-call | tf_op jit(solution)/shard_map/pallas_call | solution.py:872
  100.4 1.9 slice.13
  102.3 63.7 %shard_map.366 = (bf16[128,2048]{1,0:T(8,128)(2,1)}, bf16[8,256,2048]{2,1,0:T(8,128)(2,1)}, bf16[256,2048]{1,0:T(8,128)(2,1)}, f32[2,4,1024]{2,1,0:T(4,128)}, bf...) custom-call(bf16[128,2048]{1,0:T(8,128)(2,1)} %get-tuple-element.84., ...), custom_call_target="tpu_custom_call", output_to_operand_aliasing={{6}: (5, {}), {7}: (6, {})} | custom-call | tf_op jit(solution)/shard_map/pallas_call | solution.py:872
  166.0 66.8 %shard_map.367 = (f32[256,2048]{1,0:T(8,128)}, bf16[256,2048]{1,0:T(8,128)(2,1)}, bf16[4,1,704,512]{3,2,1,0:T(8,128)(2,1)}, bf16[4,1,704,512]{3,2,1,0:T(8,128)(2,1)}) custom-call(bf16[256,2048]{1,0:T(8,128)(2,1)} %get-tuple-element.88.refs_0_.refs_1_, bf16[4,256,512]{2,1,0:T(8,128)(2,1)} %bitcast.68, ...), custom_call_target="tpu_custom_call", output_to_operand_aliasing={{2}: (4, {})} | custom-call | tf_op jit(solution)/shard_map/pallas_call | solution.py:872
  232.8 49.7 %shard_map.368 = (bf16[8,256,2048]{2,1,0:T(8,128)(2,1)}, bf16[8,256,704]{2,1,0:T(8,128)(2,1)}, bf16[8,256,704]{2,1,0:T(8,128)(2,1)}, bf16[8,256,704]{2,1,0:T(8,128)(2,1)}, bf16[4,1,704,512]{3,2,1,0:T(8,128)(2,1)}) custom-call(bf16[256,2048]{1,0:T(8,128)(2,1)} %get-tuple-element.92.refs_0_, ...), custom_call_target="tpu_custom_call", output_to_operand_aliasing={{4}: (3, {})} | custom-call | tf_op jit(solution)/shard_map/pallas_call | solution.py:872
  282.5 48.1 %shard_map.369 = (bf16[8,256,704]{2,1,0:T(8,128)(2,1)}, bf16[8,256,704]{2,1,0:T(8,128)(2,1)}, bf16[4,704,512]{2,1,0:T(8,128)(2,1)}, bf16[256,2048]{1,0:T(8,128)(2,1)}) custom-call(bf16[8,256,704]{2,1,0:T(8,128)(2,1)} %get-tuple-element.96.refs_0_, bf16[4,704,512]{2,1,0:T(8,128)(2,1)} %bitcast.66, bf16[8,256,704]{2,1,0:T(8,128)(2,1)} %get-tuple-element.98.refs_2_, ...), custom_call_target="tpu_custom_call" | custom-call | tf_op jit(solution)/shard_map/pallas_call | solution.py:872
  330.6 53.3 %shard_map.370 = (f32[256,2048]{1,0:T(8,128)}, bf16[4,704,512]{2,1,0:T(8,128)(2,1)}, bf16[256,2048]{1,0:T(8,128)(2,1)}, f32[8,2048]{1,0:T(8,128)}, bf16[2,704,512]{2,1,0:T(8,128)(2,1)}) custom-call(bf16[8,256,704]{2,1,0:T(8,128)(2,1)} %get-tuple-element.103.refs_0_, bf16[8,256,704]{2,1,0:T(8,128)(2,1)} %get-tuple-element.104.refs_1_.refs_3_, ...), custom_call_target="tpu_custom_call" | custom-call | tf_op jit(solution)/shard_map/pallas_call | solution.py:872
  383.9 62.3 %shard_map.371 = (bf16[256,2048]{1,0:T(8,128)(2,1)}, bf16[4,256,512]{2,1,0:T(8,128)(2,1)}, bf16[4,704,512]{2,1,0:T(8,128)(2,1)}, bf16[2,704,512]{2,1,0:T(8,128)(2,1)}, bf16[2,704,512]{2,1,0:T(8,128)(2,1)}) custom-call(bf16[256,2048]{1,0:T(8,128)(2,1)} %get-tuple-element.107.refs_0_, bf16[256,2048]{1,0:T(8,128)(2,1)} %get-tuple-element.88.refs_0_.refs_1_, ...), custom_call_target="tpu_custom_call" | custom-call | tf_op jit(solution)/shard_map/pallas_call | solution.py:872
  446.2 2.2 fusion.refs_12_
  448.3 51.5 %shard_map.372 = (bf16[256,2048]{1,0:T(8,128)(2,1)}, bf16[128,2048]{1,0:T(8,128)(2,1)}, bf16[2,256,512]{2,1,0:T(8,128)(2,1)}, bf16[2,704,512]{2,1,0:T(8,128)(2,1...) custom-call(bf16[256,2048]{1,0:T(8,128)(2,1)} %get-tuple-element.85.refs_2_.refs_0_, ...), custom_call_target="tpu_custom_call" | custom-call | tf_op jit(solution)/shard_map/pallas_call | solution.py:872
  499.9 2.2 fusion.1.refs_11_
  502.0 84.8 %shard_map.373 = (f32[256,2048]{1,0:T(8,128)}, bf16[512,256]{1,0:T(8,128)(2,1)}, f32[4,64,128]{2,1,0:T(8,128)}, f32[16,128]{1,0:T(8,128)}, bf16[2,704,512]{2,1,0...) custom-call(bf16[256,2048]{1,0:T(8,128)(2,1)} %get-tuple-element.118.refs_0_, ...), custom_call_target="tpu_custom_call" | custom-call | tf_op jit(solution)/shard_map/pallas_call | solution.py:872
  586.9 1.4 fusion.2
  588.3 2.2 collective-permute-start.2
  590.5 0.6 pad_add_fusion.place_ref
  591.8 0.6 maximum_divide_fusion.fix_ref
  592.4 0.1 fusion.3
  592.5 1.3 collective-permute-start.1
  593.8 1.3 add_subtract_fusion
  595.2 0.2 reshape.176
  595.4 0.2 copy.47
  595.6 0.2 reshape.177
  595.7 5.4 shard_map.377
  601.2 3.3 shard_map.374
  604.5 0.8 multiply_subtract_fusion
  605.3 0.7 copy-done.11
  606.0 3.6 shard_map.375
  609.7 0.9 copy-done.9
  610.5 9.9 %shard_map.376 = (f32[2,704,512]{2,1,0:T(8,128)}, f32[2,704,512]{2,1,0:T(8,128)}, f32[2,704,512]{2,1,0:T(8,128)}) custom-call(s32[2]{0:T(128)} %pad_add_fusion.place_ref, f32[2]{0:T(128)} %maximum_divide_fusion.fix_ref, f32[2,704,512]{2,1,0:T(8,128)} %bitcast.67, f32[2,704,512]{2,1,0:T(8,128)} %bitcast.71, f32[2,704,512]{2,1,0:T(8,128)} %bitcast.72, ...), custom_call_target="tpu_custom_call" | custom-call | tf_op jit(solution)/shard_map/pallas_call | solution.py:119
  620.4 1.0 copy.62
  621.4 1.0 copy-done.6
  622.4 1.3 copy.63
  (44 shorter events, 0.1 us)
Async XLA Ops:
  0.7 5.5 copy-start.4
  0.7 8.8 %collective-permute-start = (s32[1,2048]{1,0:T(1,128)}, s32[1,2048]{1,0:T(1,128)S(1)}, u32[]{:S(2)}, u32[]{:S(2)}) collective-permute-start(s32[1,2048]{1,0:T(1,128)} %param.24), channel_id=1, source_target_pairs={{0,8},{8,0},{1,9},{9,1},{2,10},{10,2},{3,11},{11,3},{4,12},{12,4},... | collective-permute-start | bytes 24584 | tf_op jit(solution)/shard_map/ppermute | solution.py:1636
  4.2 2.9 copy-start
  7.3 1.2 copy-start.16
  7.3 2.1 copy-start.15
  383.9 62.3 %copy-start.1 = (bf16[2,704,512]{2,1,0:T(8,128)(2,1)S(1)}, bf16[2,704,512]{2,1,0:T(8,128)(2,1)}, u32[]{:S(2)}) copy-start(bf16[2,704,512]{2,1,0:T(8,128)(2,1)} %get-tuple-element.109.refs_6_.refs_0_) | copy-start | bytes 4325380
  448.3 51.5 %copy-start.2 = (bf16[2,704,512]{2,1,0:T(8,128)(2,1)S(1)}, bf16[2,704,512]{2,1,0:T(8,128)(2,1)}, u32[]{:S(2)}) copy-start(bf16[2,704,512]{2,1,0:T(8,128)(2,1)} %get-tuple-element.116.refs_11_.refs_0_) | copy-start | bytes 4325380
  502.0 84.8 %copy-start.3 = (bf16[2,704,512]{2,1,0:T(8,128)(2,1)S(1)}, bf16[2,704,512]{2,1,0:T(8,128)(2,1)}, u32[]{:S(2)}) copy-start(bf16[2,704,512]{2,1,0:T(8,128)(2,1)} %get-tuple-element.125.refs_9_.refs_3_) | copy-start | bytes 4325380
  586.8 5.6 copy-start.5
  586.9 5.6 copy-start.7
  586.9 6.9 %copy-start.17 = (f32[2,64]{1,0:T(2,128)S(1)}, f32[2,64]{1,0:T(2,128)}, u32[]{:S(2)}) copy-start(f32[2,64]{1,0:T(2,128)} %param.43) | copy-start | bytes 1540
  586.9 6.9 %copy-start.18 = (f32[2,64]{1,0:T(2,128)S(1)}, f32[2,64]{1,0:T(2,128)}, u32[]{:S(2)}) copy-start(f32[2,64]{1,0:T(2,128)} %param.37) | copy-start | bytes 1540
  586.9 8.3 %copy-start.12 = (f32[4,64,128]{2,1,0:T(8,128)S(1)}, f32[4,64,128]{2,1,0:T(8,128)}, u32[]{:S(2)}) copy-start(f32[4,64,128]{2,1,0:T(8,128)} %get-tuple-element.131) | copy-start | bytes 393220
  588.3 21.4 %collective-permute-start.2 = (bf16[704,512]{1,0:T(8,128)(2,1)S(1)}, bf16[704,512]{1,0:T(8,128)(2,1)S(1)}, u32[]{:S(2)}, u32[]{:S(2)}) collective-permute-start(bf16[704,512]{1,0:T(8,128)(2,1)S(1)} %fusion.2), channel_id=1, source_target_pairs={{0,8},{12,4},{1,9},{13,5},{2,10},{14,6},{3,11},{15,7},{16,24},{28,... | collective-permute-start | bytes 2162696 | tf_op jit(solution)/shard_map/ppermute | solution.py:1934
  592.5 12.8 %collective-permute-start.1 = (bf16[256,512]{1,0:T(8,128)(2,1)S(1)}, bf16[256,512]{1,0:T(8,128)(2,1)S(1)}, u32[]{:S(2)}, u32[]{:S(2)}) collective-permute-start(bf16[256,512]{1,0:T(8,128)(2,1)S(1)} %fusion.3), channel_id=1, source_target_pairs={{0,8},{12,4},{1,9},{13,5},{2,10},{14,6},{3,11},{15,7},{16,24},{28,... | collective-permute-start | bytes 786440 | tf_op jit(solution)/shard_map/ppermute | solution.py:1934
  601.1 3.3 copy-start.10
  601.2 3.3 copy-start.13
  601.2 3.3 copy-start.14
  605.3 0.7 copy-start.11
  609.7 0.9 copy-start.9
  610.5 9.9 %copy-start.8 = (bf16[256,2048]{1,0:T(8,128)(2,1)S(1)}, bf16[256,2048]{1,0:T(8,128)(2,1)}, u32[]{:S(2)}) copy-start(bf16[256,2048]{1,0:T(8,128)(2,1)} %get-tuple-element.185) | copy-start | bytes 3145732
  620.4 2.0 copy-start.6

commit v12 on v10

--- a/solution.py
+++ b/solution.py
@@ -287,7 +287,7 @@
         swap.start()
         keep.start()
 
-    def finish(self, *refs):
+    def middle(self, *refs):
         came, kept = refs[3]
         swap, keep, back = self.copies(*refs)
         keep.wait()
@@ -301,6 +301,9 @@
                 kept[n, at] = total.astype(kept.dtype)
 
         back.start()
+
+    def finish(self, *refs):
+        swap, _, back = self.copies(*refs)
         swap.wait_send()
         back.wait()
 

time: 627 us -> 620 us (0.989)
  no operation moved by 1% of the time
where the time goes in v12:
time: 620 us; the launch traced here: 615 us
  Pallas kernels  583 us (94%)
  other arithmetic  17.6 us (3%)
  local copies, waits for them, and re-layouts  9.72 us (2%)
    pallas_call x9, Pallas kernels, run(): pl.pallas_call(kernel, in_specs=in_specs, out_specs=out_specs, out_shape=...  560 us
    pallas_call x4, Pallas kernels, adam_shard(): pl.pallas_call(functools.partial(adam_kernel, rate, DECAY, groups), grid_...  22.3 us
  transfers between devices with their start and end apart: 3, of which 0 were waited for; matrix products, arithmetic and copies ran while one was open for 2% of the time, Pallas kernels for 2%

profile of v12, /device:TPU:0, one launch (start us, length us, event | category | flops | bytes accessed | tf_op | source)
XLA Modules:
  0.0 615.5 jit_solution(10083419794552420139)
XLA Ops:
  0.7 0.5 collective-permute-start
  1.2 0.9 convert.15
  2.1 0.1 reshape.169
  2.2 0.1 copy.51
  2.3 0.1 reshape.170
  2.5 1.8 convert_bitcast_fusion.2.refs_1_
  4.2 1.9 convert_bitcast_fusion.1.refs_5_
  6.2 0.9 convert_bitcast_fusion.refs_5_
  7.1 0.2 bitcast_convert_fusion
  7.3 1.2 fusion.13
  8.5 0.3 dynamic_update_slice.5
  8.8 0.6 pad_maximum_fusion.refs_0_
  9.5 0.2 fusion.5
  9.7 0.1 subtract_bitcast_fusion
  9.7 0.6 copy.48
  10.4 1.8 multiply_sine_fusion
  12.2 88.2 %shard_map.365 = (bf16[32,80,128]{2,1,0:T(8,128)(2,1)}, bf16[4,1,512,256]{3,2,1,0:T(8,128)(2,1)}, f32[16,2048]{1,0:T(8,128)}, bf16[8,256,2048]{2,1,0:T(8,128)(2,...) custom-call(bf16[4,80,128]{2,1,0:T(8,128)(2,1)} %pad_maximum_fusion., ...), custom_call_target="tpu_custom_call" | custom-call | tf_op jit(solution)/shard_map/pallas_call | solution.py:872
  100.4 1.9 slice.13
  102.3 63.7 %shard_map.366 = (bf16[128,2048]{1,0:T(8,128)(2,1)}, bf16[8,256,2048]{2,1,0:T(8,128)(2,1)}, bf16[256,2048]{1,0:T(8,128)(2,1)}, f32[2,4,1024]{2,1,0:T(4,128)}, bf...) custom-call(bf16[128,2048]{1,0:T(8,128)(2,1)} %get-tuple-element.83., ...), custom_call_target="tpu_custom_call", output_to_operand_aliasing={{6}: (5, {}), {7}: (6, {})} | custom-call | tf_op jit(solution)/shard_map/pallas_call | solution.py:872
  166.0 66.8 %shard_map.367 = (f32[256,2048]{1,0:T(8,128)}, bf16[256,2048]{1,0:T(8,128)(2,1)}, bf16[4,1,704,512]{3,2,1,0:T(8,128)(2,1)}, bf16[4,1,704,512]{3,2,1,0:T(8,128)(2,1)}) custom-call(bf16[256,2048]{1,0:T(8,128)(2,1)} %get-tuple-element.87.refs_0_.refs_1_, bf16[4,256,512]{2,1,0:T(8,128)(2,1)} %bitcast.67, ...), custom_call_target="tpu_custom_call", output_to_operand_aliasing={{2}: (4, {})} | custom-call | tf_op jit(solution)/shard_map/pallas_call | solution.py:872
  232.8 50.3 %shard_map.368 = (bf16[8,256,2048]{2,1,0:T(8,128)(2,1)}, bf16[8,256,704]{2,1,0:T(8,128)(2,1)}, bf16[8,256,704]{2,1,0:T(8,128)(2,1)}, bf16[8,256,704]{2,1,0:T(8,128)(2,1)}) custom-call(bf16[256,2048]{1,0:T(8,128)(2,1)} %get-tuple-element.91.refs_0_, bf16[4,704,512]{2,1,0:T(8,128)(2,1)} %bitcast.62, bf16[4,704,512]{2,1,0:T(8,128)(2,1)} %bitcast.64), custom_call_target="tpu_custom_call" | custom-call | tf_op jit(solution)/shard_map/pallas_call | solution.py:872
  283.1 47.5 %shard_map.369 = (bf16[8,256,704]{2,1,0:T(8,128)(2,1)}, bf16[8,256,704]{2,1,0:T(8,128)(2,1)}, bf16[4,704,512]{2,1,0:T(8,128)(2,1)}, bf16[256,2048]{1,0:T(8,128)(2,1)}) custom-call(bf16[8,256,704]{2,1,0:T(8,128)(2,1)} %get-tuple-element.94.refs_0_, bf16[4,704,512]{2,1,0:T(8,128)(2,1)} %bitcast.70, bf16[8,256,704]{2,1,0:T(8,128)(2,1)} %get-tuple-element.96.refs_2_, ...), custom_call_target="tpu_custom_call" | custom-call | tf_op jit(solution)/shard_map/pallas_call | solution.py:872
  330.5 51.9 %shard_map.370 = (f32[256,2048]{1,0:T(8,128)}, bf16[4,704,512]{2,1,0:T(8,128)(2,1)}, bf16[4,704,512]{2,1,0:T(8,128)(2,1)}, bf16[256,2048]{1,0:T(8,128)(2,1)}, f3...) custom-call(bf16[8,256,704]{2,1,0:T(8,128)(2,1)} %get-tuple-element.101.refs_0_, ...), custom_call_target="tpu_custom_call" | custom-call | tf_op jit(solution)/shard_map/pallas_call | solution.py:872
  382.4 58.2 %shard_map.371 = (bf16[256,2048]{1,0:T(8,128)(2,1)}, bf16[4,256,512]{2,1,0:T(8,128)(2,1)}, bf16[2,704,512]{2,1,0:T(8,128)(2,1)}, bf16[2,704,512]{2,1,0:T(8,128)(2,1)}) custom-call(bf16[256,2048]{1,0:T(8,128)(2,1)} %get-tuple-element.105.refs_0_, bf16[256,2048]{1,0:T(8,128)(2,1)} %get-tuple-element.87.refs_0_.refs_1_, bf16[4,256,512]{2,1,0:T(8,128)(2,1)} %bitcast.68, ...), custom_call_target="tpu_custom_call" | custom-call | tf_op jit(solution)/shard_map/pallas_call | solution.py:872
  440.6 2.2 fusion.refs_12_
  442.7 49.8 %shard_map.372 = (bf16[256,2048]{1,0:T(8,128)(2,1)}, bf16[128,2048]{1,0:T(8,128)(2,1)}, bf16[2,256,512]{2,1,0:T(8,128)(2,1)}, bf16[2,704,512]{2,1,0:T(8,128)(2,1...) custom-call(bf16[256,2048]{1,0:T(8,128)(2,1)} %get-tuple-element.84.refs_2_.refs_0_, ...), custom_call_target="tpu_custom_call" | custom-call | tf_op jit(solution)/shard_map/pallas_call | solution.py:872
  492.5 2.2 fusion.1.refs_11_
  494.7 84.1 %shard_map.373 = (f32[256,2048]{1,0:T(8,128)}, bf16[512,256]{1,0:T(8,128)(2,1)}, f32[4,64,128]{2,1,0:T(8,128)}, f32[16,128]{1,0:T(8,128)}, bf16[2,704,512]{2,1,0...) custom-call(bf16[256,2048]{1,0:T(8,128)(2,1)} %get-tuple-element.116.refs_0_, ...), custom_call_target="tpu_custom_call" | custom-call | tf_op jit(solution)/shard_map/pallas_call | solution.py:872
  578.9 1.4 fusion.2
  580.3 1.7 collective-permute-start.2
  582.0 0.6 pad_add_fusion.place_ref
  583.3 0.6 maximum_divide_fusion.fix_ref
  584.0 0.1 fusion.3
  584.0 1.3 collective-permute-start.1
  585.4 1.3 add_subtract_fusion
  586.7 0.2 reshape.176
  586.9 0.2 copy.46
  587.1 0.2 reshape.177
  587.3 5.4 shard_map.377
  592.8 3.3 shard_map.374
  596.1 0.8 multiply_subtract_fusion
  596.9 0.7 copy-done.11
  597.6 3.6 shard_map.375
  601.2 0.9 copy-done.9
  602.1 9.9 %shard_map.376 = (f32[2,704,512]{2,1,0:T(8,128)}, f32[2,704,512]{2,1,0:T(8,128)}, f32[2,704,512]{2,1,0:T(8,128)}) custom-call(s32[2]{0:T(128)} %pad_add_fusion.place_ref, f32[2]{0:T(128)} %maximum_divide_fusion.fix_ref, f32[2,704,512]{2,1,0:T(8,128)} %bitcast.66, f32[2,704,512]{2,1,0:T(8,128)} %bitcast.71, f32[2,704,512]{2,1,0:T(8,128)} %bitcast.72, ...), custom_call_target="tpu_custom_call" | custom-call | tf_op jit(solution)/shard_map/pallas_call | solution.py:119
  612.0 1.0 copy.60
  613.0 1.0 copy-done.6
  613.9 1.3 copy.61
  (44 shorter events, 0.1 us)
Async XLA Ops:
  0.7 5.5 copy-start.4
  0.7 8.8 %collective-permute-start = (s32[1,2048]{1,0:T(1,128)}, s32[1,2048]{1,0:T(1,128)S(1)}, u32[]{:S(2)}, u32[]{:S(2)}) collective-permute-start(s32[1,2048]{1,0:T(1,128)} %param.24), channel_id=1, source_target_pairs={{0,8},{8,0},{1,9},{9,1},{2,10},{10,2},{3,11},{11,3},{4,12},{12,4},... | collective-permute-start | bytes 24584 | tf_op jit(solution)/shard_map/ppermute | solution.py:1616
  4.2 2.9 copy-start
  7.3 1.2 copy-start.16
  7.3 2.1 copy-start.15
  382.4 58.2 %copy-start.1 = (bf16[2,704,512]{2,1,0:T(8,128)(2,1)S(1)}, bf16[2,704,512]{2,1,0:T(8,128)(2,1)}, u32[]{:S(2)}) copy-start(bf16[2,704,512]{2,1,0:T(8,128)(2,1)} %get-tuple-element.107.refs_4_.refs_0_) | copy-start | bytes 4325380
  442.7 49.8 %copy-start.2 = (bf16[2,704,512]{2,1,0:T(8,128)(2,1)S(1)}, bf16[2,704,512]{2,1,0:T(8,128)(2,1)}, u32[]{:S(2)}) copy-start(bf16[2,704,512]{2,1,0:T(8,128)(2,1)} %get-tuple-element.114.refs_11_.refs_0_) | copy-start | bytes 4325380
  494.7 84.2 %copy-start.3 = (bf16[2,704,512]{2,1,0:T(8,128)(2,1)S(1)}, bf16[2,704,512]{2,1,0:T(8,128)(2,1)}, u32[]{:S(2)}) copy-start(bf16[2,704,512]{2,1,0:T(8,128)(2,1)} %get-tuple-element.123.refs_9_.refs_3_) | copy-start | bytes 4325380
  578.8 5.1 copy-start.5
  578.9 5.1 copy-start.7
  578.9 6.5 %copy-start.17 = (f32[2,64]{1,0:T(2,128)S(1)}, f32[2,64]{1,0:T(2,128)}, u32[]{:S(2)}) copy-start(f32[2,64]{1,0:T(2,128)} %param.43) | copy-start | bytes 1540
  578.9 6.5 %copy-start.18 = (f32[2,64]{1,0:T(2,128)S(1)}, f32[2,64]{1,0:T(2,128)}, u32[]{:S(2)}) copy-start(f32[2,64]{1,0:T(2,128)} %param.37) | copy-start | bytes 1540
  578.9 7.8 %copy-start.12 = (f32[4,64,128]{2,1,0:T(8,128)S(1)}, f32[4,64,128]{2,1,0:T(8,128)}, u32[]{:S(2)}) copy-start(f32[4,64,128]{2,1,0:T(8,128)} %get-tuple-element.129) | copy-start | bytes 393220
  580.3 20.9 %collective-permute-start.2 = (bf16[704,512]{1,0:T(8,128)(2,1)S(1)}, bf16[704,512]{1,0:T(8,128)(2,1)S(1)}, u32[]{:S(2)}, u32[]{:S(2)}) collective-permute-start(bf16[704,512]{1,0:T(8,128)(2,1)S(1)} %fusion.2), channel_id=1, source_target_pairs={{0,8},{12,4},{1,9},{13,5},{2,10},{14,6},{3,11},{15,7},{16,24},{28,... | collective-permute-start | bytes 2162696 | tf_op jit(solution)/shard_map/ppermute | solution.py:1908
  584.0 12.8 %collective-permute-start.1 = (bf16[256,512]{1,0:T(8,128)(2,1)S(1)}, bf16[256,512]{1,0:T(8,128)(2,1)S(1)}, u32[]{:S(2)}, u32[]{:S(2)}) collective-permute-start(bf16[256,512]{1,0:T(8,128)(2,1)S(1)} %fusion.3), channel_id=1, source_target_pairs={{0,8},{12,4},{1,9},{13,5},{2,10},{14,6},{3,11},{15,7},{16,24},{28,... | collective-permute-start | bytes 786440 | tf_op jit(solution)/shard_map/ppermute | solution.py:1908
  592.7 3.3 copy-start.10
  592.7 3.3 copy-start.13
  592.7 3.3 copy-start.14
  596.9 0.7 copy-start.11
  601.2 0.9 copy-start.9
  602.1 9.9 %copy-start.8 = (bf16[256,2048]{1,0:T(8,128)(2,1)S(1)}, bf16[256,2048]{1,0:T(8,128)(2,1)}, u32[]{:S(2)}) copy-start(bf16[256,2048]{1,0:T(8,128)(2,1)} %get-tuple-element.183) | copy-start | bytes 3145732
  612.0 2.0 copy-start.6

commit v13 on v12

--- a/solution.py
+++ b/solution.py
@@ -1278,11 +1278,6 @@
         self.swap(refs).start()
 
     def fill_two(self, refs):
-        @pl.loop(1, self.devices)
-        def _(step):
-            self.send(refs, 0, step).start()
-
-        pltpu.sync_copy(self.pair_part(refs, my_number()), refs.pair_in.at[my_number()])
         self.swap(refs).wait_recv()
         mine = 2 * lax.axis_index("y")
         for n in range(2):
@@ -1292,6 +1287,12 @@
         @pl.when(not_home())
         def _():
             self.deep(refs).start()
+
+        @pl.loop(1, self.devices)
+        def _(step):
+            self.send(refs, 0, step).start()
+
+        pltpu.sync_copy(self.pair_part(refs, my_number()), refs.pair_in.at[my_number()])
 
     def summed(self, refs, out):
         refs.sums[...] = jnp.zeros_like(refs.sums)

time: 620 us -> 620 us (level)
  no operation moved by 1% of the time
where the time goes in v13:
time: 620 us; the launch traced here: 615 us
  Pallas kernels  583 us (94%)
  other arithmetic  17.6 us (3%)
  local copies, waits for them, and re-layouts  9.72 us (2%)
    pallas_call x9, Pallas kernels, run(): pl.pallas_call(kernel, in_specs=in_specs, out_specs=out_specs, out_shape=...  560 us
    pallas_call x4, Pallas kernels, adam_shard(): pl.pallas_call(functools.partial(adam_kernel, rate, DECAY, groups), grid_...  22.3 us
  transfers between devices with their start and end apart: 3, of which 0 were waited for; matrix products, arithmetic and copies ran while one was open for 2% of the time, Pallas kernels for 2%

profile of v13, /device:TPU:0, one launch (start us, length us, event | category | flops | bytes accessed | tf_op | source)
XLA Modules:
  0.0 615.5 jit_solution(14186001161943365989)
XLA Ops:
  0.7 0.5 collective-permute-start
  1.2 0.9 convert.15
  2.1 0.1 reshape.169
  2.2 0.1 copy.51
  2.3 0.1 reshape.170
  2.5 1.8 convert_bitcast_fusion.2.refs_1_
  4.2 1.9 convert_bitcast_fusion.1.refs_5_
  6.2 0.9 convert_bitcast_fusion.refs_5_
  7.1 0.2 bitcast_convert_fusion
  7.3 1.2 fusion.13
  8.5 0.3 dynamic_update_slice.5
  8.8 0.6 pad_maximum_fusion.refs_0_
  9.5 0.2 fusion.5
  9.7 0.1 subtract_bitcast_fusion
  9.7 0.6 copy.48
  10.4 1.8 multiply_sine_fusion
  12.2 88.2 %shard_map.365 = (bf16[32,80,128]{2,1,0:T(8,128)(2,1)}, bf16[4,1,512,256]{3,2,1,0:T(8,128)(2,1)}, f32[16,2048]{1,0:T(8,128)}, bf16[8,256,2048]{2,1,0:T(8,128)(2,...) custom-call(bf16[4,80,128]{2,1,0:T(8,128)(2,1)} %pad_maximum_fusion., ...), custom_call_target="tpu_custom_call" | custom-call | tf_op jit(solution)/shard_map/pallas_call | solution.py:872
  100.4 1.9 slice.13
  102.3 63.7 %shard_map.366 = (bf16[128,2048]{1,0:T(8,128)(2,1)}, bf16[8,256,2048]{2,1,0:T(8,128)(2,1)}, bf16[256,2048]{1,0:T(8,128)(2,1)}, f32[2,4,1024]{2,1,0:T(4,128)}, bf...) custom-call(bf16[128,2048]{1,0:T(8,128)(2,1)} %get-tuple-element.83., ...), custom_call_target="tpu_custom_call", output_to_operand_aliasing={{6}: (5, {}), {7}: (6, {})} | custom-call | tf_op jit(solution)/shard_map/pallas_call | solution.py:872
  166.0 66.8 %shard_map.367 = (f32[256,2048]{1,0:T(8,128)}, bf16[256,2048]{1,0:T(8,128)(2,1)}, bf16[4,1,704,512]{3,2,1,0:T(8,128)(2,1)}, bf16[4,1,704,512]{3,2,1,0:T(8,128)(2,1)}) custom-call(bf16[256,2048]{1,0:T(8,128)(2,1)} %get-tuple-element.87.refs_0_.refs_1_, bf16[4,256,512]{2,1,0:T(8,128)(2,1)} %bitcast.67, ...), custom_call_target="tpu_custom_call", output_to_operand_aliasing={{2}: (4, {})} | custom-call | tf_op jit(solution)/shard_map/pallas_call | solution.py:872
  232.8 50.3 %shard_map.368 = (bf16[8,256,2048]{2,1,0:T(8,128)(2,1)}, bf16[8,256,704]{2,1,0:T(8,128)(2,1)}, bf16[8,256,704]{2,1,0:T(8,128)(2,1)}, bf16[8,256,704]{2,1,0:T(8,128)(2,1)}) custom-call(bf16[256,2048]{1,0:T(8,128)(2,1)} %get-tuple-element.91.refs_0_, bf16[4,704,512]{2,1,0:T(8,128)(2,1)} %bitcast.62, bf16[4,704,512]{2,1,0:T(8,128)(2,1)} %bitcast.64), custom_call_target="tpu_custom_call" | custom-call | tf_op jit(solution)/shard_map/pallas_call | solution.py:872
  283.1 47.5 %shard_map.369 = (bf16[8,256,704]{2,1,0:T(8,128)(2,1)}, bf16[8,256,704]{2,1,0:T(8,128)(2,1)}, bf16[4,704,512]{2,1,0:T(8,128)(2,1)}, bf16[256,2048]{1,0:T(8,128)(2,1)}) custom-call(bf16[8,256,704]{2,1,0:T(8,128)(2,1)} %get-tuple-element.94.refs_0_, bf16[4,704,512]{2,1,0:T(8,128)(2,1)} %bitcast.70, bf16[8,256,704]{2,1,0:T(8,128)(2,1)} %get-tuple-element.96.refs_2_, ...), custom_call_target="tpu_custom_call" | custom-call | tf_op jit(solution)/shard_map/pallas_call | solution.py:872
  330.5 51.9 %shard_map.370 = (f32[256,2048]{1,0:T(8,128)}, bf16[4,704,512]{2,1,0:T(8,128)(2,1)}, bf16[4,704,512]{2,1,0:T(8,128)(2,1)}, bf16[256,2048]{1,0:T(8,128)(2,1)}, f3...) custom-call(bf16[8,256,704]{2,1,0:T(8,128)(2,1)} %get-tuple-element.101.refs_0_, ...), custom_call_target="tpu_custom_call" | custom-call | tf_op jit(solution)/shard_map/pallas_call | solution.py:872
  382.4 58.2 %shard_map.371 = (bf16[256,2048]{1,0:T(8,128)(2,1)}, bf16[4,256,512]{2,1,0:T(8,128)(2,1)}, bf16[2,704,512]{2,1,0:T(8,128)(2,1)}, bf16[2,704,512]{2,1,0:T(8,128)(2,1)}) custom-call(bf16[256,2048]{1,0:T(8,128)(2,1)} %get-tuple-element.105.refs_0_, bf16[256,2048]{1,0:T(8,128)(2,1)} %get-tuple-element.87.refs_0_.refs_1_, bf16[4,256,512]{2,1,0:T(8,128)(2,1)} %bitcast.68, ...), custom_call_target="tpu_custom_call" | custom-call | tf_op jit(solution)/shard_map/pallas_call | solution.py:872
  440.6 2.2 fusion.refs_12_
  442.7 49.8 %shard_map.372 = (bf16[256,2048]{1,0:T(8,128)(2,1)}, bf16[128,2048]{1,0:T(8,128)(2,1)}, bf16[2,256,512]{2,1,0:T(8,128)(2,1)}, bf16[2,704,512]{2,1,0:T(8,128)(2,1...) custom-call(bf16[256,2048]{1,0:T(8,128)(2,1)} %get-tuple-element.84.refs_2_.refs_0_, ...), custom_call_target="tpu_custom_call" | custom-call | tf_op jit(solution)/shard_map/pallas_call | solution.py:872
  492.5 2.2 fusion.1.refs_11_
  494.7 84.1 %shard_map.373 = (f32[256,2048]{1,0:T(8,128)}, bf16[512,256]{1,0:T(8,128)(2,1)}, f32[4,64,128]{2,1,0:T(8,128)}, f32[16,128]{1,0:T(8,128)}, bf16[2,704,512]{2,1,0...) custom-call(bf16[256,2048]{1,0:T(8,128)(2,1)} %get-tuple-element.116.refs_0_, ...), custom_call_target="tpu_custom_call" | custom-call | tf_op jit(solution)/shard_map/pallas_call | solution.py:872
  578.9 1.4 fusion.2
  580.3 1.7 collective-permute-start.2
  582.0 0.6 pad_add_fusion.place_ref
  583.3 0.6 maximum_divide_fusion.fix_ref
  584.0 0.1 fusion.3
  584.0 1.3 collective-permute-start.1
  585.4 1.3 add_subtract_fusion
  586.7 0.2 reshape.176
  586.9 0.2 copy.46
  587.1 0.2 reshape.177
  587.3 5.4 shard_map.377
  592.8 3.3 shard_map.374
  596.1 0.8 multiply_subtract_fusion
  596.9 0.7 copy-done.11
  597.6 3.6 shard_map.375
  601.2 0.9 copy-done.9
  602.1 9.9 %shard_map.376 = (f32[2,704,512]{2,1,0:T(8,128)}, f32[2,704,512]{2,1,0:T(8,128)}, f32[2,704,512]{2,1,0:T(8,128)}) custom-call(s32[2]{0:T(128)} %pad_add_fusion.place_ref, f32[2]{0:T(128)} %maximum_divide_fusion.fix_ref, f32[2,704,512]{2,1,0:T(8,128)} %bitcast.66, f32[2,704,512]{2,1,0:T(8,128)} %bitcast.71, f32[2,704,512]{2,1,0:T(8,128)} %bitcast.72, ...), custom_call_target="tpu_custom_call" | custom-call | tf_op jit(solution)/shard_map/pallas_call | solution.py:119
  612.0 1.0 copy.60
  613.0 1.0 copy-done.6
  613.9 1.3 copy.61
  (44 shorter events, 0.1 us)
Async XLA Ops:
  0.7 5.5 copy-start.4
  0.7 8.8 %collective-permute-start = (s32[1,2048]{1,0:T(1,128)}, s32[1,2048]{1,0:T(1,128)S(1)}, u32[]{:S(2)}, u32[]{:S(2)}) collective-permute-start(s32[1,2048]{1,0:T(1,128)} %param.24), channel_id=1, source_target_pairs={{0,8},{8,0},{1,9},{9,1},{2,10},{10,2},{3,11},{11,3},{4,12},{12,4},... | collective-permute-start | bytes 24584 | tf_op jit(solution)/shard_map/ppermute | solution.py:1617
  4.2 2.9 copy-start
  7.3 1.2 copy-start.16
  7.3 2.1 copy-start.15
  382.4 58.2 %copy-start.1 = (bf16[2,704,512]{2,1,0:T(8,128)(2,1)S(1)}, bf16[2,704,512]{2,1,0:T(8,128)(2,1)}, u32[]{:S(2)}) copy-start(bf16[2,704,512]{2,1,0:T(8,128)(2,1)} %get-tuple-element.107.refs_4_.refs_0_) | copy-start | bytes 4325380
  442.7 49.8 %copy-start.2 = (bf16[2,704,512]{2,1,0:T(8,128)(2,1)S(1)}, bf16[2,704,512]{2,1,0:T(8,128)(2,1)}, u32[]{:S(2)}) copy-start(bf16[2,704,512]{2,1,0:T(8,128)(2,1)} %get-tuple-element.114.refs_11_.refs_0_) | copy-start | bytes 4325380
  494.7 84.2 %copy-start.3 = (bf16[2,704,512]{2,1,0:T(8,128)(2,1)S(1)}, bf16[2,704,512]{2,1,0:T(8,128)(2,1)}, u32[]{:S(2)}) copy-start(bf16[2,704,512]{2,1,0:T(8,128)(2,1)} %get-tuple-element.123.refs_9_.refs_3_) | copy-start | bytes 4325380
  578.8 5.1 copy-start.5
  578.9 5.1 copy-start.7
  578.9 6.5 %copy-start.17 = (f32[2,64]{1,0:T(2,128)S(1)}, f32[2,64]{1,0:T(2,128)}, u32[]{:S(2)}) copy-start(f32[2,64]{1,0:T(2,128)} %param.43) | copy-start | bytes 1540
  578.9 6.5 %copy-start.18 = (f32[2,64]{1,0:T(2,128)S(1)}, f32[2,64]{1,0:T(2,128)}, u32[]{:S(2)}) copy-start(f32[2,64]{1,0:T(2,128)} %param.37) | copy-start | bytes 1540
  578.9 7.8 %copy-start.12 = (f32[4,64,128]{2,1,0:T(8,128)S(1)}, f32[4,64,128]{2,1,0:T(8,128)}, u32[]{:S(2)}) copy-start(f32[4,64,128]{2,1,0:T(8,128)} %get-tuple-element.129) | copy-start | bytes 393220
  580.3 20.9 %collective-permute-start.2 = (bf16[704,512]{1,0:T(8,128)(2,1)S(1)}, bf16[704,512]{1,0:T(8,128)(2,1)S(1)}, u32[]{:S(2)}, u32[]{:S(2)}) collective-permute-start(bf16[704,512]{1,0:T(8,128)(2,1)S(1)} %fusion.2), channel_id=1, source_target_pairs={{0,8},{12,4},{1,9},{13,5},{2,10},{14,6},{3,11},{15,7},{16,24},{28,... | collective-permute-start | bytes 2162696 | tf_op jit(solution)/shard_map/ppermute | solution.py:1909
  584.0 12.8 %collective-permute-start.1 = (bf16[256,512]{1,0:T(8,128)(2,1)S(1)}, bf16[256,512]{1,0:T(8,128)(2,1)S(1)}, u32[]{:S(2)}, u32[]{:S(2)}) collective-permute-start(bf16[256,512]{1,0:T(8,128)(2,1)S(1)} %fusion.3), channel_id=1, source_target_pairs={{0,8},{12,4},{1,9},{13,5},{2,10},{14,6},{3,11},{15,7},{16,24},{28,... | collective-permute-start | bytes 786440 | tf_op jit(solution)/shard_map/ppermute | solution.py:1909
  592.7 3.3 copy-start.10
  592.7 3.3 copy-start.13
  592.7 3.3 copy-start.14
  596.9 0.7 copy-start.11
  601.2 0.9 copy-start.9
  602.1 9.9 %copy-start.8 = (bf16[256,2048]{1,0:T(8,128)(2,1)S(1)}, bf16[256,2048]{1,0:T(8,128)(2,1)}, u32[]{:S(2)}) copy-start(bf16[256,2048]{1,0:T(8,128)(2,1)} %get-tuple-element.183) | copy-start | bytes 3145732
  612.0 2.0 copy-start.6
